TPU v7x, 32 devices: a whole 2x2x4 slice. The times are simulated.
32 devices in a mesh: section: 4 (over y, core), batch: 8 (over z, x).
Axes of the slice: x: 2, y: 2, z: 4, core: 2. Of those that a mesh axis runs over, the one named last changes fastest.
Arguments:
- stream_in: bfloat16 [16384, 768], P(('section', 'batch')), may hold values from -6 to 6
- history: bfloat16 [20, 16384, 768], P(None, ('section', 'batch')), may hold values from -6 to 6
- cotangent: bfloat16 [16384, 768], P(('section', 'batch')), may hold values from -6 to 6
- group: int32 [16], P('batch'), may hold values from 0 to 1, as said below
- params: float32 [4, 4723968], P('section', 'batch'), may hold values from -3 to 3, as said below
- first_moment: float32 [4, 4723968], P('section', 'batch'), may hold values from -0.6 to 0.6
- second_moment: float32 [4, 4723968], P('section', 'batch'), may hold values from 0.01 to 1
- mix_weights: float32 [43], replicated, may hold values from -0.3 to 1.2
- mix_first: float32 [43], replicated, may hold values from -0.6 to 0.6
- mix_second: float32 [43], replicated, may hold values from 7.68 to 768
Outputs:
- stream_out: bfloat16 [16384, 768], P(('section', 'batch'))
- stream_grad: float32 [16384, 768], P(('section', 'batch'))
- history_grad: bfloat16 [20, 16384, 768], P(None, ('section', 'batch'))
- params_grad: float32 [4, 4723968], P('section', 'batch')
- params_step: float32 [4, 4723968], P('section', 'batch')
- first_new: float32 [4, 4723968], P('section', 'batch')
- second_new: float32 [4, 4723968], P('section', 'batch')
- mix_grad: float32 [43], replicated
- mix_step: float32 [43], replicated
- mix_first_new: float32 [43], replicated
- mix_second_new: float32 [43], replicated
- branch_bias_grad: float32 [4, 768], P('section')
Inputs may be any that keep to these rules, and one draw needn't show every extreme that they name: 0: the micro-batch is one sequence of 1024 tokens; 1: it is 4 sequences of 256 tokens. Among the 2 micro-batches of each group at least one is of kind 0. `params`: the unused entries of each row are zero.
All inputs are finite; a program needn't handle non-finite values.
Results may differ from a plain program's by a relative error of at most 0.017.
Values may be sent and summed in bfloat16 or wider, within the bound.
A program may use at most 640 MiB of HBM per device.

v0:
```python
from functools import partial

import jax
import jax.numpy as jnp
from jax import lax
from jax.sharding import PartitionSpec as P

D = 768
HEADS = 12
HEAD = 64
FF = 3072
HIST = 20
SEQ_LONG = 1024
SEQ_SHORT = 256


eps_norm = 1e-05
rope_base = 10000.0
masked_score = -1e30
beta_one = 0.9
beta_two = 0.95
weight_decay = 0.1
adam_eps = 1e-08
adam_steps = 1000.0
float_type = jnp.float32
brain_type = jnp.bfloat16


def from_behind(array, axis, by):
    devices = lax.axis_size(axis)
    pairs = [(i, i + by) for i in range(devices) if 0 <= i + by < devices]
    return lax.ppermute(array, axis, pairs)


def attention_shapes():
    return [(D,), (D,), (D, 3 * D), (3 * D,), (D, D), (D,)]


def mlp_shapes():
    return [(D,), (D,), (D, FF), (FF,), (FF, D), (D,)]


def total_entries(shapes):
    entry_count = 0
    for shape_item in shapes:
        length = 1
        for extent in shape_item:
            length = length * extent
        entry_count = entry_count + length
    return entry_count


def slice_row(row_vector, shapes):
    segments = []
    offset = 0
    for shape_item in shapes:
        length = 1
        for extent in shape_item:
            length = length * extent
        segments.append(row_vector[offset : offset + length].reshape(shape_item))
        offset = offset + length
    return segments


def unpack(attention_row, mlp_row):
    return slice_row(attention_row, attention_shapes()) + slice_row(mlp_row, mlp_shapes())


def layer_norm(values, gain_row, bias_row):
    center = values - jnp.mean(values, axis=-1, keepdims=True)
    spread = jnp.mean(center * center, axis=-1, keepdims=True)
    return center * lax.rsqrt(spread + eps_norm) * gain_row + bias_row


def rotate(tensor, position):
    half_width = tensor.shape[-1] // 2
    inverse = rope_base ** (-jnp.arange(half_width, dtype=jnp.float32) / half_width)
    angles = position.astype(jnp.float32)[:, None] * inverse[None, :]
    cosine = jnp.cos(angles)[:, None, :]
    sine_value = jnp.sin(angles)[:, None, :]
    first_half = tensor[..., :half_width]
    second_half = tensor[..., half_width:]
    return jnp.concatenate(
        [
            first_half * cosine - second_half * sine_value,
            first_half * sine_value + second_half * cosine,
        ],
        axis=-1,
    )


def positions(group_kind):
    row_index = jnp.arange(SEQ_LONG, dtype=jnp.int32)
    position = jnp.where(group_kind == 1, row_index % SEQ_SHORT, row_index)
    sequence = jnp.where(group_kind == 1, row_index // SEQ_SHORT, jnp.zeros_like(row_index))
    return (position, sequence)


def weighted(coefficients, history_stack):
    weighted_sum = jnp.zeros(history_stack.shape[1:], float_type)
    for entry_index in range(history_stack.shape[0]):
        weighted_sum = weighted_sum + coefficients[entry_index] * history_stack[entry_index].astype(
            float_type
        )
    return weighted_sum


def to_slots(array, section_count, micro_count):
    span = array.shape[0] // (section_count * micro_count)
    shaped = array.reshape(section_count, micro_count, span, array.shape[-1])
    return shaped.transpose(1, 0, 2, 3).reshape(micro_count, section_count * span, array.shape[-1])


def to_owners(array, section_count):
    micro_count = array.shape[0]
    span = array.shape[1] // section_count
    shaped = array.reshape(micro_count, section_count, span, array.shape[-1])
    return shaped.transpose(1, 0, 2, 3).reshape(section_count * micro_count * span, array.shape[-1])


def store_slot(store, leaf, slot_index, active):
    return lax.dynamic_update_index_in_dim(
        store, jnp.where(active, leaf, store[slot_index]), slot_index, 0
    )


def select_branch(section_kinds, parity, attention_case, mlp_case, operands):
    if section_kinds == (0,):
        return attention_case(operands)
    if section_kinds == (1,):
        return mlp_case(operands)
    return lax.cond(parity == 0, attention_case, mlp_case, operands)


def empty_saved(row_count):
    return (
        jnp.zeros((row_count, D), brain_type),
        jnp.zeros((row_count, 3 * D), brain_type),
        jnp.zeros((HEADS, row_count), float_type),
        jnp.zeros((row_count, D), brain_type),
        jnp.zeros((row_count, FF), float_type),
        jnp.zeros((row_count, FF), brain_type),
        jnp.zeros((row_count, D), float_type),
    )


def score_block(queries, keys, sequence, block_start, block_rows):
    key_count = block_start + block_rows
    query_part = queries[block_start:key_count]
    scores = jnp.einsum(
        "qhe,khe->hqk", query_part, keys[:key_count], preferred_element_type=float_type
    )
    row_index = block_start + jnp.arange(block_rows)
    column_index = jnp.arange(key_count)
    row_sequence = sequence[block_start:key_count]
    allowed = (row_sequence[:, None] == sequence[None, :key_count]) & (
        column_index[None, :] <= row_index[:, None]
    )
    return jnp.where(allowed[None], scores, masked_score)


def attention_inputs(weight_parts, stream, position):
    row_count = stream.shape[0]
    normed = layer_norm(
        stream, weight_parts[0].astype(float_type), weight_parts[1].astype(float_type)
    )
    normed_low = normed.astype(brain_type)
    joint = jnp.dot(normed_low, weight_parts[2], preferred_element_type=float_type) + weight_parts[
        3
    ].astype(float_type)
    joint = joint.reshape(row_count, 3, HEADS, HEAD)
    queries = (rotate(joint[:, 0], position) * HEAD ** (-0.5)).astype(brain_type)
    keys = rotate(joint[:, 1], position).astype(brain_type)
    values = joint[:, 2].astype(brain_type)
    return (normed_low, queries, keys, values)


def attention_core(queries, keys, values, sequence):
    row_count = queries.shape[0]
    block_rows = min(512, row_count)
    outputs = []
    log_parts = []
    for block_start in range(0, row_count, block_rows):
        key_count = block_start + block_rows
        scores = score_block(queries, keys, sequence, block_start, block_rows)
        top_score = jnp.max(scores, axis=-1, keepdims=True)
        exp_scores = jnp.exp(scores - top_score)
        row_total = jnp.sum(exp_scores, axis=-1, keepdims=True)
        prob_rows = (exp_scores / row_total).astype(brain_type)
        outputs.append(
            jnp.einsum(
                "hqk,khe->qhe", prob_rows, values[:key_count], preferred_element_type=float_type
            )
        )
        log_parts.append((top_score + jnp.log(row_total))[..., 0])
    return (jnp.concatenate(outputs, axis=0), jnp.concatenate(log_parts, axis=1))


def attention_forward(weight_parts, stream, position, sequence):
    row_count = stream.shape[0]
    normed_low, queries, keys, values = attention_inputs(weight_parts, stream, position)
    mixed, log_totals = attention_core(queries, keys, values, sequence)
    mixed_low = mixed.reshape(row_count, -1).astype(brain_type)
    state_rows = (
        stream
        + jnp.dot(mixed_low, weight_parts[4], preferred_element_type=float_type)
        + weight_parts[5].astype(float_type)
    )
    joint_low = jnp.stack([queries, keys, values], axis=1).reshape(row_count, 3 * D)
    return (state_rows, normed_low, joint_low, log_totals, mixed_low)


def attention_backward(weight_parts, stream, kept_arrays, position, sequence, grad_out):
    row_count = stream.shape[0]
    joint_parts = kept_arrays[1].reshape(row_count, 3, HEADS, HEAD)
    queries = joint_parts[:, 0]
    keys = joint_parts[:, 1]
    values = joint_parts[:, 2]
    log_totals = kept_arrays[2]
    grad_branch = grad_out.astype(brain_type)
    grad_mixed = jnp.einsum(
        "tf,df->td", grad_branch, weight_parts[4], preferred_element_type=float_type
    )
    grad_mixed = grad_mixed.reshape(queries.shape).astype(brain_type)
    block_rows = min(512, row_count)
    query_grads = []
    grad_keys = jnp.zeros(keys.shape, float_type)
    grad_values = jnp.zeros(values.shape, float_type)
    for block_start in range(0, row_count, block_rows):
        key_count = block_start + block_rows
        scores = score_block(queries, keys, sequence, block_start, block_rows)
        prob_rows = jnp.exp(scores - log_totals[:, block_start:key_count][..., None])
        grad_part = grad_mixed[block_start:key_count]
        query_part = queries[block_start:key_count]
        grad_probs = jnp.einsum(
            "qhe,khe->hqk", grad_part, values[:key_count], preferred_element_type=float_type
        )
        inner_sum = jnp.sum(prob_rows * grad_probs, axis=-1, keepdims=True)
        grad_scores = (prob_rows * (grad_probs - inner_sum)).astype(brain_type)
        query_grads.append(
            jnp.einsum(
                "hqk,khe->qhe", grad_scores, keys[:key_count], preferred_element_type=float_type
            )
        )
        grad_keys = grad_keys.at[:key_count].add(
            jnp.einsum("hqk,qhe->khe", grad_scores, query_part, preferred_element_type=float_type)
        )
        grad_values = grad_values.at[:key_count].add(
            jnp.einsum(
                "hqk,qhe->khe",
                prob_rows.astype(brain_type),
                grad_part,
                preferred_element_type=float_type,
            )
        )
    grad_queries = jnp.concatenate(query_grads, axis=0)
    zero_joint = jnp.zeros(queries.shape, float_type)
    unused, turn_query = jax.vjp(
        lambda tensor_in: rotate(tensor_in, position) * HEAD ** (-0.5), zero_joint
    )
    unused, turn_key = jax.vjp(lambda tensor_in: rotate(tensor_in, position), zero_joint)
    grad_joint = jnp.stack(
        [turn_query(grad_queries)[0], turn_key(grad_keys)[0], grad_values], axis=1
    )
    grad_joint = grad_joint.reshape(row_count, -1).astype(brain_type)
    grad_normed = jnp.einsum(
        "tf,df->td", grad_joint, weight_parts[2], preferred_element_type=float_type
    )
    unused, norm_pull = jax.vjp(
        layer_norm, stream, weight_parts[0].astype(float_type), weight_parts[1].astype(float_type)
    )
    grad_norm_stream, grad_gain, grad_bias = norm_pull(grad_normed)
    return (grad_out + grad_norm_stream, jnp.stack([grad_gain, grad_bias]), grad_branch, grad_joint)


def mlp_hidden(weight_parts, stream):
    normed = layer_norm(
        stream, weight_parts[6].astype(float_type), weight_parts[7].astype(float_type)
    )
    normed_low = normed.astype(brain_type)
    hidden = jnp.dot(normed_low, weight_parts[8], preferred_element_type=float_type) + weight_parts[
        9
    ].astype(float_type)
    active_low = jax.nn.gelu(hidden, approximate=False).astype(brain_type)
    layer_out = (
        stream
        + jnp.dot(active_low, weight_parts[10], preferred_element_type=float_type)
        + weight_parts[11].astype(float_type)
    )
    return (normed_low, hidden, active_low, layer_out)


def mlp_backward(weight_parts, stream, kept_arrays, grad_out):
    hidden = kept_arrays[4]
    grad_branch = grad_out.astype(brain_type)
    grad_active = jnp.einsum(
        "td,fd->tf", grad_branch, weight_parts[10], preferred_element_type=float_type
    )
    unused, gelu_pull = jax.vjp(partial(jax.nn.gelu, approximate=False), hidden)
    grad_hidden = gelu_pull(grad_active)[0].astype(brain_type)
    grad_normed = jnp.einsum(
        "tf,df->td", grad_hidden, weight_parts[8], preferred_element_type=float_type
    )
    unused, norm_pull = jax.vjp(
        layer_norm, stream, weight_parts[6].astype(float_type), weight_parts[7].astype(float_type)
    )
    grad_norm_stream, grad_gain, grad_bias = norm_pull(grad_normed)
    return (
        grad_out + grad_norm_stream,
        jnp.stack([grad_gain, grad_bias]),
        grad_branch,
        grad_hidden,
    )


def mix_factors(mix_weights, layer_index):
    own_weight = jnp.where(layer_index == 0, mix_weights[HIST], mix_weights[2 * HIST + 2])
    carry_weight = jnp.where(layer_index == 0, 0.0, mix_weights[2 * HIST + 1])
    return (own_weight, carry_weight)


def section_forward(
    section_kinds,
    parity,
    weight_parts,
    layer_index,
    mix_weights,
    act_in,
    carry_in,
    past_rows,
    position,
    sequence,
):
    empty_kept = empty_saved(act_in.shape[0])

    def attention_case(operands):
        act_value, carry_value = operands
        state_rows, normed_low, joint_low, log_totals, mixed_low = attention_forward(
            weight_parts, act_value.astype(float_type), position, sequence
        )
        kept_arrays = (
            normed_low,
            joint_low,
            log_totals,
            mixed_low,
            empty_kept[4],
            empty_kept[5],
            empty_kept[6],
        )
        return (state_rows.astype(brain_type), carry_value, state_rows, kept_arrays)

    def mlp_case(operands):
        act_value, carry_value = operands
        normed_low, hidden, active_low, layer_out = mlp_hidden(
            weight_parts, act_value.astype(float_type)
        )
        own_weight, carry_weight = mix_factors(mix_weights, layer_index)
        averaged = (
            past_rows + own_weight * layer_out + carry_weight * carry_value.astype(float_type)
        )
        carry_out = jnp.where(layer_index == 0, layer_out.astype(brain_type), carry_value)
        kept_arrays = (
            normed_low,
            empty_kept[1],
            empty_kept[2],
            empty_kept[3],
            hidden,
            active_low,
            layer_out,
        )
        return (averaged.astype(brain_type), carry_out, averaged, kept_arrays)

    return select_branch(section_kinds, parity, attention_case, mlp_case, (act_in, carry_in))


def section_backward(
    section_kinds,
    parity,
    weight_parts,
    layer_index,
    mix_weights,
    act_in,
    carry_in,
    kept_arrays,
    grad_act,
    grad_carry,
    position,
    sequence,
):
    mix_count = mix_weights.shape[0]
    wide_count = max(FF, 3 * D)

    def attention_case(operands):
        act_value, carry_value, grad_value, grad_carried = operands
        grad_stream, norm_part, grad_branch, grad_joint = attention_backward(
            weight_parts, act_value.astype(float_type), kept_arrays, position, sequence, grad_value
        )
        grad_wide = jnp.pad(grad_joint, ((0, 0), (0, wide_count - 3 * D)))
        return (
            grad_stream,
            grad_carried,
            norm_part,
            jnp.zeros((mix_count,), float_type),
            grad_stream,
            grad_branch,
            grad_wide,
        )

    def mlp_case(operands):
        act_value, carry_value, grad_value, grad_carried = operands
        stream = act_value.astype(float_type)
        layer_out = kept_arrays[6]
        own_weight, carry_weight = mix_factors(mix_weights, layer_index)
        first_layer = layer_index == 0
        grad_layer = own_weight * grad_value + jnp.where(
            first_layer, grad_carried.astype(float_type), 0.0
        )
        grad_carry_in = (carry_weight * grad_value).astype(brain_type)
        own_sum = jnp.sum(grad_value * layer_out)
        carry_sum = jnp.where(
            first_layer, 0.0, jnp.sum(grad_value * carry_value.astype(float_type))
        )
        own_slot = jnp.where(first_layer, HIST, 2 * HIST + 2)
        entry_index = jnp.arange(mix_count)
        mix_part = jnp.where(entry_index == own_slot, own_sum, 0.0) + jnp.where(
            entry_index == 2 * HIST + 1, carry_sum, 0.0
        )
        grad_stream, norm_part, grad_branch, grad_hidden = mlp_backward(
            weight_parts, stream, kept_arrays, grad_layer
        )
        return (
            grad_stream,
            grad_carry_in,
            norm_part,
            mix_part,
            grad_value,
            grad_branch,
            grad_hidden,
        )

    return select_branch(
        section_kinds, parity, attention_case, mlp_case, (act_in, carry_in, grad_act, grad_carry)
    )


def weight_gradients(parity, saved, branch_store, wide_store, norm_total, row_length, branch_bias):
    all_rows = branch_store.shape[0] * branch_store.shape[1]
    branch_rows = branch_store.reshape(all_rows, D)
    normed_rows = saved[0].reshape(all_rows, D)
    wide_rows = wide_store.reshape(all_rows, -1)

    def attention_case(operand):
        joint_rows = wide_rows[:, : 3 * D]
        mixed_rows = saved[3].reshape(all_rows, D)
        grad_joint_weight = jnp.einsum(
            "td,tf->df", normed_rows, joint_rows, preferred_element_type=float_type
        )
        grad_joint_bias = jnp.sum(joint_rows.astype(float_type), axis=0)
        grad_out_weight = jnp.einsum(
            "td,tf->df", mixed_rows, branch_rows, preferred_element_type=float_type
        )
        spare_count = row_length - total_entries(attention_shapes())
        return jnp.concatenate(
            [
                norm_total[0],
                norm_total[1],
                grad_joint_weight.reshape(-1),
                grad_joint_bias,
                grad_out_weight.reshape(-1),
                branch_bias,
                jnp.zeros((spare_count,), float_type),
            ]
        )

    def mlp_case(operand):
        active_rows = saved[5].reshape(all_rows, FF)
        grad_up_weight = jnp.einsum(
            "td,tf->df", normed_rows, wide_rows, preferred_element_type=float_type
        )
        grad_up_bias = jnp.sum(wide_rows.astype(float_type), axis=0)
        grad_down_weight = jnp.einsum(
            "tf,td->fd", active_rows, branch_rows, preferred_element_type=float_type
        )
        spare_count = row_length - total_entries(mlp_shapes())
        return jnp.concatenate(
            [
                norm_total[0],
                norm_total[1],
                grad_up_weight.reshape(-1),
                grad_up_bias,
                grad_down_weight.reshape(-1),
                branch_bias,
                jnp.zeros((spare_count,), float_type),
            ]
        )

    return lax.cond(parity == 0, attention_case, mlp_case, jnp.zeros((), float_type))


def adamw(param, grad, first, second, decay):
    first_new = beta_one * first + (1.0 - beta_one) * grad
    second_new = beta_two * second + (1.0 - beta_two) * grad * grad
    first_hat = first_new / (1.0 - beta_one**adam_steps)
    second_hat = second_new / (1.0 - beta_two**adam_steps)
    direction = first_hat / (jnp.sqrt(second_hat) + adam_eps) + decay * param
    return (direction, first_new, second_new)


def local(
    stream_in,
    history,
    cotangent,
    group,
    params,
    first_moment,
    second_moment,
    mix_weights,
    mix_first,
    mix_second,
):
    section_count = lax.axis_size("section")
    batch_count = lax.axis_size("batch")
    section_index = lax.axis_index("section")
    parity = section_index % 2
    layer_index = section_index // 2
    micro_count = group.shape[0]
    local_rows = stream_in.shape[0]
    model_width = stream_in.shape[1]
    row_count = section_count * local_rows // micro_count
    total_tokens = local_rows * section_count * batch_count
    grad_scale = float(total_tokens) ** (-0.5)
    mix_count = mix_weights.shape[0]
    row_length = params.shape[1] * batch_count
    wide_count = max(FF, 3 * D)
    own_low = params.astype(brain_type).reshape(-1)
    weight_row = lax.all_gather(own_low, "batch", axis=0, tiled=True)
    weight_parts = unpack(weight_row, weight_row)
    stream_all, cotangent_all = (
        lax.all_gather(stream_in, "section", axis=0, tiled=True),
        lax.all_gather(cotangent, "section", axis=0, tiled=True),
    )
    stream_slots = to_slots(stream_all, section_count, micro_count)
    cotangent_slots = to_slots(cotangent_all, section_count, micro_count)
    past_one_weights = mix_weights[:HIST]
    past_two_weights = mix_weights[HIST + 1 : 2 * HIST + 1]
    history_stack = lax.all_gather(history, "section", axis=1, tiled=True)
    past_one = weighted(past_one_weights, history_stack)
    past_two = weighted(past_two_weights, history_stack)
    past_slots = to_slots(
        jnp.where(layer_index == 0, past_one, past_two), section_count, micro_count
    )
    zero_rows = jnp.zeros((row_count, model_width), brain_type)
    message = (zero_rows, zero_rows)
    saved = tuple(
        (jnp.zeros((micro_count,) + leaf.shape, leaf.dtype) for leaf in empty_saved(row_count))
    )
    saved_act = jnp.zeros((micro_count, row_count, model_width), brain_type)
    saved_carry = jnp.zeros((micro_count, row_count, model_width), brain_type)
    results = jnp.zeros((micro_count, row_count, model_width), float_type)
    tick_count = micro_count + section_count - 1
    for time_step in range(tick_count):
        section_kinds = tuple(
            sorted(
                set(
                    (
                        s_value % 2
                        for s_value in range(section_count)
                        if 0 <= time_step - s_value < micro_count
                    )
                )
            )
        )
        micro_index = time_step - section_index
        active = (micro_index >= 0) & (micro_index < micro_count)
        slot_index = jnp.clip(micro_index, 0, micro_count - 1)
        fresh_rows = stream_slots[slot_index]
        act_in = jnp.where(section_index == 0, fresh_rows, message[0])
        carry_in = message[1]
        position, sequence = positions(group[slot_index])
        past_rows = past_slots[slot_index]
        act_out, carry_out, result_rows, kept_arrays = section_forward(
            section_kinds,
            parity,
            weight_parts,
            layer_index,
            mix_weights,
            act_in,
            carry_in,
            past_rows,
            position,
            sequence,
        )
        saved = tuple(
            (store_slot(store, leaf, slot_index, active) for store, leaf in zip(saved, kept_arrays))
        )
        saved_act = store_slot(saved_act, act_in, slot_index, active)
        saved_carry = store_slot(saved_carry, carry_in, slot_index, active)
        results = store_slot(results, result_rows, slot_index, active)
        if time_step + 1 < tick_count:
            message = from_behind((act_out, carry_out), "section", 1)
    norm_total = jnp.zeros((2, model_width), float_type)
    mix_total = jnp.zeros((mix_count,), float_type)
    keep_store = jnp.zeros((micro_count, row_count, model_width), float_type)
    branch_store = jnp.zeros((micro_count, row_count, model_width), brain_type)
    wide_store = jnp.zeros((micro_count, row_count, wide_count), brain_type)
    message = (zero_rows, zero_rows)
    for time_step in range(tick_count):
        section_kinds = tuple(
            sorted(
                set(
                    (
                        s_value % 2
                        for s_value in range(section_count)
                        if 0 <= time_step - (section_count - 1 - s_value) < micro_count
                    )
                )
            )
        )
        micro_index = time_step - (section_count - 1 - section_index)
        active = (micro_index >= 0) & (micro_index < micro_count)
        slot_index = jnp.clip(micro_index, 0, micro_count - 1)
        kept_arrays = tuple((store[slot_index] for store in saved))
        act_in = saved_act[slot_index]
        carry_in = saved_carry[slot_index]
        position, sequence = positions(group[slot_index])
        outer_grad = cotangent_slots[slot_index].astype(float_type) * grad_scale
        grad_act = jnp.where(
            section_index == section_count - 1, outer_grad, message[0].astype(float_type)
        )
        grad_stream, grad_carry_in, norm_part, mix_part, keep_rows, grad_branch, grad_wide = (
            section_backward(
                section_kinds,
                parity,
                weight_parts,
                layer_index,
                mix_weights,
                act_in,
                carry_in,
                kept_arrays,
                grad_act,
                message[1],
                position,
                sequence,
            )
        )
        norm_total = norm_total + jnp.where(active, norm_part, 0.0)
        mix_total = mix_total + jnp.where(active, mix_part, 0.0)
        keep_store = store_slot(keep_store, keep_rows, slot_index, active)
        branch_store = store_slot(branch_store, grad_branch, slot_index, active)
        wide_store = store_slot(wide_store, grad_wide, slot_index, active)
        if time_step + 1 < tick_count:
            message = from_behind((grad_stream.astype(brain_type), grad_carry_in), "section", -1)
    branch_bias = jnp.sum(branch_store.reshape(-1, model_width).astype(float_type), axis=0)
    flat_total = weight_gradients(
        parity, saved, branch_store, wide_store, norm_total, row_length, branch_bias
    )
    sent_out = jnp.where(section_index == section_count - 1, to_owners(results, section_count), 0.0)
    sent_input_grad = jnp.where(section_index == 0, to_owners(keep_store, section_count), 0.0)
    sent_average_grad = jnp.where(section_index == 1, to_owners(keep_store, section_count), 0.0)
    stream_sum, input_sum, average_sum = (
        lax.psum_scatter(
            sent_out.astype(jnp.bfloat16), "section", scatter_dimension=0, tiled=True
        ).astype(jnp.float32),
        lax.psum_scatter(
            sent_input_grad.astype(jnp.bfloat16), "section", scatter_dimension=0, tiled=True
        ).astype(jnp.float32),
        lax.psum_scatter(
            sent_average_grad.astype(jnp.bfloat16), "section", scatter_dimension=0, tiled=True
        ).astype(jnp.float32),
    )
    outer_own = cotangent.astype(float_type) * grad_scale
    history_grad = (
        past_one_weights[:, None, None] * average_sum[None]
        + past_two_weights[:, None, None] * outer_own[None]
    ).astype(brain_type)
    own_one = jnp.einsum("td,jtd->j", average_sum, history, preferred_element_type=float_type)
    own_two = jnp.einsum("td,jtd->j", outer_own, history, preferred_element_type=float_type)
    own_mix = jnp.concatenate(
        [own_one, jnp.zeros((1,), float_type), own_two, jnp.zeros((2,), float_type)]
    )
    mix_total = mix_total + own_mix
    mix_rows = jnp.broadcast_to(mix_total, (batch_count, mix_count))
    bias_rows = jnp.broadcast_to(branch_bias, (batch_count, model_width))
    grad_flat, mix_sum, bias_sum = (
        lax.psum_scatter(flat_total, "batch", scatter_dimension=0, tiled=True),
        lax.psum_scatter(mix_rows, "batch", scatter_dimension=0, tiled=True),
        lax.psum_scatter(bias_rows, "batch", scatter_dimension=0, tiled=True),
    )
    mix_grad = lax.psum(mix_sum[0], "section")
    grad_shard = grad_flat.reshape(params.shape)
    params_step, first_new, second_new = adamw(
        params, grad_shard, first_moment, second_moment, weight_decay
    )
    mix_step, mix_first_new, mix_second_new = adamw(
        mix_weights, mix_grad, mix_first, mix_second, 0.0
    )
    return (
        stream_sum.astype(brain_type),
        input_sum,
        history_grad,
        grad_shard,
        params_step,
        first_new,
        second_new,
        mix_grad,
        mix_step,
        mix_first_new,
        mix_second_new,
        bias_sum,
    )


def solution(mesh):
    placed = (
        P(("section", "batch"), None),
        P(None, ("section", "batch"), None),
        P(("section", "batch"), None),
        P("batch"),
        P("section", "batch"),
        P("section", "batch"),
        P("section", "batch"),
        P(),
        P(),
        P(),
    )
    return jax.shard_map(
        local,
        mesh=mesh,
        in_specs=placed,
        out_specs=(
            P(("section", "batch"), None),
            P(("section", "batch"), None),
            P(None, ("section", "batch"), None),
            P("section", "batch"),
            P("section", "batch"),
            P("section", "batch"),
            P("section", "batch"),
            P(),
            P(),
            P(),
            P(),
            P("section", None),
        ),
        check_vma=False,
    )
```

profile of v0, /device:TPU:0, one launch (start us, length us, event | category | flops | bytes accessed | tf_op | source)
XLA Modules:
  0.0 3356.4 jit_solution(5499693580763665499)
XLA Ops:
  11.6 23.9 convert_reduce_fusion.19
  39.6 19.0 dynamic-update-slice.46
  85.4 20.5 broadcast_in_dim.931
  115.9 13.6 constant_dynamic-slice_fusion.48
  147.8 212.7 %all-reduce.36.cloned.1.call-done = bf16[4723968]{0:T(1024)(128)(2,1)} async-done(((bf16[4723968]{0:T(1024)(128)(2,1)}), bf16[4723968]{0:T(1024)(128)(2,1)}) %all-reduce.36.cloned.1.call-update) | async-done | bytes 9447952
  360.5 113.8 %while.24 = (u32[]{:T(128)}, bf16[4723968]{0:T(1024)(128)(2,1)}, bf16[1,1,4723968]{2,1,0:T(2,128)(2,1)}) while((u32[]{:T(128)}, bf16[4723968]{0:T(1024)(128)(2,1)}, bf16[1,1,4723968]{2,1,0:T(2,128)(2,1)}) %tuple.572), condition=%cond, body=%body | while | flops 9 | bytes 37791892
  365.7 108.6 %reshape_dynamic-update-slice_fusion = bf16[1,1,4723968]{2,1,0:T(2,128)(2,1)} fusion(bf16[1,1,4723968]{2,1,0:T(2,128)(2,1)} %get-tuple-element.3317, u32[]{:T(128)S(6)} %multiply.486, u32[]{:T(128)S(6)} %multiply.487, bf16[4723968]{0:T(1024)(128)(2,1)S(1)} %dynamic-slice.115), kind=kLoop, calls=%fused_computation.1336 | loop fusion | bytes 18895880
  476.2 72.2 %slice_reduce_fusion.6 = bf16[1769472]{0:T(1024)(128)(2,1)} fusion(bf16[1,4723968]{1,0:T(2,128)(2,1)} %bitcast.1374), kind=kLoop, calls=%fused_computation.879 | loop fusion | bytes 7077888 | tf_op jit(solution)/shard_map/slice | solution.py:60
  580.3 25.0 slice_reduce_fusion.7
  618.4 13.8 select_reduce_fusion.6
  648.0 13.0 fusion.555
  669.0 104.9 %slice_reduce_fusion.4 = (bf16[2359296]{0:T(1024)(128)(2,1)}, bf16[2359296]{0:T(1024)(128)(2,1)}) fusion(bf16[1,4723968]{1,0:T(2,128)(2,1)} %bitcast.1377), kind=kLoop, calls=%fused_computation.835 | loop fusion | bytes 18874368 | tf_op jit(solution)/shard_map/slice | solution.py:60
  834.6 28.0 convert_multiply_fusion.14
  862.6 28.5 fusion.477
  891.2 28.5 fusion.463
  919.8 28.5 fusion.481
  948.3 104.4 %conditional.20 = (f32[1024,768]{1,0:T(8,128)S(1)}, bf16[1024,768]{1,0:T(8,128)(2,1)}, bf16[1024,2304]{1,0:T(8,128)(2,1)}, f32[12,1024]{1,0:T(8,128)S(1)}, bf16[...) conditional(s32[]{:T(128)} %convert_element_type.1294, ...), branch_computations={%region_6.9_spmd, %region_9.16_spmd} | conditional | flops 9888602112 | bytes 340647712
  1000.6 13.5 fusion.41
  1096.7 15.0 bitcast_dynamic-update-slice_fusion.10
  1136.5 100.2 %conditional.21 = (f32[1024,768]{1,0:T(8,128)S(1)}, bf16[1024,768]{1,0:T(8,128)(2,1)}, bf16[1024,2304]{1,0:T(8,128)(2,1)}, f32[12,1024]{1,0:T(8,128)S(1)}, bf16[...) conditional(s32[]{:T(128)} %convert_element_type.1294, ...), branch_computations={%region_16.19_spmd, %region_19.26_spmd} | conditional | flops 9888602112 | bytes 346939200
  1189.0 13.5 fusion.97
  1319.1 99.4 %conditional.22 = (f32[1024,768]{1,0:T(8,128)S(1)}, bf16[1024,768]{1,0:T(8,128)(2,1)}, bf16[1024,2304]{1,0:T(8,128)(2,1)}, f32[12,1024]{1,0:T(8,128)S(1)}, bf16[...) conditional(s32[]{:T(128)} %convert_element_type.1294, ...), branch_computations={%region_26.29_spmd, %region_29.36_spmd} | conditional | flops 9888602112 | bytes 359522176
  1372.1 13.7 fusion.153
  1482.8 36.7 %fusion.412 = (bf16[1024,3072]{1,0:T(8,128)(2,1)}, f32[1024,3072]{1,0:T(8,128)S(1)}) fusion(f32[3072]{0:T(1024)S(1)} %copy-done.245, bf16[768,3072]{1,0:T(8,128)(2,1)} %reshape.3118, bf16[1024,768]{1,0:T(8,128)(2,1)S(1)} %get-tuple-element.3021, f32[768]{0:T(1024)S(1)} %copy-done.265, f32[768]{0:T(1024)S(1)} %copy-done.231, f32[1024]{0:T(1024)S(1)} %add_rsqrt_fusion.6, ...), kind=kOutput, calls=%fused_computation.770 | convolution fusion | flops 5044174848 | bytes 25192448 | tf_op jit(solution)/shard_map/dot_general | solution.py:281
  1532.1 36.9 %bitcast_dynamic-update-slice_fusion.14 = (bf16[2,1024,3072]{2,1,0:T(8,128)(2,1)}, bf16[1024,3072]{1,0:T(8,128)(2,1)S(1)}) fusion(bf16[2,1024,3072]{2,1,0:T(8,128)(2,1)} %broadcast.4228, s32[]{:T(128)S(6)} %min.36, pred[]{:T(512)S(6)} %and.357, bf16[3072,768]{1,0:T(8,128)(2,1)} %slice.1541, f32[]{:T(128)S(6)} %select_n.1411, pred[]{:T(512)S(6)} %eq.536, ...), kind=kOutput, calls=%fused_computation.918 | convolution fusion | flops 5065408512 | bytes 31459840 | tf_op jit(solution)/shard_map/td,fd->tf/dot_general | solution.py:296
  1635.1 159.4 %conditional.16 = (bf16[1024,768]{1,0:T(8,128)(2,1)}, f32[2,768]{1,0:T(2,128)S(1)}, f32[43]{0:T(128)S(1)}, f32[1024,768]{1,0:T(8,128)}, f32[1024,768]{1,0:T(8,12...) conditional(s32[]{:T(128)} %convert_element_type.1294, ...), branch_computations={%region_43.51_spmd, %region_51.60_spmd} | conditional | flops 11025808384 | bytes 686651008
  1667.6 12.5 fusion.233
  1680.1 17.7 multiply_reduce_fusion
  1697.8 22.0 multiply_convert_fusion.1
  1820.8 159.3 %conditional.17 = (bf16[1024,768]{1,0:T(8,128)(2,1)}, f32[2,768]{1,0:T(2,128)S(1)}, f32[43]{0:T(128)S(1)}, f32[1024,768]{1,0:T(8,128)}, f32[1024,768]{1,0:T(8,12...) conditional(s32[]{:T(128)} %convert_element_type.1294, ...), branch_computations={%region_61.69_spmd, %region_69.78_spmd} | conditional | flops 11025808384 | bytes 686651008
  1865.7 18.0 multiply_reduce_fusion.2
  1883.6 22.0 multiply_convert_fusion.4
  1989.5 13.5 fusion.558
  2009.7 153.6 %conditional.18 = (f32[2,768]{1,0:T(2,128)S(1)}, f32[43]{0:T(128)S(1)}, f32[1024,768]{1,0:T(8,128)}, f32[1024,768]{1,0:T(8,128)}, bf16[1024,3072]{1,0:T(8,128)(2...) conditional(s32[]{:T(128)} %convert_element_type.1294, (bf16[1024,768]{1,0:T(8,128)(2,1)}, ...), branch_computations={%region_79.87_spmd, %region_87.96_spmd} | conditional | flops 11025808384 | bytes 676689280
  2053.2 19.7 multiply_reduce_fusion.4
  2072.9 21.8 multiply_convert_fusion.6
  2213.0 17.6 multiply_reduce_fusion.6
  2230.6 13.1 fusion.525
  2243.7 16.7 multiply_convert_fusion.8
  2417.3 224.2 %conditional.19 = (f32[4723968]{0:T(1024)}) conditional(s32[]{:T(128)} %convert_element_type.1294, (f32[2,768]{1,0:T(2,128)S(1)}, bf16[2048,768]{1,0:T(8,128)(2,1)S(1)}, bf16[2048,3072]{1,0:T(8,128)(2,1)}, pred[]{:T(512)}, bf16[]{:T(256)}, /*index=5*/s32[]{:T(128)}, bf16[1024,3072]{1,0:T(8,128)(2,1)}, pred[]{:T(512)}, s32[]{:T(128)}, ...), branch_computations={%region_110.112_spmd.clone, %region_112.114_spmd.clone} | conditional | flops 19352514560 | bytes 283191296 | solution.py:497
  2428.6 12.7 fusion.402
  2449.3 60.7 %dynamic-update-slice.55 = f32[4723968]{0:T(1024)} dynamic-update-slice(f32[4723968]{0:T(1024)} %constant_dynamic-update-slice_fusion.6, f32[1769472]{0:T(1024)} %reshape.3199, s32[]{} %constant.2617) | dynamic-update-slice | bytes 14155780 | tf_op jit(solution)/shard_map/cond
  2535.3 20.3 dynamic-update-slice.57
  2560.7 80.4 %dynamic-update-slice.59 = f32[4723968]{0:T(1024)} dynamic-update-slice(f32[4723968]{0:T(1024)} %constant_dynamic-update-slice_fusion.4, f32[2360064]{0:T(1024)} %broadcast.4241, s32[]{} %constant.2621) | dynamic-update-slice | bytes 18880516 | tf_op jit(solution)/shard_map/cond/branch_1_fun/concatenate | solution.py:463
  2659.4 34.7 %all-reduce.32 = (f32[8,43]{1,0:T(8,128)S(1)}, f32[8,768]{1,0:T(8,128)S(1)}) all-reduce(f32[8,43]{1,0:T(8,128)S(1)} %broadcast_in_dim.988, f32[8,768]{1,0:T(8,128)S(1)} %broadcast_in_dim.989), channel_id=7, replica_groups=mesh['section'=4,'batch'=8] {'batch'}, use_global_device_ids=true, to_apply=%region_117.118.clone | all-reduce | flops 6488 | bytes 51904
  2694.7 100.3 %psum.7 = f32[43]{0:T(128)S(1)} all-reduce(f32[43]{0:T(128)S(1)} %fusion.593), channel_id=1, replica_groups=mesh['section'=4,'batch'=8] {'section'}, use_global_device_ids=true, to_apply=%region_118.119 | all-reduce | flops 43 | bytes 344 | tf_op jit(solution)/shard_map/psum | solution.py:689
  2805.4 501.1 %all-reduce.38.cloned.1.call-done = f32[4723968]{0:T(1024)} async-done(((f32[4723968]{0:T(1024)}), f32[4723968]{0:T(1024)}) %all-reduce.38.cloned.1.call-update) | async-done | bytes 18895888
  3309.6 27.4 multiply_add_fusion.21
  (1233 shorter events, 1410.6 us)
Async XLA Ops:
  8.0 124.9 %all-gather.5.cloned.1.call-start = ((), (), s32[]{:S(2)}) async-start(), calls=%async_computation.3 | async-start | bytes 3932160 | tf_op jit(solution)/shard_map/all_gather | solution.py:539
  8.7 135.1 %all-gather.9.cloned.1.call-start = ((), (), s32[]{:S(2)}) async-start(), calls=%async_computation.6 | async-start | bytes 3932160 | tf_op jit(solution)/shard_map/all_gather | solution.py:540
  9.5 351.0 %all-reduce.36.cloned.1.call-start = ((), (), s32[]{:S(2)}) async-start(), calls=%async_computation.9 | async-start | bytes 18898944
  58.7 770.5 %all-gather.7.cloned.1.call-start = ((), (), s32[]{:S(2)}) async-start(), calls=%async_computation.4 | async-start | bytes 78643200 | tf_op jit(solution)/shard_map/all_gather | solution.py:546
  60.0 69.5 %collective-permute-start.1 = (bf16[1024,768]{1,0:T(8,128)(2,1)}, bf16[1024,768]{1,0:T(8,128)(2,1)}, u32[]{:S(2)}, u32[]{:S(2)}) collective-permute-start(bf16[1024,768]{1,0:T(8,128)(2,1)} %broadcast.4186), channel_id=1, source_target_pairs={{0,8},{8,16},{16,24},{1,9},{9,17},{17,25},{2,10},{10,18},{18,26},{... | collective-permute-start | bytes 4718600 | tf_op jit(solution)/shard_map/ppermute | solution.py:32
  63.7 2583.3 %reduce-scatter.8.cloned.1.call-start = ((), (), s32[]{:S(2)}) async-start(), calls=%async_computation.8 | async-start | bytes 3932160 | tf_op jit(solution)/shard_map/reduce_scatter | solution.py:667
  135.8 688.4 %copy-start.4 = (bf16[4,2,256,768]{3,2,0,1:T(8,128)(2,1)}, bf16[4,2,256,768]{3,2,0,1:T(8,128)(2,1)S(1)}, u32[]{:S(2)}) copy-start(bf16[4,2,256,768]{3,2,0,1:T(8,128)(2,1)S(1)} %copy.222) | copy-start | bytes 9437188
  142.6 414.8 %copy-start.248 = (f32[1024]{0:T(1024)}, f32[1024]{0:T(1024)S(1)}, u32[]{:S(2)}) copy-start(f32[1024]{0:T(1024)S(1)} %broadcast_multiply_fusion.10) | copy-start | bytes 12292
  475.0 82.3 %copy-start.233 = (bf16[768]{0:T(1024)(128)(2,1)}, bf16[768]{0:T(1024)(128)(2,1)S(1)}, u32[]{:S(2)}) copy-start(bf16[768]{0:T(1024)(128)(2,1)S(1)} %get-tuple-element.2978) | copy-start | bytes 4612
  475.0 82.3 %copy-start.208 = (bf16[768]{0:T(1024)(128)(2,1)}, bf16[768]{0:T(1024)(128)(2,1)S(1)}, u32[]{:S(2)}) copy-start(bf16[768]{0:T(1024)(128)(2,1)S(1)} %get-tuple-element.2979) | copy-start | bytes 4612
  475.1 316.3 %copy-start.237 = (bf16[768]{0:T(1024)(128)(2,1)}, bf16[768]{0:T(1024)(128)(2,1)S(1)}, u32[]{:S(2)}) copy-start(bf16[768]{0:T(1024)(128)(2,1)S(1)} %get-tuple-element.2976) | copy-start | bytes 4612
  666.3 157.9 %collective-permute-start = (bf16[1024,768]{1,0:T(8,128)(2,1)}, bf16[1024,768]{1,0:T(8,128)(2,1)}, u32[]{:S(2)}, u32[]{:S(2)}) collective-permute-start(bf16[1024,768]{1,0:T(8,128)(2,1)} %get-tuple-element.3291), channel_id=1, source_target_pairs={{0,8},{8,16},{16,24},{1,9},{9,17},{17,25},{2,10},{10,18},{18,26},{... | collective-permute-start | bytes 4718600 | tf_op jit(solution)/shard_map/ppermute | solution.py:32
  793.0 155.3 %copy-start.227 = (bf16[3072]{0:T(1024)(128)(2,1)}, bf16[3072]{0:T(1024)(128)(2,1)S(1)}, u32[]{:S(2)}) copy-start(bf16[3072]{0:T(1024)(128)(2,1)S(1)} %slice_reduce_fusion.8) | copy-start | bytes 18436
  826.5 492.6 %copy-start.221 = (s32[1024]{0:T(1024)}, s32[1024]{0:T(1024)S(1)}, u32[]{:S(2)}) copy-start(s32[1024]{0:T(1024)S(1)} %ne.157) | copy-start | bytes 12292
  919.7 28.6 copy-start.32
  919.7 28.5 copy-start.182
  919.7 28.5 copy-start.209
  919.7 28.5 copy-start.217
  919.7 28.5 copy-start.219
  1056.7 77.8 %collective-permute-start.2 = (bf16[1024,768]{1,0:T(8,128)(2,1)}, bf16[1024,768]{1,0:T(8,128)(2,1)}, u32[]{:S(2)}, u32[]{:S(2)}) collective-permute-start(bf16[1024,768]{1,0:T(8,128)(2,1)} %convert_element_type.1316), channel_id=1, source_target_pairs={{0,8},{8,16},{16,24},{1,9},{9,17},{17,25},{2,10},{10,18},{18,26},{... | collective-permute-start | bytes 4718600 | tf_op jit(solution)/shard_map/ppermute | solution.py:32
  1059.3 77.2 %collective-permute-start.3 = (bf16[1024,768]{1,0:T(8,128)(2,1)}, bf16[1024,768]{1,0:T(8,128)(2,1)}, u32[]{:S(2)}, u32[]{:S(2)}) collective-permute-start(bf16[1024,768]{1,0:T(8,128)(2,1)} %get-tuple-element.2603), channel_id=1, source_target_pairs={{0,8},{8,16},{16,24},{1,9},{9,17},{17,25},{2,10},{10,18},{18,26},{... | collective-permute-start | bytes 4718600 | tf_op jit(solution)/shard_map/ppermute | solution.py:32
  1236.9 78.7 %collective-permute-start.4 = (bf16[1024,768]{1,0:T(8,128)(2,1)S(1)}, bf16[1024,768]{1,0:T(8,128)(2,1)}, u32[]{:S(2)}, u32[]{:S(2)}) collective-permute-start(bf16[1024,768]{1,0:T(8,128)(2,1)S(1)} %convert_element_type.1317), channel_id=1, source_target_pairs={{0,8},{8,16},{16,24},{1,9},{9,17},{17,25},{2,10},{10,18},{18,26},{... | collective-permute-start | bytes 4718600 | tf_op jit(solution)/shard_map/ppermute | solution.py:32
  1239.6 79.4 %collective-permute-start.5 = (bf16[1024,768]{1,0:T(8,128)(2,1)}, bf16[1024,768]{1,0:T(8,128)(2,1)S(1)}, u32[]{:S(2)}, u32[]{:S(2)}) collective-permute-start(bf16[1024,768]{1,0:T(8,128)(2,1)} %get-tuple-element.2605), channel_id=1, source_target_pairs={{0,8},{8,16},{16,24},{1,9},{9,17},{17,25},{2,10},{10,18},{18,26},{... | collective-permute-start | bytes 4718600 | tf_op jit(solution)/shard_map/ppermute | solution.py:32
  1434.8 36.0 %collective-permute-start.6 = (bf16[1024,768]{1,0:T(8,128)(2,1)}, bf16[1024,768]{1,0:T(8,128)(2,1)}, u32[]{:S(2)}, u32[]{:S(2)}) collective-permute-start(bf16[1024,768]{1,0:T(8,128)(2,1)} %convert_element_type.1318), channel_id=1, source_target_pairs={{0,8},{8,16},{16,24},{1,9},{9,17},{17,25},{2,10},{10,18},{18,26},{... | collective-permute-start | bytes 4718600 | tf_op jit(solution)/shard_map/ppermute | solution.py:32
  1439.6 145.0 %collective-permute-start.7 = (bf16[1024,768]{1,0:T(8,128)(2,1)}, bf16[1024,768]{1,0:T(8,128)(2,1)}, u32[]{:S(2)}, u32[]{:S(2)}) collective-permute-start(bf16[1024,768]{1,0:T(8,128)(2,1)} %get-tuple-element.2607), channel_id=1, source_target_pairs={{0,8},{8,16},{16,24},{1,9},{9,17},{17,25},{2,10},{10,18},{18,26},{... | collective-permute-start | bytes 4718600 | tf_op jit(solution)/shard_map/ppermute | solution.py:32
  1475.4 44.1 %copy-start.48 = (bf16[1024,768]{1,0:T(8,128)(2,1)}, bf16[1024,768]{1,0:T(8,128)(2,1)S(1)}, u32[]{:S(2)}) copy-start(bf16[1024,768]{1,0:T(8,128)(2,1)S(1)} %get-tuple-element.3021) | copy-start | bytes 4718596
  1475.7 43.8 %copy-start.267 = (f32[1024]{0:T(1024)}, f32[1024]{0:T(1024)S(1)}, u32[]{:S(2)}) copy-start(f32[1024]{0:T(1024)S(1)} %broadcast_multiply_fusion.9) | copy-start | bytes 12292
  1477.0 42.5 %copy-start.287 = (f32[1024]{0:T(1024)}, f32[1024]{0:T(1024)S(1)}, u32[]{:S(2)}) copy-start(f32[1024]{0:T(1024)S(1)} %add_rsqrt_fusion.6) | copy-start | bytes 12292
  1477.0 42.5 %slice-start.35 = ((s8[12582912]{0:T(1024)(128)(4,1)}), s8[4194304]{0:T(1024)(128)(4,1)S(1)}, s32[]{:S(2)}) async-start(s8[12582912]{0:T(1024)(128)(4,1)} %bitcast.1371), calls=%async_computation.46 | async-start | bytes 8388608
  1480.1 39.4 %copy-start.246 = (f32[1024]{0:T(1024)}, f32[1024]{0:T(1024)S(1)}, u32[]{:S(2)}) copy-start(f32[1024]{0:T(1024)S(1)} %broadcast_multiply_fusion.8) | copy-start | bytes 12292
  1482.2 37.4 %copy-start.262 = (f32[1024]{0:T(1024)}, f32[1024]{0:T(1024)S(1)}, u32[]{:S(2)}) copy-start(f32[1024]{0:T(1024)S(1)} %fusion.502) | copy-start | bytes 12292
  1482.8 36.8 %slice-start.36 = ((s8[12582912]{0:T(1024)(128)(4,1)}), s8[4194304]{0:T(1024)(128)(4,1)S(1)}, s32[]{:S(2)}) async-start(s8[12582912]{0:T(1024)(128)(4,1)} %bitcast.1371), calls=%async_computation.47 | async-start | bytes 8388608
  1482.8 36.8 %slice-start.37 = ((s8[12582912]{0:T(1024)(128)(4,1)}), s8[4194304]{0:T(1024)(128)(4,1)S(1)}, s32[]{:S(2)}) async-start(s8[12582912]{0:T(1024)(128)(4,1)} %bitcast.1371), calls=%async_computation.48 | async-start | bytes 8388608
  1532.1 36.9 %copy-start.247 = (f32[1024]{0:T(1024)S(1)}, f32[1024]{0:T(1024)}, u32[]{:S(2)}) copy-start(f32[1024]{0:T(1024)} %copy-done.246) | copy-start | bytes 12292
  1532.1 36.9 %copy-start.277 = (f32[1024]{0:T(1024)S(1)}, f32[1024]{0:T(1024)}, u32[]{:S(2)}) copy-start(f32[1024]{0:T(1024)} %fusion.590) | copy-start | bytes 12292
  1583.1 48.3 %collective-permute-start.8 = (bf16[1024,768]{1,0:T(8,128)(2,1)}, bf16[1024,768]{1,0:T(8,128)(2,1)}, u32[]{:S(2)}, u32[]{:S(2)}) collective-permute-start(bf16[1024,768]{1,0:T(8,128)(2,1)} %fusion.526), channel_id=1, source_target_pairs={{8,0},{16,8},{24,16},{9,1},{17,9},{25,17},{10,2},{18,10},{26,18},{... | collective-permute-start | bytes 4718600 | tf_op jit(solution)/shard_map/ppermute | solution.py:32
  1606.2 28.8 collective-permute-start.9
  1801.0 16.2 collective-permute-start.10
  1802.3 18.4 collective-permute-start.11
  1985.4 22.1 collective-permute-start.12
  1988.2 21.5 collective-permute-start.13
  2168.7 17.0 collective-permute-start.14
  2298.2 504.8 %reduce-scatter.6.cloned.1.call-start = ((), (), s32[]{:S(2)}) async-start(), calls=%async_computation.7 | async-start | bytes 3932160 | tf_op jit(solution)/shard_map/reduce_scatter | solution.py:664
  2340.0 966.5 %all-reduce.38.cloned.1.call-start = ((), (), s32[]{:S(2)}) async-start(), calls=%async_computation.10 | async-start | bytes 37797888
  2641.5 707.2 %reduce-scatter.4.cloned.1.call-start = ((), (), s32[]{:S(2)}) async-start(), calls=%async_computation.5 | async-start | bytes 3932160 | tf_op jit(solution)/shard_map/reduce_scatter | solution.py:661
  2648.6 147.6 %copy-start.303 = (f32[43]{0:T(128)S(1)}, f32[43]{0:T(128)}, u32[]{:S(2)}) copy-start(f32[43]{0:T(128)} %param.81) | copy-start | bytes 520
  2648.6 147.6 %copy-start.304 = (f32[43]{0:T(128)S(1)}, f32[43]{0:T(128)}, u32[]{:S(2)}) copy-start(f32[43]{0:T(128)} %param.80) | copy-start | bytes 520
  2805.4 503.8 %copy-start.105 = (f32[1,590496]{1,0:T(1,128)S(1)}, f32[1,590496]{1,0:T(1,128)}, u32[]{:S(2)}) copy-start(f32[1,590496]{1,0:T(1,128)} %param.76) | copy-start | bytes 7085956
  (287 other events, 1706.1 us)
Sparse Core Ops, SparseCore 0:
  10.4 31.2 all-gather.4
  43.2 28.5 all-gather.8
  73.4 370.1 all-gather.6
  2298.3 78.2 reduce-scatter.7
  2379.2 42.6 reduce-scatter.5
  2646.5 134.7 reduce-scatter.3
Sparse Core Ops, SparseCore 1:
  58.8 301.6 all-reduce.35
  2641.6 664.8 all-reduce.37
where the time goes:
time: 3380 us; the launch traced here: 3360 us
  local copies, waits for them, and re-layouts  1130 us (33%)
  waiting for transfers between devices  715 us (21%)
  other arithmetic  683 us (20%)
  matrix products  617 us (18%)
  blocking collectives  135 us (4%)
  starting transfers between devices  34.5 us (1%)
    unnamed x10, waiting for transfers between devices  715 us
    slice x8, local copies, waits for them, and re-layouts, slice_row(): segments.append(row_vector[offset:offset + length].reshape(shape_item))  217 us
    unnamed x503, local copies, waits for them, and re-layouts  205 us
    dynamic_slice x49, local copies, waits for them, and re-layouts, store_slot(): store[slot_index]  187 us
    dynamic_update_slice x46, other arithmetic, store_slot(): lax.dynamic_update_index_in_dim(store, jnp.where(active, leaf, store[slot...  150 us
    dot_general x16, matrix products, score_block(): jnp.einsum('qhe,khe->hqk', query_part, keys[:key_count], preferred_elemen...  114 us
    convert_element_type x8, other arithmetic, attention_backward(): grad_scores = (prob_rows * (grad_probs - inner_sum)).astype(brain_type)  111 us
    dot_general x8, matrix products, attention_backward(): jnp.einsum('qhe,khe->hqk', grad_part, values[:key_count], preferred_eleme...  104 us
  transfers between devices with their start and end apart: 23, of which 2 were waited for; matrix products, arithmetic and copies ran while one was open for 41% of the time, Pallas kernels for 0%

commit v1 on v0

v1 whole, which is shorter than its diff:
```python
import jax
import jax.numpy as jnp
from jax import lax
from jax.sharding import PartitionSpec as P

D = 768
HEADS = 12
HEAD = 64
FF = 3072
HIST = 20
SEQ_SHORT = 256
VEC = 7 * D

eps_norm = 1e-05
rope_base = 10000.0
masked_score = -1e30
beta_one = 0.9
beta_two = 0.95
weight_decay = 0.1
adam_eps = 1e-08
adam_steps = 1000.0
f32 = jnp.float32
bf16 = jnp.bfloat16

ATT_VECS = [(0, D), (D, D), (2 * D + 3 * D * D, 3 * D), (5 * D + 4 * D * D, D)]
MLP_VECS = [(0, D), (D, D), (2 * D + D * FF, FF), (2 * D + FF + 2 * D * FF, D)]


class Plan:
    def __init__(self, batch_count, shard):
        self.nb = batch_count
        self.shard = shard
        self.tile = 8 * D * D // batch_count
        nb, tile = self.nb, self.tile
        self.rows = tile // D
        self.up_rows = tile // FF
        self.joint_rows = tile // (3 * D)
        self.mlp_start = [2 * D + tile * b + (FF if 2 * b >= nb else 0) for b in range(nb)]
        self.att_start = [2 * D + tile * b + (3 * D if 8 * b >= 3 * nb else 0) for b in range(nb)]
        low = high = 0
        for starts, count in ((self.mlp_start, nb), (self.att_start, nb // 2)):
            for b in range(count):
                low = max(low, shard * b - starts[b])
                high = max(high, starts[b] + tile - shard * (b + 1))
        self.low, self.high = low, high


def swap_sections(array):
    return lax.ppermute(array, "section", [(i, 3 - i) for i in range(4)])


def swap_cores(array):
    return lax.ppermute(array, "section", [(i, i ^ 1) for i in range(4)])


def swap_planes(array):
    return lax.ppermute(array, "section", [(i, i ^ 2) for i in range(4)])


def layer_norm(values, gain_row, bias_row):
    center = values - jnp.mean(values, axis=-1, keepdims=True)
    scale = lax.rsqrt(jnp.mean(center * center, axis=-1, keepdims=True) + eps_norm)
    return center * scale * gain_row + bias_row


def norm_back(values, gain_row, grad):
    center = values - jnp.mean(values, axis=-1, keepdims=True)
    scale = lax.rsqrt(jnp.mean(center * center, axis=-1, keepdims=True) + eps_norm)
    unit = center * scale
    inner = grad * gain_row
    out = scale * (
        inner
        - jnp.mean(inner, axis=-1, keepdims=True)
        - unit * jnp.mean(inner * unit, axis=-1, keepdims=True)
    )
    return out, jnp.sum(grad * unit, axis=0), jnp.sum(grad, axis=0)


def rotate(tensor, cosine, sine):
    half = HEAD // 2
    first, second = tensor[..., :half], tensor[..., half:]
    return jnp.concatenate(
        [first * cosine - second * sine, first * sine + second * cosine], axis=-1
    )


def rotation(position):
    half = HEAD // 2
    inverse = rope_base ** (-jnp.arange(half, dtype=f32) / half)
    angles = position.astype(f32)[:, None] * inverse[None, :]
    return jnp.cos(angles)[:, None, :], jnp.sin(angles)[:, None, :]


def adamw(param, grad, first, second, decay):
    first_new = beta_one * first + (1.0 - beta_one) * grad
    second_new = beta_two * second + (1.0 - beta_two) * grad * grad
    first_hat = first_new / (1.0 - beta_one**adam_steps)
    second_hat = second_new / (1.0 - beta_two**adam_steps)
    direction = first_hat / (jnp.sqrt(second_hat) + adam_eps) + decay * param
    return (direction, first_new, second_new)


def dot(a, b):
    return jnp.dot(a, b, preferred_element_type=f32)


def dot_tn(a, b):
    return lax.dot_general(a, b, (((0,), (0,)), ((), ())), preferred_element_type=f32)


def dot_nt(a, b):
    return lax.dot_general(a, b, (((1,), (1,)), ((), ())), preferred_element_type=f32)


class Place:
    pass


def pack_weights(plan, place, params):
    nb, shard, tile = plan.nb, plan.shard, plan.tile
    own = params.reshape(-1).astype(bf16)
    parts = []
    if plan.low:
        parts.append(lax.ppermute(own[-plan.low :], "batch", [(i, i + 1) for i in range(nb - 1)]))
    parts.append(own)
    if plan.high:
        parts.append(lax.ppermute(own[: plan.high], "batch", [(i, i - 1) for i in range(1, nb)]))
    wide = jnp.concatenate(parts)
    b, mlp = place.b, place.mlp
    mlp_offset = jnp.array([plan.low + plan.mlp_start[i] - shard * i for i in range(nb)])
    att_offset = jnp.array(
        [plan.low + (plan.att_start[i] - shard * i if 2 * i < nb else 0) for i in range(nb)]
    )
    offset = jnp.where(mlp, mlp_offset[b], att_offset[b])
    flat = lax.dynamic_slice(wide, (offset,), (tile,))
    rows = plan.rows
    plain = flat.reshape(rows, D)
    up = flat.reshape(plan.up_rows, FF // D, D).transpose(1, 0, 2).reshape(rows, D)
    joint = flat.reshape(2, plan.joint_rows // 2, 3, D).transpose(0, 2, 1, 3).reshape(rows, D)
    is_up = mlp & (2 * b < nb)
    is_joint = jnp.logical_not(mlp) & (8 * b < 3 * nb)
    block = jnp.where(is_up, up, jnp.where(is_joint, joint, plain))
    padded = jnp.concatenate([jnp.zeros((FF,), bf16), own, jnp.zeros((FF,), bf16)])

    def vectors(pieces):
        out = []
        for start, length in pieces:
            at = jnp.clip(start - shard * b + FF, 0, shard + FF)
            out.append(lax.dynamic_slice(padded, (at,), (length,)))
        total = sum(length for _, length in pieces)
        out.append(jnp.zeros((VEC - total,), bf16))
        return jnp.concatenate(out)

    vecs = jnp.where(mlp, vectors(MLP_VECS), vectors(ATT_VECS))
    return block, vecs.reshape(VEC // D, D)


def split_vecs(lines, pieces):
    flat = lines.reshape(-1)
    out, at = [], 0
    for _, length in pieces:
        out.append(flat[at : at + length])
        at += length
    return out


def attention_parts(place, mine):
    other = swap_cores(mine)
    span = place.span
    outer = jnp.where(place.outer, mine, other)
    inner = jnp.where(place.outer, other, mine)
    return jnp.concatenate([outer[:span], inner, outer[span:]], axis=0)


def masks(place, width):
    out = []
    for part, start in enumerate(place.starts):
        rows = start + jnp.arange(place.span)
        columns = jnp.arange(width[part])
        lowest = jnp.where(place.kind == 1, rows - rows % SEQ_SHORT, 0)
        out.append((columns[None, :] <= rows[:, None]) & (columns[None, :] >= lowest[:, None]))
    return out


def attention(place, queries, keys, values):
    span = place.span
    width = (2 * span, 4 * span)
    allowed = masks(place, width)
    outs, logs = [], []
    for part in range(2):
        q = queries[part * span : (part + 1) * span]
        scores = jnp.einsum("qhe,khe->hqk", q, keys[: width[part]], preferred_element_type=f32)
        scores = jnp.where(allowed[part][None], scores, masked_score)
        top = jnp.max(scores, axis=-1, keepdims=True)
        expo = jnp.exp(scores - top)
        total = jnp.sum(expo, axis=-1, keepdims=True)
        prob = (expo / total).astype(bf16)
        outs.append(
            jnp.einsum("hqk,khe->qhe", prob, values[: width[part]], preferred_element_type=f32)
        )
        logs.append(top + jnp.log(total))
    return jnp.concatenate(outs, axis=0), logs


def attention_grad(place, queries, keys, values, logs, datt):
    span = place.span
    width = (2 * span, 4 * span)
    allowed = masks(place, width)
    dqs = []
    dk = jnp.zeros(keys.shape, f32)
    dv = jnp.zeros(keys.shape, f32)
    for part in range(2):
        w = width[part]
        q = queries[part * span : (part + 1) * span]
        do = datt[part * span : (part + 1) * span]
        scores = jnp.einsum("qhe,khe->hqk", q, keys[:w], preferred_element_type=f32)
        scores = jnp.where(allowed[part][None], scores, masked_score)
        prob = jnp.exp(scores - logs[part])
        dp = jnp.einsum("qhe,khe->hqk", do, values[:w], preferred_element_type=f32)
        inner = jnp.sum(prob * dp, axis=-1, keepdims=True)
        ds = (prob * (dp - inner)).astype(bf16)
        dqs.append(jnp.einsum("hqk,khe->qhe", ds, keys[:w], preferred_element_type=f32))
        dk = dk.at[:w].add(jnp.einsum("hqk,qhe->khe", ds, q, preferred_element_type=f32))
        dv = dv.at[:w].add(
            jnp.einsum("hqk,qhe->khe", prob.astype(bf16), do, preferred_element_type=f32)
        )
    return jnp.concatenate(dqs, axis=0), dk, dv


def att_forward(place, weights, stream):
    gain, bias, joint_w, joint_b, out_w, out_b = weights
    rows = stream.shape[0]
    stream = stream.astype(f32)
    normed = layer_norm(stream, gain, bias).astype(bf16)
    joint = (dot(normed, joint_w) + joint_b).reshape(rows, 3, HEADS, HEAD)
    cosine, sine = place.turn
    q = (rotate(joint[:, 0], cosine, sine) * HEAD**-0.5).astype(bf16)
    k = rotate(joint[:, 1], cosine, sine).astype(bf16)
    kv = jnp.stack([k, joint[:, 2].astype(bf16)], axis=1)
    kv = attention_parts(place, kv.reshape(rows, 2 * D)).reshape(2 * rows, 2, HEADS, HEAD)
    mixed, logs = attention(place, q, kv[:, 0], kv[:, 1])
    mixed = mixed.reshape(rows, D).astype(bf16)
    out = stream + dot(mixed, out_w) + out_b
    return out.astype(bf16), (normed, q, kv, logs, mixed)


def att_backward(place, weights, stream, kept, grad):
    gain, bias, joint_w, joint_b, out_w, out_b = weights
    normed, q, kv, logs, mixed = kept
    rows = stream.shape[0]
    datt = dot_nt(grad, out_w).astype(bf16).reshape(rows, HEADS, HEAD)
    dq, dk, dv = attention_grad(place, q, kv[:, 0], kv[:, 1], logs, datt)
    span = place.span
    both = jnp.stack([dk, dv], axis=1).reshape(2 * rows, 2 * D)
    outer = jnp.concatenate([both[:span], both[3 * span :]], axis=0)
    inner = both[span : 3 * span]
    got = swap_cores(jnp.where(place.outer, inner, outer).astype(bf16)).astype(f32)
    dkv = (jnp.where(place.outer, outer, inner) + got).reshape(rows, 2, HEADS, HEAD)
    cosine, sine = place.turn
    djoint = jnp.concatenate(
        [
            (rotate(dq, cosine, -sine) * HEAD**-0.5).reshape(rows, D),
            rotate(dkv[:, 0], cosine, -sine).reshape(rows, D),
            dkv[:, 1].reshape(rows, D),
        ],
        axis=1,
    ).astype(bf16)
    dn = dot_nt(djoint, joint_w)
    back, dgain, dbias = norm_back(stream.astype(f32), gain, dn)
    out = grad.astype(f32) + back
    vecs = (dgain, dbias, jnp.sum(djoint.astype(f32), axis=0), jnp.sum(grad.astype(f32), axis=0))
    c = place.core
    half = D // 2

    def pick(array, pieces):
        wide = array.reshape(rows, pieces, 2, array.shape[1] // (2 * pieces))
        return jnp.where(c == 0, wide[:, :, 0], wide[:, :, 1]).reshape(rows, -1), jnp.where(
            c == 0, wide[:, :, 1], wide[:, :, 0]
        ).reshape(rows, -1)

    blocks = place.plan.nb * 3 // 8
    n_mine, n_other = pick(normed, blocks)
    m_mine, m_other = pick(mixed, place.plan.nb // 8)
    got = swap_cores(jnp.concatenate([n_other, m_other, djoint, grad], axis=1))
    n_all = jnp.concatenate([n_mine, got[:, :half]], axis=0)
    m_all = jnp.concatenate([m_mine, got[:, half:D]], axis=0)
    j_all = jnp.concatenate([djoint, got[:, D : 4 * D]], axis=0)
    g_all = jnp.concatenate([grad, got[:, 4 * D :]], axis=0)
    d_joint = dot_tn(n_all, j_all).astype(bf16)
    d_out = dot_tn(m_all, g_all).astype(bf16)
    tile = place.plan.rows // 2
    d_joint = d_joint.reshape(blocks, place.plan.joint_rows // 2, 3, D).transpose(0, 2, 1, 3)
    tiles = jnp.concatenate([d_joint.reshape(-1, D), d_out], axis=0).reshape(-1, tile, D)
    return out, vecs, tiles


def mlp_forward(place, weights, stream):
    gain, bias, up_w, up_b, down_w, down_b = weights
    stream = stream.astype(f32)
    normed = layer_norm(stream, gain, bias).astype(bf16)
    hidden = dot(normed, up_w) + up_b
    cdf = 0.5 * (1.0 + lax.erf(hidden * (2.0**-0.5)))
    active = (hidden * cdf).astype(bf16)
    slope = (cdf + hidden * jnp.exp(-0.5 * hidden * hidden) * (2.0 * jnp.pi) ** -0.5).astype(bf16)
    out = stream + dot(active, down_w) + down_b
    return out, (normed, active, slope)


def mlp_backward(place, weights, stream, kept, grad):
    gain, bias, up_w, up_b, down_w, down_b = weights
    normed, active, slope = kept
    rows = stream.shape[0]
    er = grad.astype(bf16)
    dpre = (dot_nt(er, down_w) * slope.astype(f32)).astype(bf16)
    dn = dot_nt(dpre, up_w)
    back, dgain, dbias = norm_back(stream.astype(f32), gain, dn)
    out = grad + back
    vecs = (dgain, dbias, jnp.sum(dpre.astype(f32), axis=0), jnp.sum(er.astype(f32), axis=0))
    c = place.core
    half = FF // 2
    p_mine = jnp.where(c == 0, dpre[:, :half], dpre[:, half:])
    p_other = jnp.where(c == 0, dpre[:, half:], dpre[:, :half])
    wide = active.reshape(rows, place.plan.nb // 2, 2, -1)
    a_mine = jnp.where(c == 0, wide[:, :, 0], wide[:, :, 1]).reshape(rows, half)
    a_other = jnp.where(c == 0, wide[:, :, 1], wide[:, :, 0]).reshape(rows, half)
    got = swap_cores(jnp.concatenate([p_other, a_other, normed, er], axis=1))
    p_all = jnp.concatenate([p_mine, got[:, :half]], axis=0)
    a_all = jnp.concatenate([a_mine, got[:, half:FF]], axis=0)
    n_all = jnp.concatenate([normed, got[:, FF : FF + D]], axis=0)
    e_all = jnp.concatenate([er, got[:, FF + D :]], axis=0)
    d_up = dot_tn(n_all, p_all).astype(bf16)
    d_down = dot_tn(a_all, e_all).astype(bf16)
    plan = place.plan
    d_up = d_up.reshape(plan.nb // 2, plan.up_rows, FF // D // 2, D).transpose(0, 2, 1, 3)
    tiles = jnp.concatenate([d_up.reshape(-1, D), d_down], axis=0).reshape(-1, plan.rows // 2, D)
    return out, vecs, tiles


def local(
    stream_in,
    history,
    cotangent,
    group,
    params,
    first_moment,
    second_moment,
    mix_weights,
    mix_first,
    mix_second,
):
    nb = lax.axis_size("batch")
    plan = Plan(nb, params.shape[1])
    place = Place()
    place.plan = plan
    section = lax.axis_index("section")
    b = place.b = lax.axis_index("batch")
    plane = section // 2
    place.core = section % 2
    place.mlp = section % 2 == 1
    place.outer = (section == 0) | (section == 3)
    span = place.span = stream_in.shape[0] // 2
    low_half = plane == 0
    place.kind = jnp.where(low_half, group[0], group[1])
    place.starts = (
        jnp.where(place.outer, 0, 1) * span,
        jnp.where(place.outer, 3, 2) * span,
    )
    tokens = stream_in.shape[0] * 4 * nb
    grad_scale = float(tokens) ** -0.5

    def to_compute(array):
        mine = jnp.where(low_half, array[..., :span, :], array[..., span:, :])
        other = jnp.where(low_half, array[..., span:, :], array[..., :span, :])
        got = swap_sections(other)
        return jnp.concatenate(
            [jnp.where(low_half, mine, got), jnp.where(low_half, got, mine)], axis=-2
        )

    to_owner = to_compute

    block, vecs = pack_weights(plan, place, params)
    pad = -(block.shape[0] + vecs.shape[0]) % 16
    sent = jnp.concatenate([block, vecs, jnp.zeros((pad, D), bf16)], axis=0)
    gathered = lax.all_gather(sent, ("section", "batch"), axis=0, tiled=False)
    gathered = gathered.reshape(4, nb, sent.shape[0], D)
    all_vecs = jnp.sum(gathered[:, :, plan.rows : plan.rows + VEC // D].astype(f32), axis=1)
    att_weights, mlp_weights = [], []
    for layer in range(2):
        v = split_vecs(all_vecs[2 * layer], ATT_VECS)
        tiles = gathered[2 * layer, :, : plan.rows]
        blocks = nb * 3 // 8
        joint_w = (
            tiles[:blocks]
            .reshape(blocks, 2, 3, plan.joint_rows // 2, D)
            .transpose(0, 1, 3, 2, 4)
            .reshape(D, 3 * D)
        )
        out_w = tiles[blocks : nb // 2].reshape(D, D)
        att_weights.append((v[0], v[1], joint_w, v[2], out_w, v[3]))
        v = split_vecs(all_vecs[2 * layer + 1], MLP_VECS)
        tiles = gathered[2 * layer + 1, :, : plan.rows]
        up_w = (
            tiles[: nb // 2]
            .reshape(nb // 2, FF // D, plan.up_rows, D)
            .transpose(0, 2, 1, 3)
            .reshape(D, FF)
        )
        down_w = tiles[nb // 2 :].reshape(FF, D)
        mlp_weights.append((v[0], v[1], up_w, v[2], down_w, v[3]))

    first_mix = mix_weights[:HIST]
    second_mix = mix_weights[HIST + 1 : 2 * HIST + 1]
    past_one = jnp.zeros(stream_in.shape, f32)
    past_two = jnp.zeros(stream_in.shape, f32)
    for j in range(HIST):
        row = history[j].astype(f32)
        past_one = past_one + first_mix[j] * row
        past_two = past_two + second_mix[j] * row
    stream = to_compute(stream_in)
    cot, past_one, past_two = to_compute(
        jnp.stack([cotangent, past_one.astype(bf16), past_two.astype(bf16)])
    )
    row_index = jnp.concatenate([s + jnp.arange(span) for s in place.starts])
    position = jnp.where(place.kind == 1, row_index % SEQ_SHORT, row_index)
    place.turn = rotation(position)
    w20, w41, w42 = mix_weights[HIST], mix_weights[2 * HIST + 1], mix_weights[2 * HIST + 2]

    h20, kept_a20 = att_forward(place, att_weights[0], stream)
    x20, kept_m20 = mlp_forward(place, mlp_weights[0], h20)
    y20 = (past_one.astype(f32) + w20 * x20).astype(bf16)
    c20 = x20.astype(bf16)
    h21, kept_a21 = att_forward(place, att_weights[1], y20)
    x21, kept_m21 = mlp_forward(place, mlp_weights[1], h21)
    y21 = past_two.astype(f32) + w41 * c20.astype(f32) + w42 * x21
    stream_out = to_owner(y21.astype(bf16))

    g21 = cot.astype(f32) * grad_scale
    mix42 = jnp.sum(g21 * x21)
    mix41 = jnp.sum(g21 * c20.astype(f32))
    dh21, vec_m21, tiles_m21 = mlp_backward(place, mlp_weights[1], h21, kept_m21, w42 * g21)
    dy20, vec_a21, tiles_a21 = att_backward(
        place, att_weights[1], y20, kept_a21, dh21.astype(bf16)
    )
    dy20 = dy20.astype(bf16)
    mix20 = jnp.sum(dy20.astype(f32) * x20)
    e20 = w20 * dy20.astype(f32) + (w41 * g21).astype(bf16).astype(f32)
    dh20, vec_m20, tiles_m20 = mlp_backward(place, mlp_weights[0], h20, kept_m20, e20)
    dstream, vec_a20, tiles_a20 = att_backward(
        place, att_weights[0], stream, kept_a20, dh20.astype(bf16)
    )
    dy20_own = to_owner(dy20)
    stream_grad = to_owner(dstream.astype(bf16)).astype(f32)

    def reduce_rows(tiles):
        if tiles.shape[0] < nb:
            tiles = jnp.concatenate(
                [tiles, jnp.zeros((nb - tiles.shape[0],) + tiles.shape[1:], bf16)], axis=0
            )
        return lax.psum_scatter(tiles, "batch", scatter_dimension=0, tiled=True)[0]

    parts = [reduce_rows(t) for t in (tiles_a20, tiles_m20, tiles_a21, tiles_m21)]
    upper = jnp.stack(parts[:2])
    lower = jnp.stack(parts[2:])
    keep = jnp.where(low_half, upper, lower)
    give = jnp.where(low_half, lower, upper)
    keep = keep.astype(f32) + swap_planes(give).astype(f32)
    mine = jnp.where(place.core == 0, keep[0], keep[1])
    other = jnp.where(place.core == 0, keep[1], keep[0])
    got = swap_cores(other.astype(bf16)).astype(f32)
    first = jnp.where(place.core == 0, mine, got)
    second = jnp.where(place.core == 0, got, mine)
    tile_grad = jnp.concatenate([first, second], axis=0)

    own_g = cotangent.astype(f32) * grad_scale
    own_dy = dy20_own.astype(f32)
    history_grad = (
        first_mix[:, None, None] * own_dy[None] + second_mix[:, None, None] * own_g[None]
    ).astype(bf16)
    mix_one = jnp.sum(own_dy[None] * history.astype(f32), axis=(1, 2))
    mix_two = jnp.sum(own_g[None] * history.astype(f32), axis=(1, 2))
    own_mix = jnp.concatenate([mix_one, mix20[None], mix_two, mix41[None], mix42[None]])

    def flat_vec(v):
        out = jnp.concatenate(v)
        return jnp.concatenate([out, jnp.zeros((VEC - out.shape[0],), f32)])

    small = jnp.concatenate(
        [flat_vec(v) for v in (vec_a20, vec_m20, vec_a21, vec_m21)] + [own_mix]
    )
    small = lax.psum(small, ("section", "batch"))
    mix_grad = small[4 * VEC :]
    vec_rows = small[: 4 * VEC].reshape(4, VEC)
    vec_own = lax.dynamic_index_in_dim(vec_rows, section, 0, keepdims=False)

    rows = plan.rows
    plain = tile_grad.reshape(-1)
    up = tile_grad.reshape(FF // D, plan.up_rows, D).transpose(1, 0, 2).reshape(-1)
    joint = tile_grad.reshape(2, 3, plan.joint_rows // 2, D).transpose(0, 2, 1, 3).reshape(-1)
    is_up = place.mlp & (2 * b < nb)
    is_joint = jnp.logical_not(place.mlp) & (8 * b < 3 * nb)
    flat = jnp.where(is_up, up, jnp.where(is_joint, joint, plain))
    flat = jnp.where(place.mlp | (2 * b < nb), flat, 0.0)
    halo = max(
        [0]
        + [
            max(s[i] + plan.tile - plan.shard * (i + 1), plan.shard * i - s[i])
            for s, n in ((plan.mlp_start, nb), (plan.att_start, nb // 2))
            for i in range(n)
        ]
    )
    before = lax.ppermute(flat[-halo:], "batch", [(i, i + 1) for i in range(nb - 1)])
    after = lax.ppermute(flat[:halo], "batch", [(i, i - 1) for i in range(1, nb)])
    starts = jnp.array([plan.att_start, plan.mlp_start])[place.mlp.astype(jnp.int32)]
    margin = 4 * D + halo
    shift = margin - plan.shard * b
    window = jnp.zeros((plan.shard + 2 * margin,), f32)

    def put(window, piece, at):
        at = jnp.clip(at, 0, window.shape[0] - piece.shape[0])
        return lax.dynamic_update_slice(window, piece, (at,))

    window = put(window, before, starts[jnp.maximum(b - 1, 0)] + plan.tile - halo + shift)
    window = put(window, after, starts[jnp.minimum(b + 1, nb - 1)] + shift)
    window = put(window, flat, starts[b] + shift)

    def with_vecs(window, pieces):
        at = 0
        for start, length in pieces:
            window = put(window, vec_own[at : at + length], start + shift)
            at += length
        return window[margin : margin + plan.shard]

    grad = jnp.where(place.mlp, with_vecs(window, MLP_VECS), with_vecs(window, ATT_VECS))
    grad = grad.reshape(params.shape)
    bias_grad = jnp.where(place.mlp, vec_own[6 * D : 7 * D], vec_own[5 * D : 6 * D])[None]

    params_step, first_new, second_new = adamw(
        params, grad, first_moment, second_moment, weight_decay
    )
    mix_step, mix_first_new, mix_second_new = adamw(
        mix_weights, mix_grad, mix_first, mix_second, 0.0
    )
    return (
        stream_out,
        stream_grad,
        history_grad,
        grad,
        params_step,
        first_new,
        second_new,
        mix_grad,
        mix_step,
        mix_first_new,
        mix_second_new,
        bias_grad,
    )


def solution(mesh):
    rows = P(("section", "batch"), None)
    hist = P(None, ("section", "batch"), None)
    weights = P("section", "batch")
    return jax.shard_map(
        local,
        mesh=mesh,
        in_specs=(rows, hist, rows, P("batch"), weights, weights, weights, P(), P(), P()),
        out_specs=(
            rows,
            rows,
            hist,
            weights,
            weights,
            weights,
            weights,
            P(),
            P(),
            P(),
            P(),
            P("section", None),
        ),
        check_vma=False,
    )
```

time: 3380 us -> 1340 us (0.40)
  local copies, waits for them, and re-layouts: 1130 us -> 363 us
  other arithmetic: 683 us -> 246 us
  matrix products: 617 us -> 207 us
  waiting for transfers between devices: 715 us -> 466 us
  blocking collectives: 135 us -> 0 us
    unnamed x10 -> x6, waiting for transfers between devices: 715 us -> 0.1 us
    dot_general x78 -> x48, matrix products: 617 us -> 207 us  [the longest x8 43.3 us: dot_tn(): lax.dot_general(a, b, (((0,), (0,)), ((), ())), preferred_element_type=f32)]
    dynamic_slice x60 -> x7, local copies, waits for them, and re-layouts: 195 us -> 3.94 us  [the longest x1 1.93 us: pack_weights(): flat = lax.dynamic_slice(wide, (offset,), (tile,))]
    slice x32 -> x44, local copies, waits for them, and re-layouts: 231 us -> 69.3 us  [the longest x1 12.7 us: local(): down_w = tiles[nb // 2:].reshape(FF, D)]
    dynamic_update_slice x46 -> x0, other arithmetic: 150 us -> none  [store_slot(): lax.dynamic_update_index_in_dim(store, jnp.where(active, leaf, store[slot...]
    reduce_scatter x3 -> x4, waiting for transfers between devices: 0.02 us -> 149 us  [reduce_rows(): return lax.psum_scatter(tiles, 'batch', scatter_dimension=0, tiled=True)[0]]
    unnamed x503 -> x515, local copies, waits for them, and re-layouts: 205 us -> 66.1 us
    all_gather x3 -> x1, waiting for transfers between devices: 0.01 us -> 125 us  [local(): gathered = lax.all_gather(sent, ('section', 'batch'), axis=0, tiled=False)]
  transfers between devices with their start and end apart: 23 -> 25, of which waited for: 2 -> 9; matrix products, arithmetic and copies ran while one was open for 41% -> 40% of each run, Pallas kernels for 0% -> 0%
where the time goes in v1:
time: 1340 us; the launch traced here: 1330 us
  waiting for transfers between devices  466 us (35%)
  local copies, waits for them, and re-layouts  363 us (27%)
  other arithmetic  246 us (18%)
  matrix products  207 us (15%)
  between operations  23.5 us (2%)
  starting transfers between devices  19.8 us (1%)
    reduce_scatter x4, waiting for transfers between devices, reduce_rows(): return lax.psum_scatter(tiles, 'batch', scatter_dimension=0, tiled=True)[0]  149 us
    all_gather x1, waiting for transfers between devices, local(): gathered = lax.all_gather(sent, ('section', 'batch'), axis=0, tiled=False)  125 us
    psum x1, waiting for transfers between devices, local(): small = lax.psum(small, ('section', 'batch'))  116 us
    unnamed x515, local copies, waits for them, and re-layouts  66.1 us
    ppermute x5, waiting for transfers between devices, swap_sections(): return lax.ppermute(array, 'section', [(i, 3 - i) for i in range(4)])  64.6 us
    dot_general x8, matrix products, dot_tn(): lax.dot_general(a, b, (((0,), (0,)), ((), ())), preferred_element_type=f32)  43.3 us
    dot_general x8, matrix products, dot(): return jnp.dot(a, b, preferred_element_type=f32)  39.7 us
    dot_general x8, matrix products, dot_nt(): lax.dot_general(a, b, (((1,), (1,)), ((), ())), preferred_element_type=f32)  32.7 us
  transfers between devices with their start and end apart: 25, of which 9 were waited for; matrix products, arithmetic and copies ran while one was open for 40% of the time, Pallas kernels for 0%

profile of v1, /device:TPU:0, one launch (start us, length us, event | category | flops | bytes accessed | tf_op | source)
XLA Modules:
  0.0 1325.5 jit_solution(8395708792433220573)
XLA Ops:
  12.1 5.4 collective-permute-start.2
  19.5 22.1 %convert_reduce_fusion.13 = bf16[590496]{0:T(1024)(128)(2,1)S(1)} fusion(f32[1,590496]{1,0:T(1,128)S(1)} %copy-done.18), kind=kLoop, calls=%fused_computation.664 | loop fusion | flops 590496 | bytes 3542976 | tf_op jit(solution)/shard_map/convert_element_type | solution.py:121
  41.7 5.7 concatenate.262
  52.0 15.8 %concatenate.261 = bf16[592224]{0:T(1024)(128)(2,1)} concatenate(bf16[480]{0:T(512)(128)(2,1)} %collective-permute-done.2, bf16[590496]{0:T(1024)(128)(2,1)S(1)} %convert_reduce_fusion.13, bf16[1248]{0:T(1024)(128)(2,1)S(1)} %collective-permute-done.3), dimensions={0} | concatenate | bytes 2368896 | tf_op jit(solution)/shard_map/concatenate | solution.py:128
  79.4 20.0 %fusion.230 = bf16[1,512,768]{2,1,0:T(8,128)(2,1)S(1)} fusion(f32[]{:T(128)} %bitcast.40, f32[]{:T(128)} %bitcast.39, f32[]{:T(128)} %bitcast.38, f32[]{:T(128)} %bitcast.37, f32[]{:T(128)} %bitcast.36, f32[]{:T(128)} %bitcast.35, f32[]{:T(128)} %bitcast.34, f32[]{:T(128)} %bitcast.33, f32[]{:T(128)} %bitcast.32, f32[]{:T(128)} %bitcast.31, f32[]{:T(128)} %bitcast.30, ...), kind=kLoop, calls=%fused_computation.406 | loop fusion | flops 23592960 | bytes 16515152 | tf_op jit(solution)/shard_map/convert_element_type | solution.py:421
  99.3 19.9 %fusion.231 = bf16[1,512,768]{2,1,0:T(8,128)(2,1)S(1)} fusion(f32[]{:T(128)} %bitcast.20, f32[]{:T(128)} %bitcast.19, f32[]{:T(128)} %bitcast.18, f32[]{:T(128)} %bitcast.17, f32[]{:T(128)} %bitcast.16, f32[]{:T(128)} %bitcast.15, f32[]{:T(128)} %bitcast.14, f32[]{:T(128)} %bitcast.13, f32[]{:T(128)} %bitcast.12, f32[]{:T(128)} %bitcast.11, f32[]{:T(128)} %bitcast.10, ...), kind=kLoop, calls=%fused_computation.407 | loop fusion | flops 23592960 | bytes 16515152 | tf_op jit(solution)/shard_map/convert_element_type | solution.py:421
  126.5 48.4 %collective-permute-done.1 = bf16[256,768]{1,0:T(8,128)(2,1)} collective-permute-done((bf16[256,768]{1,0:T(8,128)(2,1)S(1)}, bf16[256,768]{1,0:T(8,128)(2,1)}, u32[]{:S(2)}, u32[]{:S(2)}) %collective-permute-start.1) | collective-permute-done | bytes 393248 | tf_op jit(solution)/shard_map/ppermute | solution.py:49
  177.3 125.2 %all-gather.3.cloned.1.call-done = bf16[25088,768]{1,0:T(8,128)(2,1)} async-done(((bf16[784,768]{1,0:T(8,128)(2,1)}), bf16[25088,768]{1,0:T(8,128)(2,1)}) %all-gather.3.cloned.1.call-update) | async-done | bytes 38535184 | tf_op jit(solution)/shard_map/all_gather | solution.py:384
  303.6 6.5 fusion.351
  312.0 12.0 copy.103
  324.0 8.9 reshape.1150
  334.2 6.3 convolution_add_fusion.1
  340.5 6.0 copy.104
  365.5 12.7 fusion.350
  385.0 12.0 copy.106
  397.0 9.0 reshape.1159
  435.9 5.6 convert_reduce_fusion.10
  446.8 6.1 copy.107
  461.1 6.0 copy.108
  519.8 5.2 convert_reduce_fusion
  534.4 5.5 fusion.232
  540.0 5.3 multiply_reduce_fusion.3
  547.3 10.5 multiply_reduce_fusion.1
  557.8 7.3 fusion.76
  570.8 6.7 multiply_convert_fusion.1
  588.4 7.1 reshape.1182
  620.1 5.8 fusion.251
  643.9 9.1 fusion.190
  654.8 5.5 convert_reduce_fusion.1
  667.2 14.0 %fusion.46 = bf16[384,2304]{1,0:T(8,128)(2,1)} fusion(bf16[512,2304]{1,0:T(8,128)(2,1)S(1)} %slice.1308, bf16[512,768]{1,0:T(8,128)(2,1)S(1)} %copy.113, bf16[512,768]{1,0:T(8,128)(2,1)S(1)} %copy.112, bf16[512,768]{1,0:T(8,128)(2,1)S(1)} %copy.111, bf16[512,384]{1,0:T(8,128)(2,1)S(1)} %get-tuple-element.226, bf16[512,384]{1,0:T(8,128)(2,1)S(1)} %copy-done.134), kind=kOutput, calls=%fused_computation.89 | convolution fusion | flops 1833271296 | bytes 7274496 | tf_op jit(solution)/shard_map/dot_general | solution.py:108
  702.6 5.4 multiply_reduce_fusion.2
  714.6 7.4 multiply_reduce_fusion
  722.0 6.8 multiply_convert_fusion
  752.6 6.1 reshape.1183
  782.0 5.9 fusion.252
  804.8 7.3 reshape.1174
  817.1 14.0 %fusion.49 = bf16[384,2304]{1,0:T(8,128)(2,1)} fusion(bf16[512,2304]{1,0:T(8,128)(2,1)S(1)} %slice.1292, bf16[512,768]{1,0:T(8,128)(2,1)S(1)} %copy-done.46, bf16[512,768]{1,0:T(8,128)(2,1)S(1)} %copy-done.49, bf16[512,768]{1,0:T(8,128)(2,1)S(1)} %copy-done.52, bf16[512,384]{1,0:T(8,128)(2,1)S(1)} %get-tuple-element.224, bf16[512,384]{1,0:T(8,128)(2,1)S(1)} %copy-done.135), kind=kOutput, calls=%fused_computation.90 | convolution fusion | flops 1833271296 | bytes 7274496 | tf_op jit(solution)/shard_map/dot_general | solution.py:108
  854.6 6.5 collective-permute-done.12
  885.7 8.8 collective-permute-done.6
  895.6 7.4 collective-permute-done.10
  903.2 23.6 %fusion.1 = (f32[20]{0:T(128)S(1)}, f32[20]{0:T(128)S(1)}, bf16[20,512,768]{2,1,0:T(8,128)(2,1)}) fusion(bf16[20,512,768]{2,1,0:T(8,128)(2,1)} %param.38, f32[512,768]{1,0:T(8,128)S(1)} %convert_multiply_fusion.49, f32[512,768]{1,0:T(8,128)S(1)} %maximum_convert_fusion.1, f32[20]{0:T(128)S(1)} %get-tuple-element.318, f32[20]{0:T(128)S(1)} %get-tuple-element.317), kind=kLoop, calls=%fused_computation.3 | loop fusion | flops 70778840 | bytes 34603328 | tf_op jit(solution)/shard_map/reduce_sum | solution.py:480
  929.0 51.8 %reduce-scatter.5.cloned.1.call-done = bf16[1,384,768]{2,1,0:T(8,128)(2,1)} async-done(((bf16[8,384,768]{2,1,0:T(8,128)(2,1)}), bf16[1,384,768]{2,1,0:T(8,128)(2,1)}) %reduce-scatter.5.cloned.1.call-update) | async-done | bytes 589840 | tf_op jit(solution)/shard_map/reduce_scatter | solution.py:459
  981.9 97.4 %reduce-scatter.7.cloned.1.call-done = bf16[1,384,768]{2,1,0:T(8,128)(2,1)} async-done(((bf16[8,384,768]{2,1,0:T(8,128)(2,1)}), bf16[1,384,768]{2,1,0:T(8,128)(2,1)}) %reduce-scatter.7.cloned.1.call-update) | async-done | bytes 589840 | tf_op jit(solution)/shard_map/reduce_scatter | solution.py:459
  1083.2 5.4 fusion.147
  1095.4 115.8 %all-reduce.8.cloned.1.call-done = f32[21547]{0:T(1024)} async-done(((f32[21547]{0:T(1024)}), f32[21547]{0:T(1024)}) %all-reduce.8.cloned.1.call-update) | async-done | bytes 86204 | tf_op jit(solution)/shard_map/psum | solution.py:490
  1246.0 22.4 %dynamic_update_slice.31 = f32[599136]{0:T(1024)S(1)} dynamic-update-slice(f32[599136]{0:T(1024)S(1)} %dynamic_update_slice.30, f32[589824]{0:T(1024)} %copy-done.32, s32[]{:T(128)S(6)} %min.62) | dynamic-update-slice | bytes 4718596 | tf_op jit(solution)/shard_map/dynamic_update_slice | solution.py:520
  1276.7 11.8 reshape.1192
  1290.9 27.6 %multiply_add_fusion = (f32[1,590496]{1,0:T(1,128)}, f32[1,590496]{1,0:T(1,128)}, f32[1,590496]{1,0:T(1,128)}) fusion(f32[1,590496]{1,0:T(1,128)S(1)} %copy-done.19, f32[590496]{0:T(1024)S(1)} %get-tuple-element.184, f32[1,590496]{1,0:T(1,128)S(1)} %copy-done.107, f32[590496]{0:T(1024)S(1)} %broadcast_multiply_fusion, f32[1,590496]{1,0:T(1,128)S(1)} %copy-done.108), kind=kLoop, calls=%fused_computation.147 | loop fusion | flops 4723968 | bytes 18895872 | tf_op jit(solution)/shard_map/add | solution.py:99
  (844 shorter events, 435.3 us)
Async XLA Ops:
  7.2 295.3 %all-gather.3.cloned.1.call-start = ((), (), s32[]{:S(2)}) async-start(), calls=%async_computation.9 | async-start | bytes 39739392 | tf_op jit(solution)/shard_map/all_gather | solution.py:384
  12.1 39.9 %collective-permute-start.2 = (bf16[480]{0:T(512)(128)(2,1)}, bf16[480]{0:T(512)(128)(2,1)}, u32[]{:S(2)}, u32[]{:S(2)}) collective-permute-start(bf16[480]{0:T(512)(128)(2,1)} %slice_reduce_fusion.11), channel_id=1, source_target_pairs={{0,1},{1,2},{2,3},{3,4},{4,5},{5,6},{6,7},{8,9},{9,10},{10,11},{11... | collective-permute-start | bytes 2888 | tf_op jit(solution)/shard_map/ppermute | solution.py:124
  18.2 33.9 %collective-permute-start.3 = (bf16[1248]{0:T(1024)(128)(2,1)}, bf16[1248]{0:T(1024)(128)(2,1)S(1)}, u32[]{:S(2)}, u32[]{:S(2)}) collective-permute-start(bf16[1248]{0:T(1024)(128)(2,1)} %slice_reduce_fusion), channel_id=1, source_target_pairs={{1,0},{2,1},{3,2},{4,3},{5,4},{6,5},{7,6},{9,8},{10,9},{11,10},{12... | collective-permute-start | bytes 7496 | tf_op jit(solution)/shard_map/ppermute | solution.py:127
  19.5 30.6 %copy-start.213 = (s32[8]{0:T(128)S(1)}, s32[8]{0:T(128)}, u32[]{:S(2)}) copy-start(s32[8]{0:T(128)} %constant.485.clone) | copy-start | bytes 100
  77.2 849.6 %reduce-scatter.9.cloned.1.call-start = ((), (), s32[]{:S(2)}) async-start(), calls=%async_computation.6 | async-start | bytes 5308416 | tf_op jit(solution)/shard_map/reduce_scatter | solution.py:459
  99.3 19.9 %copy-start.89 = (bf16[512,768]{1,0:T(8,128)(2,1)S(1)}, bf16[512,768]{1,0:T(8,128)(2,1)}, u32[]{:S(2)}) copy-start(bf16[512,768]{1,0:T(8,128)(2,1)} %param.39) | copy-start | bytes 2359300
  120.7 240.0 %collective-permute-start = (bf16[3,256,768]{2,1,0:T(8,128)(2,1)}, bf16[3,256,768]{2,1,0:T(8,128)(2,1)}, u32[]{:S(2)}, u32[]{:S(2)}) collective-permute-start(bf16[3,256,768]{2,1,0:T(8,128)(2,1)} %broadcast_select_fusion.15), channel_id=1, source_target_pairs={{0,24},{8,16},{16,8},{24,0},{1,25},{9,17},{17,9},{25,1},{2,26},{10... | collective-permute-start | bytes 3538952 | tf_op jit(solution)/shard_map/ppermute | solution.py:49
  121.4 53.4 %collective-permute-start.1 = (bf16[256,768]{1,0:T(8,128)(2,1)S(1)}, bf16[256,768]{1,0:T(8,128)(2,1)}, u32[]{:S(2)}, u32[]{:S(2)}) collective-permute-start(bf16[256,768]{1,0:T(8,128)(2,1)S(1)} %broadcast_select_fusion.35), channel_id=1, source_target_pairs={{0,24},{8,16},{16,8},{24,0},{1,25},{9,17},{17,9},{25,1},{2,26},{10... | collective-permute-start | bytes 1179656 | tf_op jit(solution)/shard_map/ppermute | solution.py:49
  125.5 224.8 %copy-start.109 = (f32[512,32]{0,1:T(8,128)}, f32[512,32]{0,1:T(8,128)S(1)}, u32[]{:S(2)}) copy-start(f32[512,32]{0,1:T(8,128)S(1)} %get-tuple-element.313) | copy-start | bytes 196612
  125.5 224.8 %copy-start.132 = (f32[512,32]{0,1:T(8,128)}, f32[512,32]{0,1:T(8,128)S(1)}, u32[]{:S(2)}) copy-start(f32[512,32]{0,1:T(8,128)S(1)} %get-tuple-element.312) | copy-start | bytes 196612
  176.2 250.9 %copy-start.28 = (bf16[256,768]{1,0:T(8,128)(2,1)}, bf16[256,768]{1,0:T(8,128)(2,1)S(1)}, u32[]{:S(2)}) copy-start(bf16[256,768]{1,0:T(8,128)(2,1)S(1)} %get-tuple-element.280) | copy-start | bytes 1179652
  176.2 250.9 %copy-start.30 = (bf16[256,768]{1,0:T(8,128)(2,1)}, bf16[256,768]{1,0:T(8,128)(2,1)S(1)}, u32[]{:S(2)}) copy-start(bf16[256,768]{1,0:T(8,128)(2,1)S(1)} %get-tuple-element.281) | copy-start | bytes 1179652
  176.4 157.8 %copy-start.162 = (f32[512]{0:T(512)}, f32[512]{0:T(512)S(1)}, u32[]{:S(2)}) copy-start(f32[512]{0:T(512)S(1)} %broadcast_multiply_fusion.12) | copy-start | bytes 6148
  353.2 54.9 %collective-permute-start.4 = (bf16[512,1536]{0,1:T(8,128)(2,1)}, bf16[512,1536]{0,1:T(8,128)(2,1)}, u32[]{:S(2)}, u32[]{:S(2)}) collective-permute-start(bf16[512,1536]{0,1:T(8,128)(2,1)} %bitcast.58), channel_id=1, source_target_pairs={{0,8},{8,0},{16,24},{24,16},{1,9},{9,1},{17,25},{25,17},{2,10},{10... | collective-permute-start | bytes 4718600 | tf_op jit(solution)/shard_map/ppermute | solution.py:53
  441.4 87.1 %copy-start.64 = (bf16[1,512,768]{2,1,0:T(8,128)(2,1)}, bf16[1,512,768]{2,1,0:T(8,128)(2,1)S(1)}, u32[]{:S(2)}) copy-start(bf16[1,512,768]{2,1,0:T(8,128)(2,1)S(1)} %get-tuple-element.189) | copy-start | bytes 2359300
  458.5 35.4 %collective-permute-start.5 = (bf16[512,1536]{0,1:T(8,128)(2,1)S(1)}, bf16[512,1536]{0,1:T(8,128)(2,1)}, u32[]{:S(2)}, u32[]{:S(2)}) collective-permute-start(bf16[512,1536]{0,1:T(8,128)(2,1)S(1)} %bitcast.479), channel_id=1, source_target_pairs={{0,8},{8,0},{16,24},{24,16},{1,9},{9,1},{17,25},{25,17},{2,10},{10... | collective-permute-start | bytes 4718600 | tf_op jit(solution)/shard_map/ppermute | solution.py:53
  545.2 19.8 %slice-start.10 = ((s8[6291456]{0:T(1024)(128)(4,1)}), s8[2097152]{0:T(1024)(128)(4,1)S(1)}, s32[]{:S(2)}) async-start(s8[6291456]{0:T(1024)(128)(4,1)} %bitcast.430), calls=%async_computation.20 | async-start | bytes 4194304
  547.3 17.8 %slice-start.11 = ((s8[6291456]{0:T(1024)(128)(4,1)}), s8[4194304]{0:T(1024)(128)(4,1)S(1)}, s32[]{:S(2)}) async-start(s8[6291456]{0:T(1024)(128)(4,1)} %bitcast.430), calls=%async_computation.21 | async-start | bytes 8388608
  588.2 37.8 %collective-permute-start.7 = (bf16[512,1536]{0,1:T(8,128)(2,1)}, bf16[512,1536]{0,1:T(8,128)(2,1)}, u32[]{:S(2)}, u32[]{:S(2)}) collective-permute-start(bf16[512,1536]{0,1:T(8,128)(2,1)} %fusion.75), channel_id=1, source_target_pairs={{0,8},{8,0},{16,24},{24,16},{1,9},{9,1},{17,25},{25,17},{2,10},{10... | collective-permute-start | bytes 4718600 | tf_op jit(solution)/shard_map/ppermute | solution.py:53
  611.1 131.8 %collective-permute-start.14 = (bf16[512,4608]{1,0:T(8,128)(2,1)}, bf16[512,4608]{1,0:T(8,128)(2,1)}, u32[]{:S(2)}, u32[]{:S(2)}) collective-permute-start(bf16[512,4608]{1,0:T(8,128)(2,1)} %pad_maximum_fusion.2), channel_id=1, source_target_pairs={{0,8},{8,0},{16,24},{24,16},{1,9},{9,1},{17,25},{25,17},{2,10},{10... | collective-permute-start | bytes 14155784 | tf_op jit(solution)/shard_map/ppermute | solution.py:53
  628.8 38.3 %copy-start.39 = (bf16[512,768]{1,0:T(8,128)(2,1)}, bf16[512,768]{1,0:T(8,128)(2,1)S(1)}, u32[]{:S(2)}) copy-start(bf16[512,768]{1,0:T(8,128)(2,1)S(1)} %copy.113) | copy-start | bytes 2359300
  632.7 34.3 %copy-start.41 = (bf16[512,768]{1,0:T(8,128)(2,1)}, bf16[512,768]{1,0:T(8,128)(2,1)S(1)}, u32[]{:S(2)}) copy-start(bf16[512,768]{1,0:T(8,128)(2,1)S(1)} %copy.112) | copy-start | bytes 2359300
  635.1 31.9 %copy-start.43 = (bf16[512,768]{1,0:T(8,128)(2,1)}, bf16[512,768]{1,0:T(8,128)(2,1)S(1)}, u32[]{:S(2)}) copy-start(bf16[512,768]{1,0:T(8,128)(2,1)S(1)} %copy.111) | copy-start | bytes 2359300
  639.2 25.8 %collective-permute-start.13 = (bf16[512,3840]{1,0:T(8,128)(2,1)}, bf16[512,3840]{1,0:T(8,128)(2,1)S(1)}, u32[]{:S(2)}, u32[]{:S(2)}) collective-permute-start(bf16[512,3840]{1,0:T(8,128)(2,1)} %constant_dynamic-update-slice_fusion.7), channel_id=1, source_target_pairs={{0,8},{8,0},{16,24},{24,16},{1,9},{9,1},{17,25},{25,17},{2,10},{10... | collective-permute-start | bytes 11796488 | tf_op jit(solution)/shard_map/ppermute | solution.py:53
  639.5 15.2 %slice-start.14 = ((s8[4718592]{0:T(1024)(128)(4,1)}), s8[4194304]{0:T(1024)(128)(4,1)S(1)}, s32[]{:S(2)}) async-start(s8[4718592]{0:T(1024)(128)(4,1)} %bitcast.484), calls=%async_computation.24 | async-start | bytes 8388608
  643.9 16.4 %slice-start.22 = ((s8[4718592]{0:T(1024)(128)(4,1)}), s8[524288]{0:T(1024)(128)(4,1)S(1)}, s32[]{:S(2)}) async-start(s8[4718592]{0:T(1024)(128)(4,1)} %bitcast.496), calls=%async_computation.32 | async-start | bytes 1048576
  653.0 36.7 %copy-start.26 = (bf16[512,768]{1,0:T(8,128)(2,1)}, bf16[512,768]{1,0:T(8,128)(2,1)S(1)}, u32[]{:S(2)}) copy-start(bf16[512,768]{1,0:T(8,128)(2,1)S(1)} %get-tuple-element.186) | copy-start | bytes 2359300
  689.7 238.2 %reduce-scatter.11.cloned.1.call-start = ((), (), s32[]{:S(2)}) async-start(), calls=%async_computation.7 | async-start | bytes 5308416 | tf_op jit(solution)/shard_map/reduce_scatter | solution.py:459
  714.6 18.5 %slice-start.6 = ((s8[6291456]{0:T(1024)(128)(4,1)}), s8[4194304]{0:T(1024)(128)(4,1)S(1)}, s32[]{:S(2)}) async-start(s8[6291456]{0:T(1024)(128)(4,1)} %bitcast.408), calls=%async_computation.16 | async-start | bytes 8388608
  740.6 27.1 %copy-start.12 = (f32[512,2,12,64]{0,3,2,1:T(8,128)}, f32[512,2,12,64]{0,3,2,1:T(8,128)S(1)}, u32[]{:S(2)}) copy-start(f32[512,2,12,64]{0,3,2,1:T(8,128)S(1)} %pad_maximum_fusion.4) | copy-start | bytes 9437188
  767.6 213.1 %reduce-scatter.5.cloned.1.call-start = ((), (), s32[]{:S(2)}) async-start(), calls=%async_computation.4 | async-start | bytes 5308416 | tf_op jit(solution)/shard_map/reduce_scatter | solution.py:459
  771.8 16.1 %collective-permute-start.8 = (bf16[512,1536]{0,1:T(8,128)(2,1)}, bf16[512,1536]{0,1:T(8,128)(2,1)}, u32[]{:S(2)}, u32[]{:S(2)}) collective-permute-start(bf16[512,1536]{0,1:T(8,128)(2,1)} %fusion.71), channel_id=1, source_target_pairs={{0,8},{8,0},{16,24},{24,16},{1,9},{9,1},{17,25},{25,17},{2,10},{10... | collective-permute-start | bytes 4718600 | tf_op jit(solution)/shard_map/ppermute | solution.py:53
  802.7 11.2 collective-permute-start.11
  842.9 236.4 %reduce-scatter.7.cloned.1.call-start = ((), (), s32[]{:S(2)}) async-start(), calls=%async_computation.5 | async-start | bytes 5308416 | tf_op jit(solution)/shard_map/reduce_scatter | solution.py:459
  853.1 8.0 collective-permute-start.12
  879.9 331.3 %all-reduce.8.cloned.1.call-start = ((), (), s32[]{:S(2)}) async-start(), calls=%async_computation.8 | async-start | bytes 180224 | tf_op jit(solution)/shard_map/psum | solution.py:490
  883.4 11.2 collective-permute-start.6
  884.7 18.3 %collective-permute-start.10 = (bf16[256,768]{1,0:T(8,128)(2,1)S(1)}, bf16[256,768]{1,0:T(8,128)(2,1)S(1)}, u32[]{:S(2)}, u32[]{:S(2)}) collective-permute-start(bf16[256,768]{1,0:T(8,128)(2,1)S(1)} %broadcast_select_fusion.23), channel_id=1, source_target_pairs={{0,24},{8,16},{16,8},{24,0},{1,25},{9,17},{17,9},{25,1},{2,26},{10... | collective-permute-start | bytes 1179656 | tf_op jit(solution)/shard_map/ppermute | solution.py:49
  981.9 101.3 %copy-start.29 = (bf16[256,768]{1,0:T(8,128)(2,1)S(1)}, bf16[256,768]{1,0:T(8,128)(2,1)}, u32[]{:S(2)}) copy-start(bf16[256,768]{1,0:T(8,128)(2,1)} %copy-done.28) | copy-start | bytes 1179652
  981.9 101.3 %copy-start.31 = (bf16[256,768]{1,0:T(8,128)(2,1)S(1)}, bf16[256,768]{1,0:T(8,128)(2,1)}, u32[]{:S(2)}) copy-start(bf16[256,768]{1,0:T(8,128)(2,1)} %copy-done.30) | copy-start | bytes 1179652
  981.9 101.3 %copy-start.164 = (f32[512]{0:T(512)S(1)}, f32[512]{0:T(512)}, u32[]{:S(2)}) copy-start(f32[512]{0:T(512)} %copy-done.162) | copy-start | bytes 6148
  981.9 101.3 %copy-start.168 = (f32[512]{0:T(512)S(1)}, f32[512]{0:T(512)}, u32[]{:S(2)}) copy-start(f32[512]{0:T(512)} %add_rsqrt_fusion.3) | copy-start | bytes 6148
  981.9 101.3 %copy-start.173 = (f32[768]{0:T(1024)S(1)}, f32[768]{0:T(1024)}, u32[]{:S(2)}) copy-start(f32[768]{0:T(1024)} %get-tuple-element.162) | copy-start | bytes 9220
  1081.7 130.6 %collective-permute-start.15 = (bf16[2,384,768]{2,1,0:T(8,128)(2,1)}, bf16[2,384,768]{2,1,0:T(8,128)(2,1)}, u32[]{:S(2)}, u32[]{:S(2)}) collective-permute-start(bf16[2,384,768]{2,1,0:T(8,128)(2,1)} %broadcast_select_fusion.12), channel_id=1, source_target_pairs={{0,16},{8,24},{16,0},{24,8},{1,17},{9,25},{17,1},{25,9},{2,18},{10... | collective-permute-start | bytes 3538952 | tf_op jit(solution)/shard_map/ppermute | solution.py:57
  1095.3 121.0 %collective-permute-start.9 = (bf16[256,768]{1,0:T(8,128)(2,1)S(1)}, bf16[256,768]{1,0:T(8,128)(2,1)S(1)}, u32[]{:S(2)}, u32[]{:S(2)}) collective-permute-start(bf16[256,768]{1,0:T(8,128)(2,1)S(1)} %broadcast_select_fusion.27), channel_id=1, source_target_pairs={{0,24},{8,16},{16,8},{24,0},{1,25},{9,17},{17,9},{25,1},{2,26},{10... | collective-permute-start | bytes 1179656 | tf_op jit(solution)/shard_map/ppermute | solution.py:49
  1214.2 2.1 collective-permute-start.16
  1235.2 5.9 collective-permute-start.17
  1238.5 7.2 collective-permute-start.18
  (222 other events, 944.5 us)
Sparse Core Ops, SparseCore 0:
  77.3 225.1 all-gather.2
  689.8 93.5 reduce-scatter.8
  787.1 95.0 reduce-scatter.10
  885.7 95.0 reduce-scatter.4
  984.3 94.9 reduce-scatter.6
  1092.1 118.9 all-reduce.7

commit v2 on v1

v2 whole, which is shorter than its diff:
```python
import functools
import math

import jax
import jax.numpy as jnp
from jax import lax
from jax.experimental import pallas as pl
from jax.experimental.pallas import tpu as pltpu
from jax.sharding import PartitionSpec as P

D = 768
HEADS = 12
HEAD = 64
FF = 3072
HIST = 20
SEQ_SHORT = 256
VEC = 7 * D

eps_norm = 1e-05
rope_base = 10000.0
masked_score = -1e30
beta_one = 0.9
beta_two = 0.95
weight_decay = 0.1
adam_eps = 1e-08
adam_steps = 1000.0
f32 = jnp.float32
bf16 = jnp.bfloat16

ATT_VECS = [(0, D), (D, D), (2 * D + 3 * D * D, 3 * D), (5 * D + 4 * D * D, D)]
MLP_VECS = [(0, D), (D, D), (2 * D + D * FF, FF), (2 * D + FF + 2 * D * FF, D)]


class Plan:
    def __init__(self, batch_count, shard):
        self.nb = batch_count
        self.shard = shard
        self.tile = 8 * D * D // batch_count
        nb, tile = self.nb, self.tile
        self.rows = tile // D
        self.up_rows = tile // FF
        self.joint_rows = tile // (3 * D)
        self.mlp_start = [2 * D + tile * b + (FF if 2 * b >= nb else 0) for b in range(nb)]
        self.att_start = [2 * D + tile * b + (3 * D if 8 * b >= 3 * nb else 0) for b in range(nb)]
        low = high = 0
        for starts, count in ((self.mlp_start, nb), (self.att_start, nb // 2)):
            for b in range(count):
                low = max(low, shard * b - starts[b])
                high = max(high, starts[b] + tile - shard * (b + 1))
        self.low, self.high = low, high


def swap_sections(array):
    return lax.ppermute(array, "section", [(i, 3 - i) for i in range(4)])


def swap_cores(array):
    return lax.ppermute(array, "section", [(i, i ^ 1) for i in range(4)])


def swap_planes(array):
    return lax.ppermute(array, "section", [(i, i ^ 2) for i in range(4)])


def rotation(position):
    half = HEAD // 2
    inverse = rope_base ** (-jnp.arange(half, dtype=f32) / half)
    angles = position.astype(f32)[:, None] * inverse[None, :]
    cosine, sine = jnp.cos(angles), jnp.sin(angles)
    return jnp.concatenate([cosine] * 4, axis=1), jnp.concatenate([-sine, sine] * 2, axis=1)


def adamw(param, grad, first, second, decay):
    first_new = beta_one * first + (1.0 - beta_one) * grad
    second_new = beta_two * second + (1.0 - beta_two) * grad * grad
    first_hat = first_new / (1.0 - beta_one**adam_steps)
    second_hat = second_new / (1.0 - beta_two**adam_steps)
    direction = first_hat / (jnp.sqrt(second_hat) + adam_eps) + decay * param
    return (direction, first_new, second_new)


def dot(a, b):
    return jnp.dot(a, b, preferred_element_type=f32)


def dot_tn(a, b):
    return lax.dot_general(a, b, (((0,), (0,)), ((), ())), preferred_element_type=f32)


def dot_nt(a, b):
    return lax.dot_general(a, b, (((1,), (1,)), ((), ())), preferred_element_type=f32)


def gather_blocks(plan, block, vecs):
    nb, rows = plan.nb, plan.rows
    sent = jnp.concatenate([block, vecs], axis=0)
    gathered = lax.all_gather(sent, ("section", "batch"), axis=0, tiled=False)
    gathered = gathered.reshape(2, 2, nb, sent.shape[0], D)
    blocks = nb * 3 // 8
    tiles = gathered[:, 0, :, :rows]
    joint = tiles[:, :blocks].reshape(2, blocks, 2, 3, plan.joint_rows // 2, D)
    joint = joint.transpose(0, 1, 2, 4, 3, 5).reshape(2, 6, 128, 3, D)
    joint = joint.transpose(0, 1, 3, 2, 4).reshape(2, 3, D, D)
    att = jnp.concatenate([joint, tiles[:, blocks : nb // 2].reshape(2, 1, D, D)], axis=1)
    tiles = gathered[:, 1, :, :rows]
    up = tiles[:, : nb // 2].reshape(2, nb // 2, FF // D, plan.up_rows, D)
    up = up.transpose(0, 1, 3, 2, 4).reshape(2, 4, 192, 4, D)
    up = up.transpose(0, 1, 3, 2, 4).reshape(2, 4, D, D)
    mlp = jnp.concatenate([up, tiles[:, nb // 2 :].reshape(2, 4, D, D)], axis=1)
    return att, mlp, gathered[:, :, :, rows:].reshape(4, nb, -1, D)


class Place:
    pass


def pack_weights(plan, place, params):
    nb, shard, tile = plan.nb, plan.shard, plan.tile
    own = params.reshape(-1).astype(bf16)
    parts = []
    if plan.low:
        parts.append(lax.ppermute(own[-plan.low :], "batch", [(i, i + 1) for i in range(nb - 1)]))
    parts.append(own)
    if plan.high:
        parts.append(lax.ppermute(own[: plan.high], "batch", [(i, i - 1) for i in range(1, nb)]))
    wide = jnp.concatenate(parts)
    b, mlp = place.b, place.mlp
    mlp_offset = jnp.array([plan.low + plan.mlp_start[i] - shard * i for i in range(nb)])
    att_offset = jnp.array(
        [plan.low + (plan.att_start[i] - shard * i if 2 * i < nb else 0) for i in range(nb)]
    )
    offset = jnp.where(mlp, mlp_offset[b], att_offset[b])
    flat = lax.dynamic_slice(wide, (offset,), (tile,))
    rows = plan.rows
    plain = flat.reshape(rows, D)
    up = flat.reshape(plan.up_rows, FF // D, D).transpose(1, 0, 2).reshape(rows, D)
    joint = flat.reshape(2, plan.joint_rows // 2, 3, D).transpose(0, 2, 1, 3).reshape(rows, D)
    is_up = mlp & (2 * b < nb)
    is_joint = jnp.logical_not(mlp) & (8 * b < 3 * nb)
    block = jnp.where(is_up, up, jnp.where(is_joint, joint, plain))
    padded = jnp.concatenate([jnp.zeros((FF,), bf16), own, jnp.zeros((FF,), bf16)])

    def vectors(pieces):
        out = []
        for start, length in pieces:
            at = jnp.clip(start - shard * b + FF, 0, shard + FF)
            out.append(lax.dynamic_slice(padded, (at,), (length,)))
        total = sum(length for _, length in pieces)
        out.append(jnp.zeros((VEC - total,), bf16))
        return jnp.concatenate(out)

    vecs = jnp.where(mlp, vectors(MLP_VECS), vectors(ATT_VECS))
    lines = vecs.reshape(VEC // D, D)
    return block, jnp.concatenate([lines, jnp.zeros((16 - VEC // D, D), bf16)], axis=0)


def split_vecs(lines, pieces):
    flat = lines.reshape(-1)
    out, at = [], 0
    for _, length in pieces:
        out.append(flat[at : at + length])
        at += length
    return out


MESH = pl.DeviceIdType.MESH


def gather_kernel(plan, block_ref, vec_ref, att_ref, mlp_ref, vecs_ref, att_in, mlp_in, vec_in, vec_out, sent, kept):
    section, b = lax.axis_index("section"), lax.axis_index("batch")
    plane, core = section // 2, section % 2
    z, x = b // 2, b % 2
    nb = plan.nb
    count = 4 * nb
    me = section * nb + b

    barrier = pltpu.get_barrier_semaphore()

    def greet(k, carry):
        to = lax.rem(me + k, count)
        pl.semaphore_signal(barrier, 1, device_id=(to // nb, to % nb), device_id_type=MESH)
        return carry

    lax.fori_loop(1, count, greet, 0)
    pl.semaphore_wait(barrier, count - 1)

    def vec_copy(k):
        to = lax.rem(me + k, count)
        return pltpu.make_async_remote_copy(
            vec_ref,
            vecs_ref.at[me],
            vec_out.at[k],
            vec_in.at[k],
            device_id=(to // nb, to % nb),
            device_id_type=MESH,
        )

    def each(fn):
        def body(k, carry):
            fn(vec_copy(k))
            return carry

        lax.fori_loop(1, count, body, 0)

    half = plan.rows // 2
    pending = []
    slot = [0]

    def when(cond, fn):
        if cond is True:
            fn()
        else:
            pl.when(cond)(fn)

    def run(out_ref, arrive, first, second):
        def part(layer, tile, unit):
            return out_ref.at[layer, tile, pl.ds(unit * half, half)]

        def send(cond, src, layer, tile, unit, to):
            index = slot[0]
            slot[0] += 1
            copy = pltpu.make_async_remote_copy(
                src,
                part(layer, tile, unit),
                sent.at[index],
                arrive.at[layer, tile, unit],
                device_id=to,
                device_id_type=MESH,
            )
            when(cond, copy.start)
            mine.append((cond, copy))

        def wait(cond, layer, tile, unit):
            copy = pltpu.make_async_remote_copy(
                part(layer, tile, unit),
                part(layer, tile, unit),
                sent.at[0],
                arrive.at[layer, tile, unit],
                device_id=(section, b ^ 1),
                device_id_type=MESH,
            )
            when(cond, copy.wait_recv)

        mine = []
        to_x, to_y, to_core = (section, b ^ 1), (section ^ 2, b), (section ^ 1, b)
        far = 1 - plane

        def spread(step, cond, from_block):
            column, owned, hops = first[step], second[step][0], second[step][1]
            tile = 2 * column + x
            for unit in range(2):
                if not from_block:
                    wait(cond if owned is None else jnp.logical_not(owned) & cond, plane, tile, unit)
            for unit in range(2):
                for source_cond, src in (
                    (owned, block_ref.at[pl.ds(unit * half, half)]),
                    (None if owned is True else (True if owned is None else jnp.logical_not(owned)), part(plane, tile, unit)),
                ):
                    if source_cond is None:
                        continue

                    def both(c):
                        return c if source_cond is True else (source_cond if c is True else c & source_cond)

                    for hop_cond, to in hops:
                        send(both(hop_cond), src, plane, tile, unit, to)
                    send(both(True), src, plane, tile, unit, to_x)
                    send(both(True), src, plane, tile, unit, to_y)
                    send(both(True), src, plane, tile, unit, to_core)

        def corner(step):
            column = first[step]
            across, same = 2 * column + (1 - x), 2 * column + x
            for unit in range(2):
                wait(True, plane, across, unit)
                if unit == 0:
                    send(True, part(plane, across, unit), plane, across, unit, to_y)
                send(True, part(plane, across, unit), plane, across, unit, to_core)
            for unit in range(2):
                wait(True, far, same, unit)
                if unit == 1:
                    send(True, part(far, same, unit), far, same, unit, to_x)
                send(True, part(far, same, unit), far, same, unit, to_core)

        def last(step):
            tile = 2 * first[step] + (1 - x)
            for unit in range(2):
                wait(True, far, tile, unit)
                send(True, part(far, tile, unit), far, tile, unit, to_core)

        steps = len(first)
        for step in range(steps):
            spread(step, True, second[step][0] is True)
            if step:
                corner(step - 1)
        corner(steps - 1)
        for step in range(steps):
            last(step)
        pending.append(mine)

    each(lambda copy: copy.start())
    up, down = (section, jnp.minimum(b + 2, nb - 1)), (section, jnp.maximum(b - 2, 0))

    @pl.when(core == 0)
    def _():
        own = pltpu.make_async_copy(block_ref, att_ref.at[plane, jnp.minimum(b, nb // 2 - 1)], kept)
        pl.when(z < 2)(own.start)
        first = [jnp.where(z == 0, 0, 1), jnp.where(z == 0, 1, 0)]
        slot[0] = 0
        run(
            att_ref,
            att_in,
            first,
            [
                (z < 2, [(z < 3, up), (z == 1, down)]),
                (None, [((z == 1) | (z == 2), up)]),
            ],
        )
        for layer in range(2):
            for tile in range(nb):
                for unit in range(2):
                    other = mlp_ref.at[layer, tile, pl.ds(unit * half, half)]
                    pltpu.make_async_remote_copy(
                        other, other, sent.at[0], mlp_in.at[layer, tile, unit],
                        device_id=(section ^ 1, b), device_id_type=MESH,
                    ).wait_recv()
        for cond, copy in pending[-1]:
            when(cond, copy.wait_send)
        pl.when(z < 2)(own.wait)

    @pl.when(core == 1)
    def _():
        own = pltpu.make_async_copy(block_ref, mlp_ref.at[plane, b], kept)
        own.start()
        low = z < 2
        end = (z == 0) | (z == 3)
        middle = jnp.logical_not(end)

        def at(t):
            return jnp.where(low, t, 3 - t)

        inward = (section, jnp.where(low, jnp.minimum(b + 2, nb - 1), jnp.maximum(b - 2, 0)))
        outward = (section, jnp.where(low, jnp.maximum(b - 2, 0), jnp.minimum(b + 2, nb - 1)))
        slot[0] = 0
        run(
            mlp_ref,
            mlp_in,
            [z, jnp.where(end, at(1), at(0)), at(2), at(3)],
            [
                (True, [(True, inward), (middle, outward)]),
                (None, [(middle, inward)]),
                (None, [(middle, outward)]),
                (None, [(middle, outward)]),
            ],
        )
        for layer in range(2):
            for tile in range(nb // 2):
                for unit in range(2):
                    other = att_ref.at[layer, tile, pl.ds(unit * half, half)]
                    pltpu.make_async_remote_copy(
                        other, other, sent.at[0], att_in.at[layer, tile, unit],
                        device_id=(section ^ 1, b), device_id_type=MESH,
                    ).wait_recv()
        for cond, copy in pending[-1]:
            when(cond, copy.wait_send)
        own.wait()

    each(lambda copy: copy.wait())
    here = pltpu.make_async_copy(vec_ref, vecs_ref.at[me], kept)
    here.start()
    here.wait()


def gather_weights(plan, block, vecs):
    nb, rows = plan.nb, plan.rows
    body = functools.partial(gather_kernel, plan)
    any_spec = pl.BlockSpec(memory_space=pltpu.HBM)
    return pl.pallas_call(
        body,
        in_specs=[any_spec] * 2,
        out_specs=[any_spec] * 3,
        out_shape=[
            jax.ShapeDtypeStruct((2, nb // 2, rows, D), bf16),
            jax.ShapeDtypeStruct((2, nb, rows, D), bf16),
            jax.ShapeDtypeStruct((4 * nb,) + vecs.shape, bf16),
        ],
        scratch_shapes=[
            pltpu.SemaphoreType.DMA((2, nb // 2, 2)),
            pltpu.SemaphoreType.DMA((2, nb, 2)),
            pltpu.SemaphoreType.DMA((4 * nb,)),
            pltpu.SemaphoreType.DMA((4 * nb,)),
            pltpu.SemaphoreType.DMA((96,)),
            pltpu.SemaphoreType.DMA,
        ],
        name="gather_weights",
        compiler_params=pltpu.CompilerParams(collective_id=0, has_side_effects=True),
    )(block, vecs)


VMEM_LIMIT = 56 * 1024 * 1024


def row_spec(width):
    return pl.BlockSpec((1, width), lambda *i: (0, 0))


def whole_spec(shape):
    return pl.BlockSpec(shape, lambda *i: (0,) * len(shape))


SMEM_SPEC = pl.BlockSpec(memory_space=pltpu.SMEM)


def call(body, name, grid, in_specs, outs, scratch, flops):
    return pl.pallas_call(
        body,
        grid=grid,
        in_specs=in_specs,
        out_specs=[spec for _, _, spec in outs],
        out_shape=[jax.ShapeDtypeStruct(shape, dtype) for shape, dtype, _ in outs],
        scratch_shapes=scratch,
        name=name,
        cost_estimate=pl.CostEstimate(
            flops=int(flops), bytes_accessed=4 * D * D, transcendentals=0
        ),
        compiler_params=pltpu.CompilerParams(vmem_limit_bytes=VMEM_LIMIT),
    )


def partner(x):
    width = x.shape[-1]
    lane = lax.broadcasted_iota(jnp.int32, x.shape, x.ndim - 1)
    ahead = pltpu.roll(x, width - HEAD // 2, x.ndim - 1)
    behind = pltpu.roll(x, HEAD // 2, x.ndim - 1)
    return jnp.where(lane % HEAD < HEAD // 2, ahead, behind)


def turned(x, cosine, sine, back):
    parts = []
    for at in range(0, x.shape[-1], 128):
        piece = x[:, at : at + 128]
        other = partner(piece) * sine
        parts.append(piece * cosine - other if back else piece * cosine + other)
    return jnp.concatenate(parts, axis=-1) if len(parts) > 1 else parts[0]


def unit_rows(values):
    center = values - jnp.mean(values, axis=-1, keepdims=True)
    scale = lax.rsqrt(jnp.mean(center * center, axis=-1, keepdims=True) + eps_norm)
    return center * scale, scale


def column_sum(x):
    return jnp.sum(x, axis=0, keepdims=True)


def qkv_kernel(x_ref, gain_ref, bias_ref, w_ref, b_ref, cos_ref, sin_ref, n_ref, q_ref, kv_ref):
    step = pl.program_id(0)

    @pl.when(step == 0)
    def _():
        unit, _ = unit_rows(x_ref[...].astype(f32))
        n_ref[...] = (unit * gain_ref[...] + bias_ref[...]).astype(bf16)

    joint = dot(n_ref[...], matrix(w_ref)) + b_ref[...]

    @pl.when(step < 2)
    def _():
        q_ref[...] = (turned(joint, cos_ref[...], sin_ref[...], False) * HEAD**-0.5).astype(bf16)

    @pl.when((step >= 2) & (step < 4))
    def _():
        kv_ref[...] = turned(joint, cos_ref[...], sin_ref[...], False).astype(bf16)

    @pl.when(step >= 4)
    def _():
        kv_ref[...] = joint.astype(bf16)


def qkv_call(layer, x, gain, bias, att, b, cosine, sine):
    rows = x.shape[0]
    wide = D // 2
    return call(
        qkv_kernel,
        "qkv_rows",
        (6,),
        [
            whole_spec((rows, D)),
            row_spec(D),
            row_spec(D),
            joint_spec(layer, wide),
            pl.BlockSpec((1, wide), lambda i: (0, i)),
            whole_spec((rows, 128)),
            whole_spec((rows, 128)),
        ],
        [
            ((rows, D), bf16, whole_spec((rows, D))),
            ((rows, D), bf16, pl.BlockSpec((rows, wide), lambda i: (0, jnp.minimum(i, 1)))),
            ((rows, 2 * D), bf16, pl.BlockSpec((rows, wide), lambda i: (0, jnp.maximum(i - 2, 0)))),
        ],
        [],
        2 * rows * D * 3 * D,
    )(x, gain, bias, att.reshape(2, 8, 3, 128, D), b, cosine, sine)


def joint_spec(layer, wide):
    per = D // wide

    def index(i):
        return (layer, 0, i // per, 0, i % per)

    return pl.BlockSpec((1, 6, 1, 128, wide), index)


def out_spec(layer):
    return pl.BlockSpec((1, 1, D, D), lambda i: (layer, 3, 0, 0))


def up_spec(layer):
    per = D // FF_BLOCK
    return pl.BlockSpec(
        (1, 4, 1, 192, FF_BLOCK), lambda i: (layer, 0, i // per, 0, i % per)
    )


def down_spec(layer):
    return pl.BlockSpec((1, FF_BLOCK, D), lambda i: (layer, FF // FF_BLOCK + i, 0))


def matrix(ref):
    return ref[...].reshape(-1, ref.shape[-1])


def fill_mask(meta_ref, mask_ref, span):
    for part in range(2):
        width = (2 + 2 * part) * span
        shape = (span, width)
        rows = meta_ref[2 + part] + lax.broadcasted_iota(jnp.int32, shape, 0)
        columns = lax.broadcasted_iota(jnp.int32, shape, 1)
        lowest = jnp.where(meta_ref[1] == 1, rows - rows % SEQ_SHORT, 0)
        ok = (columns <= rows) & (columns >= lowest)
        mask_ref[pl.ds(part * span, span), pl.ds(0, width)] = jnp.where(ok, 0.0, masked_score)


def fill_keys(meta_ref, own_ref, other_ref, full_ref, span):
    @pl.when(meta_ref[0] == 1)
    def _():
        full_ref[:span] = own_ref[:span]
        full_ref[span : 3 * span] = other_ref[...]
        full_ref[3 * span :] = own_ref[span:]

    @pl.when(meta_ref[0] != 1)
    def _():
        full_ref[:span] = other_ref[:span]
        full_ref[span : 3 * span] = own_ref[...]
        full_ref[3 * span :] = other_ref[span:]


def head_lanes(x, head):
    lane = lax.broadcasted_iota(jnp.int32, x.shape, 1)
    return jnp.where(lane // HEAD == head, x, jnp.zeros_like(x))


def att_kernel(meta_ref, q_ref, k_ref, v_ref, ko_ref, vo_ref, o_ref, lse_ref, mask, kf, vf):
    span = q_ref.shape[0] // 2

    @pl.when(pl.program_id(0) == 0)
    def _():
        fill_mask(meta_ref, mask, span)

    fill_keys(meta_ref, k_ref, ko_ref, kf, span)
    fill_keys(meta_ref, v_ref, vo_ref, vf, span)
    for part in range(2):
        width = (2 + 2 * part) * span
        rows = pl.ds(part * span, span)
        outs, lses = [], []
        for head in range(2):
            q = head_lanes(q_ref[rows], head)
            scores = dot_nt(q, kf[:width]) + mask[rows, :width]
            top = jnp.max(scores, axis=-1, keepdims=True)
            expo = jnp.exp(scores - top)
            total = jnp.sum(expo, axis=-1, keepdims=True)
            outs.append(dot(expo.astype(bf16), vf[:width]) * (1.0 / total))
            lses.append(top + jnp.log(total))
        lane = lax.broadcasted_iota(jnp.int32, (span, 128), 1)
        o_ref[rows] = jnp.where(lane < HEAD, outs[0], outs[1]).astype(bf16)
        lse_ref[0, rows] = jnp.where(lane < HEAD, lses[0], lses[1])


def pair_spec(rows, shift=0):
    return pl.BlockSpec((rows, 128), lambda i: (0, i + shift))


def att_call(meta, q, kv, kv_other):
    rows = q.shape[0]
    pairs = HEADS // 2
    return call(
        att_kernel,
        "attention_rows",
        (pairs,),
        [
            SMEM_SPEC,
            pair_spec(rows),
            pair_spec(rows),
            pair_spec(rows, pairs),
            pair_spec(rows),
            pair_spec(rows, pairs),
        ],
        [
            ((rows, D), bf16, pair_spec(rows)),
            ((pairs, rows, 128), f32, pl.BlockSpec((1, rows, 128), lambda i: (i, 0, 0))),
        ],
        [
            pltpu.VMEM((rows, 2 * rows), f32),
            pltpu.VMEM((2 * rows, 128), bf16),
            pltpu.VMEM((2 * rows, 128), bf16),
        ],
        20 * rows * rows * D,
    )(meta, q, kv, kv, kv_other, kv_other)


FF_BLOCK = 384


def mlp_kernel(
    last_layer,
    mix_ref,
    x_ref,
    o_ref,
    ow_ref,
    ob_ref,
    gain_ref,
    bias_ref,
    up_ref,
    ub_ref,
    down_ref,
    db_ref,
    past_ref,
    *rest,
):
    if last_layer:
        c_ref, cot_ref, h_ref, n_ref, act_ref, slope_ref, y_ref, sums_ref, acc = rest
    else:
        h_ref, n_ref, act_ref, slope_ref, y_ref, c_ref, acc = rest
    step = pl.program_id(0)

    @pl.when(step == 0)
    def _():
        h = x_ref[...].astype(f32) + dot(o_ref[...], matrix(ow_ref)) + ob_ref[...]
        h_ref[...] = h.astype(bf16)
        unit, _ = unit_rows(h_ref[...].astype(f32))
        n_ref[...] = (unit * gain_ref[...] + bias_ref[...]).astype(bf16)
        acc[...] = h_ref[...].astype(f32) + db_ref[...]

    pre = dot(n_ref[...], matrix(up_ref)) + ub_ref[...]
    cdf = 0.5 + 0.5 * lax.erf(pre * (2.0**-0.5))
    act = (pre * cdf).astype(bf16)
    act_ref[...] = act
    slope_ref[...] = (cdf + pre * jnp.exp(-0.5 * pre * pre) * (2.0 * math.pi) ** -0.5).astype(bf16)
    acc[...] += dot(act, matrix(down_ref))

    @pl.when(step == pl.num_programs(0) - 1)
    def _():
        x = acc[...]
        past = past_ref[...].astype(f32)
        if last_layer:
            carried = c_ref[...].astype(f32)
            y_ref[...] = (past + mix_ref[1] * carried + mix_ref[2] * x).astype(bf16)
            g = cot_ref[...].astype(f32) * mix_ref[3]
            sums_ref[0:1] = column_sum(g * carried)
            sums_ref[1:2] = column_sum(g * x)
            sums_ref[2:] = jnp.zeros((6, D), f32)
        else:
            y_ref[...] = (past + mix_ref[0] * x).astype(bf16)
            c_ref[...] = x.astype(bf16)


def mlp_call(layer, mix, x, o, att, out_b, gain, bias, mlp, up_b, down_b, past, extra):
    rows = x.shape[0]
    last_layer = layer == 1
    full = whole_spec((rows, D))
    blocks = pl.BlockSpec((rows, FF_BLOCK), lambda i: (0, i))
    outs = [
        ((rows, D), bf16, full),
        ((rows, D), bf16, full),
        ((rows, FF), bf16, blocks),
        ((rows, FF), bf16, blocks),
        ((rows, D), bf16, full),
    ]
    outs.append(((8, D), f32, whole_spec((8, D))) if last_layer else ((rows, D), bf16, full))
    return call(
        functools.partial(mlp_kernel, last_layer),
        "feed_forward_rows",
        (FF // FF_BLOCK,),
        [
            SMEM_SPEC,
            full,
            full,
            out_spec(layer),
            row_spec(D),
            row_spec(D),
            row_spec(D),
            up_spec(layer),
            pl.BlockSpec((1, FF_BLOCK), lambda i: (0, i)),
            down_spec(layer),
            row_spec(D),
            full,
        ]
        + [full] * len(extra),
        outs,
        [pltpu.VMEM((rows, D), f32)],
        2 * rows * D * (D + 2 * FF),
    )(
        mix,
        x,
        o,
        att,
        out_b,
        gain,
        bias,
        mlp.reshape(2, 8, 4, 192, D),
        up_b,
        mlp.reshape(2, 8 * D, D),
        down_b,
        past,
        *extra,
    )


def norm_back(values, gain, grad):
    unit, scale = unit_rows(values)
    inner = grad * gain
    back = scale * (
        inner
        - jnp.mean(inner, axis=-1, keepdims=True)
        - unit * jnp.mean(inner * unit, axis=-1, keepdims=True)
    )
    return back, column_sum(grad * unit), column_sum(grad)


def mlp_back_kernel(
    last_layer,
    mix_ref,
    cot_ref,
    dy_ref,
    h_ref,
    gain_ref,
    up_ref,
    down_ref,
    slope_ref,
    ow_ref,
    er_ref,
    dpre_ref,
    dub_ref,
    dh_ref,
    datt_ref,
    sums_ref,
    e_s,
    acc,
):
    step = pl.program_id(0)

    @pl.when(step == 0)
    def _():
        g = cot_ref[...].astype(f32) * mix_ref[3]
        if last_layer:
            e = mix_ref[2] * g
        else:
            carried = (mix_ref[1] * g).astype(bf16).astype(f32)
            e = mix_ref[0] * dy_ref[...].astype(f32) + carried
        e_s[...] = e
        er_ref[...] = e.astype(bf16)
        acc[...] = jnp.zeros_like(acc)

    dact = dot_nt(er_ref[...], matrix(down_ref))
    dpre = (dact * slope_ref[...].astype(f32)).astype(bf16)
    dpre_ref[...] = dpre
    dub_ref[...] = column_sum(dpre.astype(f32))
    acc[...] += dot_nt(dpre, matrix(up_ref))

    @pl.when(step == pl.num_programs(0) - 1)
    def _():
        back, dgain, dbias = norm_back(h_ref[...].astype(f32), gain_ref[...], acc[...])
        dh = (e_s[...] + back).astype(bf16)
        dh_ref[...] = dh
        sums_ref[0:1] = dgain
        sums_ref[1:2] = dbias
        sums_ref[2:3] = column_sum(er_ref[...].astype(f32))
        sums_ref[3:4] = column_sum(dh.astype(f32))
        sums_ref[4:] = jnp.zeros((4, D), f32)
        datt_ref[...] = dot_nt(dh, matrix(ow_ref)).astype(bf16)


def mlp_back_call(layer, mix, cot, dy, h, gain, mlp, slope, att):
    rows = h.shape[0]
    last_layer = layer == 1
    full = whole_spec((rows, D))
    blocks = pl.BlockSpec((rows, FF_BLOCK), lambda i: (0, i))
    return call(
        functools.partial(mlp_back_kernel, last_layer),
        "feed_forward_grad_rows",
        (FF // FF_BLOCK,),
        [
            SMEM_SPEC,
            full,
            full,
            full,
            row_spec(D),
            up_spec(layer),
            down_spec(layer),
            blocks,
            out_spec(layer),
        ],
        [
            ((rows, D), bf16, full),
            ((rows, FF), bf16, blocks),
            ((1, FF), f32, pl.BlockSpec((1, FF_BLOCK), lambda i: (0, i))),
            ((rows, D), bf16, full),
            ((rows, D), bf16, full),
            ((8, D), f32, whole_spec((8, D))),
        ],
        [pltpu.VMEM((rows, D), f32), pltpu.VMEM((rows, D), f32)],
        2 * rows * D * (D + 2 * FF),
    )(
        mix,
        cot,
        dy,
        h,
        gain,
        mlp.reshape(2, 8, 4, 192, D),
        mlp.reshape(2, 8 * D, D),
        slope,
        att,
    )


def att_back_kernel(
    meta_ref,
    q_ref,
    k_ref,
    v_ref,
    ko_ref,
    vo_ref,
    do_ref,
    o_ref,
    lse_ref,
    cos_ref,
    sin_ref,
    dq_ref,
    own_ref,
    give_ref,
    mask,
    kf,
    vf,
    dkf,
    dvf,
):
    span = q_ref.shape[0] // 2

    @pl.when(pl.program_id(0) == 0)
    def _():
        fill_mask(meta_ref, mask, span)

    fill_keys(meta_ref, k_ref, ko_ref, kf, span)
    fill_keys(meta_ref, v_ref, vo_ref, vf, span)
    lane = lax.broadcasted_iota(jnp.int32, (span, 128), 1)
    for part in (1, 0):
        width = (2 + 2 * part) * span
        rows = pl.ds(part * span, span)
        product = do_ref[rows].astype(f32) * o_ref[rows].astype(f32)
        dqs = []
        dk = dv = None
        for head in range(2):
            q = head_lanes(q_ref[rows], head)
            do = head_lanes(do_ref[rows], head)
            delta = jnp.sum(head_lanes(product, head), axis=-1, keepdims=True)
            scores = dot_nt(q, kf[:width]) + mask[rows, :width]
            prob = jnp.exp(scores - lse_ref[0, rows, head * HEAD : head * HEAD + 1])
            dp = dot_nt(do, vf[:width])
            ds = (prob * (dp - delta)).astype(bf16)
            dqs.append(dot(ds, kf[:width]))
            dk_new = dot_tn(ds, q)
            dv_new = dot_tn(prob.astype(bf16), do)
            dk = dk_new if dk is None else dk + dk_new
            dv = dv_new if dv is None else dv + dv_new
        dq = jnp.where(lane < HEAD, dqs[0], dqs[1])
        dq = turned(dq, cos_ref[rows], sin_ref[rows], True) * HEAD**-0.5
        dq_ref[rows] = dq.astype(bf16)
        if part == 1:
            dkf[...] = dk
            dvf[...] = dv
        else:
            dkf[:width] += dk
            dvf[:width] += dv
    for at, full in enumerate((dkf, dvf)):

        @pl.when(meta_ref[0] == 1)
        def _():
            own_ref[at, :span] = full[:span]
            own_ref[at, span:] = full[3 * span :]
            give_ref[at] = full[span : 3 * span].astype(bf16)

        @pl.when(meta_ref[0] != 1)
        def _():
            own_ref[at] = full[span : 3 * span]
            give_ref[at, :span] = full[:span].astype(bf16)
            give_ref[at, span:] = full[3 * span :].astype(bf16)


def att_back_call(meta, q, kv, kv_other, datt, mixed, lse, cosine, sine):
    rows = q.shape[0]
    pairs = HEADS // 2
    both = pl.BlockSpec((2, rows, 128), lambda i: (0, 0, i))
    return call(
        att_back_kernel,
        "attention_grad_rows",
        (pairs,),
        [
            SMEM_SPEC,
            pair_spec(rows),
            pair_spec(rows),
            pair_spec(rows, pairs),
            pair_spec(rows),
            pair_spec(rows, pairs),
            pair_spec(rows),
            pair_spec(rows),
            pl.BlockSpec((1, rows, 128), lambda i: (i, 0, 0)),
            whole_spec((rows, 128)),
            whole_spec((rows, 128)),
        ],
        [
            ((rows, D), bf16, pair_spec(rows)),
            ((2, rows, D), f32, both),
            ((2, rows, D), bf16, both),
        ],
        [
            pltpu.VMEM((rows, 2 * rows), f32),
            pltpu.VMEM((2 * rows, 128), bf16),
            pltpu.VMEM((2 * rows, 128), bf16),
            pltpu.VMEM((2 * rows, 128), f32),
            pltpu.VMEM((2 * rows, 128), f32),
        ],
        50 * rows * rows * D,
    )(meta, q, kv, kv, kv_other, kv_other, datt, mixed, lse, cosine, sine)


def qkv_back_kernel(
    dq_ref,
    own_ref,
    got_ref,
    cos_ref,
    sin_ref,
    w_ref,
    x_ref,
    gain_ref,
    dh_ref,
    c_ref,
    dj_ref,
    djb_ref,
    dx_ref,
    sums_ref,
    acc,
):
    step = pl.program_id(0)

    @pl.when(step == 0)
    def _():
        acc[...] = jnp.zeros_like(acc)
        dj_ref[...] = dq_ref[...]

    @pl.when(step == 1)
    def _():
        dk = own_ref[0] + got_ref[0].astype(f32)
        dj_ref[...] = turned(dk, cos_ref[...], sin_ref[...], True).astype(bf16)

    @pl.when(step == 2)
    def _():
        dj_ref[...] = (own_ref[1] + got_ref[1].astype(f32)).astype(bf16)

    dj = dj_ref[...]
    djb_ref[...] = column_sum(dj.astype(f32))
    acc[...] += dot_nt(dj, matrix(w_ref))

    @pl.when(step == 2)
    def _():
        back, dgain, dbias = norm_back(x_ref[...].astype(f32), gain_ref[...], acc[...])
        dx = (dh_ref[...].astype(f32) + back).astype(bf16)
        dx_ref[...] = dx
        sums_ref[0:1] = dgain
        sums_ref[1:2] = dbias
        sums_ref[2:3] = column_sum(dx.astype(f32) * c_ref[...].astype(f32))
        sums_ref[3:] = jnp.zeros((5, D), f32)


def qkv_back_call(layer, dq, own, got, cosine, sine, att, x, gain, dh, carried):
    rows = x.shape[0]
    full = whole_spec((rows, D))
    return call(
        qkv_back_kernel,
        "qkv_grad_rows",
        (3,),
        [
            full,
            whole_spec((2, rows, D)),
            whole_spec((2, rows, D)),
            whole_spec((rows, 128)),
            whole_spec((rows, 128)),
            joint_spec(layer, D),
            full,
            row_spec(D),
            full,
            full,
        ],
        [
            ((rows, 3 * D), bf16, pl.BlockSpec((rows, D), lambda i: (0, i))),
            ((1, 3 * D), f32, pl.BlockSpec((1, D), lambda i: (0, i))),
            ((rows, D), bf16, full),
            ((8, D), f32, whole_spec((8, D))),
        ],
        [pltpu.VMEM((rows, D), f32)],
        2 * rows * D * 3 * D,
    )(
        dq,
        own,
        got,
        cosine,
        sine,
        att.reshape(2, 8, 3, 128, D),
        x,
        gain,
        dh,
        carried,
    )


def weight_grad_kernel(a_ref, b_ref, out_ref):
    out_ref[...] = dot_tn(a_ref[...], b_ref[...]).astype(bf16).reshape(out_ref.shape)


def weight_grad_call(name, a, b, a_step, b_step, out_shape, block, index):
    rows = a.shape[0]
    steps = max(a.shape[1] if a_step else D, b.shape[1] if b_step else D) // D
    return call(
        weight_grad_kernel,
        name,
        (steps,),
        [
            pl.BlockSpec((rows, D), (lambda i: (0, i)) if a_step else (lambda i: (0, 0))),
            pl.BlockSpec((rows, D), (lambda i: (0, i)) if b_step else (lambda i: (0, 0))),
        ],
        [(out_shape, bf16, pl.BlockSpec(block, index))],
        [],
        2 * rows * a.shape[1] * b.shape[1],
    )(a, b)[0]


def mlp_tiles(plan, normed, dpre, active, er):
    count = plan.nb // 2
    up = weight_grad_call(
        "up_grad",
        normed,
        dpre,
        False,
        True,
        (count, FF // D, plan.up_rows, D),
        (count, 1, plan.up_rows, D),
        lambda i: (0, i, 0, 0),
    )
    down = weight_grad_call(
        "down_grad", active, er, True, False, (FF, D), (D, D), lambda i: (i, 0)
    )
    return up.reshape(count, plan.rows, D), down.reshape(count, plan.rows, D)


def att_tiles(plan, normed, djoint, mixed, dh):
    count = plan.nb * 3 // 8
    part = plan.joint_rows // 2
    joint = weight_grad_call(
        "joint_grad",
        normed,
        djoint,
        False,
        True,
        (count, 2, 3, part, D),
        (count, 2, 1, part, D),
        lambda i: (0, 0, i, 0, 0),
    )
    out = weight_grad_call(
        "out_grad", mixed, dh, True, False, (D, D), (D, D), lambda i: (0, 0)
    )
    return joint.reshape(count, plan.rows, D), out.reshape(plan.nb // 8, plan.rows, D)


def reduce_tiles(place, tiles):
    plan = place.plan
    nb, half = plan.nb, plan.rows // 2
    tiles = jnp.concatenate(tiles, axis=0).reshape(-1, 2, half, D)
    first = place.core == 0
    keep = jnp.where(first, tiles[:, 0], tiles[:, 1])
    give = jnp.where(first, tiles[:, 1], tiles[:, 0])
    total = keep.astype(f32) + swap_cores(give).astype(f32)
    total = total.astype(bf16)
    if nb != 8:
        if total.shape[0] < nb:
            empty = jnp.zeros((nb - total.shape[0],) + total.shape[1:], bf16)
            total = jnp.concatenate([total, empty], axis=0)
        return lax.psum_scatter(total, "batch", scatter_dimension=0, tiled=True)[0]
    b = place.b

    def halve(total, bit, axis):
        low = (b & bit) == 0
        zero = lax.index_in_dim(total, 0, axis, keepdims=False)
        one = lax.index_in_dim(total, 1, axis, keepdims=False)
        got = lax.ppermute(
            jnp.where(low, one, zero), "batch", [(i, i ^ bit) for i in range(nb)]
        )
        return (jnp.where(low, zero, one).astype(f32) + got.astype(f32)).astype(bf16)

    total = halve(total.reshape(-1, 2, half, D), 1, 1)
    if total.shape[0] == 4:
        total = halve(total.reshape(2, 2, half, D), 4, 0)
    else:
        got = lax.ppermute(total, "batch", [(i, i - 4) for i in range(4, nb)])
        total = (total.astype(f32) + got.astype(f32)).astype(bf16)
    return halve(total, 2, 0)


def local(
    stream_in,
    history,
    cotangent,
    group,
    params,
    first_moment,
    second_moment,
    mix_weights,
    mix_first,
    mix_second,
):
    nb = lax.axis_size("batch")
    plan = Plan(nb, params.shape[1])
    place = Place()
    place.plan = plan
    section = lax.axis_index("section")
    b = place.b = lax.axis_index("batch")
    plane = section // 2
    place.core = section % 2
    place.mlp = section % 2 == 1
    place.outer = (section == 0) | (section == 3)
    span = place.span = stream_in.shape[0] // 2
    low_half = plane == 0
    place.kind = jnp.where(low_half, group[0], group[1])
    place.starts = (
        jnp.where(place.outer, 0, 1) * span,
        jnp.where(place.outer, 3, 2) * span,
    )
    tokens = stream_in.shape[0] * 4 * nb
    grad_scale = float(tokens) ** -0.5

    def to_compute(array):
        mine = jnp.where(low_half, array[..., :span, :], array[..., span:, :])
        other = jnp.where(low_half, array[..., span:, :], array[..., :span, :])
        got = swap_sections(other)
        return jnp.concatenate(
            [jnp.where(low_half, mine, got), jnp.where(low_half, got, mine)], axis=-2
        )

    to_owner = to_compute

    block, vecs = pack_weights(plan, place, params)
    if nb == 8:
        att, mlp, vec_parts = gather_weights(plan, block, vecs)
        vec_parts = vec_parts.reshape(4, nb, -1, D)
    else:
        att, mlp, vec_parts = gather_blocks(plan, block, vecs)
    all_vecs = jnp.sum(vec_parts.astype(f32), axis=1)
    att_vecs = [split_vecs(all_vecs[2 * layer], ATT_VECS) for layer in range(2)]
    mlp_vecs = [split_vecs(all_vecs[2 * layer + 1], MLP_VECS) for layer in range(2)]

    first_mix = mix_weights[:HIST]
    second_mix = mix_weights[HIST + 1 : 2 * HIST + 1]
    past_one = jnp.zeros(stream_in.shape, f32)
    past_two = jnp.zeros(stream_in.shape, f32)
    for j in range(HIST):
        row = history[j].astype(f32)
        past_one = past_one + first_mix[j] * row
        past_two = past_two + second_mix[j] * row
    stream = to_compute(stream_in)
    cot, past_one, past_two = to_compute(
        jnp.stack([cotangent, past_one.astype(bf16), past_two.astype(bf16)])
    )
    row_index = jnp.concatenate([s + jnp.arange(span) for s in place.starts])
    position = jnp.where(place.kind == 1, row_index % SEQ_SHORT, row_index)
    place.turn = rotation(position)
    w20, w41, w42 = mix_weights[HIST], mix_weights[2 * HIST + 1], mix_weights[2 * HIST + 2]
    mix = jnp.stack([w20, w41, w42, jnp.full((), grad_scale, f32)])
    meta = jnp.stack(
        [place.outer.astype(jnp.int32), place.kind, place.starts[0], place.starts[1]]
    ).astype(jnp.int32)
    cosine, sine = place.turn

    def line(v):
        return v.reshape(1, -1)

    def forward(layer, x, past, extra):
        gain, bias, joint_b, out_b = att_vecs[layer]
        normed, q, kv = qkv_call(
            layer, x, line(gain), line(bias), att, line(joint_b), cosine, sine
        )
        kv_other = swap_cores(kv)
        mixed, lse = att_call(meta, q, kv, kv_other)
        gain, bias, up_b, down_b = mlp_vecs[layer]
        outs = mlp_call(
            layer,
            mix,
            x,
            mixed,
            att,
            line(out_b),
            line(gain),
            line(bias),
            mlp,
            line(up_b),
            line(down_b),
            past,
            extra,
        )
        return (x, normed, q, kv, kv_other, mixed, lse), outs

    def backward(layer, dy, kept, outs, carried):
        x, normed, q, kv, kv_other, mixed, lse = kept
        h, n_m, act, slope = outs[:4]
        er, dpre, dub, dh, datt, sums = mlp_back_call(
            layer, mix, cot, dy, h, line(mlp_vecs[layer][0]), mlp, slope, att
        )
        mlp_part = reduce_tiles(place, mlp_tiles(plan, n_m, dpre, act, er))
        dq, own, give = att_back_call(meta, q, kv, kv_other, datt, mixed, lse, cosine, sine)
        gain = line(att_vecs[layer][0])
        dj, djb, dx, sums_a = qkv_back_call(
            layer, dq, own, swap_cores(give), cosine, sine, att, x, gain, dh, carried
        )
        att_part = reduce_tiles(place, att_tiles(plan, normed, dj, mixed, dh))
        vec_m = (sums[0], sums[1], dub[0], sums[2])
        vec_a = (sums_a[0], sums_a[1], djb[0], sums[3])
        return dx, sums_a[2], vec_a, vec_m, att_part, mlp_part

    kept20, outs20 = forward(0, stream, past_one, ())
    y20, c20 = outs20[4:]
    kept21, outs21 = forward(1, y20, past_two, (c20, cot))
    y21, sums21 = outs21[4:]
    stream_out = to_owner(y21)
    mix41, mix42 = jnp.sum(sums21[0]), jnp.sum(sums21[1])
    dy20, mix20, vec_a21, vec_m21, att21, mlp21 = backward(1, y20, kept21, outs21, c20)
    mix20 = jnp.sum(mix20)
    dstream, _, vec_a20, vec_m20, att20, mlp20 = backward(0, dy20, kept20, outs20, c20)
    dy20_own = to_owner(dy20)
    stream_grad = to_owner(dstream).astype(f32)

    upper = jnp.stack([att20, mlp20])
    lower = jnp.stack([att21, mlp21])
    keep = jnp.where(low_half, upper, lower)
    give = jnp.where(low_half, lower, upper)
    keep = keep.astype(f32) + swap_planes(give).astype(f32)
    mine = jnp.where(place.core == 0, keep[0], keep[1])
    other = jnp.where(place.core == 0, keep[1], keep[0])
    got = swap_cores(other.astype(bf16)).astype(f32)
    first = jnp.where(place.core == 0, mine, got)
    second = jnp.where(place.core == 0, got, mine)
    tile_grad = jnp.concatenate([first, second], axis=0)

    own_g = cotangent.astype(f32) * grad_scale
    own_dy = dy20_own.astype(f32)
    history_grad = (
        first_mix[:, None, None] * own_dy[None] + second_mix[:, None, None] * own_g[None]
    ).astype(bf16)
    mix_one = jnp.sum(own_dy[None] * history.astype(f32), axis=(1, 2))
    mix_two = jnp.sum(own_g[None] * history.astype(f32), axis=(1, 2))
    own_mix = jnp.concatenate([mix_one, mix20[None], mix_two, mix41[None], mix42[None]])

    def flat_vec(v):
        out = jnp.concatenate(v)
        return jnp.concatenate([out, jnp.zeros((VEC - out.shape[0],), f32)])

    small = jnp.concatenate(
        [flat_vec(v) for v in (vec_a20, vec_m20, vec_a21, vec_m21)] + [own_mix]
    )
    small = lax.psum(small, ("section", "batch"))
    mix_grad = small[4 * VEC :]
    vec_rows = small[: 4 * VEC].reshape(4, VEC)
    vec_own = lax.dynamic_index_in_dim(vec_rows, section, 0, keepdims=False)

    rows = plan.rows
    plain = tile_grad.reshape(-1)
    up = tile_grad.reshape(FF // D, plan.up_rows, D).transpose(1, 0, 2).reshape(-1)
    joint = tile_grad.reshape(2, 3, plan.joint_rows // 2, D).transpose(0, 2, 1, 3).reshape(-1)
    is_up = place.mlp & (2 * b < nb)
    is_joint = jnp.logical_not(place.mlp) & (8 * b < 3 * nb)
    flat = jnp.where(is_up, up, jnp.where(is_joint, joint, plain))
    flat = jnp.where(place.mlp | (2 * b < nb), flat, 0.0)
    halo = max(
        [0]
        + [
            max(s[i] + plan.tile - plan.shard * (i + 1), plan.shard * i - s[i])
            for s, n in ((plan.mlp_start, nb), (plan.att_start, nb // 2))
            for i in range(n)
        ]
    )
    before = lax.ppermute(flat[-halo:], "batch", [(i, i + 1) for i in range(nb - 1)])
    after = lax.ppermute(flat[:halo], "batch", [(i, i - 1) for i in range(1, nb)])
    starts = jnp.array([plan.att_start, plan.mlp_start])[place.mlp.astype(jnp.int32)]
    margin = 4 * D + halo
    shift = margin - plan.shard * b
    window = jnp.zeros((plan.shard + 2 * margin,), f32)

    def put(window, piece, at):
        at = jnp.clip(at, 0, window.shape[0] - piece.shape[0])
        return lax.dynamic_update_slice(window, piece, (at,))

    window = put(window, before, starts[jnp.maximum(b - 1, 0)] + plan.tile - halo + shift)
    window = put(window, after, starts[jnp.minimum(b + 1, nb - 1)] + shift)
    window = put(window, flat, starts[b] + shift)

    def with_vecs(window, pieces):
        at = 0
        for start, length in pieces:
            window = put(window, vec_own[at : at + length], start + shift)
            at += length
        return window[margin : margin + plan.shard]

    grad = jnp.where(place.mlp, with_vecs(window, MLP_VECS), with_vecs(window, ATT_VECS))
    grad = grad.reshape(params.shape)
    bias_grad = jnp.where(place.mlp, vec_own[6 * D : 7 * D], vec_own[5 * D : 6 * D])[None]

    params_step, first_new, second_new = adamw(
        params, grad, first_moment, second_moment, weight_decay
    )
    mix_step, mix_first_new, mix_second_new = adamw(
        mix_weights, mix_grad, mix_first, mix_second, 0.0
    )
    return (
        stream_out,
        stream_grad,
        history_grad,
        grad,
        params_step,
        first_new,
        second_new,
        mix_grad,
        mix_step,
        mix_first_new,
        mix_second_new,
        bias_grad,
    )


def solution(mesh):
    rows = P(("section", "batch"), None)
    hist = P(None, ("section", "batch"), None)
    weights = P("section", "batch")
    return jax.shard_map(
        local,
        mesh=mesh,
        in_specs=(rows, hist, rows, P("batch"), weights, weights, weights, P(), P(), P()),
        out_specs=(
            rows,
            rows,
            hist,
            weights,
            weights,
            weights,
            weights,
            P(),
            P(),
            P(),
            P(),
            P("section", None),
        ),
        check_vma=False,
    )
```

time: 1340 us -> 1110 us (0.83)
  Pallas kernels: 0 us -> 361 us
  local copies, waits for them, and re-layouts: 363 us -> 110 us
  matrix products: 207 us -> 0 us
  waiting for transfers between devices: 466 us -> 346 us
  other arithmetic: 246 us -> 199 us
  starting transfers between devices: 19.8 us -> 57.2 us
    pallas_call x0 -> x21, Pallas kernels: none -> 361 us  [the longest x1 143 us: gather_weights(): pl.pallas_call(body, in_specs=[any_spec] * 2, out_specs=[any_spec] * 3, o...]
    ppermute x0 -> x12, waiting for transfers between devices: none -> 223 us  [the longest x10 154 us: halve(): lax.ppermute(jnp.where(low, one, zero), 'batch', [(i, i ^ bit) for i in r...]
    dot_general x48 -> x0, matrix products: 207 us -> none  [the longest x8 43.3 us: dot_tn(): lax.dot_general(a, b, (((0,), (0,)), ((), ())), preferred_element_type=f32)]
    reduce_scatter x4 -> x0, waiting for transfers between devices: 149 us -> none  [reduce_rows(): return lax.psum_scatter(tiles, 'batch', scatter_dimension=0, tiled=True)[0]]
    all_gather x1 -> x0, waiting for transfers between devices: 125 us -> none  [local(): gathered = lax.all_gather(sent, ('section', 'batch'), axis=0, tiled=False)]
    ppermute x5, waiting for transfers between devices: 64.6 us -> 0.01 us  [swap_sections(): return lax.ppermute(array, 'section', [(i, 3 - i) for i in range(4)])]
    slice x33 -> x3, local copies, waits for them, and re-layouts: 64.1 us -> 1.48 us  [the longest x1 0.84 us: backward(): vec_a = (sums_a[0], sums_a[1], djb[0], sums[3])]
    reshape x11 -> x1, local copies, waits for them, and re-layouts: 54.6 us -> 0.64 us  [line(): return v.reshape(1, -1)]
  transfers between devices with their start and end apart: 25 -> 32, of which waited for: 9 -> 13; matrix products, arithmetic and copies ran while one was open for 40% -> 19% of each run, Pallas kernels for 0% -> 23%
where the time goes in v2:
time: 1110 us; the launch traced here: 1090 us
  Pallas kernels  361 us (33%)
  waiting for transfers between devices  346 us (31%)
  other arithmetic  199 us (18%)
  local copies, waits for them, and re-layouts  110 us (10%)
  starting transfers between devices  57.2 us (5%)
  between operations  20.1 us (2%)
    ppermute x10, waiting for transfers between devices, halve(): lax.ppermute(jnp.where(low, one, zero), 'batch', [(i, i ^ bit) for i in r...  154 us
    pallas_call x1, Pallas kernels, gather_weights(): pl.pallas_call(body, in_specs=[any_spec] * 2, out_specs=[any_spec] * 3, o...  143 us
    psum x1, waiting for transfers between devices, local(): small = lax.psum(small, ('section', 'batch'))  117 us
    ppermute x2, waiting for transfers between devices, reduce_tiles(): got = lax.ppermute(total, 'batch', [(i, i - 4) for i in range(4, nb)])  69.8 us
    pallas_call x8, Pallas kernels, weight_grad_call(): call(weight_grad_kernel, name, (steps,), [pl.BlockSpec((rows, D), (lambda...  44.3 us
    pallas_call x2, Pallas kernels, att_back_call(): call(att_back_kernel, 'attention_grad_rows', (pairs,), [SMEM_SPEC, pair_s...  39.5 us
    ppermute x10, starting transfers between devices, halve(): lax.ppermute(jnp.where(low, one, zero), 'batch', [(i, i ^ bit) for i in r...  35 us
    pallas_call x2, Pallas kernels, mlp_call(): call(functools.partial(mlp_kernel, last_layer), 'feed_forward_rows', (FF...  34.1 us
  transfers between devices with their start and end apart: 32, of which 13 were waited for; matrix products, arithmetic and copies ran while one was open for 19% of the time, Pallas kernels for 23%

profile of v2, /device:TPU:0, one launch (start us, length us, event | category | flops | bytes accessed | tf_op | source)
XLA Modules:
  0.0 1092.7 jit_solution(4439311027728242729)
XLA Ops:
  11.6 4.1 convert_element_type.346
  16.3 4.0 collective-permute-start.1
  24.2 20.9 %fusion.56 = bf16[1,512,768]{2,1,0:T(8,128)(2,1)S(1)} fusion(f32[]{:T(128)} %bitcast.62, f32[]{:T(128)} %bitcast.61, f32[]{:T(128)} %bitcast.60, f32[]{:T(128)} %bitcast.59, f32[]{:T(128)} %bitcast.58, f32[]{:T(128)} %bitcast.57, f32[]{:T(128)} %bitcast.56, f32[]{:T(128)} %bitcast.55, f32[]{:T(128)} %bitcast.54, f32[]{:T(128)} %bitcast.53, f32[]{:T(128)} %bitcast.52, ...), kind=kLoop, calls=%fused_computation.149 | loop fusion | flops 23592960 | bytes 16515152 | tf_op jit(solution)/shard_map/convert_element_type | solution.py:1190
  45.1 15.6 %fusion.57 = bf16[1,512,768]{2,1,0:T(8,128)(2,1)S(1)} fusion(f32[]{:T(128)} %bitcast.42, f32[]{:T(128)} %bitcast.41, f32[]{:T(128)} %bitcast.40, f32[]{:T(128)} %bitcast.39, f32[]{:T(128)} %bitcast.38, f32[]{:T(128)} %bitcast.37, f32[]{:T(128)} %bitcast.36, f32[]{:T(128)} %bitcast.35, f32[]{:T(128)} %bitcast.34, f32[]{:T(128)} %bitcast.33, f32[]{:T(128)} %bitcast.32, ...), kind=kLoop, calls=%fused_computation.150 | loop fusion | flops 23592960 | bytes 16515152 | tf_op jit(solution)/shard_map/convert_element_type | solution.py:1190
  64.5 22.1 %convert_reduce_fusion.1 = bf16[590496]{0:T(1024)(128)(2,1)S(1)} fusion(f32[1,590496]{1,0:T(1,128)S(1)} %copy-done.3), kind=kLoop, calls=%fused_computation.277 | loop fusion | flops 590496 | bytes 3542976 | tf_op jit(solution)/shard_map/convert_element_type | solution.py:119
  88.0 5.7 concatenate.96
  102.5 9.8 concatenate.95
  119.7 142.8 %gather_weights.1 = (bf16[2,4,768,768]{3,2,1,0:T(8,128)(2,1)}, bf16[2,8,768,768]{3,2,1,0:T(8,128)(2,1)}, bf16[32,16,768]{2,1,0:T(8,128)(2,1)}) custom-call(bf16[768,768]{1,0:T(8,128)(2,1)} %fusion.64.block_ref, bf16[16,768]{1,0:T(8,128)(2,1)} %concatenate.99.vec_ref), custom_call_target="tpu_custom_call" | custom-call | tf_op jit(solution)/shard_map/gather_weights/pallas_call | solution.py:378
  267.1 9.9 qkv_rows.2
  283.1 13.5 %attention_rows.2 = (bf16[512,768]{1,0:T(8,128)(2,1)}, f32[6,512,128]{2,1,0:T(8,128)}) custom-call(s32[4]{0:T(128)} %pad_add_fusion.1.meta_ref, bf16[512,768]{1,0:T(8,128)(2,1)} %get-tuple-element.65.q_ref, bf16[512,1536]{1,0:T(8,128)(2,1)} %get-tuple-element.66.k_ref.v_ref, bf16[512,1536]{1,0:T(8,128)(2,1)} %get-tuple-element.66.k_ref.v_ref, ...), custom_call_target="tpu_custom_call" | custom-call | flops 4026531840 | bytes 2359296 | tf_op jit(solution)/shard_map/attention_rows/pallas_call | solution.py:597
  296.7 16.8 %feed_forward_rows.2 = (bf16[512,768]{1,0:T(8,128)(2,1)}, bf16[512,768]{1,0:T(8,128)(2,1)}, bf16[512,3072]{1,0:T(8,128)(2,1)}, bf16[512,3072]{1,0:T(8,128)(2,1)}...) custom-call(f32[4]{0:T(128)} %pad_maximum_fusion.13.mix_ref, bf16[512,768]{1,0:T(8,128)(2,1)} %pad_maximum_fusion.9.x_ref, ...), custom_call_target="tpu_custom_call" | custom-call | flops 5435817984 | bytes 2359296 | tf_op jit(solution)/shard_map/feed_forward_rows/pallas_call | solution.py:691
  313.5 9.8 qkv_rows.3
  328.1 13.7 %attention_rows.3 = (bf16[512,768]{1,0:T(8,128)(2,1)}, f32[6,512,128]{2,1,0:T(8,128)}) custom-call(s32[4]{0:T(128)} %pad_add_fusion.1.meta_ref, bf16[512,768]{1,0:T(8,128)(2,1)} %get-tuple-element.70.q_ref, bf16[512,1536]{1,0:T(8,128)(2,1)} %get-tuple-element.71.k_ref.v_ref, bf16[512,1536]{1,0:T(8,128)(2,1)} %get-tuple-element.71.k_ref.v_ref, ...), custom_call_target="tpu_custom_call" | custom-call | flops 4026531840 | bytes 2359296 | tf_op jit(solution)/shard_map/attention_rows/pallas_call | solution.py:597
  341.8 17.3 %feed_forward_rows.3 = (bf16[512,768]{1,0:T(8,128)(2,1)}, bf16[512,768]{1,0:T(8,128)(2,1)}, bf16[512,3072]{1,0:T(8,128)(2,1)}, bf16[512,3072]{1,0:T(8,128)(2,1)}...) custom-call(f32[4]{0:T(128)} %pad_maximum_fusion.13.mix_ref, bf16[512,768]{1,0:T(8,128)(2,1)} %get-tuple-element.69.x_ref.dy_ref, ...), custom_call_target="tpu_custom_call" | custom-call | flops 5435817984 | bytes 2359296 | tf_op jit(solution)/shard_map/feed_forward_rows/pallas_call | solution.py:691
  359.1 16.4 %feed_forward_grad_rows.2 = (bf16[512,768]{1,0:T(8,128)(2,1)}, bf16[512,3072]{1,0:T(8,128)(2,1)}, f32[1,3072]{1,0:T(1,128)}, bf16[512,768]{1,0:T(8,128)(2,1)}, b...) custom-call(f32[4]{0:T(128)} %pad_maximum_fusion.13.mix_ref, bf16[512,768]{1,0:T(8,128)(2,1)} %get-tuple-element.151.rest_1_.cot_ref, ...), custom_call_target="tpu_custom_call" | custom-call | flops 5435817984 | bytes 2359296 | tf_op jit(solution)/shard_map/feed_forward_grad_rows/pallas_call | solution.py:799
  375.5 19.6 %attention_grad_rows.2 = (bf16[512,768]{1,0:T(8,128)(2,1)}, f32[2,512,768]{2,1,0:T(8,128)}, bf16[2,512,768]{2,1,0:T(8,128)(2,1)}) custom-call(s32[4]{0:T(128)} %pad_add_fusion.1.meta_ref, bf16[512,768]{1,0:T(8,128)(2,1)} %get-tuple-element.70.q_ref, bf16[512,1536]{1,0:T(8,128)(2,1)} %get-tuple-element.71.k_ref.v_ref, ...), custom_call_target="tpu_custom_call" | custom-call | flops 10066329600 | bytes 2359296 | tf_op jit(solution)/shard_map/attention_grad_rows/pallas_call | solution.py:914
  400.2 6.7 down_grad.3
  407.0 6.7 up_grad.3
  413.6 5.6 select_bitcast_fusion
  424.5 10.2 qkv_grad_rows.2
  434.7 16.6 %feed_forward_grad_rows.3 = (bf16[512,768]{1,0:T(8,128)(2,1)}, bf16[512,3072]{1,0:T(8,128)(2,1)}, f32[1,3072]{1,0:T(1,128)}, bf16[512,768]{1,0:T(8,128)(2,1)}, b...) custom-call(f32[4]{0:T(128)} %pad_maximum_fusion.13.mix_ref, bf16[512,768]{1,0:T(8,128)(2,1)} %get-tuple-element.151.rest_1_.cot_ref, ...), custom_call_target="tpu_custom_call" | custom-call | flops 5435817984 | bytes 2359296 | tf_op jit(solution)/shard_map/feed_forward_grad_rows/pallas_call | solution.py:799
  451.3 19.9 %attention_grad_rows.3 = (bf16[512,768]{1,0:T(8,128)(2,1)}, f32[2,512,768]{2,1,0:T(8,128)}, bf16[2,512,768]{2,1,0:T(8,128)(2,1)}) custom-call(s32[4]{0:T(128)} %pad_add_fusion.1.meta_ref, bf16[512,768]{1,0:T(8,128)(2,1)} %get-tuple-element.65.q_ref, bf16[512,1536]{1,0:T(8,128)(2,1)} %get-tuple-element.66.k_ref.v_ref, ...), custom_call_target="tpu_custom_call" | custom-call | flops 10066329600 | bytes 2359296 | tf_op jit(solution)/shard_map/attention_grad_rows/pallas_call | solution.py:914
  471.6 5.7 joint_grad.3
  482.2 6.5 down_grad.2
  488.7 6.6 up_grad.2
  495.3 6.6 select_bitcast_fusion.1
  507.4 10.2 qkv_grad_rows.3
  517.7 5.7 joint_grad.2
  530.8 4.0 fusion.2
  537.7 19.7 %collective-permute-done.20 = bf16[2,384,768]{2,1,0:T(8,128)(2,1)S(1)} collective-permute-done((bf16[2,384,768]{2,1,0:T(8,128)(2,1)S(1)}, bf16[2,384,768]{2,1,0:T(8,128)(2,1)S(1)}, u32[]{:S(2)}, u32[]{:S(2)}) %collective-permute-start.20) | collective-permute-done | bytes 1179680 | tf_op jit(solution)/shard_map/ppermute | solution.py:1114
  564.6 4.0 fusion.3
  577.7 38.1 %collective-permute-done.21 = bf16[2,384,768]{2,1,0:T(8,128)(2,1)} collective-permute-done((bf16[2,384,768]{2,1,0:T(8,128)(2,1)}, bf16[2,384,768]{2,1,0:T(8,128)(2,1)}, u32[]{:S(2)}, u32[]{:S(2)}) %collective-permute-start.21) | collective-permute-done | bytes 1179680 | tf_op jit(solution)/shard_map/ppermute | solution.py:1123
  617.7 19.4 %collective-permute-done.12 = bf16[2,384,768]{2,1,0:T(8,128)(2,1)} collective-permute-done((bf16[2,384,768]{2,1,0:T(8,128)(2,1)}, bf16[2,384,768]{2,1,0:T(8,128)(2,1)}, u32[]{:S(2)}, u32[]{:S(2)}) %collective-permute-start.12) | collective-permute-done | bytes 1179680 | tf_op jit(solution)/shard_map/ppermute | solution.py:1114
  647.0 39.0 %collective-permute-done.16 = bf16[4,384,768]{2,1,0:T(8,128)(2,1)} collective-permute-done((bf16[4,384,768]{2,1,0:T(8,128)(2,1)}, bf16[4,384,768]{2,1,0:T(8,128)(2,1)}, u32[]{:S(2)}, u32[]{:S(2)}) %collective-permute-start.16) | collective-permute-done | bytes 2359328 | tf_op jit(solution)/shard_map/ppermute | solution.py:1114
  690.0 25.0 %collective-permute-start.22 = (bf16[384,768]{1,0:T(8,128)(2,1)S(1)}, bf16[384,768]{1,0:T(8,128)(2,1)S(1)}, u32[]{:S(2)}, u32[]{:S(2)}) collective-permute-start(bf16[384,768]{1,0:T(8,128)(2,1)S(1)} %select_bitcast_fusion.8), channel_id=1, source_target_pairs={{0,2},{1,3},{2,0},{3,1},{4,6},{5,7},{6,4},{7,5},{8,10},{9,11},{10,... | collective-permute-start | bytes 1769480 | tf_op jit(solution)/shard_map/ppermute | solution.py:1114
  715.0 31.7 %collective-permute-done.13 = bf16[2,384,768]{2,1,0:T(8,128)(2,1)S(1)} collective-permute-done((bf16[2,384,768]{2,1,0:T(8,128)(2,1)S(1)}, bf16[2,384,768]{2,1,0:T(8,128)(2,1)S(1)}, u32[]{:S(2)}, u32[]{:S(2)}) %collective-permute-start.13) | collective-permute-done | bytes 1179680 | tf_op jit(solution)/shard_map/ppermute | solution.py:1123
  747.2 24.9 %collective-permute-done.25 = bf16[2,384,768]{2,1,0:T(8,128)(2,1)S(1)} collective-permute-done((bf16[2,384,768]{2,1,0:T(8,128)(2,1)S(1)}, bf16[2,384,768]{2,1,0:T(8,128)(2,1)S(1)}, u32[]{:S(2)}, u32[]{:S(2)}) %collective-permute-start.25) | collective-permute-done | bytes 1179680 | tf_op jit(solution)/shard_map/ppermute | solution.py:1114
  772.7 20.4 %collective-permute-done.17 = bf16[2,384,768]{2,1,0:T(8,128)(2,1)S(1)} collective-permute-done((bf16[2,384,768]{2,1,0:T(8,128)(2,1)S(1)}, bf16[2,384,768]{2,1,0:T(8,128)(2,1)S(1)}, u32[]{:S(2)}, u32[]{:S(2)}) %collective-permute-start.17) | collective-permute-done | bytes 1179680 | tf_op jit(solution)/shard_map/ppermute | solution.py:1114
  793.9 11.6 %collective-permute-done.14 = bf16[384,768]{1,0:T(8,128)(2,1)S(1)} collective-permute-done((bf16[384,768]{1,0:T(8,128)(2,1)S(1)}, bf16[384,768]{1,0:T(8,128)(2,1)S(1)}, u32[]{:S(2)}, u32[]{:S(2)}) %collective-permute-start.14) | collective-permute-done | bytes 589856 | tf_op jit(solution)/shard_map/ppermute | solution.py:1114
  805.7 12.4 %collective-permute-done.26 = bf16[384,768]{1,0:T(8,128)(2,1)S(1)} collective-permute-done((bf16[384,768]{1,0:T(8,128)(2,1)S(1)}, bf16[384,768]{1,0:T(8,128)(2,1)S(1)}, u32[]{:S(2)}, u32[]{:S(2)}) %collective-permute-start.26) | collective-permute-done | bytes 589856 | tf_op jit(solution)/shard_map/ppermute | solution.py:1114
  818.3 6.2 collective-permute-done.18
  828.1 21.4 %fusion.1 = (f32[20]{0:T(128)S(1)}, f32[20]{0:T(128)S(1)}, bf16[20,512,768]{2,1,0:T(8,128)(2,1)}) fusion(bf16[20,512,768]{2,1,0:T(8,128)(2,1)S(1)} %bitcast.310, f32[512,768]{1,0:T(8,128)S(1)} %copy-done.15, f32[512,768]{1,0:T(8,128)S(1)} %maximum_convert_fusion.1, f32[20]{0:T(128)S(1)} %copy-done.42, f32[20]{0:T(128)S(1)} %copy-done.41), kind=kLoop, calls=%fused_computation.3 | loop fusion | flops 70778840 | bytes 34603328 | tf_op jit(solution)/shard_map/reduce_sum | solution.py:1277
  853.3 117.2 %all-reduce.3.cloned.1.call-done = f32[21547]{0:T(1024)} async-done(((f32[21547]{0:T(1024)}), f32[21547]{0:T(1024)}) %all-reduce.3.cloned.1.call-update) | async-done | bytes 86204 | tf_op jit(solution)/shard_map/psum | solution.py:1287
  995.2 4.7 reshape.422
  1008.8 3.9 collective-permute-done.30
  1012.9 22.4 %dynamic_update_slice.31 = f32[599136]{0:T(1024)S(1)} dynamic-update-slice(f32[599136]{0:T(1024)S(1)} %dynamic_update_slice.30, f32[589824]{0:T(1024)} %copy-done.11, s32[]{:T(128)S(6)} %min.62) | dynamic-update-slice | bytes 4718596 | tf_op jit(solution)/shard_map/dynamic_update_slice | solution.py:1317
  1043.7 11.8 %reshape.425 = f32[1,590496]{1,0:T(1,128)} reshape(f32[590496]{0:T(1024)S(1)} %get-tuple-element.143) | data formatting | bytes 4723968 | tf_op jit(solution)/shard_map/reshape | solution.py:1331
  1057.9 27.6 %multiply_add_fusion = (f32[1,590496]{1,0:T(1,128)}, f32[1,590496]{1,0:T(1,128)}, f32[1,590496]{1,0:T(1,128)}) fusion(f32[1,590496]{1,0:T(1,128)S(1)} %copy-done.4, f32[590496]{0:T(1024)S(1)} %get-tuple-element.142, f32[1,590496]{1,0:T(1,128)S(1)} %copy-done.24, f32[590496]{0:T(1024)S(1)} %broadcast_multiply_fusion, f32[1,590496]{1,0:T(1,128)S(1)} %copy-done.25), kind=kLoop, calls=%fused_computation.41 | loop fusion | flops 4723968 | bytes 18895872 | tf_op jit(solution)/shard_map/add | solution.py:78
  (317 shorter events, 158.1 us)
Async XLA Ops:
  7.2 963.2 %all-reduce.3.cloned.1.call-start = ((), (), s32[]{:S(2)}) async-start(), calls=%async_computation | async-start | bytes 180224 | tf_op jit(solution)/shard_map/psum | solution.py:1287
  9.1 256.0 %collective-permute-start = (bf16[256,768]{1,0:T(8,128)(2,1)}, bf16[256,768]{1,0:T(8,128)(2,1)}, u32[]{:S(2)}, u32[]{:S(2)}) collective-permute-start(bf16[256,768]{1,0:T(8,128)(2,1)} %broadcast_select_fusion.21), channel_id=1, source_target_pairs={{0,24},{8,16},{16,8},{24,0},{1,25},{9,17},{17,9},{25,1},{2,26},{10... | collective-permute-start | bytes 1179656 | tf_op jit(solution)/shard_map/ppermute | solution.py:54
  16.3 86.2 %collective-permute-start.1 = (bf16[480]{0:T(512)(128)(2,1)}, bf16[480]{0:T(512)(128)(2,1)}, u32[]{:S(2)}, u32[]{:S(2)}) collective-permute-start(bf16[480]{0:T(512)(128)(2,1)} %slice_reduce_fusion.16), channel_id=1, source_target_pairs={{0,1},{1,2},{2,3},{3,4},{4,5},{5,6},{6,7},{8,9},{9,10},{10,11},{11... | collective-permute-start | bytes 2888 | tf_op jit(solution)/shard_map/ppermute | solution.py:122
  20.9 81.6 %collective-permute-start.2 = (bf16[1248]{0:T(1024)(128)(2,1)}, bf16[1248]{0:T(1024)(128)(2,1)S(1)}, u32[]{:S(2)}, u32[]{:S(2)}) collective-permute-start(bf16[1248]{0:T(1024)(128)(2,1)} %slice_reduce_fusion), channel_id=1, source_target_pairs={{1,0},{2,1},{3,2},{4,3},{5,4},{6,5},{7,6},{9,8},{10,9},{11,10},{12... | collective-permute-start | bytes 7496 | tf_op jit(solution)/shard_map/ppermute | solution.py:125
  63.5 216.7 %collective-permute-start.4 = (bf16[3,256,768]{2,1,0:T(8,128)(2,1)}, bf16[3,256,768]{2,1,0:T(8,128)(2,1)}, u32[]{:S(2)}, u32[]{:S(2)}) collective-permute-start(bf16[3,256,768]{2,1,0:T(8,128)(2,1)} %broadcast_select_fusion.5), channel_id=1, source_target_pairs={{0,24},{8,16},{16,8},{24,0},{1,25},{9,17},{17,9},{25,1},{2,26},{10... | collective-permute-start | bytes 3538952 | tf_op jit(solution)/shard_map/ppermute | solution.py:54
  118.4 146.7 %copy-start.18 = (bf16[512,768]{1,0:T(8,128)(2,1)S(1)}, bf16[512,768]{1,0:T(8,128)(2,1)}, u32[]{:S(2)}) copy-start(bf16[512,768]{1,0:T(8,128)(2,1)} %param.13) | copy-start | bytes 2359300
  277.0 6.1 collective-permute-start.3
  323.3 3.7 collective-permute-start.5
  375.5 23.3 %copy-start.21 = (bf16[512,768]{1,0:T(8,128)(2,1)S(1)}, bf16[512,768]{1,0:T(8,128)(2,1)}, u32[]{:S(2)}) copy-start(bf16[512,768]{1,0:T(8,128)(2,1)} %get-tuple-element.74) | copy-start | bytes 2359300
  395.2 28.2 %collective-permute-start.7 = (bf16[2,512,768]{2,1,0:T(8,128)(2,1)}, bf16[2,512,768]{2,1,0:T(8,128)(2,1)S(1)}, u32[]{:S(2)}, u32[]{:S(2)}) collective-permute-start(bf16[2,512,768]{2,1,0:T(8,128)(2,1)} %get-tuple-element.81), channel_id=1, source_target_pairs={{0,8},{8,0},{16,24},{24,16},{1,9},{9,1},{17,25},{25,17},{2,10},{10... | collective-permute-start | bytes 4718600 | tf_op jit(solution)/shard_map/ppermute | solution.py:58
  399.7 171.8 %collective-permute-start.6 = (bf16[256,768]{1,0:T(8,128)(2,1)}, bf16[256,768]{1,0:T(8,128)(2,1)}, u32[]{:S(2)}, u32[]{:S(2)}) collective-permute-start(bf16[256,768]{1,0:T(8,128)(2,1)} %broadcast_select_fusion.17), channel_id=1, source_target_pairs={{0,24},{8,16},{16,8},{24,0},{1,25},{9,17},{17,9},{25,1},{2,26},{10... | collective-permute-start | bytes 1179656 | tf_op jit(solution)/shard_map/ppermute | solution.py:54
  419.2 110.1 %collective-permute-start.23 = (bf16[8,384,768]{2,1,0:T(8,128)(2,1)}, bf16[8,384,768]{2,1,0:T(8,128)(2,1)}, u32[]{:S(2)}, u32[]{:S(2)}) collective-permute-start(bf16[8,384,768]{2,1,0:T(8,128)(2,1)} %select_bitcast_fusion), channel_id=1, source_target_pairs={{0,8},{8,0},{16,24},{24,16},{1,9},{9,1},{17,25},{25,17},{2,10},{10... | collective-permute-start | bytes 14155784 | tf_op jit(solution)/shard_map/ppermute | solution.py:58
  471.2 35.1 %collective-permute-start.8 = (bf16[2,512,768]{2,1,0:T(8,128)(2,1)}, bf16[2,512,768]{2,1,0:T(8,128)(2,1)S(1)}, u32[]{:S(2)}, u32[]{:S(2)}) collective-permute-start(bf16[2,512,768]{2,1,0:T(8,128)(2,1)} %get-tuple-element.90), channel_id=1, source_target_pairs={{0,8},{8,0},{16,24},{24,16},{1,9},{9,1},{17,25},{25,17},{2,10},{10... | collective-permute-start | bytes 4718600 | tf_op jit(solution)/shard_map/ppermute | solution.py:58
  480.6 45.3 %collective-permute-start.19 = (bf16[4,384,768]{2,1,0:T(8,128)(2,1)}, bf16[4,384,768]{2,1,0:T(8,128)(2,1)}, u32[]{:S(2)}, u32[]{:S(2)}) collective-permute-start(bf16[4,384,768]{2,1,0:T(8,128)(2,1)} %select_bitcast_fusion.3), channel_id=1, source_target_pairs={{0,8},{8,0},{16,24},{24,16},{1,9},{9,1},{17,25},{25,17},{2,10},{10... | collective-permute-start | bytes 7077896 | tf_op jit(solution)/shard_map/ppermute | solution.py:58
  501.9 62.0 %collective-permute-start.15 = (bf16[8,384,768]{2,1,0:T(8,128)(2,1)}, bf16[8,384,768]{2,1,0:T(8,128)(2,1)}, u32[]{:S(2)}, u32[]{:S(2)}) collective-permute-start(bf16[8,384,768]{2,1,0:T(8,128)(2,1)} %select_bitcast_fusion.1), channel_id=1, source_target_pairs={{0,8},{8,0},{16,24},{24,16},{1,9},{9,1},{17,25},{25,17},{2,10},{10... | collective-permute-start | bytes 14155784 | tf_op jit(solution)/shard_map/ppermute | solution.py:58
  506.3 70.2 %collective-permute-start.10 = (bf16[256,768]{1,0:T(8,128)(2,1)}, bf16[256,768]{1,0:T(8,128)(2,1)}, u32[]{:S(2)}, u32[]{:S(2)}) collective-permute-start(bf16[256,768]{1,0:T(8,128)(2,1)} %broadcast_select_fusion.9), channel_id=1, source_target_pairs={{0,24},{8,16},{16,8},{24,0},{1,25},{9,17},{17,9},{25,1},{2,26},{10... | collective-permute-start | bytes 1179656 | tf_op jit(solution)/shard_map/ppermute | solution.py:54
  525.9 34.4 %collective-permute-start.11 = (bf16[4,384,768]{2,1,0:T(8,128)(2,1)S(1)}, bf16[4,384,768]{2,1,0:T(8,128)(2,1)S(1)}, u32[]{:S(2)}, u32[]{:S(2)}) collective-permute-start(bf16[4,384,768]{2,1,0:T(8,128)(2,1)S(1)} %select_bitcast_fusion.5), channel_id=1, source_target_pairs={{0,8},{8,0},{16,24},{24,16},{1,9},{9,1},{17,25},{25,17},{2,10},{10... | collective-permute-start | bytes 7077896 | tf_op jit(solution)/shard_map/ppermute | solution.py:58
  529.3 28.1 %collective-permute-start.20 = (bf16[2,384,768]{2,1,0:T(8,128)(2,1)S(1)}, bf16[2,384,768]{2,1,0:T(8,128)(2,1)S(1)}, u32[]{:S(2)}, u32[]{:S(2)}) collective-permute-start(bf16[2,384,768]{2,1,0:T(8,128)(2,1)S(1)} %select_bitcast_fusion.6), channel_id=1, source_target_pairs={{0,1},{1,0},{2,3},{3,2},{4,5},{5,4},{6,7},{7,6},{8,9},{9,8},{10,11... | collective-permute-start | bytes 3538952 | tf_op jit(solution)/shard_map/ppermute | solution.py:1114
  537.7 24.1 %copy-start.8 = (bf16[3,2,3,128,768]{4,3,2,1,0:T(8,128)(2,1)S(1)}, bf16[3,2,3,128,768]{4,3,2,1,0:T(8,128)(2,1)}, u32[]{:S(2)}) copy-start(bf16[3,2,3,128,768]{4,3,2,1,0:T(8,128)(2,1)} %joint_grad.2) | copy-start | bytes 10616836
  557.4 83.1 %collective-permute-start.24 = (bf16[4,384,768]{2,1,0:T(8,128)(2,1)}, bf16[4,384,768]{2,1,0:T(8,128)(2,1)}, u32[]{:S(2)}, u32[]{:S(2)}) collective-permute-start(bf16[4,384,768]{2,1,0:T(8,128)(2,1)} %select_bitcast_fusion.2), channel_id=1, source_target_pairs={{0,1},{1,0},{2,3},{3,2},{4,5},{5,4},{6,7},{7,6},{8,9},{9,8},{10,11... | collective-permute-start | bytes 7077896 | tf_op jit(solution)/shard_map/ppermute | solution.py:1114
  560.3 55.6 %collective-permute-start.21 = (bf16[2,384,768]{2,1,0:T(8,128)(2,1)}, bf16[2,384,768]{2,1,0:T(8,128)(2,1)}, u32[]{:S(2)}, u32[]{:S(2)}) collective-permute-start(bf16[2,384,768]{2,1,0:T(8,128)(2,1)} %fusion.16), channel_id=1, source_target_pairs={{4,0},{5,1},{6,2},{7,3},{12,8},{13,9},{14,10},{15,11},{20,16},{21,... | collective-permute-start | bytes 3538952 | tf_op jit(solution)/shard_map/ppermute | solution.py:1123
  564.0 73.2 %collective-permute-start.12 = (bf16[2,384,768]{2,1,0:T(8,128)(2,1)}, bf16[2,384,768]{2,1,0:T(8,128)(2,1)}, u32[]{:S(2)}, u32[]{:S(2)}) collective-permute-start(bf16[2,384,768]{2,1,0:T(8,128)(2,1)} %fusion.58), channel_id=1, source_target_pairs={{0,1},{1,0},{2,3},{3,2},{4,5},{5,4},{6,7},{7,6},{8,9},{9,8},{10,11... | collective-permute-start | bytes 3538952 | tf_op jit(solution)/shard_map/ppermute | solution.py:1114
  571.5 114.6 %collective-permute-start.16 = (bf16[4,384,768]{2,1,0:T(8,128)(2,1)}, bf16[4,384,768]{2,1,0:T(8,128)(2,1)}, u32[]{:S(2)}, u32[]{:S(2)}) collective-permute-start(bf16[4,384,768]{2,1,0:T(8,128)(2,1)} %select_bitcast_fusion.4), channel_id=1, source_target_pairs={{0,1},{1,0},{2,3},{3,2},{4,5},{5,4},{6,7},{7,6},{8,9},{9,8},{10,11... | collective-permute-start | bytes 7077896 | tf_op jit(solution)/shard_map/ppermute | solution.py:1114
  577.6 62.9 %slice-start.4 = ((s8[4718592]{0:T(1024)(128)(4,1)}), s8[4194304]{0:T(1024)(128)(4,1)S(1)}, s32[]{:S(2)}) async-start(s8[4718592]{0:T(1024)(128)(4,1)} %bitcast.312), calls=%async_computation.5 | async-start | bytes 8388608
  577.7 62.8 %slice-start.5 = ((s8[4718592]{0:T(1024)(128)(4,1)}), s8[524288]{0:T(1024)(128)(4,1)S(1)}, s32[]{:S(2)}) async-start(s8[4718592]{0:T(1024)(128)(4,1)} %bitcast.312), calls=%async_computation.6 | async-start | bytes 1048576
  637.2 48.9 %slice-start.6 = ((s8[4718592]{0:T(1024)(128)(4,1)}), s8[4194304]{0:T(1024)(128)(4,1)S(1)}, s32[]{:S(2)}) async-start(s8[4718592]{0:T(1024)(128)(4,1)} %bitcast.316), calls=%async_computation.7 | async-start | bytes 8388608
  639.0 47.0 %slice-start.7 = ((s8[4718592]{0:T(1024)(128)(4,1)}), s8[524288]{0:T(1024)(128)(4,1)S(1)}, s32[]{:S(2)}) async-start(s8[4718592]{0:T(1024)(128)(4,1)} %bitcast.316), calls=%async_computation.8 | async-start | bytes 1048576
  639.0 107.7 %collective-permute-start.13 = (bf16[2,384,768]{2,1,0:T(8,128)(2,1)S(1)}, bf16[2,384,768]{2,1,0:T(8,128)(2,1)S(1)}, u32[]{:S(2)}, u32[]{:S(2)}) collective-permute-start(bf16[2,384,768]{2,1,0:T(8,128)(2,1)S(1)} %fusion.17), channel_id=1, source_target_pairs={{4,0},{5,1},{6,2},{7,3},{12,8},{13,9},{14,10},{15,11},{20,16},{21,... | collective-permute-start | bytes 3538952 | tf_op jit(solution)/shard_map/ppermute | solution.py:1123
  643.3 128.8 %collective-permute-start.25 = (bf16[2,384,768]{2,1,0:T(8,128)(2,1)S(1)}, bf16[2,384,768]{2,1,0:T(8,128)(2,1)S(1)}, u32[]{:S(2)}, u32[]{:S(2)}) collective-permute-start(bf16[2,384,768]{2,1,0:T(8,128)(2,1)S(1)} %broadcast_select_fusion), channel_id=1, source_target_pairs={{0,4},{1,5},{2,6},{3,7},{4,0},{5,1},{6,2},{7,3},{8,12},{9,13},{10,... | collective-permute-start | bytes 3538952 | tf_op jit(solution)/shard_map/ppermute | solution.py:1114
  688.9 104.2 %collective-permute-start.17 = (bf16[2,384,768]{2,1,0:T(8,128)(2,1)S(1)}, bf16[2,384,768]{2,1,0:T(8,128)(2,1)S(1)}, u32[]{:S(2)}, u32[]{:S(2)}) collective-permute-start(bf16[2,384,768]{2,1,0:T(8,128)(2,1)S(1)} %broadcast_select_fusion.1), channel_id=1, source_target_pairs={{0,4},{1,5},{2,6},{3,7},{4,0},{5,1},{6,2},{7,3},{8,12},{9,13},{10,... | collective-permute-start | bytes 3538952 | tf_op jit(solution)/shard_map/ppermute | solution.py:1114
  690.0 138.0 %slice-start = ((s8[15728640]{0:T(1024)(128)(4,1)}), s8[4194304]{0:T(1024)(128)(4,1)S(1)}, s32[]{:S(2)}) async-start(s8[15728640]{0:T(1024)(128)(4,1)} %bitcast.309), calls=%async_computation.1 | async-start | bytes 8388608
  690.0 103.6 %collective-permute-start.22 = (bf16[384,768]{1,0:T(8,128)(2,1)S(1)}, bf16[384,768]{1,0:T(8,128)(2,1)S(1)}, u32[]{:S(2)}, u32[]{:S(2)}) collective-permute-start(bf16[384,768]{1,0:T(8,128)(2,1)S(1)} %select_bitcast_fusion.8), channel_id=1, source_target_pairs={{0,2},{1,3},{2,0},{3,1},{4,6},{5,7},{6,4},{7,5},{8,10},{9,11},{10,... | collective-permute-start | bytes 1769480 | tf_op jit(solution)/shard_map/ppermute | solution.py:1114
  747.1 80.9 %slice-start.1 = ((s8[15728640]{0:T(1024)(128)(4,1)}), s8[4194304]{0:T(1024)(128)(4,1)S(1)}, s32[]{:S(2)}) async-start(s8[15728640]{0:T(1024)(128)(4,1)} %bitcast.309), calls=%async_computation.2 | async-start | bytes 8388608
  747.1 58.4 %collective-permute-start.14 = (bf16[384,768]{1,0:T(8,128)(2,1)S(1)}, bf16[384,768]{1,0:T(8,128)(2,1)S(1)}, u32[]{:S(2)}, u32[]{:S(2)}) collective-permute-start(bf16[384,768]{1,0:T(8,128)(2,1)S(1)} %select_bitcast_fusion.10), channel_id=1, source_target_pairs={{0,2},{1,3},{2,0},{3,1},{4,6},{5,7},{6,4},{7,5},{8,10},{9,11},{10,... | collective-permute-start | bytes 1769480 | tf_op jit(solution)/shard_map/ppermute | solution.py:1114
  772.6 55.4 %slice-start.2 = ((s8[15728640]{0:T(1024)(128)(4,1)}), s8[4194304]{0:T(1024)(128)(4,1)S(1)}, s32[]{:S(2)}) async-start(s8[15728640]{0:T(1024)(128)(4,1)} %bitcast.309), calls=%async_computation.3 | async-start | bytes 8388608
  772.6 45.5 %collective-permute-start.26 = (bf16[384,768]{1,0:T(8,128)(2,1)S(1)}, bf16[384,768]{1,0:T(8,128)(2,1)S(1)}, u32[]{:S(2)}, u32[]{:S(2)}) collective-permute-start(bf16[384,768]{1,0:T(8,128)(2,1)S(1)} %select_bitcast_fusion.7), channel_id=1, source_target_pairs={{0,2},{1,3},{2,0},{3,1},{4,6},{5,7},{6,4},{7,5},{8,10},{9,11},{10,... | collective-permute-start | bytes 1769480 | tf_op jit(solution)/shard_map/ppermute | solution.py:1114
  793.6 31.0 %collective-permute-start.18 = (bf16[384,768]{1,0:T(8,128)(2,1)S(1)}, bf16[384,768]{1,0:T(8,128)(2,1)S(1)}, u32[]{:S(2)}, u32[]{:S(2)}) collective-permute-start(bf16[384,768]{1,0:T(8,128)(2,1)S(1)} %select_bitcast_fusion.9), channel_id=1, source_target_pairs={{0,2},{1,3},{2,0},{3,1},{4,6},{5,7},{6,4},{7,5},{8,10},{9,11},{10,... | collective-permute-start | bytes 1769480 | tf_op jit(solution)/shard_map/ppermute | solution.py:1114
  805.7 22.3 %slice-start.3 = ((s8[15728640]{0:T(1024)(128)(4,1)}), s8[3145728]{0:T(1024)(128)(4,1)S(1)}, s32[]{:S(2)}) async-start(s8[15728640]{0:T(1024)(128)(4,1)} %bitcast.309), calls=%async_computation.4 | async-start | bytes 6291456
  826.0 150.5 %collective-permute-start.27 = (bf16[2,384,768]{2,1,0:T(8,128)(2,1)}, bf16[2,384,768]{2,1,0:T(8,128)(2,1)}, u32[]{:S(2)}, u32[]{:S(2)}) collective-permute-start(bf16[2,384,768]{2,1,0:T(8,128)(2,1)} %broadcast_select_fusion.2), channel_id=1, source_target_pairs={{0,16},{8,24},{16,0},{24,8},{1,17},{9,25},{17,1},{25,9},{2,18},{10... | collective-permute-start | bytes 3538952 | tf_op jit(solution)/shard_map/ppermute | solution.py:62
  828.0 22.4 %copy-start.32 = (f32[768]{0:T(1024)S(1)}, f32[768]{0:T(1024)}, u32[]{:S(2)}) copy-start(f32[768]{0:T(1024)} %get-tuple-element.128) | copy-start | bytes 9220
  828.1 22.4 %copy-start.34 = (f32[1,3072]{1,0:T(1,128)S(1)}, f32[1,3072]{1,0:T(1,128)}, u32[]{:S(2)}) copy-start(f32[1,3072]{1,0:T(1,128)} %get-tuple-element.112) | copy-start | bytes 36868
  828.1 22.4 %copy-start.35 = (f32[1,3072]{1,0:T(1,128)S(1)}, f32[1,3072]{1,0:T(1,128)}, u32[]{:S(2)}) copy-start(f32[1,3072]{1,0:T(1,128)} %get-tuple-element.108) | copy-start | bytes 36868
  828.1 25.0 %copy-start.23 = (bf16[512,768]{1,0:T(8,128)(2,1)S(1)}, bf16[512,768]{1,0:T(8,128)(2,1)}, u32[]{:S(2)}) copy-start(bf16[512,768]{1,0:T(8,128)(2,1)} %get-tuple-element.92) | copy-start | bytes 2359300
  853.2 128.5 %collective-permute-start.9 = (bf16[256,768]{1,0:T(8,128)(2,1)S(1)}, bf16[256,768]{1,0:T(8,128)(2,1)}, u32[]{:S(2)}, u32[]{:S(2)}) collective-permute-start(bf16[256,768]{1,0:T(8,128)(2,1)S(1)} %broadcast_select_fusion.13), channel_id=1, source_target_pairs={{0,24},{8,16},{16,8},{24,0},{1,25},{9,17},{17,9},{25,1},{2,26},{10... | collective-permute-start | bytes 1179656 | tf_op jit(solution)/shard_map/ppermute | solution.py:54
  978.2 5.2 collective-permute-start.28
  1002.1 6.0 collective-permute-start.29
  1005.5 7.2 collective-permute-start.30
  1012.9 22.4 %copy-start.33 = (f32[768]{0:T(1024)S(1)}, f32[768]{0:T(1024)}, u32[]{:S(2)}) copy-start(f32[768]{0:T(1024)} %get-tuple-element.118) | copy-start | bytes 9220
  (48 other events, 293.9 us)
Sparse Core Ops, SparseCore 0:
  853.2 117.1 all-reduce.2

commit v3 on v2

--- a/solution.py
+++ b/solution.py
@@ -93,74 +93,25 @@
 
 def gather_blocks(plan, block, vecs):
     nb, rows = plan.nb, plan.rows
-    sent = jnp.concatenate([block, vecs], axis=0)
-    gathered = lax.all_gather(sent, ("section", "batch"), axis=0, tiled=False)
-    gathered = gathered.reshape(2, 2, nb, sent.shape[0], D)
+    gathered = lax.all_gather(block, ("section", "batch"), axis=0, tiled=False)
+    gathered = gathered.reshape(2, 2, nb, rows, D)
+    vecs = lax.all_gather(vecs, ("section", "batch"), axis=0, tiled=False)
     blocks = nb * 3 // 8
-    tiles = gathered[:, 0, :, :rows]
+    tiles = gathered[:, 0]
     joint = tiles[:, :blocks].reshape(2, blocks, 2, 3, plan.joint_rows // 2, D)
     joint = joint.transpose(0, 1, 2, 4, 3, 5).reshape(2, 6, 128, 3, D)
     joint = joint.transpose(0, 1, 3, 2, 4).reshape(2, 3, D, D)
     att = jnp.concatenate([joint, tiles[:, blocks : nb // 2].reshape(2, 1, D, D)], axis=1)
-    tiles = gathered[:, 1, :, :rows]
+    tiles = gathered[:, 1]
     up = tiles[:, : nb // 2].reshape(2, nb // 2, FF // D, plan.up_rows, D)
     up = up.transpose(0, 1, 3, 2, 4).reshape(2, 4, 192, 4, D)
     up = up.transpose(0, 1, 3, 2, 4).reshape(2, 4, D, D)
     mlp = jnp.concatenate([up, tiles[:, nb // 2 :].reshape(2, 4, D, D)], axis=1)
-    return att, mlp, gathered[:, :, :, rows:].reshape(4, nb, -1, D)
+    return att, mlp, vecs
 
 
 class Place:
     pass
-
-
-def pack_weights(plan, place, params):
-    nb, shard, tile = plan.nb, plan.shard, plan.tile
-    own = params.reshape(-1).astype(bf16)
-    parts = []
-    if plan.low:
-        parts.append(lax.ppermute(own[-plan.low :], "batch", [(i, i + 1) for i in range(nb - 1)]))
-    parts.append(own)
-    if plan.high:
-        parts.append(lax.ppermute(own[: plan.high], "batch", [(i, i - 1) for i in range(1, nb)]))
-    wide = jnp.concatenate(parts)
-    b, mlp = place.b, place.mlp
-    mlp_offset = jnp.array([plan.low + plan.mlp_start[i] - shard * i for i in range(nb)])
-    att_offset = jnp.array(
-        [plan.low + (plan.att_start[i] - shard * i if 2 * i < nb else 0) for i in range(nb)]
-    )
-    offset = jnp.where(mlp, mlp_offset[b], att_offset[b])
-    flat = lax.dynamic_slice(wide, (offset,), (tile,))
-    rows = plan.rows
-    plain = flat.reshape(rows, D)
-    up = flat.reshape(plan.up_rows, FF // D, D).transpose(1, 0, 2).reshape(rows, D)
-    joint = flat.reshape(2, plan.joint_rows // 2, 3, D).transpose(0, 2, 1, 3).reshape(rows, D)
-    is_up = mlp & (2 * b < nb)
-    is_joint = jnp.logical_not(mlp) & (8 * b < 3 * nb)
-    block = jnp.where(is_up, up, jnp.where(is_joint, joint, plain))
-    padded = jnp.concatenate([jnp.zeros((FF,), bf16), own, jnp.zeros((FF,), bf16)])
-
-    def vectors(pieces):
-        out = []
-        for start, length in pieces:
-            at = jnp.clip(start - shard * b + FF, 0, shard + FF)
-            out.append(lax.dynamic_slice(padded, (at,), (length,)))
-        total = sum(length for _, length in pieces)
-        out.append(jnp.zeros((VEC - total,), bf16))
-        return jnp.concatenate(out)
-
-    vecs = jnp.where(mlp, vectors(MLP_VECS), vectors(ATT_VECS))
-    lines = vecs.reshape(VEC // D, D)
-    return block, jnp.concatenate([lines, jnp.zeros((16 - VEC // D, D), bf16)], axis=0)
-
-
-def split_vecs(lines, pieces):
-    flat = lines.reshape(-1)
-    out, at = [], 0
-    for _, length in pieces:
-        out.append(flat[at : at + length])
-        at += length
-    return out
 
 
 MESH = pl.DeviceIdType.MESH
@@ -1054,6 +1005,291 @@
     )(a, b)[0]
 
 
+EDGE = 16 * 128
+UNDER = 40
+
+
+def take_shifted(ref, start, shift, rows):
+    lane = lax.broadcasted_iota(jnp.int32, (rows, 128), 1)
+    turn = lax.rem(128 - shift, 128)
+    here = pltpu.roll(ref[pl.ds(start, rows)], turn, 1)
+    after = pltpu.roll(ref[pl.ds(start + 1, rows)], turn, 1)
+    return jnp.where(lane < 128 - shift, here, after)
+
+
+def line_pieces(plan, role):
+    if role == 0:
+        return [(j * plan.up_rows, plan.up_rows, j, 4) for j in range(4)]
+    if role == 1:
+        part = plan.joint_rows // 2
+        return [
+            ((3 * k + j) * part, part, 3 * part * k + j, 3) for k in range(2) for j in range(3)
+        ]
+    return [(0, plan.rows, 0, 1)]
+
+
+def pack_kernel(plan, meta_ref, p_ref, before_ref, after_ref, out_ref, wide, flat, block):
+    full = plan.shard // 128
+    wide[:16] = before_ref[...].astype(f32)
+    wide[16 : 16 + full] = p_ref[:, : full * 128].reshape(full, 128)
+    wide[16 + full : 32 + full] = after_ref[...].astype(f32)
+    flat[...] = take_shifted(wide, meta_ref[1], meta_ref[2], plan.tile // 128)
+    for role in range(3):
+
+        @pl.when(meta_ref[0] == role)
+        def _():
+            for row, rows, line, stride in line_pieces(plan, role):
+                for j in range(6):
+                    block[row : row + rows, 128 * j : 128 * j + 128] = flat[
+                        pl.ds(6 * line + j, rows, stride=6 * stride)
+                    ]
+
+    out_ref[...] = block[...].astype(bf16)
+
+
+def pack_call(plan, meta, params, before, after):
+    full = plan.shard // 128
+    return pl.pallas_call(
+        functools.partial(pack_kernel, plan),
+        grid=(1,),
+        in_specs=[
+            SMEM_SPEC,
+            whole_spec((1, plan.shard)),
+            whole_spec((16, 128)),
+            whole_spec((16, 128)),
+        ],
+        out_specs=whole_spec((plan.rows, D)),
+        out_shape=jax.ShapeDtypeStruct((plan.rows, D), bf16),
+        scratch_shapes=[
+            pltpu.VMEM((full + 48, 128), f32),
+            pltpu.VMEM((plan.tile // 128, 128), f32),
+            pltpu.VMEM((plan.rows, D), f32),
+        ],
+        name="pack_weights",
+        compiler_params=pltpu.CompilerParams(vmem_limit_bytes=VMEM_LIMIT),
+    )(meta, params, before, after)
+
+
+def pack_weights(plan, place, params):
+    nb, shard = plan.nb, plan.shard
+    full = shard // 128 * 128
+    head = params[0, :EDGE].astype(bf16)
+    tail = params[0, shard - EDGE :].astype(bf16)
+    before = lax.ppermute(tail.reshape(16, 128), "batch", [(i, i + 1) for i in range(nb - 1)])
+    after = lax.ppermute(head.reshape(16, 128), "batch", [(i, i - 1) for i in range(1, nb)])
+    rest = shard - full
+    after = jnp.concatenate([tail[EDGE - rest :], after.reshape(-1)[: EDGE - rest]])
+    offsets = [
+        [EDGE + starts[i] - shard * i if 2 * i < nb or k else EDGE for i in range(nb)]
+        for k, starts in enumerate((plan.att_start, plan.mlp_start))
+    ]
+    offset = jnp.array(offsets, jnp.int32)[place.core, place.b]
+    meta = jnp.stack([place.role, offset // 128, offset % 128]).astype(jnp.int32)
+    block = pack_call(plan, meta, params, before, after.reshape(16, 128))
+    return block, jnp.concatenate([head, tail]).reshape(32, 128)
+
+
+def split_ends(plan, ends):
+    nb = plan.nb
+    head, tail = ends[:, :, :16].reshape(4, nb, EDGE), ends[:, :, 16:].reshape(4, nb, EDGE)
+
+    def piece(row, start, length):
+        first = start // plan.shard
+        inside = (first + 1) * plan.shard - start
+        at = start - first * plan.shard
+        if inside >= length:
+            if at + length <= EDGE:
+                return head[row, first, at : at + length]
+            at -= plan.shard - EDGE
+            return tail[row, first, at : at + length]
+        return jnp.concatenate(
+            [tail[row, first, EDGE - inside :], head[row, first + 1, : length - inside]]
+        )
+
+    rows = [ATT_VECS, MLP_VECS] * 2
+    return [[piece(i, *where).astype(f32)[None] for where in rows[i]] for i in range(4)]
+
+
+def past_kernel(w_ref, h_ref, out_ref):
+    one = jnp.zeros(h_ref.shape[1:], f32)
+    two = one
+    for j in range(HIST):
+        row = h_ref[j].astype(f32)
+        one = one + w_ref[j] * row
+        two = two + w_ref[HIST + 1 + j] * row
+    out_ref[0] = one.astype(bf16)
+    out_ref[1] = two.astype(bf16)
+
+
+HIST_ROWS = 32
+
+
+def past_call(mix_weights, history):
+    rows = history.shape[1]
+    return call(
+        past_kernel,
+        "past_averages",
+        (rows // HIST_ROWS,),
+        [SMEM_SPEC, pl.BlockSpec((HIST, HIST_ROWS, D), lambda i: (0, i, 0))],
+        [((2, rows, D), bf16, pl.BlockSpec((2, HIST_ROWS, D), lambda i: (0, i, 0)))],
+        [],
+        4 * HIST * rows * D,
+    )(mix_weights, history)[0]
+
+
+def history_kernel(scale, w_ref, h_ref, dy_ref, cot_ref, out_ref, sums_ref):
+    @pl.when(pl.program_id(0) == 0)
+    def _():
+        sums_ref[...] = jnp.zeros_like(sums_ref)
+
+    dy = dy_ref[...].astype(f32)
+    g = cot_ref[...].astype(f32) * scale
+    for j in range(HIST):
+        row = h_ref[j].astype(f32)
+        out_ref[j] = (w_ref[j] * dy + w_ref[HIST + 1 + j] * g).astype(bf16)
+        sums_ref[j : j + 1] += column_sum(dy * row)
+        sums_ref[HIST + j : HIST + j + 1] += column_sum(g * row)
+
+
+def history_call(scale, mix_weights, history, dy, cotangent):
+    rows = history.shape[1]
+    block = pl.BlockSpec((HIST, HIST_ROWS, D), lambda i: (0, i, 0))
+    part = pl.BlockSpec((HIST_ROWS, D), lambda i: (i, 0))
+    return call(
+        functools.partial(history_kernel, scale),
+        "history_grads",
+        (rows // HIST_ROWS,),
+        [SMEM_SPEC, block, part, part],
+        [
+            (history.shape, bf16, block),
+            ((2 * HIST, D), f32, whole_spec((2 * HIST, D))),
+        ],
+        [],
+        8 * HIST * rows * D,
+    )(mix_weights, history, dy, cotangent)
+
+
+STEP_ROWS = 1024
+
+
+def update_kernel(
+    plan, meta_ref, tile_ref, before_ref, after_ref, p_ref, m_ref, v_ref, g_ref, s_ref, mn_ref, vn_ref, wide
+):
+    step = pl.program_id(0)
+    end = UNDER + plan.tile // 128
+
+    @pl.when(step == 0)
+    def _():
+        for j in range(6):
+            columns = pl.ds(128 * j, 128)
+            wide[pl.ds(UNDER - 36 + j, 6, stride=6)] = before_ref[:, columns]
+            wide[pl.ds(end + j, 6, stride=6)] = after_ref[:, columns]
+        for role in range(3):
+
+            @pl.when(meta_ref[0] == role)
+            def _():
+                for row, rows, line, stride in line_pieces(plan, role):
+                    for j in range(6):
+                        wide[pl.ds(UNDER + 6 * line + j, rows, stride=6 * stride)] = tile_ref[
+                            row : row + rows, 128 * j : 128 * j + 128
+                        ]
+
+    size = g_ref.shape[1] // 128
+    grad = take_shifted(wide, meta_ref[1] + step * size, meta_ref[2], size)
+    grad = grad.reshape(1, size * 128)
+    g_ref[...] = grad
+    s_ref[...], mn_ref[...], vn_ref[...] = adamw(
+        p_ref[...], grad, m_ref[...], v_ref[...], weight_decay
+    )
+
+
+def update_call(plan, meta, tile, before, after, params, first, second):
+    size = min(STEP_ROWS, -(-plan.shard // 1024) * 8)
+    steps = pl.cdiv(plan.shard, size * 128)
+    flat = pl.BlockSpec((1, size * 128), lambda i: (0, i))
+    out = (params.shape, f32, flat)
+    return call(
+        functools.partial(update_kernel, plan),
+        "adamw_step",
+        (steps,),
+        [
+            SMEM_SPEC,
+            whole_spec((plan.rows, D)),
+            whole_spec((6, D)),
+            whole_spec((6, D)),
+            flat,
+            flat,
+            flat,
+        ],
+        [out] * 4,
+        [pltpu.VMEM((steps * size + 2 * UNDER + 8, 128), f32)],
+        20 * plan.shard,
+    )(meta, tile, before, after, params, first, second)
+
+
+def update_weights(plan, place, tile, vecs, params, first, second):
+    nb, b = plan.nb, place.b
+    tile = tile.astype(f32)
+
+    def lines(rows):
+        return jnp.concatenate([tile[r : r + 1] for r in rows], axis=0)
+
+    def ends(role):
+        pieces = line_pieces(plan, role)
+        if role == 0:
+            return [r for r, _, _, _ in pieces[:3]], [r + n - 1 for r, n, _, _ in pieces[1:]]
+        if role == 1:
+            return [r for r, _, _, _ in pieces[:3]], [r + n - 1 for r, n, _, _ in pieces[3:]]
+        return [0, 1, 2], [plan.rows - 3, plan.rows - 2, plan.rows - 1]
+
+    heads = jnp.stack([lines(ends(role)[0]) for role in range(3)])[place.role]
+    tails = jnp.stack([lines(ends(role)[1]) for role in range(3)])[place.role]
+    tails = lax.ppermute(tails, "batch", [(i, i + 1) for i in range(nb - 1)])
+    heads = lax.ppermute(heads, "batch", [(i, i - 1) for i in range(1, nb)])
+    none = jnp.zeros((6, D), f32)
+    last = none.at[3:].set(tails)
+    next_ = none.at[:3].set(heads)
+    first_two = none.at[4:].set(vecs[:2])
+    three, four = 3 * nb // 8, nb // 2
+    att = jnp.logical_not(place.mlp)
+    wide_b = vecs[2:5]
+    before = jnp.where(
+        b == 0,
+        first_two,
+        jnp.where(
+            place.mlp & (b == four),
+            jnp.concatenate([tails[1:], vecs[2:6]], axis=0),
+            jnp.where(att & (b == three), jnp.concatenate([tails, wide_b], axis=0), last),
+        ),
+    )
+    after = jnp.where(
+        place.mlp,
+        jnp.where(
+            b == four - 1,
+            jnp.concatenate([vecs[2:6], heads[:2]], axis=0),
+            jnp.where(b == nb - 1, none.at[:1].set(vecs[6:7]), next_),
+        ),
+        jnp.where(
+            b == three - 1,
+            jnp.concatenate([wide_b, heads], axis=0),
+            jnp.where(b == four - 1, none.at[:1].set(vecs[5:6]), next_),
+        ),
+    )
+    empty = att & (b >= four)
+    line = jnp.arange(plan.rows)[:, None]
+    tile = jnp.where(empty, jnp.where((line == 0) & (b == four), vecs[5:6], 0.0), tile)
+    offsets = [
+        [UNDER * 128 + shard_at - starts[i] for i, shard_at in enumerate(range(0, nb * plan.shard, plan.shard))]
+        for starts in (plan.att_start, plan.mlp_start)
+    ]
+    for i in range(four + 1, nb):
+        offsets[0][i] = offsets[0][four]
+    offset = jnp.array(offsets, jnp.int32)[place.core, b]
+    meta = jnp.stack([place.role, offset // 128, offset % 128]).astype(jnp.int32)
+    before = jnp.where(att & (b > four), none, before)
+    return update_call(plan, meta, tile, before, after, params, first, second)
+
+
 def mlp_tiles(plan, normed, dpre, active, er):
     count = plan.nb // 2
     up = weight_grad_call(
@@ -1091,6 +1327,275 @@
     return joint.reshape(count, plan.rows, D), out.reshape(plan.nb // 8, plan.rows, D)
 
 
+class Kind:
+    def __init__(self, refs):
+        self.sum, self.c, self.y, self.x, self.z, self.w, self.end = refs[:7]
+        self.load, self.sent, self.got = refs[7:]
+
+
+def reduce_kernel(tile_count, *refs):
+    inputs, refs = refs[:8], refs[8:]
+    small_ref, tile_ref, total_ref = refs[:3]
+    refs = refs[3:]
+    kinds = [Kind(refs[:10]), Kind(refs[10:20])]
+    fin, other_half, acc, part, fin_sem, small_sem = refs[20:]
+    section, b = lax.axis_index("section"), lax.axis_index("batch")
+    plane, core = section // 2, section % 2
+    x, z = b % 2, b // 2
+    low, high = z % 2, z // 2
+    to_core, to_plane = (section ^ 1, b), (section ^ 2, b)
+    to_x, to_low, to_high = (section, b ^ 1), (section, b ^ 2), (section, b ^ 4)
+    peers = [to_core, to_plane, to_x, to_high, to_low]
+    barrier = pltpu.get_barrier_semaphore()
+    for peer in peers:
+        pl.semaphore_signal(barrier, 1, device_id=peer, device_id_type=MESH)
+    pl.semaphore_wait(barrier, len(peers))
+
+    mine = []
+
+    def remote(src, dst, sent, got, to, cond=None):
+        copy = pltpu.make_async_remote_copy(
+            src, dst, sent, got, device_id=to, device_id_type=MESH
+        )
+        if cond is None:
+            copy.start()
+        else:
+            pl.when(cond)(copy.start)
+        mine.append((cond, copy))
+
+    def landed(dst, got):
+        pltpu.make_async_remote_copy(
+            dst, dst, kinds[0].sent.at[0, 0, 0], got, device_id=to_core, device_id_type=MESH
+        ).wait_recv()
+
+    def add(dst, at, src, src_at, rows):
+        def body(i, carry):
+            to = pl.ds(pl.multiple_of(at + i * 64, 64), 64)
+            fro = pl.ds(pl.multiple_of(src_at + i * 64, 64), 64)
+            dst[to, :] = (dst[to, :].astype(f32) + src[fro, :].astype(f32)).astype(bf16)
+            return carry
+
+        lax.fori_loop(0, rows // 64, body, 0)
+
+    loads = {}
+    order = [(layer, k) for layer in (1, 0) for k in (0, 1)]
+    for layer, k in order:
+        kind = kinds[k]
+        for tile in range(tile_count[k]):
+            first, second = inputs[4 * layer + 2 * k : 4 * layer + 2 * k + 2]
+            split = first.shape[0]
+            src = first.at[tile] if tile < split else second.at[tile - split]
+            here = src.at[pl.ds(pl.multiple_of(384 * core, 384), 384)]
+            there = src.at[pl.ds(pl.multiple_of(384 * (1 - core), 384), 384)]
+            remote(there, kind.c.at[layer, tile], kind.sent.at[0, layer, tile], kind.got.at[0, layer, tile], to_core)
+            pltpu.make_async_copy(here, kind.sum.at[layer, tile], kind.load.at[layer, tile]).start()
+
+    keep_at = pl.multiple_of(128 * plane, 128)
+    keep = pl.ds(keep_at, 256)
+
+    def column(k, step):
+        if k == 1:
+            return 1 - low if step == 0 else low
+        return 2 * step + (1 - low) if step < 2 else 2 * (step - 2) + low
+
+    def stage_core(layer, k, step):
+        kind = kinds[k]
+        zz = column(k, step)
+        for tile in (2 * zz + (1 - x), 2 * zz + x):
+            pltpu.make_async_copy(
+                inputs[0].at[0, pl.ds(0, 384)], kind.sum.at[layer, tile], kind.load.at[layer, tile]
+            ).wait()
+            landed(kind.c.at[layer, tile], kind.got.at[0, layer, tile])
+            add(kind.sum.at[layer, tile], 0, kind.c.at[layer, tile], 0, 384)
+            give = pl.ds(pl.multiple_of(256 * (1 - plane), 128), 128)
+            remote(
+                kind.sum.at[layer, tile, give],
+                kind.y.at[layer, tile],
+                kind.sent.at[1, layer, tile],
+                kind.got.at[1, layer, tile],
+                to_plane,
+            )
+
+    def stage_plane(layer, k, step):
+        kind = kinds[k]
+        zz = column(k, step)
+        for turn, tile in enumerate((2 * zz + (1 - x), 2 * zz + x)):
+            landed(kind.y.at[layer, tile], kind.got.at[1, layer, tile])
+            add(kind.sum.at[layer, tile], 256 * plane, kind.y.at[layer, tile], 0, 128)
+            if turn == 0:
+                remote(
+                    kind.sum.at[layer, tile, keep],
+                    kind.x.at[layer, zz],
+                    kind.sent.at[2, layer, zz],
+                    kind.got.at[2, layer, zz],
+                    to_x,
+                )
+
+    def stage_x(layer, k, step):
+        kind = kinds[k]
+        zz = column(k, step)
+        tile = 2 * zz + x
+        landed(kind.x.at[layer, zz], kind.got.at[2, layer, zz])
+        add(kind.sum.at[layer, tile], keep_at, kind.x.at[layer, zz], 0, 256)
+
+        half = 2 - k
+        if step < half:
+            remote(
+                kind.sum.at[layer, tile, keep],
+                kind.z.at[layer, step],
+                kind.sent.at[3, layer, step],
+                kind.got.at[3, layer, step],
+                to_low,
+            )
+        else:
+            landed(kind.z.at[layer, step - half], kind.got.at[3, layer, step - half])
+            add(kind.sum.at[layer, tile], keep_at, kind.z.at[layer, step - half], 0, 256)
+
+    def stage_high(layer, k):
+        kind = kinds[k]
+        zz = 2 * (1 - high) + low if k == 0 else low
+        remote(
+            kind.sum.at[layer, 2 * zz + x, keep],
+            kind.w.at[layer],
+            kind.sent.at[4, layer, 0],
+            kind.got.at[4, layer, 0],
+            to_high,
+            None if k == 0 else high == 1,
+        )
+
+    def stage_end(layer, k):
+        kind = kinds[k]
+        tile = 2 * (2 * high + low if k == 0 else low) + x
+
+        def take():
+            landed(kind.w.at[layer], kind.got.at[4, layer, 0])
+            add(kind.sum.at[layer, tile], keep_at, kind.w.at[layer], 0, 256)
+
+        cond = plane != layer
+        if k == 0:
+            take()
+        else:
+            pl.when(high == 0)(take)
+            cond = cond & (high == 0)
+        remote(
+            kind.sum.at[layer, tile, keep],
+            kind.end,
+            kind.sent.at[5, layer, 0],
+            kind.got.at[5, 0, 0],
+            to_plane,
+            cond,
+        )
+
+    def stage_small(step):
+        if step == 0:
+            acc[0] = small_ref[...]
+        else:
+            landed(part.at[step - 1], small_sem.at[1, step - 1])
+            acc[step] = acc[step - 1] + part[step - 1]
+        if step < len(peers):
+            remote(acc.at[step], part.at[step], small_sem.at[0, step], small_sem.at[1, step], peers[step])
+        else:
+            total_ref[...] = acc[step]
+
+    steps = [(layer, k, step) for layer, k in order for step in range(tile_count[k] // 2)]
+    later = {}
+    for at in range(len(steps) + 8):
+        if at < len(steps):
+            stage_core(*steps[at])
+        if at % 2 == 0 and at // 2 <= len(peers):
+            stage_small(at // 2)
+        if 0 <= at - 2 < len(steps):
+            stage_plane(*steps[at - 2])
+        if 0 <= at - 4 < len(steps):
+            layer, k, step = steps[at - 4]
+            stage_x(layer, k, step)
+            if step == tile_count[k] // 2 - 1:
+                stage_high(layer, k)
+                later[at + 2] = (layer, k)
+        if at in later:
+            stage_end(*later.pop(at))
+    for layer, k in later.values():
+        stage_end(layer, k)
+
+    def finish(k):
+        kind = kinds[k]
+        tile = 2 * (2 * high + low if k == 0 else low) + x
+        landed(kind.end, kind.got.at[5, 0, 0])
+        own = kind.sum.at[plane, tile]
+        here = pl.ds(pl.multiple_of(256 * plane, 128), 128)
+        there = pl.ds(pl.multiple_of(256 * (1 - plane), 128), 128)
+        fin[k, here] = own[here]
+        fin[k, there] = kind.end[pl.ds(pl.multiple_of(128 * (1 - plane), 128), 128)]
+        shared = kind.end[pl.ds(pl.multiple_of(128 * plane, 128), 128)].astype(f32)
+        fin[k, 128:256] = (own[128:256].astype(f32) + shared).astype(bf16)
+
+    owner = high == 0
+    pl.when(owner)(lambda: finish(1))
+    cond = jnp.logical_and(core == 1, owner)
+    remote(fin.at[1], other_half, fin_sem.at[0], fin_sem.at[2], to_core, cond)
+    finish(0)
+    remote(fin.at[0], other_half, fin_sem.at[1], fin_sem.at[2], to_core, core == 0)
+
+    def store(k):
+        tile_ref[pl.ds(pl.multiple_of(384 * core, 384), 384)] = fin[k]
+        landed(other_half, fin_sem.at[2])
+        tile_ref[pl.ds(pl.multiple_of(384 * (1 - core), 384), 384)] = other_half[...]
+
+    pl.when(core == 1)(lambda: store(0))
+    pl.when(jnp.logical_and(core == 0, owner))(lambda: store(1))
+
+    @pl.when(jnp.logical_and(core == 0, jnp.logical_not(owner)))
+    def _():
+        tile_ref[...] = jnp.zeros_like(tile_ref)
+
+    for cond, copy in mine:
+        if cond is None:
+            copy.wait_send()
+        else:
+            pl.when(cond)(copy.wait_send)
+
+
+def reduce_call(tiles, small):
+    counts = (8, 4)
+    scratch = []
+    for count in counts:
+        scratch += [
+            pltpu.VMEM((2, count, 384, D), bf16),
+            pltpu.VMEM((2, count, 384, D), bf16),
+            pltpu.VMEM((2, count, 128, D), bf16),
+            pltpu.VMEM((2, count // 2, 256, D), bf16),
+            pltpu.VMEM((2, 2, 256, D), bf16),
+            pltpu.VMEM((2, 256, D), bf16),
+            pltpu.VMEM((256, D), bf16),
+            pltpu.SemaphoreType.DMA((2, count)),
+            pltpu.SemaphoreType.DMA((6, 2, count)),
+            pltpu.SemaphoreType.DMA((6, 2, count)),
+        ]
+    scratch += [
+        pltpu.VMEM((2, 384, D), bf16),
+        pltpu.VMEM((384, D), bf16),
+        pltpu.VMEM((6,) + small.shape, f32),
+        pltpu.VMEM((5,) + small.shape, f32),
+        pltpu.SemaphoreType.DMA((3,)),
+        pltpu.SemaphoreType.DMA((2, 5)),
+    ]
+    return pl.pallas_call(
+        functools.partial(reduce_kernel, counts),
+        in_specs=[pl.BlockSpec(memory_space=pltpu.HBM)] * 8
+        + [pl.BlockSpec(memory_space=pltpu.VMEM)],
+        out_specs=[pl.BlockSpec(memory_space=pltpu.VMEM)] * 2,
+        out_shape=[
+            jax.ShapeDtypeStruct((D, D), bf16),
+            jax.ShapeDtypeStruct(small.shape, f32),
+        ],
+        scratch_shapes=scratch,
+        name="reduce_gradients",
+        compiler_params=pltpu.CompilerParams(
+            collective_id=1, has_side_effects=True, vmem_limit_bytes=60 * 1024 * 1024
+        ),
+    )(*tiles, small)
+
+
 def reduce_tiles(place, tiles):
     plan = place.plan
     nb, half = plan.nb, plan.rows // 2
@@ -1100,29 +1605,25 @@
     give = jnp.where(first, tiles[:, 1], tiles[:, 0])
     total = keep.astype(f32) + swap_cores(give).astype(f32)
     total = total.astype(bf16)
-    if nb != 8:
-        if total.shape[0] < nb:
-            empty = jnp.zeros((nb - total.shape[0],) + total.shape[1:], bf16)
-            total = jnp.concatenate([total, empty], axis=0)
-        return lax.psum_scatter(total, "batch", scatter_dimension=0, tiled=True)[0]
-    b = place.b
-
-    def halve(total, bit, axis):
-        low = (b & bit) == 0
-        zero = lax.index_in_dim(total, 0, axis, keepdims=False)
-        one = lax.index_in_dim(total, 1, axis, keepdims=False)
-        got = lax.ppermute(
-            jnp.where(low, one, zero), "batch", [(i, i ^ bit) for i in range(nb)]
-        )
-        return (jnp.where(low, zero, one).astype(f32) + got.astype(f32)).astype(bf16)
-
-    total = halve(total.reshape(-1, 2, half, D), 1, 1)
-    if total.shape[0] == 4:
-        total = halve(total.reshape(2, 2, half, D), 4, 0)
-    else:
-        got = lax.ppermute(total, "batch", [(i, i - 4) for i in range(4, nb)])
-        total = (total.astype(f32) + got.astype(f32)).astype(bf16)
-    return halve(total, 2, 0)
+    if total.shape[0] < nb:
+        empty = jnp.zeros((nb - total.shape[0],) + total.shape[1:], bf16)
+        total = jnp.concatenate([total, empty], axis=0)
+    return lax.psum_scatter(total, "batch", scatter_dimension=0, tiled=True)[0]
+
+
+def reduce_blocks(place, tiles):
+    parts = [reduce_tiles(place, pair) for layer in tiles for pair in (layer[2:], layer[:2])]
+    upper, lower = jnp.stack(parts[:2]), jnp.stack(parts[2:])
+    first_plane, first_core = place.plane == 0, place.core == 0
+    keep = jnp.where(first_plane, upper, lower)
+    give = jnp.where(first_plane, lower, upper)
+    keep = keep.astype(f32) + swap_planes(give).astype(f32)
+    mine = jnp.where(first_core, keep[0], keep[1])
+    other = jnp.where(first_core, keep[1], keep[0])
+    got = swap_cores(other.astype(bf16)).astype(f32)
+    first = jnp.where(first_core, mine, got)
+    second = jnp.where(first_core, got, mine)
+    return jnp.concatenate([first, second], axis=0).astype(bf16)
 
 
 def local(
@@ -1143,9 +1644,11 @@
     place.plan = plan
     section = lax.axis_index("section")
     b = place.b = lax.axis_index("batch")
-    plane = section // 2
+    plane = place.plane = section // 2
     place.core = section % 2
     place.mlp = section % 2 == 1
+    b_role = jnp.where(8 * b < 3 * nb, 1, 2)
+    place.role = jnp.where(place.mlp, jnp.where(2 * b < nb, 0, 2), b_role)
     place.outer = (section == 0) | (section == 3)
     span = place.span = stream_in.shape[0] // 2
     low_half = plane == 0
@@ -1167,27 +1670,16 @@
 
     to_owner = to_compute
 
-    block, vecs = pack_weights(plan, place, params)
-    if nb == 8:
-        att, mlp, vec_parts = gather_weights(plan, block, vecs)
-        vec_parts = vec_parts.reshape(4, nb, -1, D)
-    else:
-        att, mlp, vec_parts = gather_blocks(plan, block, vecs)
-    all_vecs = jnp.sum(vec_parts.astype(f32), axis=1)
-    att_vecs = [split_vecs(all_vecs[2 * layer], ATT_VECS) for layer in range(2)]
-    mlp_vecs = [split_vecs(all_vecs[2 * layer + 1], MLP_VECS) for layer in range(2)]
-
-    first_mix = mix_weights[:HIST]
-    second_mix = mix_weights[HIST + 1 : 2 * HIST + 1]
-    past_one = jnp.zeros(stream_in.shape, f32)
-    past_two = jnp.zeros(stream_in.shape, f32)
-    for j in range(HIST):
-        row = history[j].astype(f32)
-        past_one = past_one + first_mix[j] * row
-        past_two = past_two + second_mix[j] * row
+    block, ends = pack_weights(plan, place, params)
+    gather = gather_weights if nb == 8 else gather_blocks
+    att, mlp, ends = gather(plan, block, ends)
+    all_vecs = split_ends(plan, ends.reshape(4, nb, 32, 128))
+    att_vecs, mlp_vecs = all_vecs[::2], all_vecs[1::2]
+
+    past = past_call(mix_weights, history)
     stream = to_compute(stream_in)
     cot, past_one, past_two = to_compute(
-        jnp.stack([cotangent, past_one.astype(bf16), past_two.astype(bf16)])
+        jnp.concatenate([cotangent[None], past], axis=0)
     )
     row_index = jnp.concatenate([s + jnp.arange(span) for s in place.starts])
     position = jnp.where(place.kind == 1, row_index % SEQ_SHORT, row_index)
@@ -1199,13 +1691,10 @@
     ).astype(jnp.int32)
     cosine, sine = place.turn
 
-    def line(v):
-        return v.reshape(1, -1)
-
     def forward(layer, x, past, extra):
         gain, bias, joint_b, out_b = att_vecs[layer]
         normed, q, kv = qkv_call(
-            layer, x, line(gain), line(bias), att, line(joint_b), cosine, sine
+            layer, x, gain, bias, att, joint_b, cosine, sine
         )
         kv_other = swap_cores(kv)
         mixed, lse = att_call(meta, q, kv, kv_other)
@@ -1216,12 +1705,12 @@
             x,
             mixed,
             att,
-            line(out_b),
-            line(gain),
-            line(bias),
+            out_b,
+            gain,
+            bias,
             mlp,
-            line(up_b),
-            line(down_b),
+            up_b,
+            down_b,
             past,
             extra,
         )
@@ -1231,18 +1720,18 @@
         x, normed, q, kv, kv_other, mixed, lse = kept
         h, n_m, act, slope = outs[:4]
         er, dpre, dub, dh, datt, sums = mlp_back_call(
-            layer, mix, cot, dy, h, line(mlp_vecs[layer][0]), mlp, slope, att
+            layer, mix, cot, dy, h, mlp_vecs[layer][0], mlp, slope, att
         )
-        mlp_part = reduce_tiles(place, mlp_tiles(plan, n_m, dpre, act, er))
+        up_part, down_part = mlp_tiles(plan, n_m, dpre, act, er)
         dq, own, give = att_back_call(meta, q, kv, kv_other, datt, mixed, lse, cosine, sine)
-        gain = line(att_vecs[layer][0])
+        gain = att_vecs[layer][0]
         dj, djb, dx, sums_a = qkv_back_call(
             layer, dq, own, swap_cores(give), cosine, sine, att, x, gain, dh, carried
         )
-        att_part = reduce_tiles(place, att_tiles(plan, normed, dj, mixed, dh))
+        joint_part, out_part = att_tiles(plan, normed, dj, mixed, dh)
         vec_m = (sums[0], sums[1], dub[0], sums[2])
         vec_a = (sums_a[0], sums_a[1], djb[0], sums[3])
-        return dx, sums_a[2], vec_a, vec_m, att_part, mlp_part
+        return dx, sums_a[2], vec_a, vec_m, (up_part, down_part, joint_part, out_part)
 
     kept20, outs20 = forward(0, stream, past_one, ())
     y20, c20 = outs20[4:]
@@ -1250,31 +1739,15 @@
     y21, sums21 = outs21[4:]
     stream_out = to_owner(y21)
     mix41, mix42 = jnp.sum(sums21[0]), jnp.sum(sums21[1])
-    dy20, mix20, vec_a21, vec_m21, att21, mlp21 = backward(1, y20, kept21, outs21, c20)
+    dy20, mix20, vec_a21, vec_m21, tiles21 = backward(1, y20, kept21, outs21, c20)
     mix20 = jnp.sum(mix20)
-    dstream, _, vec_a20, vec_m20, att20, mlp20 = backward(0, dy20, kept20, outs20, c20)
+    dstream, _, vec_a20, vec_m20, tiles20 = backward(0, dy20, kept20, outs20, c20)
     dy20_own = to_owner(dy20)
     stream_grad = to_owner(dstream).astype(f32)
 
-    upper = jnp.stack([att20, mlp20])
-    lower = jnp.stack([att21, mlp21])
-    keep = jnp.where(low_half, upper, lower)
-    give = jnp.where(low_half, lower, upper)
-    keep = keep.astype(f32) + swap_planes(give).astype(f32)
-    mine = jnp.where(place.core == 0, keep[0], keep[1])
-    other = jnp.where(place.core == 0, keep[1], keep[0])
-    got = swap_cores(other.astype(bf16)).astype(f32)
-    first = jnp.where(place.core == 0, mine, got)
-    second = jnp.where(place.core == 0, got, mine)
-    tile_grad = jnp.concatenate([first, second], axis=0)
-
-    own_g = cotangent.astype(f32) * grad_scale
-    own_dy = dy20_own.astype(f32)
-    history_grad = (
-        first_mix[:, None, None] * own_dy[None] + second_mix[:, None, None] * own_g[None]
-    ).astype(bf16)
-    mix_one = jnp.sum(own_dy[None] * history.astype(f32), axis=(1, 2))
-    mix_two = jnp.sum(own_g[None] * history.astype(f32), axis=(1, 2))
+    history_grad, mix_sums = history_call(grad_scale, mix_weights, history, dy20_own, cotangent)
+    mix_sums = jnp.sum(mix_sums, axis=1)
+    mix_one, mix_two = mix_sums[:HIST], mix_sums[HIST:]
     own_mix = jnp.concatenate([mix_one, mix20[None], mix_two, mix41[None], mix42[None]])
 
     def flat_vec(v):
@@ -1284,55 +1757,22 @@
     small = jnp.concatenate(
         [flat_vec(v) for v in (vec_a20, vec_m20, vec_a21, vec_m21)] + [own_mix]
     )
-    small = lax.psum(small, ("section", "batch"))
-    mix_grad = small[4 * VEC :]
+    if nb == 8:
+        lines = -(-small.shape[0] // 1024) * 8
+        small = jnp.concatenate([small, jnp.zeros((lines * 128 - small.shape[0],), f32)])
+        tile_grad, small = reduce_call(tiles20 + tiles21, small.reshape(lines, 128))
+        small = small.reshape(-1)
+    else:
+        tile_grad = reduce_blocks(place, (tiles20, tiles21))
+        small = lax.psum(small, ("section", "batch"))
+    mix_grad = small[4 * VEC : 4 * VEC + own_mix.shape[0]]
     vec_rows = small[: 4 * VEC].reshape(4, VEC)
     vec_own = lax.dynamic_index_in_dim(vec_rows, section, 0, keepdims=False)
 
-    rows = plan.rows
-    plain = tile_grad.reshape(-1)
-    up = tile_grad.reshape(FF // D, plan.up_rows, D).transpose(1, 0, 2).reshape(-1)
-    joint = tile_grad.reshape(2, 3, plan.joint_rows // 2, D).transpose(0, 2, 1, 3).reshape(-1)
-    is_up = place.mlp & (2 * b < nb)
-    is_joint = jnp.logical_not(place.mlp) & (8 * b < 3 * nb)
-    flat = jnp.where(is_up, up, jnp.where(is_joint, joint, plain))
-    flat = jnp.where(place.mlp | (2 * b < nb), flat, 0.0)
-    halo = max(
-        [0]
-        + [
-            max(s[i] + plan.tile - plan.shard * (i + 1), plan.shard * i - s[i])
-            for s, n in ((plan.mlp_start, nb), (plan.att_start, nb // 2))
-            for i in range(n)
-        ]
-    )
-    before = lax.ppermute(flat[-halo:], "batch", [(i, i + 1) for i in range(nb - 1)])
-    after = lax.ppermute(flat[:halo], "batch", [(i, i - 1) for i in range(1, nb)])
-    starts = jnp.array([plan.att_start, plan.mlp_start])[place.mlp.astype(jnp.int32)]
-    margin = 4 * D + halo
-    shift = margin - plan.shard * b
-    window = jnp.zeros((plan.shard + 2 * margin,), f32)
-
-    def put(window, piece, at):
-        at = jnp.clip(at, 0, window.shape[0] - piece.shape[0])
-        return lax.dynamic_update_slice(window, piece, (at,))
-
-    window = put(window, before, starts[jnp.maximum(b - 1, 0)] + plan.tile - halo + shift)
-    window = put(window, after, starts[jnp.minimum(b + 1, nb - 1)] + shift)
-    window = put(window, flat, starts[b] + shift)
-
-    def with_vecs(window, pieces):
-        at = 0
-        for start, length in pieces:
-            window = put(window, vec_own[at : at + length], start + shift)
-            at += length
-        return window[margin : margin + plan.shard]
-
-    grad = jnp.where(place.mlp, with_vecs(window, MLP_VECS), with_vecs(window, ATT_VECS))
-    grad = grad.reshape(params.shape)
-    bias_grad = jnp.where(place.mlp, vec_own[6 * D : 7 * D], vec_own[5 * D : 6 * D])[None]
-
-    params_step, first_new, second_new = adamw(
-        params, grad, first_moment, second_moment, weight_decay
+    vec_lines = vec_own.reshape(VEC // D, D)
+    bias_grad = jnp.where(place.mlp, vec_lines[6], vec_lines[5])[None]
+    grad, params_step, first_new, second_new = update_weights(
+        plan, place, tile_grad, vec_lines, params, first_moment, second_moment
     )
     mix_step, mix_first_new, mix_second_new = adamw(
         mix_weights, mix_grad, mix_first, mix_second, 0.0

time: 1110 us -> 676 us (0.61)
  waiting for transfers between devices: 346 us -> 0.98 us
  Pallas kernels: 361 us -> 595 us
  other arithmetic: 199 us -> 32.9 us
  local copies, waits for them, and re-layouts: 110 us -> 14.3 us
  starting transfers between devices: 57.2 us -> 16.7 us
  between operations: 20.1 us -> 7.89 us
    pallas_call x0 -> x5, Pallas kernels: none -> 242 us  [the longest x1 193 us: reduce_call(): pl.pallas_call(functools.partial(reduce_kernel, counts), in_specs=[pl.Blo...]
    ppermute x17 -> x4, waiting for transfers between devices: 227 us -> 0.01 us  [the longest x1 0.01 us: pack_weights(): lax.ppermute(head.reshape(16, 128), 'batch', [(i, i - 1) for i in range(1...]
    psum x1 -> x0, waiting for transfers between devices: 117 us -> none  [local(): small = lax.psum(small, ('section', 'batch'))]
    convert_element_type x18 -> x5, other arithmetic: 86.4 us -> 5.5 us  [the longest x1 2.92 us: update_weights(): tile = tile.astype(f32)]
    ppermute x17 -> x4, starting transfers between devices: 49.8 us -> 12.1 us  [the longest x1 4.84 us: pack_weights(): lax.ppermute(tail.reshape(16, 128), 'batch', [(i, i + 1) for i in range(n...]
    add x2 -> x1, other arithmetic: 28.8 us -> 0.53 us  [adamw(): direction = first_hat / (jnp.sqrt(second_hat) + adam_eps) + decay * param]
    dynamic_update_slice x9 -> x0, local copies, waits for them, and re-layouts: 27 us -> none  [put(): return lax.dynamic_update_slice(window, piece, (at,))]
    reshape x8 -> x2, local copies, waits for them, and re-layouts: 26 us -> 0.12 us  [the longest x1 0.06 us: split_ends(): ends[:, :, 16:].reshape(4, nb, EDGE)]
  transfers between devices with their start and end apart: 32 -> 13, of which waited for: 13 -> 1; matrix products, arithmetic and copies ran while one was open for 19% -> 5% of each run, Pallas kernels for 23% -> 35%
where the time goes in v3:
time: 676 us; the launch traced here: 668 us
  Pallas kernels  595 us (88%)
  other arithmetic  32.9 us (5%)
  starting transfers between devices  16.7 us (2%)
  local copies, waits for them, and re-layouts  14.3 us (2%)
  between operations  7.89 us (1%)
    pallas_call x1, Pallas kernels, reduce_call(): pl.pallas_call(functools.partial(reduce_kernel, counts), in_specs=[pl.Blo...  193 us
    pallas_call x1, Pallas kernels, gather_weights(): pl.pallas_call(body, in_specs=[any_spec] * 2, out_specs=[any_spec] * 3, o...  135 us
    pallas_call x8, Pallas kernels, weight_grad_call(): call(weight_grad_kernel, name, (steps,), [pl.BlockSpec((rows, D), (lambda...  44.2 us
    pallas_call x2, Pallas kernels, att_back_call(): call(att_back_kernel, 'attention_grad_rows', (pairs,), [SMEM_SPEC, pair_s...  39.6 us
    pallas_call x2, Pallas kernels, mlp_call(): call(functools.partial(mlp_kernel, last_layer), 'feed_forward_rows', (FF...  34.1 us
    pallas_call x2, Pallas kernels, mlp_back_call(): call(functools.partial(mlp_back_kernel, last_layer), 'feed_forward_grad_r...  32.9 us
    pallas_call x2, Pallas kernels, att_call(): call(att_kernel, 'attention_rows', (pairs,), [SMEM_SPEC, pair_spec(rows),...  27.2 us
    pallas_call x1, Pallas kernels, history_call(): call(functools.partial(history_kernel, scale), 'history_grads', (rows //...  20.7 us
  transfers between devices with their start and end apart: 13, of which 1 were waited for; matrix products, arithmetic and copies ran while one was open for 5% of the time, Pallas kernels for 35%

profile of v3, /device:TPU:0, one launch (start us, length us, event | category | flops | bytes accessed | tf_op | source)
XLA Modules:
  0.0 668.1 jit_solution(5280604955336430508)
XLA Ops:
  1.5 4.8 collective-permute-start.1
  6.3 1.3 collective-permute-start.2
  7.6 1.9 broadcast_select_fusion.18
  10.2 14.9 %past_averages.1 = bf16[2,512,768]{2,1,0:T(8,128)(2,1)} custom-call(f32[43]{0:T(128)} %w_ref.3, bf16[20,512,768]{2,1,0:T(8,128)(2,1)} %h_ref.3), custom_call_target="tpu_custom_call" | custom-call | flops 31457280 | bytes 2359296 | tf_op jit(solution)/shard_map/past_averages/pallas_call | solution.py:1129
  25.2 2.7 broadcast_select_fusion.2
  27.9 1.1 collective-permute-start.4
  35.4 1.0 fusion.6
  39.0 1.2 pad_maximum_fusion.12.mix_ref
  42.1 4.4 pack_weights.1.block_ref
  46.5 135.1 %gather_weights.1 = (bf16[2,4,768,768]{3,2,1,0:T(8,128)(2,1)}, bf16[2,8,768,768]{3,2,1,0:T(8,128)(2,1)}, bf16[32,32,128]{2,1,0:T(8,128)(2,1)}) custom-call(bf16[768,768]{1,0:T(8,128)(2,1)} %pack_weights.1.block_ref, bf16[32,128]{1,0:T(8,128)(2,1)} %pad_maximum_fusion.11.vec_ref), custom_call_target="tpu_custom_call" | custom-call | tf_op jit(solution)/shard_map/gather_weights/pallas_call | solution.py:329
  181.5 1.0 fusion.45
  185.2 9.8 %qkv_rows.2 = (bf16[512,768]{1,0:T(8,128)(2,1)}, bf16[512,768]{1,0:T(8,128)(2,1)}, bf16[512,1536]{1,0:T(8,128)(2,1)}) custom-call(bf16[512,768]{1,0:T(8,128)(2,1)} %pad_maximum_fusion.2.x_ref, f32[1,768]{1,0:T(1,128)} %get-tuple-element.277.gain_ref, f32[1,768]{1,0:T(1,128)} %get-tuple-element.278.bias_ref, bf16[2,8,3,128,768]{4,3,2,1,0:T(8,128)(2,1)} %bitcast.151, ...), custom_call_target="tpu_custom_call" | custom-call | flops 1811939328 | bytes 2359296 | tf_op jit(solution)/shard_map/qkv_rows/pallas_call | solution.py:434
  196.3 1.5 fusion.5
  198.8 13.6 %attention_rows.2 = (bf16[512,768]{1,0:T(8,128)(2,1)}, f32[6,512,128]{2,1,0:T(8,128)}) custom-call(s32[4]{0:T(128)} %pad_add_fusion.1.meta_ref, bf16[512,768]{1,0:T(8,128)(2,1)} %get-tuple-element.133.q_ref, bf16[512,1536]{1,0:T(8,128)(2,1)} %get-tuple-element.134.k_ref.v_ref, bf16[512,1536]{1,0:T(8,128)(2,1)} %get-tuple-element.134.k_ref.v_ref, ...), custom_call_target="tpu_custom_call" | custom-call | flops 4026531840 | bytes 2359296 | tf_op jit(solution)/shard_map/attention_rows/pallas_call | solution.py:548
  212.3 16.7 %feed_forward_rows.2 = (bf16[512,768]{1,0:T(8,128)(2,1)}, bf16[512,768]{1,0:T(8,128)(2,1)}, bf16[512,3072]{1,0:T(8,128)(2,1)}, bf16[512,3072]{1,0:T(8,128)(2,1)}...) custom-call(f32[4]{0:T(128)} %pad_maximum_fusion.12.mix_ref, bf16[512,768]{1,0:T(8,128)(2,1)} %pad_maximum_fusion.2.x_ref, ...), custom_call_target="tpu_custom_call" | custom-call | flops 5435817984 | bytes 2359296 | tf_op jit(solution)/shard_map/feed_forward_rows/pallas_call | solution.py:642
  229.1 9.7 %qkv_rows.3 = (bf16[512,768]{1,0:T(8,128)(2,1)}, bf16[512,768]{1,0:T(8,128)(2,1)}, bf16[512,1536]{1,0:T(8,128)(2,1)}) custom-call(bf16[512,768]{1,0:T(8,128)(2,1)} %get-tuple-element.137.x_ref.dy_ref, f32[1,768]{1,0:T(1,128)} %get-tuple-element.282.gain_ref, f32[1,768]{1,0:T(1,128)} %get-tuple-element.283.bias_ref, bf16[2,8,3,128,768]{4,3,2,1,0:T(8,128)(2,1)} %bitcast.152, ...), custom_call_target="tpu_custom_call" | custom-call | flops 1811939328 | bytes 2359296 | tf_op jit(solution)/shard_map/qkv_rows/pallas_call | solution.py:434
  242.8 1.1 copy-done.23
  243.9 13.7 %attention_rows.3 = (bf16[512,768]{1,0:T(8,128)(2,1)}, f32[6,512,128]{2,1,0:T(8,128)}) custom-call(s32[4]{0:T(128)} %pad_add_fusion.1.meta_ref, bf16[512,768]{1,0:T(8,128)(2,1)} %get-tuple-element.138.q_ref, bf16[512,1536]{1,0:T(8,128)(2,1)} %get-tuple-element.139.k_ref.v_ref, bf16[512,1536]{1,0:T(8,128)(2,1)} %get-tuple-element.139.k_ref.v_ref, ...), custom_call_target="tpu_custom_call" | custom-call | flops 4026531840 | bytes 2359296 | tf_op jit(solution)/shard_map/attention_rows/pallas_call | solution.py:548
  257.6 17.4 %feed_forward_rows.3 = (bf16[512,768]{1,0:T(8,128)(2,1)}, bf16[512,768]{1,0:T(8,128)(2,1)}, bf16[512,3072]{1,0:T(8,128)(2,1)}, bf16[512,3072]{1,0:T(8,128)(2,1)}...) custom-call(f32[4]{0:T(128)} %pad_maximum_fusion.12.mix_ref, bf16[512,768]{1,0:T(8,128)(2,1)} %get-tuple-element.137.x_ref.dy_ref, ...), custom_call_target="tpu_custom_call" | custom-call | flops 5435817984 | bytes 2359296 | tf_op jit(solution)/shard_map/feed_forward_rows/pallas_call | solution.py:642
  275.0 16.4 %feed_forward_grad_rows.2 = (bf16[512,768]{1,0:T(8,128)(2,1)}, bf16[512,3072]{1,0:T(8,128)(2,1)}, f32[1,3072]{1,0:T(1,128)}, bf16[512,768]{1,0:T(8,128)(2,1)}, b...) custom-call(f32[4]{0:T(128)} %pad_maximum_fusion.12.mix_ref, bf16[512,768]{1,0:T(8,128)(2,1)} %get-tuple-element.219.rest_1_.cot_ref, ...), custom_call_target="tpu_custom_call" | custom-call | flops 5435817984 | bytes 2359296 | tf_op jit(solution)/shard_map/feed_forward_grad_rows/pallas_call | solution.py:750
  291.3 19.7 %attention_grad_rows.2 = (bf16[512,768]{1,0:T(8,128)(2,1)}, f32[2,512,768]{2,1,0:T(8,128)}, bf16[2,512,768]{2,1,0:T(8,128)(2,1)}) custom-call(s32[4]{0:T(128)} %pad_add_fusion.1.meta_ref, bf16[512,768]{1,0:T(8,128)(2,1)} %get-tuple-element.138.q_ref, bf16[512,1536]{1,0:T(8,128)(2,1)} %get-tuple-element.139.k_ref.v_ref, ...), custom_call_target="tpu_custom_call" | custom-call | flops 10066329600 | bytes 2359296 | tf_op jit(solution)/shard_map/attention_grad_rows/pallas_call | solution.py:865
  312.2 1.2 collective-permute-start.6
  313.5 1.4 slice_reduce_fusion
  314.9 6.7 %down_grad.3 = bf16[3072,768]{1,0:T(8,128)(2,1)} custom-call(bf16[512,3072]{1,0:T(8,128)(2,1)} %get-tuple-element.170.a_ref, bf16[512,768]{1,0:T(8,128)(2,1)} %get-tuple-element.171.b_ref), custom_call_target="tpu_custom_call" | custom-call | flops 2415919104 | bytes 2359296 | tf_op jit(solution)/shard_map/down_grad/pallas_call | solution.py:994
  321.6 3.2 out_grad.3
  324.9 6.5 up_grad.3
  332.4 1.1 copy-done.8
  333.6 10.4 %qkv_grad_rows.2 = (bf16[512,2304]{1,0:T(8,128)(2,1)}, f32[1,2304]{1,0:T(1,128)}, bf16[512,768]{1,0:T(8,128)(2,1)}, f32[8,768]{1,0:T(8,128)}) custom-call(bf16[512,768]{1,0:T(8,128)(2,1)} %get-tuple-element.147.dq_ref, f32[2,512,768]{2,1,0:T(8,128)} %get-tuple-element.148.own_ref, bf16[2,512,768]{2,1,0:T(8,128)(2,1)} %copy-done.8, ...), custom_call_target="tpu_custom_call" | custom-call | flops 1811939328 | bytes 2359296 | tf_op jit(solution)/shard_map/qkv_grad_rows/pallas_call | solution.py:949
  343.9 16.6 %feed_forward_grad_rows.3 = (bf16[512,768]{1,0:T(8,128)(2,1)}, bf16[512,3072]{1,0:T(8,128)(2,1)}, f32[1,3072]{1,0:T(1,128)}, bf16[512,768]{1,0:T(8,128)(2,1)}, b...) custom-call(f32[4]{0:T(128)} %pad_maximum_fusion.12.mix_ref, bf16[512,768]{1,0:T(8,128)(2,1)} %get-tuple-element.219.rest_1_.cot_ref, ...), custom_call_target="tpu_custom_call" | custom-call | flops 5435817984 | bytes 2359296 | tf_op jit(solution)/shard_map/feed_forward_grad_rows/pallas_call | solution.py:750
  360.5 19.9 %attention_grad_rows.3 = (bf16[512,768]{1,0:T(8,128)(2,1)}, f32[2,512,768]{2,1,0:T(8,128)}, bf16[2,512,768]{2,1,0:T(8,128)(2,1)}) custom-call(s32[4]{0:T(128)} %pad_add_fusion.1.meta_ref, bf16[512,768]{1,0:T(8,128)(2,1)} %get-tuple-element.133.q_ref, bf16[512,1536]{1,0:T(8,128)(2,1)} %get-tuple-element.134.k_ref.v_ref, ...), custom_call_target="tpu_custom_call" | custom-call | flops 10066329600 | bytes 2359296 | tf_op jit(solution)/shard_map/attention_grad_rows/pallas_call | solution.py:865
  381.3 3.2 out_grad.2
  384.5 1.5 slice_reduce_fusion.2
  386.1 6.5 down_grad.2
  392.6 5.6 joint_grad.3
  398.2 6.6 up_grad.2
  405.8 20.7 %history_grads.1 = (bf16[20,512,768]{2,1,0:T(8,128)(2,1)}, f32[40,768]{1,0:T(8,128)}) custom-call(f32[43]{0:T(128)} %w_ref.3, bf16[20,512,768]{2,1,0:T(8,128)(2,1)} %h_ref.3, bf16[512,768]{1,0:T(8,128)(2,1)} %pad_maximum_fusion.4.dy_ref, bf16[512,768]{1,0:T(8,128)(2,1)} %cot_ref.1), custom_call_target="tpu_custom_call" | custom-call | flops 62914560 | bytes 2359296 | tf_op jit(solution)/shard_map/history_grads/pallas_call | solution.py:1158
  426.5 1.0 reduce_sum.36
  427.6 1.1 copy-done.7
  428.8 10.2 %qkv_grad_rows.3 = (bf16[512,2304]{1,0:T(8,128)(2,1)}, f32[1,2304]{1,0:T(1,128)}, bf16[512,768]{1,0:T(8,128)(2,1)}, f32[8,768]{1,0:T(8,128)}) custom-call(bf16[512,768]{1,0:T(8,128)(2,1)} %get-tuple-element.156.dq_ref, f32[2,512,768]{2,1,0:T(8,128)} %get-tuple-element.157.own_ref, bf16[2,512,768]{2,1,0:T(8,128)(2,1)} %copy-done.7, ...), custom_call_target="tpu_custom_call" | custom-call | flops 1811939328 | bytes 2359296 | tf_op jit(solution)/shard_map/qkv_grad_rows/pallas_call | solution.py:949
  440.5 5.8 joint_grad.2
  446.3 2.7 concatenate.167
  449.0 192.6 %reduce_gradients.1 = (bf16[768,768]{1,0:T(8,128)(2,1)}, f32[176,128]{1,0:T(8,128)}) custom-call(bf16[4,768,768]{2,1,0:T(8,128)(2,1)} %bitcast.162, bf16[4,768,768]{2,1,0:T(8,128)(2,1)} %bitcast.161, bf16[3,768,768]{2,1,0:T(8,128)(2,1)} %bitcast.164, bf16[1,768,768]{2,1,0:T(8,128)(2,1)} %bitcast.158, bf16[4,768,768]{2,1,0:T(8,128)(2,1)} %bitcast.160, ...), custom_call_target="tpu_custom_call" | custom-call | tf_op jit(solution)/shard_map/reduce_gradients/pallas_call | solution.py:1582
  642.5 2.9 convert_element_type.258
  647.1 1.3 collective-permute-start.12
  648.5 4.7 collective-permute-start.11
  653.2 1.7 select_select_fusion.tile_ref
  657.1 9.5 %adamw_step.1 = (f32[1,590496]{1,0:T(1,128)}, f32[1,590496]{1,0:T(1,128)}, f32[1,590496]{1,0:T(1,128)}, f32[1,590496]{1,0:T(1,128)}) custom-call(s32[3]{0:T(128)} %pad_add_fusion.3.meta_ref, f32[768,768]{1,0:T(8,128)} %select_select_fusion.tile_ref, f32[6,768]{1,0:T(8,128)} %fusion.11.before_ref, f32[6,768]{1,0:T(8,128)} %fusion.8.after_ref, ...), custom_call_target="tpu_custom_call" | custom-call | flops 11809920 | bytes 2359296 | tf_op jit(solution)/shard_map/adamw_step/pallas_call | solution.py:1211
  666.6 1.3 maximum_convert_fusion
  (133 shorter events, 25.2 us)
Async XLA Ops:
  1.5 40.0 %collective-permute-start.1 = (bf16[16,128]{1,0:T(8,128)(2,1)S(1)}, bf16[16,128]{1,0:T(8,128)(2,1)S(1)}, u32[]{:S(2)}, u32[]{:S(2)}) collective-permute-start(bf16[16,128]{1,0:T(8,128)(2,1)S(1)} %bitcast.168), channel_id=1, source_target_pairs={{0,1},{1,2},{2,3},{3,4},{4,5},{5,6},{6,7},{8,9},{9,10},{10,11},{11... | collective-permute-start | bytes 12296 | tf_op jit(solution)/shard_map/ppermute | solution.py:1078
  6.3 34.5 %collective-permute-start.2 = (bf16[16,128]{1,0:T(8,128)(2,1)S(1)}, bf16[16,128]{1,0:T(8,128)(2,1)S(1)}, u32[]{:S(2)}, u32[]{:S(2)}) collective-permute-start(bf16[16,128]{1,0:T(8,128)(2,1)S(1)} %bitcast.170), channel_id=1, source_target_pairs={{1,0},{2,1},{3,2},{4,3},{5,4},{6,5},{7,6},{9,8},{10,9},{11,10},{12... | collective-permute-start | bytes 12296 | tf_op jit(solution)/shard_map/ppermute | solution.py:1079
  9.5 15.6 %copy-start.1 = (bf16[512,768]{1,0:T(8,128)(2,1)S(1)}, bf16[512,768]{1,0:T(8,128)(2,1)}, u32[]{:S(2)}) copy-start(bf16[512,768]{1,0:T(8,128)(2,1)} %cot_ref.1) | copy-start | bytes 2359300
  9.5 174.6 %collective-permute-start = (bf16[256,768]{1,0:T(8,128)(2,1)}, bf16[256,768]{1,0:T(8,128)(2,1)S(1)}, u32[]{:S(2)}, u32[]{:S(2)}) collective-permute-start(bf16[256,768]{1,0:T(8,128)(2,1)} %broadcast_select_fusion.18), channel_id=1, source_target_pairs={{0,24},{8,16},{16,8},{24,0},{1,25},{9,17},{17,9},{25,1},{2,26},{10... | collective-permute-start | bytes 1179656 | tf_op jit(solution)/shard_map/ppermute | solution.py:54
  25.2 3.8 copy-start.15
  25.2 4.3 copy-start.22
  25.2 8.2 %copy-start.18 = (s32[2]{0:T(128)S(1)}, s32[2]{0:T(128)}, u32[]{:S(2)}) copy-start(s32[2]{0:T(128)} %param.25) | copy-start | bytes 28
  27.9 167.9 %collective-permute-start.4 = (bf16[3,256,768]{2,1,0:T(8,128)(2,1)}, bf16[3,256,768]{2,1,0:T(8,128)(2,1)S(1)}, u32[]{:S(2)}, u32[]{:S(2)}) collective-permute-start(bf16[3,256,768]{2,1,0:T(8,128)(2,1)} %broadcast_select_fusion.2), channel_id=1, source_target_pairs={{0,24},{8,16},{16,8},{24,0},{1,25},{9,17},{17,9},{25,1},{2,26},{10... | collective-permute-start | bytes 3538952 | tf_op jit(solution)/shard_map/ppermute | solution.py:54
  41.5 0.6 copy-start.17
  46.5 137.7 %copy-start.4 = (bf16[512,768]{1,0:T(8,128)(2,1)S(1)}, bf16[512,768]{1,0:T(8,128)(2,1)}, u32[]{:S(2)}) copy-start(bf16[512,768]{1,0:T(8,128)(2,1)} %param.22) | copy-start | bytes 2359300
  185.2 10.6 %copy-start = (bf16[2,512,768]{2,1,0:T(8,128)(2,1)S(1)}, bf16[2,512,768]{2,1,0:T(8,128)(2,1)}, u32[]{:S(2)}) copy-start(bf16[2,512,768]{2,1,0:T(8,128)(2,1)} %past_averages.1) | copy-start | bytes 4718596
  195.0 3.8 collective-permute-start.3
  229.1 9.9 %copy-start.21 = (s32[2,8]{1,0:T(2,128)S(1)}, s32[2,8]{1,0:T(2,128)}, u32[]{:S(2)}) copy-start(s32[2,8]{1,0:T(2,128)} %constant.246.clone) | copy-start | bytes 196
  238.8 3.9 collective-permute-start.5
  242.8 1.1 copy-start.23
  291.3 20.9 %copy-start.6 = (bf16[512,768]{1,0:T(8,128)(2,1)S(1)}, bf16[512,768]{1,0:T(8,128)(2,1)}, u32[]{:S(2)}) copy-start(bf16[512,768]{1,0:T(8,128)(2,1)} %get-tuple-element.142) | copy-start | bytes 2359300
  311.0 21.4 %collective-permute-start.7 = (bf16[2,512,768]{2,1,0:T(8,128)(2,1)}, bf16[2,512,768]{2,1,0:T(8,128)(2,1)S(1)}, u32[]{:S(2)}, u32[]{:S(2)}) collective-permute-start(bf16[2,512,768]{2,1,0:T(8,128)(2,1)} %get-tuple-element.149), channel_id=1, source_target_pairs={{0,8},{8,0},{16,24},{24,16},{1,9},{9,1},{17,25},{25,17},{2,10},{10... | collective-permute-start | bytes 4718600 | tf_op jit(solution)/shard_map/ppermute | solution.py:58
  312.2 19.2 %collective-permute-start.6 = (bf16[256,768]{1,0:T(8,128)(2,1)S(1)}, bf16[256,768]{1,0:T(8,128)(2,1)S(1)}, u32[]{:S(2)}, u32[]{:S(2)}) collective-permute-start(bf16[256,768]{1,0:T(8,128)(2,1)S(1)} %broadcast_select_fusion.14), channel_id=1, source_target_pairs={{0,24},{8,16},{16,8},{24,0},{1,25},{9,17},{17,9},{25,1},{2,26},{10... | collective-permute-start | bytes 1179656 | tf_op jit(solution)/shard_map/ppermute | solution.py:54
  321.6 3.2 copy-start.13
  332.4 1.1 copy-start.8
  360.5 20.4 %copy-start.2 = (bf16[512,768]{1,0:T(8,128)(2,1)S(1)}, bf16[512,768]{1,0:T(8,128)(2,1)}, u32[]{:S(2)}) copy-start(bf16[512,768]{1,0:T(8,128)(2,1)} %get-tuple-element.151.dy_ref) | copy-start | bytes 2359300
  360.5 20.8 %copy-start.12 = (f32[1,2304]{1,0:T(1,128)S(1)}, f32[1,2304]{1,0:T(1,128)}, u32[]{:S(2)}) copy-start(f32[1,2304]{1,0:T(1,128)} %get-tuple-element.179) | copy-start | bytes 27652
  380.4 47.2 %collective-permute-start.8 = (bf16[2,512,768]{2,1,0:T(8,128)(2,1)}, bf16[2,512,768]{2,1,0:T(8,128)(2,1)S(1)}, u32[]{:S(2)}, u32[]{:S(2)}) collective-permute-start(bf16[2,512,768]{2,1,0:T(8,128)(2,1)} %get-tuple-element.158), channel_id=1, source_target_pairs={{0,8},{8,0},{16,24},{24,16},{1,9},{9,1},{17,25},{25,17},{2,10},{10... | collective-permute-start | bytes 4718600 | tf_op jit(solution)/shard_map/ppermute | solution.py:58
  381.0 5.1 copy-start.14
  381.0 23.8 %collective-permute-start.10 = (bf16[256,768]{1,0:T(8,128)(2,1)S(1)}, bf16[256,768]{1,0:T(8,128)(2,1)S(1)}, u32[]{:S(2)}, u32[]{:S(2)}) collective-permute-start(bf16[256,768]{1,0:T(8,128)(2,1)S(1)} %broadcast_select_fusion.6), channel_id=1, source_target_pairs={{0,24},{8,16},{16,8},{24,0},{1,25},{9,17},{17,9},{25,1},{2,26},{10... | collective-permute-start | bytes 1179656 | tf_op jit(solution)/shard_map/ppermute | solution.py:54
  427.6 1.1 copy-start.7
  440.5 5.8 copy-start.10
  440.5 5.8 copy-start.11
  642.5 2.9 copy-start.5
  642.5 3.1 copy-start.9
  645.4 7.8 %copy-start.3 = (bf16[768,768]{1,0:T(8,128)(2,1)S(1)}, bf16[768,768]{1,0:T(8,128)(2,1)}, u32[]{:S(2)}) copy-start(bf16[768,768]{1,0:T(8,128)(2,1)} %get-tuple-element.185) | copy-start | bytes 3538948
  645.5 21.1 %collective-permute-start.9 = (bf16[256,768]{1,0:T(8,128)(2,1)S(1)}, bf16[256,768]{1,0:T(8,128)(2,1)S(1)}, u32[]{:S(2)}, u32[]{:S(2)}) collective-permute-start(bf16[256,768]{1,0:T(8,128)(2,1)S(1)} %broadcast_select_fusion.10), channel_id=1, source_target_pairs={{0,24},{8,16},{16,8},{24,0},{1,25},{9,17},{17,9},{25,1},{2,26},{10... | collective-permute-start | bytes 1179656 | tf_op jit(solution)/shard_map/ppermute | solution.py:54
  647.1 8.7 %collective-permute-start.12 = (f32[3,768]{1,0:T(4,128)S(1)}, f32[3,768]{1,0:T(4,128)S(1)}, u32[]{:S(2)}, u32[]{:S(2)}) collective-permute-start(f32[3,768]{1,0:T(4,128)S(1)} %fusion.20), channel_id=1, source_target_pairs={{1,0},{2,1},{3,2},{4,3},{5,4},{6,5},{7,6},{9,8},{10,9},{11,10},{12... | collective-permute-start | bytes 27656 | tf_op jit(solution)/shard_map/ppermute | solution.py:1248
  648.5 6.5 copy-start.16
  648.5 6.5 copy-start.19
  648.5 6.4 copy-start.20
  648.5 7.3 %collective-permute-start.11 = (f32[3,768]{1,0:T(4,128)S(1)}, f32[3,768]{1,0:T(4,128)S(1)}, u32[]{:S(2)}, u32[]{:S(2)}) collective-permute-start(f32[3,768]{1,0:T(4,128)S(1)} %fusion.23), channel_id=1, source_target_pairs={{0,1},{1,2},{2,3},{3,4},{4,5},{5,6},{6,7},{8,9},{9,10},{10,11},{11... | collective-permute-start | bytes 27656 | tf_op jit(solution)/shard_map/ppermute | solution.py:1247

commit v4 on v3

--- a/solution.py
+++ b/solution.py
@@ -344,11 +344,12 @@
             pltpu.SemaphoreType.DMA,
         ],
         name="gather_weights",
+        cost_estimate=pl.CostEstimate(flops=10**11, bytes_accessed=10**8, transcendentals=0),
         compiler_params=pltpu.CompilerParams(collective_id=0, has_side_effects=True),
     )(block, vecs)
 
 
-VMEM_LIMIT = 56 * 1024 * 1024
+VMEM_LIMIT = 32 * 1024 * 1024
 
 
 def row_spec(width):
@@ -570,7 +571,7 @@
     )(meta, q, kv, kv, kv_other, kv_other)
 
 
-FF_BLOCK = 384
+FF_BLOCK = 768
 
 
 def mlp_kernel(
@@ -1121,7 +1122,7 @@
     out_ref[1] = two.astype(bf16)
 
 
-HIST_ROWS = 32
+HIST_ROWS = 64
 
 
 def past_call(mix_weights, history):
@@ -1137,36 +1138,26 @@
     )(mix_weights, history)[0]
 
 
-def history_kernel(scale, w_ref, h_ref, dy_ref, cot_ref, out_ref, sums_ref):
-    @pl.when(pl.program_id(0) == 0)
-    def _():
-        sums_ref[...] = jnp.zeros_like(sums_ref)
-
+def history_kernel(scale, w_ref, dy_ref, cot_ref, out_ref):
     dy = dy_ref[...].astype(f32)
     g = cot_ref[...].astype(f32) * scale
     for j in range(HIST):
-        row = h_ref[j].astype(f32)
         out_ref[j] = (w_ref[j] * dy + w_ref[HIST + 1 + j] * g).astype(bf16)
-        sums_ref[j : j + 1] += column_sum(dy * row)
-        sums_ref[HIST + j : HIST + j + 1] += column_sum(g * row)
-
-
-def history_call(scale, mix_weights, history, dy, cotangent):
-    rows = history.shape[1]
+
+
+def history_call(scale, mix_weights, dy, cotangent):
+    rows = dy.shape[0]
+    part = pl.BlockSpec((HIST_ROWS, D), lambda i: (i, 0))
     block = pl.BlockSpec((HIST, HIST_ROWS, D), lambda i: (0, i, 0))
-    part = pl.BlockSpec((HIST_ROWS, D), lambda i: (i, 0))
     return call(
         functools.partial(history_kernel, scale),
         "history_grads",
         (rows // HIST_ROWS,),
-        [SMEM_SPEC, block, part, part],
-        [
-            (history.shape, bf16, block),
-            ((2 * HIST, D), f32, whole_spec((2 * HIST, D))),
-        ],
+        [SMEM_SPEC, part, part],
+        [((HIST, rows, D), bf16, block)],
         [],
-        8 * HIST * rows * D,
-    )(mix_weights, history, dy, cotangent)
+        4 * HIST * rows * D,
+    )(mix_weights, dy, cotangent)[0]
 
 
 STEP_ROWS = 1024
@@ -1333,12 +1324,17 @@
         self.load, self.sent, self.got = refs[7:]
 
 
-def reduce_kernel(tile_count, *refs):
-    inputs, refs = refs[:8], refs[8:]
-    small_ref, tile_ref, total_ref = refs[:3]
-    refs = refs[3:]
+HIST_CHUNK = 16
+SMALL_ROWS = 176
+
+
+def reduce_kernel(tile_count, scale, small_ref, hist_ref, dy_ref, cot_ref, *refs):
+    operands, refs = refs[:16], refs[16:]
+    tile_ref, total_ref = refs[:2]
+    refs = refs[2:]
     kinds = [Kind(refs[:10]), Kind(refs[10:20])]
-    fin, other_half, acc, part, fin_sem, small_sem = refs[20:]
+    fin, other_half, acc, part, fin_sem, small_sem, left, right, op_sem, credit = refs[20:30]
+    hin, sums, hist_sem = refs[30:]
     section, b = lax.axis_index("section"), lax.axis_index("batch")
     plane, core = section // 2, section % 2
     x, z = b % 2, b // 2
@@ -1346,6 +1342,37 @@
     to_core, to_plane = (section ^ 1, b), (section ^ 2, b)
     to_x, to_low, to_high = (section, b ^ 1), (section, b ^ 2), (section, b ^ 4)
     peers = [to_core, to_plane, to_x, to_high, to_low]
+
+    products = []
+    for layer in (1, 0):
+        n_m, dpre, act, er, n_a, dj, mixed, dh = operands[8 * layer : 8 * layer + 8]
+        products += [(layer, 0, 0, "up", j, n_m, 0, dpre, j) for j in range(4)]
+        for step, near in ((1, 1 - low), (3, low)):
+            for j in range(2):
+                products.append((layer, 0, step, "down", 2 * near + j, act, 2 * near + j, er, 0))
+        products += [(layer, 1, 0, "joint", j, n_a, 0, dj, j) for j in range(3)]
+        products.append((layer, 1, 0, "out", 3, mixed, 0, dh, 0))
+
+    def operand_copies(index):
+        a, at, b_, bt = products[index][5:]
+        slot = index % 3
+
+        def columns(i):
+            return pl.ds(pl.multiple_of(i * D, 128), D)
+
+        return (
+            pltpu.make_async_copy(a.at[:, columns(at)], left.at[slot], op_sem.at[0, slot]),
+            pltpu.make_async_copy(b_.at[:, columns(bt)], right.at[slot], op_sem.at[1, slot]),
+        )
+
+    def load_operands(index):
+        if index < len(products):
+            for copy in operand_copies(index):
+                copy.start()
+
+    load_operands(0)
+    load_operands(1)
+
     barrier = pltpu.get_barrier_semaphore()
     for peer in peers:
         pl.semaphore_signal(barrier, 1, device_id=peer, device_id_type=MESH)
@@ -1362,6 +1389,7 @@
         else:
             pl.when(cond)(copy.start)
         mine.append((cond, copy))
+        return copy
 
     def landed(dst, got):
         pltpu.make_async_remote_copy(
@@ -1377,18 +1405,95 @@
 
         lax.fori_loop(0, rows // 64, body, 0)
 
-    loads = {}
+    def product(index):
+        layer, k, _, name, j = products[index][:5]
+        store = kinds[k].sum
+        slot = index % 3
+        for copy in operand_copies(index):
+            copy.wait()
+        load_operands(index + 2)
+        to = [jnp.where(core == h, layer, 2) for h in range(2)]
+
+        def body(i, carry):
+            columns = pl.ds(pl.multiple_of(i * 256, 256), 256)
+            result = dot_tn(left[slot], right[slot, :, columns]).astype(bf16)
+            if name == "up":
+                for t in range(4):
+                    row = pl.ds(192 * (j % 2), 192)
+                    store[to[j // 2], t, row, columns] = result[192 * t : 192 * t + 192]
+            elif name == "joint":
+                for t in range(3):
+                    for h in range(2):
+                        at = 256 * t + 128 * h
+                        store[to[h], t, pl.ds(128 * j, 128), columns] = result[at : at + 128]
+            else:
+                tile = 4 + j if name == "down" else 3
+                for h in range(2):
+                    store[to[h], tile, :, columns] = result[384 * h : 384 * h + 384]
+            return carry
+
+        lax.fori_loop(0, 3, body, 0)
+
+    given = {}
+
+    def stage_product(layer, k, step):
+        kind = kinds[k]
+        if layer == 0 and step == 0:
+            for copy in given[k]:
+                copy.wait_send()
+            pl.semaphore_wait(credit.at[k], 1)
+        done = []
+        for index, item in enumerate(products):
+            if item[:3] == (layer, k, step):
+                product(index)
+                done.append(item)
+        if not done:
+            return
+        tiles = range(4) if done[0][3] in ("up", "joint") else [4 + item[4] for item in done]
+        for tile in tiles:
+            copy = pltpu.make_async_remote_copy(
+                kind.sum.at[2, tile],
+                kind.c.at[tile],
+                kind.sent.at[0, layer, tile],
+                kind.got.at[0, layer, tile],
+                device_id=to_core,
+                device_id_type=MESH,
+            )
+            copy.start()
+            if layer == 1:
+                given.setdefault(k, []).append(copy)
+            else:
+                mine.append((None, copy))
+
     order = [(layer, k) for layer in (1, 0) for k in (0, 1)]
-    for layer, k in order:
-        kind = kinds[k]
-        for tile in range(tile_count[k]):
-            first, second = inputs[4 * layer + 2 * k : 4 * layer + 2 * k + 2]
-            split = first.shape[0]
-            src = first.at[tile] if tile < split else second.at[tile - split]
-            here = src.at[pl.ds(pl.multiple_of(384 * core, 384), 384)]
-            there = src.at[pl.ds(pl.multiple_of(384 * (1 - core), 384), 384)]
-            remote(there, kind.c.at[layer, tile], kind.sent.at[0, layer, tile], kind.got.at[0, layer, tile], to_core)
-            pltpu.make_async_copy(here, kind.sum.at[layer, tile], kind.load.at[layer, tile]).start()
+    chunks = hist_ref.shape[1] // HIST_CHUNK
+
+    def history_in(i, slot):
+        rows = pl.ds(pl.multiple_of(i * HIST_CHUNK, HIST_CHUNK), HIST_CHUNK)
+        return pltpu.make_async_copy(hist_ref.at[:, rows], hin.at[slot], hist_sem.at[slot])
+
+    sums[...] = jnp.zeros_like(sums)
+    history_in(0, 0).start()
+    history_in(1, 1).start()
+
+    def stage_history(pair):
+        for slot in range(2):
+            i = 2 * pair + slot
+            history_in(i, slot).wait()
+            rows = pl.ds(i * HIST_CHUNK, HIST_CHUNK)
+            dy = dy_ref[rows].astype(f32)
+            g = cot_ref[rows].astype(f32) * scale
+
+            def body(j, carry):
+                row = hin[slot, j].astype(f32)
+                one, two = dy * row, g * row
+                sums[j] += one[:8] + one[8:]
+                sums[HIST + j] += two[:8] + two[8:]
+                return carry
+
+            lax.fori_loop(0, HIST, body, 0)
+            if i + 2 < chunks:
+                history_in(i + 2, slot).start()
 
     keep_at = pl.multiple_of(128 * plane, 128)
     keep = pl.ds(keep_at, 256)
@@ -1402,11 +1507,8 @@
         kind = kinds[k]
         zz = column(k, step)
         for tile in (2 * zz + (1 - x), 2 * zz + x):
-            pltpu.make_async_copy(
-                inputs[0].at[0, pl.ds(0, 384)], kind.sum.at[layer, tile], kind.load.at[layer, tile]
-            ).wait()
-            landed(kind.c.at[layer, tile], kind.got.at[0, layer, tile])
-            add(kind.sum.at[layer, tile], 0, kind.c.at[layer, tile], 0, 384)
+            landed(kind.c.at[tile], kind.got.at[0, layer, tile])
+            add(kind.sum.at[layer, tile], 0, kind.c.at[tile], 0, 384)
             give = pl.ds(pl.multiple_of(256 * (1 - plane), 128), 128)
             remote(
                 kind.sum.at[layer, tile, give],
@@ -1415,6 +1517,8 @@
                 kind.got.at[1, layer, tile],
                 to_plane,
             )
+        if layer == 1 and step == tile_count[k] // 2 - 1:
+            pl.semaphore_signal(credit.at[k], 1, device_id=to_core, device_id_type=MESH)
 
     def stage_plane(layer, k, step):
         kind = kinds[k]
@@ -1488,7 +1592,12 @@
 
     def stage_small(step):
         if step == 0:
-            acc[0] = small_ref[...]
+            acc[0, :SMALL_ROWS] = small_ref[...]
+            lanes = jnp.sum(sums[...], axis=1)
+            total = lanes[:, :128]
+            for j in range(1, 6):
+                total = total + lanes[:, 128 * j : 128 * j + 128]
+            acc[0, SMALL_ROWS:] = total
         else:
             landed(part.at[step - 1], small_sem.at[1, step - 1])
             acc[step] = acc[step - 1] + part[step - 1]
@@ -1499,15 +1608,20 @@
 
     steps = [(layer, k, step) for layer, k in order for step in range(tile_count[k] // 2)]
     later = {}
-    for at in range(len(steps) + 8):
+    small_at = chunks // 2
+    for at in range(len(steps) + 10):
         if at < len(steps):
-            stage_core(*steps[at])
-        if at % 2 == 0 and at // 2 <= len(peers):
-            stage_small(at // 2)
-        if 0 <= at - 2 < len(steps):
-            stage_plane(*steps[at - 2])
-        if 0 <= at - 4 < len(steps):
-            layer, k, step = steps[at - 4]
+            stage_product(*steps[at])
+        if 0 <= at - 1 < len(steps):
+            stage_core(*steps[at - 1])
+        if at < chunks // 2:
+            stage_history(at)
+        if 0 <= at - small_at <= len(peers):
+            stage_small(at - small_at)
+        if 0 <= at - 3 < len(steps):
+            stage_plane(*steps[at - 3])
+        if 0 <= at - 5 < len(steps):
+            layer, k, step = steps[at - 5]
             stage_x(layer, k, step)
             if step == tile_count[k] // 2 - 1:
                 stage_high(layer, k)
@@ -1516,7 +1630,6 @@
             stage_end(*later.pop(at))
     for layer, k in later.values():
         stage_end(layer, k)
-
     def finish(k):
         kind = kinds[k]
         tile = 2 * (2 * high + low if k == 0 else low) + x
@@ -1555,45 +1668,55 @@
             pl.when(cond)(copy.wait_send)
 
 
-def reduce_call(tiles, small):
+def reduce_call(scale, small, history, dy, cotangent, operands):
     counts = (8, 4)
+    rows = dy.shape[0]
     scratch = []
     for count in counts:
         scratch += [
-            pltpu.VMEM((2, count, 384, D), bf16),
-            pltpu.VMEM((2, count, 384, D), bf16),
+            pltpu.VMEM((3, count, 384, D), bf16),
+            pltpu.VMEM((count, 384, D), bf16),
             pltpu.VMEM((2, count, 128, D), bf16),
             pltpu.VMEM((2, count // 2, 256, D), bf16),
-            pltpu.VMEM((2, 2, 256, D), bf16),
+            pltpu.VMEM((2, count // 4, 256, D), bf16),
             pltpu.VMEM((2, 256, D), bf16),
             pltpu.VMEM((256, D), bf16),
             pltpu.SemaphoreType.DMA((2, count)),
             pltpu.SemaphoreType.DMA((6, 2, count)),
             pltpu.SemaphoreType.DMA((6, 2, count)),
         ]
+    small_shape = (SMALL_ROWS + 2 * HIST, 128)
     scratch += [
         pltpu.VMEM((2, 384, D), bf16),
         pltpu.VMEM((384, D), bf16),
-        pltpu.VMEM((6,) + small.shape, f32),
-        pltpu.VMEM((5,) + small.shape, f32),
+        pltpu.VMEM((6,) + small_shape, f32),
+        pltpu.VMEM((5,) + small_shape, f32),
         pltpu.SemaphoreType.DMA((3,)),
         pltpu.SemaphoreType.DMA((2, 5)),
+        pltpu.VMEM((3, rows, D), bf16),
+        pltpu.VMEM((3, rows, D), bf16),
+        pltpu.SemaphoreType.DMA((2, 3)),
+        pltpu.SemaphoreType.REGULAR((2,)),
+        pltpu.VMEM((2, HIST, HIST_CHUNK, D), bf16),
+        pltpu.VMEM((2 * HIST, 8, D), f32),
+        pltpu.SemaphoreType.DMA((2,)),
     ]
+    in_vmem, in_hbm = (pl.BlockSpec(memory_space=space) for space in (pltpu.VMEM, pltpu.HBM))
     return pl.pallas_call(
-        functools.partial(reduce_kernel, counts),
-        in_specs=[pl.BlockSpec(memory_space=pltpu.HBM)] * 8
-        + [pl.BlockSpec(memory_space=pltpu.VMEM)],
-        out_specs=[pl.BlockSpec(memory_space=pltpu.VMEM)] * 2,
+        functools.partial(reduce_kernel, counts, scale),
+        in_specs=[in_vmem, in_hbm, in_vmem, in_vmem] + [in_hbm] * 16,
+        out_specs=[in_vmem, in_vmem],
         out_shape=[
             jax.ShapeDtypeStruct((D, D), bf16),
-            jax.ShapeDtypeStruct(small.shape, f32),
+            jax.ShapeDtypeStruct(small_shape, f32),
         ],
         scratch_shapes=scratch,
         name="reduce_gradients",
+        cost_estimate=pl.CostEstimate(flops=10**11, bytes_accessed=10**8, transcendentals=0),
         compiler_params=pltpu.CompilerParams(
             collective_id=1, has_side_effects=True, vmem_limit_bytes=60 * 1024 * 1024
         ),
-    )(*tiles, small)
+    )(small, history, dy, cotangent, *operands)
 
 
 def reduce_tiles(place, tiles):
@@ -1716,56 +1839,71 @@
         )
         return (x, normed, q, kv, kv_other, mixed, lse), outs
 
-    def backward(layer, dy, kept, outs, carried):
+    def backward(layer, dy, kept, outs, carried, moved):
         x, normed, q, kv, kv_other, mixed, lse = kept
         h, n_m, act, slope = outs[:4]
         er, dpre, dub, dh, datt, sums = mlp_back_call(
             layer, mix, cot, dy, h, mlp_vecs[layer][0], mlp, slope, att
         )
-        up_part, down_part = mlp_tiles(plan, n_m, dpre, act, er)
+        datt, moved = lax.optimization_barrier((datt, moved))
         dq, own, give = att_back_call(meta, q, kv, kv_other, datt, mixed, lse, cosine, sine)
         gain = att_vecs[layer][0]
         dj, djb, dx, sums_a = qkv_back_call(
             layer, dq, own, swap_cores(give), cosine, sine, att, x, gain, dh, carried
         )
-        joint_part, out_part = att_tiles(plan, normed, dj, mixed, dh)
         vec_m = (sums[0], sums[1], dub[0], sums[2])
         vec_a = (sums_a[0], sums_a[1], djb[0], sums[3])
-        return dx, sums_a[2], vec_a, vec_m, (up_part, down_part, joint_part, out_part)
+        return dx, moved, sums_a[2], vec_a, vec_m, (n_m, dpre, act, er, normed, dj, mixed, dh)
 
     kept20, outs20 = forward(0, stream, past_one, ())
     y20, c20 = outs20[4:]
     kept21, outs21 = forward(1, y20, past_two, (c20, cot))
     y21, sums21 = outs21[4:]
-    stream_out = to_owner(y21)
     mix41, mix42 = jnp.sum(sums21[0]), jnp.sum(sums21[1])
-    dy20, mix20, vec_a21, vec_m21, tiles21 = backward(1, y20, kept21, outs21, c20)
+    dy20, stream_out, mix20, vec_a21, vec_m21, operands21 = backward(
+        1, y20, kept21, outs21, c20, to_owner(y21)
+    )
     mix20 = jnp.sum(mix20)
-    dstream, _, vec_a20, vec_m20, tiles20 = backward(0, dy20, kept20, outs20, c20)
-    dy20_own = to_owner(dy20)
+    dstream, dy20_own, _, vec_a20, vec_m20, operands20 = backward(
+        0, dy20, kept20, outs20, c20, to_owner(dy20)
+    )
     stream_grad = to_owner(dstream).astype(f32)
 
-    history_grad, mix_sums = history_call(grad_scale, mix_weights, history, dy20_own, cotangent)
-    mix_sums = jnp.sum(mix_sums, axis=1)
-    mix_one, mix_two = mix_sums[:HIST], mix_sums[HIST:]
-    own_mix = jnp.concatenate([mix_one, mix20[None], mix_two, mix41[None], mix42[None]])
+    own_mix = jnp.stack([mix20, mix41, mix42])
 
     def flat_vec(v):
-        out = jnp.concatenate(v)
+        out = jnp.concatenate([line.reshape(-1) for line in v])
         return jnp.concatenate([out, jnp.zeros((VEC - out.shape[0],), f32)])
 
     small = jnp.concatenate(
         [flat_vec(v) for v in (vec_a20, vec_m20, vec_a21, vec_m21)] + [own_mix]
     )
+    history_grad = history_call(grad_scale, mix_weights, dy20_own, cotangent)
+
     if nb == 8:
-        lines = -(-small.shape[0] // 1024) * 8
-        small = jnp.concatenate([small, jnp.zeros((lines * 128 - small.shape[0],), f32)])
-        tile_grad, small = reduce_call(tiles20 + tiles21, small.reshape(lines, 128))
-        small = small.reshape(-1)
+        small = jnp.concatenate([small, jnp.zeros((SMALL_ROWS * 128 - small.shape[0],), f32)])
+        tile_grad, small = reduce_call(
+            grad_scale,
+            small.reshape(SMALL_ROWS, 128),
+            history,
+            dy20_own,
+            cotangent,
+            operands20 + operands21,
+        )
+        mix_sums = jnp.sum(small[SMALL_ROWS:], axis=1)
+        small = small[:SMALL_ROWS].reshape(-1)
     else:
-        tile_grad = reduce_blocks(place, (tiles20, tiles21))
-        small = lax.psum(small, ("section", "batch"))
-    mix_grad = small[4 * VEC : 4 * VEC + own_mix.shape[0]]
+        rows = [dy20_own.astype(f32), cotangent.astype(f32) * grad_scale]
+        mix_sums = [jnp.sum(r[None] * history.astype(f32), axis=(1, 2)) for r in rows]
+        tiles = [
+            mlp_tiles(plan, *ops[:4]) + att_tiles(plan, *ops[4:])
+            for ops in (operands20, operands21)
+        ]
+        tile_grad = reduce_blocks(place, tiles)
+        small = lax.psum(jnp.concatenate([small] + mix_sums), ("section", "batch"))
+        mix_sums = small[-2 * HIST :]
+    own_mix = small[4 * VEC : 4 * VEC + 3]
+    mix_grad = jnp.concatenate([mix_sums[:HIST], own_mix[:1], mix_sums[HIST:], own_mix[1:]])
     vec_rows = small[: 4 * VEC].reshape(4, VEC)
     vec_own = lax.dynamic_index_in_dim(vec_rows, section, 0, keepdims=False)
 

time: 676 us -> 619 us (0.916)
  Pallas kernels: 595 us -> 495 us
  local copies, waits for them, and re-layouts: 14.3 us -> 57.8 us
  other arithmetic: 32.9 us -> 25.7 us
    pallas_call x9 -> x1, Pallas kernels: 237 us -> 197 us  [reduce_call(): pl.pallas_call(functools.partial(reduce_kernel, counts, scale), in_specs=...]
    unnamed x48 -> x158, local copies, waits for them, and re-layouts: 4.12 us -> 39.9 us
    pallas_call x1, Pallas kernels: 20.7 us -> 8.71 us  [history_call(): call(functools.partial(history_kernel, scale), 'history_grads', (rows //...]
    pallas_call x2, Pallas kernels: 32.9 us -> 21.9 us  [mlp_back_call(): call(functools.partial(mlp_back_kernel, last_layer), 'feed_forward_grad_r...]
    pallas_call x2, Pallas kernels: 34.1 us -> 23.8 us  [mlp_call(): call(functools.partial(mlp_kernel, last_layer), 'feed_forward_rows', (FF...]
    pallas_call x2, Pallas kernels: 20.5 us -> 13.1 us  [qkv_back_call(): call(qkv_back_kernel, 'qkv_grad_rows', (3,), [full, whole_spec((2, rows,...]
    pallas_call x1, Pallas kernels: 14.9 us -> 7.78 us  [past_call(): call(past_kernel, 'past_averages', (rows // HIST_ROWS,), [SMEM_SPEC, pl.B...]
  transfers between devices with their start and end apart: 13 -> 13, of which waited for: 1 -> 2; matrix products, arithmetic and copies ran while one was open for 5% -> 5% of each run, Pallas kernels for 35% -> 31%
where the time goes in v4:
time: 619 us; the launch traced here: 611 us
  Pallas kernels  495 us (80%)
  local copies, waits for them, and re-layouts  57.8 us (9%)
  other arithmetic  25.7 us (4%)
  starting transfers between devices  17.8 us (3%)
  between operations  8.47 us (1%)
    pallas_call x1, Pallas kernels, reduce_call(): pl.pallas_call(functools.partial(reduce_kernel, counts, scale), in_specs=...  197 us
    pallas_call x1, Pallas kernels, gather_weights(): pl.pallas_call(body, in_specs=[any_spec] * 2, out_specs=[any_spec] * 3, o...  136 us
    unnamed x158, local copies, waits for them, and re-layouts  39.9 us
    pallas_call x2, Pallas kernels, att_back_call(): call(att_back_kernel, 'attention_grad_rows', (pairs,), [SMEM_SPEC, pair_s...  39.1 us
    pallas_call x2, Pallas kernels, att_call(): call(att_kernel, 'attention_rows', (pairs,), [SMEM_SPEC, pair_spec(rows),...  25.6 us
    pallas_call x2, Pallas kernels, mlp_call(): call(functools.partial(mlp_kernel, last_layer), 'feed_forward_rows', (FF...  23.8 us
    pallas_call x2, Pallas kernels, mlp_back_call(): call(functools.partial(mlp_back_kernel, last_layer), 'feed_forward_grad_r...  21.9 us
    pallas_call x2, Pallas kernels, qkv_call(): call(qkv_kernel, 'qkv_rows', (6,), [whole_spec((rows, D)), row_spec(D), r...  14.3 us
  transfers between devices with their start and end apart: 13, of which 2 were waited for; matrix products, arithmetic and copies ran while one was open for 5% of the time, Pallas kernels for 31%

profile of v4, /device:TPU:0, one launch (start us, length us, event | category | flops | bytes accessed | tf_op | source)
XLA Modules:
  0.0 611.4 jit_solution(11639988812852390378)
XLA Ops:
  1.5 4.8 collective-permute-start.2
  6.3 1.3 collective-permute-start.3
  7.6 1.9 broadcast_select_fusion.18
  10.2 5.5 copy-done.1
  16.4 7.8 %past_averages.1 = bf16[2,512,768]{2,1,0:T(8,128)(2,1)S(1)} custom-call(f32[43]{0:T(128)S(1)} %copy-done.33, bf16[20,512,768]{2,1,0:T(8,128)(2,1)S(1)} %copy-done.1), custom_call_target="tpu_custom_call" | custom-call | flops 31457280 | bytes 2359296 | tf_op jit(solution)/shard_map/past_averages/pallas_call | solution.py:1130
  24.2 1.3 broadcast_select_fusion.2
  36.3 1.7 copy-done.4
  37.9 2.2 pack_weights.1.block_ref
  41.2 135.9 %gather_weights.1 = (bf16[2,4,768,768]{3,2,1,0:T(8,128)(2,1)}, bf16[2,8,768,768]{3,2,1,0:T(8,128)(2,1)}, bf16[32,32,128]{2,1,0:T(8,128)(2,1)}) custom-call(bf16[768,768]{1,0:T(8,128)(2,1)} %copy-done.22, bf16[32,128]{1,0:T(8,128)(2,1)} %pad_maximum_fusion.11.vec_ref), custom_call_target="tpu_custom_call" | custom-call | flops 99999997952 | bytes 100000000 | tf_op jit(solution)/shard_map/gather_weights/pallas_call | solution.py:329
  177.2 1.8 fusion.45
  178.9 1.6 reshape.548
  180.5 1.6 reshape.546
  186.0 3.7 copy-done
  189.6 7.2 %qkv_rows.2 = (bf16[512,768]{1,0:T(8,128)(2,1)S(1)}, bf16[512,768]{1,0:T(8,128)(2,1)S(1)}, bf16[512,1536]{1,0:T(8,128)(2,1)S(1)}) custom-call(bf16[512,768]{1,0:T(8,128)(2,1)S(1)} %pad_maximum_fusion.2.x_ref, f32[1,768]{1,0:T(1,128)S(1)} %get-tuple-element.281.gain_ref, f32[1,768]{1,0:T(1,128)S(1)} %get-tuple-element.282.bias_ref, ...), custom_call_target="tpu_custom_call" | custom-call | flops 1811939328 | bytes 2359296 | tf_op jit(solution)/shard_map/qkv_rows/pallas_call | solution.py:435
  199.4 1.8 broadcast_select_fusion
  201.5 12.7 %attention_rows.2 = (bf16[512,768]{1,0:T(8,128)(2,1)S(1)}, f32[6,512,128]{2,1,0:T(8,128)S(1)}) custom-call(s32[4]{0:T(128)S(1)} %pad_add_fusion.1.meta_ref, bf16[512,768]{1,0:T(8,128)(2,1)S(1)} %get-tuple-element.135.q_ref, bf16[512,1536]{1,0:T(8,128)(2,1)S(1)} %get-tuple-element.136.k_ref.v_ref, bf16[512,1536]{1,0:T(8,128)(2,1)S(1)} %get-tuple-element.136.k_ref.v_ref, ...), custom_call_target="tpu_custom_call" | custom-call | flops 4026531840 | bytes 2359296 | tf_op jit(solution)/shard_map/attention_rows/pallas_call | solution.py:549
  214.3 11.9 %feed_forward_rows.2 = (bf16[512,768]{1,0:T(8,128)(2,1)S(1)}, bf16[512,768]{1,0:T(8,128)(2,1)S(1)}, bf16[512,3072]{1,0:T(8,128)(2,1)S(1)}, bf16[512,3072]{1,0:T(...) custom-call(f32[4]{0:T(128)S(1)} %pad_maximum_fusion.12.mix_ref, ...), custom_call_target="tpu_custom_call" | custom-call | flops 5435817984 | bytes 2359296 | tf_op jit(solution)/shard_map/feed_forward_rows/pallas_call | solution.py:643
  227.2 1.6 copy-done.37
  228.8 7.2 %qkv_rows.3 = (bf16[512,768]{1,0:T(8,128)(2,1)S(1)}, bf16[512,768]{1,0:T(8,128)(2,1)S(1)}, bf16[512,1536]{1,0:T(8,128)(2,1)S(1)}) custom-call(bf16[512,768]{1,0:T(8,128)(2,1)S(1)} %get-tuple-element.139.x_ref.dy_ref, f32[1,768]{1,0:T(1,128)S(1)} %get-tuple-element.286.gain_ref, f32[1,768]{1,0:T(1,128)S(1)} %get-tuple-element.287.bias_ref, ...), custom_call_target="tpu_custom_call" | custom-call | flops 1811939328 | bytes 2359296 | tf_op jit(solution)/shard_map/qkv_rows/pallas_call | solution.py:435
  236.5 3.0 collective-permute-done.5.ko_ref.vo_ref
  239.6 12.9 %attention_rows.3 = (bf16[512,768]{1,0:T(8,128)(2,1)S(1)}, f32[6,512,128]{2,1,0:T(8,128)S(1)}) custom-call(s32[4]{0:T(128)S(1)} %pad_add_fusion.1.meta_ref, bf16[512,768]{1,0:T(8,128)(2,1)S(1)} %get-tuple-element.140.q_ref, bf16[512,1536]{1,0:T(8,128)(2,1)S(1)} %get-tuple-element.141.k_ref.v_ref, bf16[512,1536]{1,0:T(8,128)(2,1)S(1)} %get-tuple-element.141.k_ref.v_ref, ...), custom_call_target="tpu_custom_call" | custom-call | flops 4026531840 | bytes 2359296 | tf_op jit(solution)/shard_map/attention_rows/pallas_call | solution.py:549
  253.6 11.9 %feed_forward_rows.3 = (bf16[512,768]{1,0:T(8,128)(2,1)S(1)}, bf16[512,768]{1,0:T(8,128)(2,1)S(1)}, bf16[512,3072]{1,0:T(8,128)(2,1)S(1)}, bf16[512,3072]{1,0:T(...) custom-call(f32[4]{0:T(128)S(1)} %pad_maximum_fusion.12.mix_ref, ...), custom_call_target="tpu_custom_call" | custom-call | flops 5435817984 | bytes 2359296 | tf_op jit(solution)/shard_map/feed_forward_rows/pallas_call | solution.py:643
  265.5 1.7 copy-done.38
  268.2 10.8 %feed_forward_grad_rows.2 = (bf16[512,768]{1,0:T(8,128)(2,1)S(1)}, bf16[512,3072]{1,0:T(8,128)(2,1)S(1)}, f32[1,3072]{1,0:T(1,128)S(1)}, bf16[512,768]{1,0:T(8,1...) custom-call(f32[4]{0:T(128)S(1)} %pad_maximum_fusion.12.mix_ref, ...), custom_call_target="tpu_custom_call" | custom-call | flops 5435817984 | bytes 2359296 | tf_op jit(solution)/shard_map/feed_forward_grad_rows/pallas_call | solution.py:751
  279.0 1.7 copy-done.39
  284.1 1.4 copy-done.64
  285.5 19.2 %attention_grad_rows.2 = (bf16[512,768]{1,0:T(8,128)(2,1)S(1)}, f32[2,512,768]{2,1,0:T(8,128)S(1)}, bf16[2,512,768]{2,1,0:T(8,128)(2,1)S(1)}) custom-call(s32[4]{0:T(128)S(1)} %pad_add_fusion.1.meta_ref, bf16[512,768]{1,0:T(8,128)(2,1)S(1)} %copy-done.60, bf16[512,1536]{1,0:T(8,128)(2,1)S(1)} %copy-done.48, bf16[512,1536]{1,0:T(8,128)(2,1)S(1)} %copy-done.48, ...), custom_call_target="tpu_custom_call" | custom-call | flops 10066329600 | bytes 2359296 | tf_op jit(solution)/shard_map/attention_grad_rows/pallas_call | solution.py:866
  305.1 3.1 collective-permute-done.7.got_ref
  308.2 5.9 qkv_grad_rows.2
  315.8 11.1 %feed_forward_grad_rows.3 = (bf16[512,768]{1,0:T(8,128)(2,1)S(1)}, bf16[512,3072]{1,0:T(8,128)(2,1)S(1)}, f32[1,3072]{1,0:T(1,128)S(1)}, bf16[512,768]{1,0:T(8,1...) custom-call(f32[4]{0:T(128)S(1)} %pad_maximum_fusion.12.mix_ref, bf16[512,768]{1,0:T(8,128)(2,1)S(1)} %copy-done.3, ...), custom_call_target="tpu_custom_call" | custom-call | flops 5435817984 | bytes 2359296 | tf_op jit(solution)/shard_map/feed_forward_grad_rows/pallas_call | solution.py:751
  327.0 1.6 copy-done.40
  331.3 19.9 %attention_grad_rows.3 = (bf16[512,768]{1,0:T(8,128)(2,1)S(1)}, f32[2,512,768]{2,1,0:T(8,128)S(1)}, bf16[2,512,768]{2,1,0:T(8,128)(2,1)}) custom-call(s32[4]{0:T(128)S(1)} %pad_add_fusion.1.meta_ref, bf16[512,768]{1,0:T(8,128)(2,1)S(1)} %copy-done.58, bf16[512,1536]{1,0:T(8,128)(2,1)S(1)} %copy-done.44, bf16[512,1536]{1,0:T(8,128)(2,1)S(1)} %copy-done.44, ...), custom_call_target="tpu_custom_call" | custom-call | flops 10066329600 | bytes 2359296 | tf_op jit(solution)/shard_map/attention_grad_rows/pallas_call | solution.py:866
  351.2 1.7 copy-done.16
  358.0 1.4 slice_reduce_fusion.1
  360.3 8.7 %history_grads.1 = bf16[20,512,768]{2,1,0:T(8,128)(2,1)} custom-call(f32[43]{0:T(128)S(1)} %copy-done.35, bf16[512,768]{1,0:T(8,128)(2,1)S(1)} %pad_maximum_fusion.4.dy_ref, bf16[512,768]{1,0:T(8,128)(2,1)S(1)} %copy-done.11), custom_call_target="tpu_custom_call" | custom-call | flops 31457280 | bytes 2359296 | tf_op jit(solution)/shard_map/history_grads/pallas_call | solution.py:1152
  369.1 1.5 copy-done.17
  370.9 7.2 %qkv_grad_rows.3 = (bf16[512,2304]{1,0:T(8,128)(2,1)S(1)}, f32[1,2304]{1,0:T(1,128)S(1)}, bf16[512,768]{1,0:T(8,128)(2,1)S(1)}, f32[8,768]{1,0:T(8,128)S(1)}) custom-call(bf16[512,768]{1,0:T(8,128)(2,1)S(1)} %copy-done.27, f32[2,512,768]{2,1,0:T(8,128)S(1)} %copy-done.17, bf16[2,512,768]{2,1,0:T(8,128)(2,1)} %collective-permute-done.9.got_ref, ...), custom_call_target="tpu_custom_call" | custom-call | flops 1811939328 | bytes 2359296 | tf_op jit(solution)/shard_map/qkv_grad_rows/pallas_call | solution.py:950
  378.1 1.4 copy-done.42
  379.6 2.7 concatenate.170
  382.3 196.9 %reduce_gradients.1 = (bf16[768,768]{1,0:T(8,128)(2,1)}, f32[216,128]{1,0:T(8,128)}) custom-call(f32[176,128]{1,0:T(8,128)} %bitcast.157, bf16[20,512,768]{2,1,0:T(8,128)(2,1)} %hist_ref.1, bf16[512,768]{1,0:T(8,128)(2,1)} %copy-done.15, bf16[512,768]{1,0:T(8,128)(2,1)} %cot_ref.3, bf16[512,768]{1,0:T(8,128)(2,1)} %copy-done.52, ...), custom_call_target="tpu_custom_call" | custom-call | flops 99999997952 | bytes 100000000 | tf_op jit(solution)/shard_map/reduce_gradients/pallas_call | solution.py:1705
  583.3 1.4 convert_element_type.258
  586.4 1.3 collective-permute-start.12
  587.8 5.4 collective-permute-start.11
  593.2 3.0 select_select_fusion.tile_ref
  597.9 1.7 copy-done.6
  599.6 1.7 copy-done.20
  601.2 1.7 copy-done.21
  602.9 6.0 adamw_step.1
  (240 shorter events, 41.6 us)
Async XLA Ops:
  1.5 34.8 %collective-permute-start.2 = (bf16[16,128]{1,0:T(8,128)(2,1)S(1)}, bf16[16,128]{1,0:T(8,128)(2,1)S(1)}, u32[]{:S(2)}, u32[]{:S(2)}) collective-permute-start(bf16[16,128]{1,0:T(8,128)(2,1)S(1)} %bitcast.158), channel_id=1, source_target_pairs={{0,1},{1,2},{2,3},{3,4},{4,5},{5,6},{6,7},{8,9},{9,10},{10,11},{11... | collective-permute-start | bytes 12296 | tf_op jit(solution)/shard_map/ppermute | solution.py:1079
  6.3 29.9 %collective-permute-start.3 = (bf16[16,128]{1,0:T(8,128)(2,1)S(1)}, bf16[16,128]{1,0:T(8,128)(2,1)S(1)}, u32[]{:S(2)}, u32[]{:S(2)}) collective-permute-start(bf16[16,128]{1,0:T(8,128)(2,1)S(1)} %bitcast.160), channel_id=1, source_target_pairs={{1,0},{2,1},{3,2},{4,3},{5,4},{6,5},{7,6},{9,8},{10,9},{11,10},{12... | collective-permute-start | bytes 12296 | tf_op jit(solution)/shard_map/ppermute | solution.py:1080
  9.5 175.2 %collective-permute-start.1 = (bf16[256,768]{1,0:T(8,128)(2,1)}, bf16[256,768]{1,0:T(8,128)(2,1)}, u32[]{:S(2)}, u32[]{:S(2)}) collective-permute-start(bf16[256,768]{1,0:T(8,128)(2,1)} %broadcast_select_fusion.18), channel_id=1, source_target_pairs={{0,24},{8,16},{16,8},{24,0},{1,25},{9,17},{17,9},{25,1},{2,26},{10... | collective-permute-start | bytes 1179656 | tf_op jit(solution)/shard_map/ppermute | solution.py:54
  25.5 173.9 %collective-permute-start = (bf16[3,256,768]{2,1,0:T(8,128)(2,1)}, bf16[3,256,768]{2,1,0:T(8,128)(2,1)}, u32[]{:S(2)}, u32[]{:S(2)}) collective-permute-start(bf16[3,256,768]{2,1,0:T(8,128)(2,1)} %broadcast_select_fusion.2), channel_id=1, source_target_pairs={{0,24},{8,16},{16,8},{24,0},{1,25},{9,17},{17,9},{25,1},{2,26},{10... | collective-permute-start | bytes 3538952 | tf_op jit(solution)/shard_map/ppermute | solution.py:54
  197.7 3.8 collective-permute-start.4
  199.4 14.9 %slice-start = ((s8[9437184]{0:T(1024)(128)(4,1)}), s8[4194304]{0:T(1024)(128)(4,1)S(1)}, s32[]{:S(2)}) async-start(s8[9437184]{0:T(1024)(128)(4,1)} %bitcast.137), calls=%async_computation | async-start | bytes 8388608
  201.3 13.0 %slice-start.1 = ((s8[9437184]{0:T(1024)(128)(4,1)}), s8[4194304]{0:T(1024)(128)(4,1)S(1)}, s32[]{:S(2)}) async-start(s8[9437184]{0:T(1024)(128)(4,1)} %bitcast.137), calls=%async_computation.1 | async-start | bytes 8388608
  201.4 66.7 %copy-start.2 = (bf16[512,768]{1,0:T(8,128)(2,1)}, bf16[512,768]{1,0:T(8,128)(2,1)S(1)}, u32[]{:S(2)}) copy-start(bf16[512,768]{1,0:T(8,128)(2,1)S(1)} %get-tuple-element.224.rest_1_.cot_ref) | copy-start | bytes 2359300
  201.5 12.8 %copy-start.45 = (bf16[512,1536]{1,0:T(8,128)(2,1)}, bf16[512,1536]{1,0:T(8,128)(2,1)S(1)}, u32[]{:S(2)}) copy-start(bf16[512,1536]{1,0:T(8,128)(2,1)S(1)} %collective-permute-done.4.ko_ref.vo_ref) | copy-start | bytes 4718596
  201.5 12.8 %slice-start.2 = ((s8[9437184]{0:T(1024)(128)(4,1)}), s8[1048576]{0:T(1024)(128)(4,1)S(1)}, s32[]{:S(2)}) async-start(s8[9437184]{0:T(1024)(128)(4,1)} %bitcast.137), calls=%async_computation.2 | async-start | bytes 2097152
  214.3 12.0 %copy-start.28 = (bf16[512,768]{1,0:T(8,128)(2,1)}, bf16[512,768]{1,0:T(8,128)(2,1)S(1)}, u32[]{:S(2)}) copy-start(bf16[512,768]{1,0:T(8,128)(2,1)S(1)} %get-tuple-element.137.o_ref.refs_6_) | copy-start | bytes 2359300
  214.3 12.0 %copy-start.61 = (f32[6,512,128]{2,1,0:T(8,128)}, f32[6,512,128]{2,1,0:T(8,128)S(1)}, u32[]{:S(2)}) copy-start(f32[6,512,128]{2,1,0:T(8,128)S(1)} %get-tuple-element.160.lse_ref) | copy-start | bytes 4718596
  228.8 24.8 %copy-start.7 = (bf16[512,768]{1,0:T(8,128)(2,1)}, bf16[512,768]{1,0:T(8,128)(2,1)S(1)}, u32[]{:S(2)}) copy-start(bf16[512,768]{1,0:T(8,128)(2,1)S(1)} %get-tuple-element.143.rest_0_.c_ref) | copy-start | bytes 2359300
  236.0 16.5 %copy-start.47 = (bf16[512,1536]{1,0:T(8,128)(2,1)}, bf16[512,1536]{1,0:T(8,128)(2,1)S(1)}, u32[]{:S(2)}) copy-start(bf16[512,1536]{1,0:T(8,128)(2,1)S(1)} %get-tuple-element.141.k_ref.v_ref) | copy-start | bytes 4718596
  236.0 16.5 %copy-start.53 = (bf16[512,768]{1,0:T(8,128)(2,1)}, bf16[512,768]{1,0:T(8,128)(2,1)S(1)}, u32[]{:S(2)}) copy-start(bf16[512,768]{1,0:T(8,128)(2,1)S(1)} %get-tuple-element.186.refs_12_) | copy-start | bytes 2359300
  236.0 16.5 %copy-start.59 = (bf16[512,768]{1,0:T(8,128)(2,1)}, bf16[512,768]{1,0:T(8,128)(2,1)S(1)}, u32[]{:S(2)}) copy-start(bf16[512,768]{1,0:T(8,128)(2,1)S(1)} %get-tuple-element.140.q_ref) | copy-start | bytes 2359300
  236.0 3.5 collective-permute-start.5
  239.6 12.9 %copy-start.49 = (bf16[512,1536]{1,0:T(8,128)(2,1)}, bf16[512,1536]{1,0:T(8,128)(2,1)S(1)}, u32[]{:S(2)}) copy-start(bf16[512,1536]{1,0:T(8,128)(2,1)S(1)} %collective-permute-done.5.ko_ref.vo_ref) | copy-start | bytes 4718596
  253.6 29.0 %copy-start.30 = (bf16[512,768]{1,0:T(8,128)(2,1)}, bf16[512,768]{1,0:T(8,128)(2,1)S(1)}, u32[]{:S(2)}) copy-start(bf16[512,768]{1,0:T(8,128)(2,1)S(1)} %get-tuple-element.142.o_ref.refs_14_) | copy-start | bytes 2359300
  267.2 14.4 %collective-permute-start.6 = (bf16[256,768]{1,0:T(8,128)(2,1)S(1)}, bf16[256,768]{1,0:T(8,128)(2,1)S(1)}, u32[]{:S(2)}, u32[]{:S(2)}) collective-permute-start(bf16[256,768]{1,0:T(8,128)(2,1)S(1)} %broadcast_select_fusion.14), channel_id=1, source_target_pairs={{0,24},{8,16},{16,8},{24,0},{1,25},{9,17},{17,9},{25,1},{2,26},{10... | collective-permute-start | bytes 1179656 | tf_op jit(solution)/shard_map/ppermute | solution.py:54
  268.2 14.5 %copy-start.60 = (bf16[512,768]{1,0:T(8,128)(2,1)S(1)}, bf16[512,768]{1,0:T(8,128)(2,1)}, u32[]{:S(2)}) copy-start(bf16[512,768]{1,0:T(8,128)(2,1)} %copy-done.59) | copy-start | bytes 2359300
  281.6 26.6 %copy-start.23 = (bf16[512,768]{1,0:T(8,128)(2,1)}, bf16[512,768]{1,0:T(8,128)(2,1)S(1)}, u32[]{:S(2)}) copy-start(bf16[512,768]{1,0:T(8,128)(2,1)S(1)} %get-tuple-element.154.dh_ref.refs_15_) | copy-start | bytes 2359300
  285.5 22.7 %copy-start.8 = (bf16[512,768]{1,0:T(8,128)(2,1)S(1)}, bf16[512,768]{1,0:T(8,128)(2,1)}, u32[]{:S(2)}) copy-start(bf16[512,768]{1,0:T(8,128)(2,1)} %copy-done.7) | copy-start | bytes 2359300
  304.7 3.5 collective-permute-start.7
  314.1 12.9 %copy-start.41 = (bf16[512,2304]{1,0:T(8,128)(2,1)}, bf16[512,2304]{1,0:T(8,128)(2,1)S(1)}, u32[]{:S(2)}) copy-start(bf16[512,2304]{1,0:T(8,128)(2,1)S(1)} %get-tuple-element.187.refs_13_) | copy-start | bytes 7077892
  314.2 14.5 %collective-permute-start.8 = (bf16[256,768]{1,0:T(8,128)(2,1)S(1)}, bf16[256,768]{1,0:T(8,128)(2,1)S(1)}, u32[]{:S(2)}, u32[]{:S(2)}) collective-permute-start(bf16[256,768]{1,0:T(8,128)(2,1)S(1)} %broadcast_select_fusion.10), channel_id=1, source_target_pairs={{0,24},{8,16},{16,8},{24,0},{1,25},{9,17},{17,9},{25,1},{2,26},{10... | collective-permute-start | bytes 1179656 | tf_op jit(solution)/shard_map/ppermute | solution.py:54
  315.8 14.0 %copy-start.46 = (bf16[512,1536]{1,0:T(8,128)(2,1)S(1)}, bf16[512,1536]{1,0:T(8,128)(2,1)}, u32[]{:S(2)}) copy-start(bf16[512,1536]{1,0:T(8,128)(2,1)} %copy-done.45) | copy-start | bytes 4718596
  315.8 14.0 %copy-start.62 = (f32[6,512,128]{2,1,0:T(8,128)S(1)}, f32[6,512,128]{2,1,0:T(8,128)}, u32[]{:S(2)}) copy-start(f32[6,512,128]{2,1,0:T(8,128)} %copy-done.61) | copy-start | bytes 4718596
  329.8 30.4 %copy-start.15 = (bf16[512,768]{1,0:T(8,128)(2,1)}, bf16[512,768]{1,0:T(8,128)(2,1)S(1)}, u32[]{:S(2)}) copy-start(bf16[512,768]{1,0:T(8,128)(2,1)S(1)} %pad_maximum_fusion.4.dy_ref) | copy-start | bytes 2359300
  331.3 22.8 %copy-start.71 = (s32[2,8]{1,0:T(2,128)S(1)}, s32[2,8]{1,0:T(2,128)}, u32[]{:S(2)}) copy-start(s32[2,8]{1,0:T(2,128)} %constant.246.clone) | copy-start | bytes 196
  331.3 28.9 %copy-start.11 = (bf16[512,768]{1,0:T(8,128)(2,1)S(1)}, bf16[512,768]{1,0:T(8,128)(2,1)}, u32[]{:S(2)}) copy-start(bf16[512,768]{1,0:T(8,128)(2,1)} %cot_ref.3) | copy-start | bytes 2359300
  331.3 28.9 %copy-start.35 = (f32[43]{0:T(128)S(1)}, f32[43]{0:T(128)}, u32[]{:S(2)}) copy-start(f32[43]{0:T(128)} %w_ref.3) | copy-start | bytes 520
  353.8 15.3 %collective-permute-start.9 = (bf16[2,512,768]{2,1,0:T(8,128)(2,1)}, bf16[2,512,768]{2,1,0:T(8,128)(2,1)}, u32[]{:S(2)}, u32[]{:S(2)}) collective-permute-start(bf16[2,512,768]{2,1,0:T(8,128)(2,1)} %get-tuple-element.163), channel_id=1, source_target_pairs={{0,8},{8,0},{16,24},{24,16},{1,9},{9,1},{17,25},{25,17},{2,10},{10... | collective-permute-start | bytes 4718600 | tf_op jit(solution)/shard_map/ppermute | solution.py:58
  360.2 8.9 %slice-start.3 = ((s8[9437184]{0:T(1024)(128)(4,1)}), s8[4194304]{0:T(1024)(128)(4,1)S(1)}, s32[]{:S(2)}) async-start(s8[9437184]{0:T(1024)(128)(4,1)} %bitcast.141), calls=%async_computation.3 | async-start | bytes 8388608
  360.2 8.8 %slice-start.4 = ((s8[9437184]{0:T(1024)(128)(4,1)}), s8[4194304]{0:T(1024)(128)(4,1)S(1)}, s32[]{:S(2)}) async-start(s8[9437184]{0:T(1024)(128)(4,1)} %bitcast.141), calls=%async_computation.4 | async-start | bytes 8388608
  360.3 8.8 %slice-start.5 = ((s8[9437184]{0:T(1024)(128)(4,1)}), s8[1048576]{0:T(1024)(128)(4,1)S(1)}, s32[]{:S(2)}) async-start(s8[9437184]{0:T(1024)(128)(4,1)} %bitcast.141), calls=%async_computation.5 | async-start | bytes 2097152
  360.3 8.8 %copy-start.9 = (bf16[512,768]{1,0:T(8,128)(2,1)S(1)}, bf16[512,768]{1,0:T(8,128)(2,1)}, u32[]{:S(2)}) copy-start(bf16[512,768]{1,0:T(8,128)(2,1)} %copy-done.7) | copy-start | bytes 2359300
  360.3 8.8 %copy-start.14 = (f32[512,128]{1,0:T(8,128)S(1)}, f32[512,128]{1,0:T(8,128)}, u32[]{:S(2)}) copy-start(f32[512,128]{1,0:T(8,128)} %pad_maximum_fusion.6.sin_ref) | copy-start | bytes 786436
  360.3 10.3 %copy-start.17 = (f32[2,512,768]{2,1,0:T(8,128)S(1)}, f32[2,512,768]{2,1,0:T(8,128)}, u32[]{:S(2)}) copy-start(f32[2,512,768]{2,1,0:T(8,128)} %copy-done.16) | copy-start | bytes 9437188
  360.3 10.4 %copy-start.25 = (bf16[512,768]{1,0:T(8,128)(2,1)S(1)}, bf16[512,768]{1,0:T(8,128)(2,1)}, u32[]{:S(2)}) copy-start(bf16[512,768]{1,0:T(8,128)(2,1)} %copy-done.24) | copy-start | bytes 2359300
  360.3 10.6 %copy-start.27 = (bf16[512,768]{1,0:T(8,128)(2,1)S(1)}, bf16[512,768]{1,0:T(8,128)(2,1)}, u32[]{:S(2)}) copy-start(bf16[512,768]{1,0:T(8,128)(2,1)} %copy-done.26) | copy-start | bytes 2359300
  370.9 8.7 %copy-start.66 = (f32[768]{0:T(1024)S(1)}, f32[768]{0:T(1024)}, u32[]{:S(2)}) copy-start(f32[768]{0:T(1024)} %get-tuple-element.200) | copy-start | bytes 9220
  584.8 8.4 %copy-start.68 = (pred[768]{0:T(1024)(128)(4,1)S(1)}, pred[768]{0:T(1024)(128)(4,1)}, u32[]{:S(2)}) copy-start(pred[768]{0:T(1024)(128)(4,1)} %fusion.25) | copy-start | bytes 2308
  586.4 22.5 %collective-permute-start.10 = (bf16[256,768]{1,0:T(8,128)(2,1)}, bf16[256,768]{1,0:T(8,128)(2,1)}, u32[]{:S(2)}, u32[]{:S(2)}) collective-permute-start(bf16[256,768]{1,0:T(8,128)(2,1)} %broadcast_select_fusion.6), channel_id=1, source_target_pairs={{0,24},{8,16},{16,8},{24,0},{1,25},{9,17},{17,9},{25,1},{2,26},{10... | collective-permute-start | bytes 1179656 | tf_op jit(solution)/shard_map/ppermute | solution.py:54
  586.4 11.3 %collective-permute-start.12 = (f32[3,768]{1,0:T(4,128)S(1)}, f32[3,768]{1,0:T(4,128)S(1)}, u32[]{:S(2)}, u32[]{:S(2)}) collective-permute-start(f32[3,768]{1,0:T(4,128)S(1)} %fusion.20), channel_id=1, source_target_pairs={{1,0},{2,1},{3,2},{4,3},{5,4},{6,5},{7,6},{9,8},{10,9},{11,10},{12... | collective-permute-start | bytes 27656 | tf_op jit(solution)/shard_map/ppermute | solution.py:1239
  587.8 8.4 %copy-start.69 = (f32[43]{0:T(128)S(1)}, f32[43]{0:T(128)}, u32[]{:S(2)}) copy-start(f32[43]{0:T(128)} %param.31) | copy-start | bytes 520
  587.8 10.1 %copy-start.5 = (f32[1,590496]{1,0:T(1,128)S(1)}, f32[1,590496]{1,0:T(1,128)}, u32[]{:S(2)}) copy-start(f32[1,590496]{1,0:T(1,128)} %p_ref.3) | copy-start | bytes 7085956
  587.8 10.0 %collective-permute-start.11 = (f32[3,768]{1,0:T(4,128)S(1)}, f32[3,768]{1,0:T(4,128)S(1)}, u32[]{:S(2)}, u32[]{:S(2)}) collective-permute-start(f32[3,768]{1,0:T(4,128)S(1)} %fusion.23), channel_id=1, source_target_pairs={{0,1},{1,2},{2,3},{3,4},{4,5},{5,6},{6,7},{8,9},{9,10},{10,11},{11... | collective-permute-start | bytes 27656 | tf_op jit(solution)/shard_map/ppermute | solution.py:1238
  (44 other events, 124.8 us)

commit v5 on v4

--- a/solution.py
+++ b/solution.py
@@ -115,15 +115,53 @@
 
 
 MESH = pl.DeviceIdType.MESH
-
-
-def gather_kernel(plan, block_ref, vec_ref, att_ref, mlp_ref, vecs_ref, att_in, mlp_in, vec_in, vec_out, sent, kept):
+HIST_CHUNK = 16
+
+
+def gather_kernel(plan, w_ref, block_ref, vec_ref, hist_ref, *refs):
+    att_ref, mlp_ref, vecs_ref, past_ref = refs[:4]
+    att_in, mlp_in, att_core, mlp_core, first_in, vec_in, vec_out, sent, kept, hin, hist_sem = refs[4:]
     section, b = lax.axis_index("section"), lax.axis_index("batch")
     plane, core = section // 2, section % 2
     z, x = b // 2, b % 2
     nb = plan.nb
     count = 4 * nb
     me = section * nb + b
+    half, quarter = plan.rows // 2, plan.rows // 4
+    far = 1 - plane
+    to_x, to_y, to_core = (section, b ^ 1), (section ^ 2, b), (section ^ 1, b)
+    up, down = (section, jnp.minimum(b + 2, nb - 1)), (section, jnp.maximum(b - 2, 0))
+
+    chunks = hist_ref.shape[1] // HIST_CHUNK
+
+    def history_in(i, slot):
+        rows = pl.ds(pl.multiple_of(i * HIST_CHUNK, HIST_CHUNK), HIST_CHUNK)
+        return pltpu.make_async_copy(hist_ref.at[:, rows], hin.at[slot], hist_sem.at[slot])
+
+    history_in(0, 0).start()
+    history_in(1, 1).start()
+    pairs = [0]
+
+    def average():
+        if pairs[0] >= chunks // 2:
+            return
+        for slot in range(2):
+            i = 2 * pairs[0] + slot
+            history_in(i, slot).wait()
+            for at in range(0, D, 256):
+                columns = slice(at, at + 256)
+
+                def body(j, totals):
+                    row = hin[slot, j, :, columns].astype(f32)
+                    return totals[0] + w_ref[j] * row, totals[1] + w_ref[HIST + 1 + j] * row
+
+                zero = jnp.zeros((HIST_CHUNK, 256), f32)
+                one, two = lax.fori_loop(0, HIST, body, (zero, zero))
+                past_ref[0, pl.ds(i * HIST_CHUNK, HIST_CHUNK), columns] = one.astype(bf16)
+                past_ref[1, pl.ds(i * HIST_CHUNK, HIST_CHUNK), columns] = two.astype(bf16)
+            if i + 2 < chunks:
+                history_in(i + 2, slot).start()
+        pairs[0] += 1
 
     barrier = pltpu.get_barrier_semaphore()
 
@@ -153,9 +191,7 @@
 
         lax.fori_loop(1, count, body, 0)
 
-    half = plan.rows // 2
-    pending = []
-    slot = [0]
+    mine = []
 
     def when(cond, fn):
         if cond is True:
@@ -163,190 +199,176 @@
         else:
             pl.when(cond)(fn)
 
-    def run(out_ref, arrive, first, second):
-        def part(layer, tile, unit):
-            return out_ref.at[layer, tile, pl.ds(unit * half, half)]
-
-        def send(cond, src, layer, tile, unit, to):
-            index = slot[0]
-            slot[0] += 1
-            copy = pltpu.make_async_remote_copy(
-                src,
-                part(layer, tile, unit),
-                sent.at[index],
-                arrive.at[layer, tile, unit],
-                device_id=to,
-                device_id_type=MESH,
-            )
-            when(cond, copy.start)
-            mine.append((cond, copy))
-
-        def wait(cond, layer, tile, unit):
-            copy = pltpu.make_async_remote_copy(
-                part(layer, tile, unit),
-                part(layer, tile, unit),
-                sent.at[0],
-                arrive.at[layer, tile, unit],
-                device_id=(section, b ^ 1),
-                device_id_type=MESH,
-            )
-            when(cond, copy.wait_recv)
-
-        mine = []
-        to_x, to_y, to_core = (section, b ^ 1), (section ^ 2, b), (section ^ 1, b)
-        far = 1 - plane
-
-        def spread(step, cond, from_block):
-            column, owned, hops = first[step], second[step][0], second[step][1]
-            tile = 2 * column + x
-            for unit in range(2):
-                if not from_block:
-                    wait(cond if owned is None else jnp.logical_not(owned) & cond, plane, tile, unit)
-            for unit in range(2):
-                for source_cond, src in (
-                    (owned, block_ref.at[pl.ds(unit * half, half)]),
-                    (None if owned is True else (True if owned is None else jnp.logical_not(owned)), part(plane, tile, unit)),
-                ):
-                    if source_cond is None:
-                        continue
-
-                    def both(c):
-                        return c if source_cond is True else (source_cond if c is True else c & source_cond)
-
-                    for hop_cond, to in hops:
-                        send(both(hop_cond), src, plane, tile, unit, to)
-                    send(both(True), src, plane, tile, unit, to_x)
-                    send(both(True), src, plane, tile, unit, to_y)
-                    send(both(True), src, plane, tile, unit, to_core)
-
-        def corner(step):
-            column = first[step]
-            across, same = 2 * column + (1 - x), 2 * column + x
-            for unit in range(2):
-                wait(True, plane, across, unit)
-                if unit == 0:
-                    send(True, part(plane, across, unit), plane, across, unit, to_y)
-                send(True, part(plane, across, unit), plane, across, unit, to_core)
-            for unit in range(2):
-                wait(True, far, same, unit)
-                if unit == 1:
-                    send(True, part(far, same, unit), far, same, unit, to_x)
-                send(True, part(far, same, unit), far, same, unit, to_core)
-
-        def last(step):
-            tile = 2 * first[step] + (1 - x)
-            for unit in range(2):
-                wait(True, far, tile, unit)
-                send(True, part(far, tile, unit), far, tile, unit, to_core)
-
-        steps = len(first)
-        for step in range(steps):
-            spread(step, True, second[step][0] is True)
-            if step:
-                corner(step - 1)
-        corner(steps - 1)
-        for step in range(steps):
-            last(step)
-        pending.append(mine)
-
+    def both(a, c):
+        return c if a is True else a if c is True else a & c
+
+    def remote(cond, src, dst, got, to):
+        copy = pltpu.make_async_remote_copy(
+            src, dst, sent.at[len(mine)], got, device_id=to, device_id_type=MESH
+        )
+        when(cond, copy.start)
+        mine.append((cond, copy))
+
+    def landed(cond, dst, got):
+        copy = pltpu.make_async_remote_copy(
+            dst, dst, sent.at[0], got, device_id=to_core, device_id_type=MESH
+        )
+        when(cond, copy.wait_recv)
+
+    tile = jnp.minimum(b, nb // 2 - 1)
+    has_att = z < 2
+    own_att = both(core == 0, has_att)
+    own_mlp = core == 1
+    places = ((own_att, att_ref.at[plane, tile], 0), (own_mlp, mlp_ref.at[plane, b], 1))
+    for cond, place, k in places:
+        remote(cond, block_ref, place, first_in.at[k], to_core)
+        when(cond, pltpu.make_async_copy(block_ref, place, kept).start)
+    for cond, place, k in places:
+        when(cond, pltpu.make_async_copy(block_ref, place, kept).wait)
+    landed(both(core == 0, True), mlp_ref.at[plane, b], first_in.at[1])
+    landed(both(core == 1, has_att), att_ref.at[plane, tile], first_in.at[0])
+
+    lower = z < 2
+    end = (z == 0) | (z == 3)
+    middle = jnp.logical_not(end)
+
+    def at(t):
+        return jnp.where(lower, t, 3 - t)
+
+    inward = (section, jnp.where(lower, up[1], down[1]))
+    outward = (section, jnp.where(lower, down[1], up[1]))
+    att_steps = [
+        (jnp.where(z == 0, 0, 1), has_att, [(z < 3, up), (z == 1, down)]),
+        (jnp.where(z == 0, 1, 0), False, [((z == 1) | (z == 2), up)]),
+    ]
+    mlp_steps = [
+        (z, True, [(True, inward), (middle, outward)]),
+        (jnp.where(end, at(1), at(0)), False, [(middle, inward)]),
+        (at(2), False, [(middle, outward)]),
+        (at(3), False, [(middle, outward)]),
+    ]
+    kinds = {
+        "a": (att_ref, att_in, att_core, att_steps),
+        "m": (mlp_ref, mlp_in, mlp_core, mlp_steps),
+    }
+    row = pl.multiple_of(half * core, half)
+
+    def part(k, layer, t, unit=None):
+        ref = kinds[k][0]
+        if unit is None:
+            return ref.at[layer, t, pl.ds(row, half)]
+        return ref.at[layer, t, pl.ds(pl.multiple_of(row + unit * quarter, quarter), quarter)]
+
+    def give(cond, k, layer, t):
+        remote(cond, part(k, layer, t), part(k, layer, t), kinds[k][2].at[layer, t], to_core)
+
+    def spread(k, step, cond=True):
+        column, owned, hops = kinds[k][3][step]
+        got = kinds[k][1]
+        t = 2 * column + x
+        src = part(k, plane, t)
+        if owned is False:
+            landed(cond, src, got.at[plane, t, 0])
+        for hop, to in hops:
+            remote(both(cond, hop), src, src, got.at[plane, t, 0], to)
+        remote(cond, src, src, got.at[plane, t, 0], to_x)
+        remote(cond, src, src, got.at[plane, t, 0], to_y)
+        if owned is False:
+            give(cond, k, plane, t)
+        average()
+
+    def corner(k, step):
+        column, got = kinds[k][3][step][0], kinds[k][1]
+        across, same = 2 * column + (1 - x), 2 * column + x
+        landed(True, part(k, plane, across), got.at[plane, across, 0])
+        src = part(k, plane, across, 0)
+        remote(True, src, src, got.at[plane, across, 0], to_y)
+        landed(True, part(k, far, same), got.at[far, same, 0])
+        src = part(k, far, same, 1)
+        remote(True, src, src, got.at[far, same, 1], to_x)
+        give(True, k, plane, across)
+        give(True, k, far, same)
+        average()
+
+    def last(k, step):
+        t = 2 * kinds[k][3][step][0] + (1 - x)
+        for unit in range(2):
+            landed(True, part(k, far, t, unit), kinds[k][1].at[far, t, unit])
+        give(True, k, far, t)
+        average()
+
+    upper = jnp.logical_not(lower)
+    column, _, hops = att_steps[0]
+    att_steps.append((column, False, hops))
     each(lambda copy: copy.start())
-    up, down = (section, jnp.minimum(b + 2, nb - 1)), (section, jnp.maximum(b - 2, 0))
-
-    @pl.when(core == 0)
-    def _():
-        own = pltpu.make_async_copy(block_ref, att_ref.at[plane, jnp.minimum(b, nb // 2 - 1)], kept)
-        pl.when(z < 2)(own.start)
-        first = [jnp.where(z == 0, 0, 1), jnp.where(z == 0, 1, 0)]
-        slot[0] = 0
-        run(
-            att_ref,
-            att_in,
-            first,
-            [
-                (z < 2, [(z < 3, up), (z == 1, down)]),
-                (None, [((z == 1) | (z == 2), up)]),
-            ],
-        )
+    spread("m", 0)
+    spread("a", 0, lower)
+    spread("m", 1)
+    corner("m", 0)
+    spread("a", 2, upper)
+    spread("m", 2)
+    corner("a", 0)
+    corner("m", 1)
+    spread("a", 1)
+    spread("m", 3)
+    corner("m", 2)
+    corner("a", 1)
+    last("m", 0)
+    last("a", 0)
+    corner("m", 3)
+    last("m", 1)
+    last("m", 2)
+    last("a", 1)
+    last("m", 3)
+    while pairs[0] < chunks // 2:
+        average()
+    for k, tiles, skip in (("a", nb // 2, has_att), ("m", nb, True)):
         for layer in range(2):
-            for tile in range(nb):
-                for unit in range(2):
-                    other = mlp_ref.at[layer, tile, pl.ds(unit * half, half)]
-                    pltpu.make_async_remote_copy(
-                        other, other, sent.at[0], mlp_in.at[layer, tile, unit],
-                        device_id=(section ^ 1, b), device_id_type=MESH,
-                    ).wait_recv()
-        for cond, copy in pending[-1]:
-            when(cond, copy.wait_send)
-        pl.when(z < 2)(own.wait)
-
-    @pl.when(core == 1)
-    def _():
-        own = pltpu.make_async_copy(block_ref, mlp_ref.at[plane, b], kept)
-        own.start()
-        low = z < 2
-        end = (z == 0) | (z == 3)
-        middle = jnp.logical_not(end)
-
-        def at(t):
-            return jnp.where(low, t, 3 - t)
-
-        inward = (section, jnp.where(low, jnp.minimum(b + 2, nb - 1), jnp.maximum(b - 2, 0)))
-        outward = (section, jnp.where(low, jnp.maximum(b - 2, 0), jnp.minimum(b + 2, nb - 1)))
-        slot[0] = 0
-        run(
-            mlp_ref,
-            mlp_in,
-            [z, jnp.where(end, at(1), at(0)), at(2), at(3)],
-            [
-                (True, [(True, inward), (middle, outward)]),
-                (None, [(middle, inward)]),
-                (None, [(middle, outward)]),
-                (None, [(middle, outward)]),
-            ],
-        )
-        for layer in range(2):
-            for tile in range(nb // 2):
-                for unit in range(2):
-                    other = att_ref.at[layer, tile, pl.ds(unit * half, half)]
-                    pltpu.make_async_remote_copy(
-                        other, other, sent.at[0], att_in.at[layer, tile, unit],
-                        device_id=(section ^ 1, b), device_id_type=MESH,
-                    ).wait_recv()
-        for cond, copy in pending[-1]:
-            when(cond, copy.wait_send)
-        own.wait()
-
+            for t in range(tiles):
+                other = pl.ds(pl.multiple_of(half * (1 - core), half), half)
+                cond = jnp.logical_not(both((plane == layer) & (b == t), skip))
+                landed(cond, kinds[k][0].at[layer, t, other], kinds[k][2].at[layer, t])
+    for cond, copy in mine:
+        when(cond, copy.wait_send)
     each(lambda copy: copy.wait())
     here = pltpu.make_async_copy(vec_ref, vecs_ref.at[me], kept)
     here.start()
     here.wait()
 
 
-def gather_weights(plan, block, vecs):
+def gather_weights(plan, mix_weights, block, vecs, history):
     nb, rows = plan.nb, plan.rows
     body = functools.partial(gather_kernel, plan)
     any_spec = pl.BlockSpec(memory_space=pltpu.HBM)
     return pl.pallas_call(
         body,
-        in_specs=[any_spec] * 2,
-        out_specs=[any_spec] * 3,
+        in_specs=[SMEM_SPEC] + [any_spec] * 3,
+        out_specs=[any_spec] * 3 + [pl.BlockSpec(memory_space=pltpu.VMEM)],
         out_shape=[
             jax.ShapeDtypeStruct((2, nb // 2, rows, D), bf16),
             jax.ShapeDtypeStruct((2, nb, rows, D), bf16),
             jax.ShapeDtypeStruct((4 * nb,) + vecs.shape, bf16),
+            jax.ShapeDtypeStruct((2,) + history.shape[1:], bf16),
         ],
         scratch_shapes=[
             pltpu.SemaphoreType.DMA((2, nb // 2, 2)),
             pltpu.SemaphoreType.DMA((2, nb, 2)),
+            pltpu.SemaphoreType.DMA((2, nb // 2)),
+            pltpu.SemaphoreType.DMA((2, nb)),
+            pltpu.SemaphoreType.DMA((2,)),
             pltpu.SemaphoreType.DMA((4 * nb,)),
             pltpu.SemaphoreType.DMA((4 * nb,)),
             pltpu.SemaphoreType.DMA((96,)),
             pltpu.SemaphoreType.DMA,
+            pltpu.VMEM((2, HIST, HIST_CHUNK, D), bf16),
+            pltpu.SemaphoreType.DMA((2,)),
         ],
         name="gather_weights",
         cost_estimate=pl.CostEstimate(flops=10**11, bytes_accessed=10**8, transcendentals=0),
-        compiler_params=pltpu.CompilerParams(collective_id=0, has_side_effects=True),
-    )(block, vecs)
+        compiler_params=pltpu.CompilerParams(
+            collective_id=0, has_side_effects=True, vmem_limit_bytes=16 * 1024 * 1024
+        ),
+    )(mix_weights, block, vecs, history)
 
 
 VMEM_LIMIT = 32 * 1024 * 1024
@@ -1324,8 +1346,9 @@
         self.load, self.sent, self.got = refs[7:]
 
 
-HIST_CHUNK = 16
 SMALL_ROWS = 176
+SPLIT, SHARE = 112, 160
+KEEP = SPLIT + SHARE
 
 
 def reduce_kernel(tile_count, scale, small_ref, hist_ref, dy_ref, cot_ref, *refs):
@@ -1393,17 +1416,29 @@
 
     def landed(dst, got):
         pltpu.make_async_remote_copy(
-            dst, dst, kinds[0].sent.at[0, 0, 0], got, device_id=to_core, device_id_type=MESH
+            dst, dst, kinds[0].sent.at[0, 0, 0, 0], got, device_id=to_core, device_id_type=MESH
         ).wait_recv()
 
-    def add(dst, at, src, src_at, rows):
+    def add(dst, at, src, src_at, rows, columns):
+        size = math.gcd(rows, 64)
+
         def body(i, carry):
-            to = pl.ds(pl.multiple_of(at + i * 64, 64), 64)
-            fro = pl.ds(pl.multiple_of(src_at + i * 64, 64), 64)
-            dst[to, :] = (dst[to, :].astype(f32) + src[fro, :].astype(f32)).astype(bf16)
+            to = pl.ds(pl.multiple_of(at + i * size, 16), size)
+            fro = pl.ds(pl.multiple_of(src_at + i * size, 16), size)
+            both = dst[to, columns].astype(f32) + src[fro, columns].astype(f32)
+            dst[to, columns] = both.astype(bf16)
             return carry
 
-        lax.fori_loop(0, rows // 64, body, 0)
+        lax.fori_loop(0, rows // size, body, 0)
+
+    def parts(layer, k):
+        wide = D // 2
+        return [pl.ds(at, wide) for at in range(0, D, wide)]
+
+    def message(kind, hop, layer, slot, p, src, dst, to, cond=None):
+        return remote(
+            src, dst, kind.sent.at[hop, layer, slot, p], kind.got.at[hop, layer, slot, p], to, cond
+        )
 
     def product(index):
         layer, k, _, name, j = products[index][:5]
@@ -1450,20 +1485,20 @@
         if not done:
             return
         tiles = range(4) if done[0][3] in ("up", "joint") else [4 + item[4] for item in done]
-        for tile in tiles:
-            copy = pltpu.make_async_remote_copy(
-                kind.sum.at[2, tile],
-                kind.c.at[tile],
-                kind.sent.at[0, layer, tile],
-                kind.got.at[0, layer, tile],
-                device_id=to_core,
-                device_id_type=MESH,
-            )
-            copy.start()
-            if layer == 1:
-                given.setdefault(k, []).append(copy)
-            else:
-                mine.append((None, copy))
+        for p, columns in enumerate(parts(layer, k)):
+            for tile in tiles:
+                copy = message(
+                    kind,
+                    0,
+                    layer,
+                    tile,
+                    p,
+                    kind.sum.at[2, tile, :, columns],
+                    kind.c.at[tile, :, columns],
+                    to_core,
+                )
+                if layer == 1:
+                    given.setdefault(k, []).append(mine.pop()[1])
 
     order = [(layer, k) for layer in (1, 0) for k in (0, 1)]
     chunks = hist_ref.shape[1] // HIST_CHUNK
@@ -1495,85 +1530,98 @@
             if i + 2 < chunks:
                 history_in(i + 2, slot).start()
 
-    keep_at = pl.multiple_of(128 * plane, 128)
-    keep = pl.ds(keep_at, 256)
+    keep_at = pl.multiple_of(SPLIT * plane, 16)
+    keep = pl.ds(keep_at, KEEP)
 
     def column(k, step):
         if k == 1:
             return 1 - low if step == 0 else low
         return 2 * step + (1 - low) if step < 2 else 2 * (step - 2) + low
 
-    def stage_core(layer, k, step):
+    def stage_core(layer, k, step, p, columns):
         kind = kinds[k]
         zz = column(k, step)
         for tile in (2 * zz + (1 - x), 2 * zz + x):
-            landed(kind.c.at[tile], kind.got.at[0, layer, tile])
-            add(kind.sum.at[layer, tile], 0, kind.c.at[tile], 0, 384)
-            give = pl.ds(pl.multiple_of(256 * (1 - plane), 128), 128)
-            remote(
-                kind.sum.at[layer, tile, give],
-                kind.y.at[layer, tile],
-                kind.sent.at[1, layer, tile],
-                kind.got.at[1, layer, tile],
+            landed(kind.c.at[tile, :, columns], kind.got.at[0, layer, tile, p])
+            add(kind.sum.at[layer, tile], 0, kind.c.at[tile], 0, 384, columns)
+            give = pl.ds(pl.multiple_of(KEEP * (1 - plane), 16), SPLIT)
+            message(
+                kind,
+                1,
+                layer,
+                tile,
+                p,
+                kind.sum.at[layer, tile, give, columns],
+                kind.y.at[layer, tile, :, columns],
                 to_plane,
             )
-        if layer == 1 and step == tile_count[k] // 2 - 1:
+        last = step == tile_count[k] // 2 - 1 and p == len(parts(layer, k)) - 1
+        if layer == 1 and last:
             pl.semaphore_signal(credit.at[k], 1, device_id=to_core, device_id_type=MESH)
 
-    def stage_plane(layer, k, step):
+    def stage_plane(layer, k, step, p, columns):
         kind = kinds[k]
         zz = column(k, step)
         for turn, tile in enumerate((2 * zz + (1 - x), 2 * zz + x)):
-            landed(kind.y.at[layer, tile], kind.got.at[1, layer, tile])
-            add(kind.sum.at[layer, tile], 256 * plane, kind.y.at[layer, tile], 0, 128)
+            landed(kind.y.at[layer, tile, :, columns], kind.got.at[1, layer, tile, p])
+            add(kind.sum.at[layer, tile], KEEP * plane, kind.y.at[layer, tile], 0, SPLIT, columns)
             if turn == 0:
-                remote(
-                    kind.sum.at[layer, tile, keep],
-                    kind.x.at[layer, zz],
-                    kind.sent.at[2, layer, zz],
-                    kind.got.at[2, layer, zz],
+                message(
+                    kind,
+                    2,
+                    layer,
+                    zz,
+                    p,
+                    kind.sum.at[layer, tile, keep, columns],
+                    kind.x.at[layer, zz, :, columns],
                     to_x,
                 )
 
-    def stage_x(layer, k, step):
+    def stage_x(layer, k, step, p, columns):
         kind = kinds[k]
         zz = column(k, step)
         tile = 2 * zz + x
-        landed(kind.x.at[layer, zz], kind.got.at[2, layer, zz])
-        add(kind.sum.at[layer, tile], keep_at, kind.x.at[layer, zz], 0, 256)
-
+        landed(kind.x.at[layer, zz, :, columns], kind.got.at[2, layer, zz, p])
+        add(kind.sum.at[layer, tile], keep_at, kind.x.at[layer, zz], 0, KEEP, columns)
         half = 2 - k
         if step < half:
-            remote(
-                kind.sum.at[layer, tile, keep],
-                kind.z.at[layer, step],
-                kind.sent.at[3, layer, step],
-                kind.got.at[3, layer, step],
+            message(
+                kind,
+                3,
+                layer,
+                step,
+                p,
+                kind.sum.at[layer, tile, keep, columns],
+                kind.z.at[layer, step, :, columns],
                 to_low,
             )
         else:
-            landed(kind.z.at[layer, step - half], kind.got.at[3, layer, step - half])
-            add(kind.sum.at[layer, tile], keep_at, kind.z.at[layer, step - half], 0, 256)
-
-    def stage_high(layer, k):
+            slot = step - half
+            landed(kind.z.at[layer, slot, :, columns], kind.got.at[3, layer, slot, p])
+            add(kind.sum.at[layer, tile], keep_at, kind.z.at[layer, slot], 0, KEEP, columns)
+
+    def stage_high(layer, k, p, columns):
         kind = kinds[k]
         zz = 2 * (1 - high) + low if k == 0 else low
-        remote(
-            kind.sum.at[layer, 2 * zz + x, keep],
-            kind.w.at[layer],
-            kind.sent.at[4, layer, 0],
-            kind.got.at[4, layer, 0],
+        message(
+            kind,
+            4,
+            layer,
+            0,
+            p,
+            kind.sum.at[layer, 2 * zz + x, keep, columns],
+            kind.w.at[layer, :, columns],
             to_high,
             None if k == 0 else high == 1,
         )
 
-    def stage_end(layer, k):
+    def stage_end(layer, k, p, columns):
         kind = kinds[k]
         tile = 2 * (2 * high + low if k == 0 else low) + x
 
         def take():
-            landed(kind.w.at[layer], kind.got.at[4, layer, 0])
-            add(kind.sum.at[layer, tile], keep_at, kind.w.at[layer], 0, 256)
+            landed(kind.w.at[layer, :, columns], kind.got.at[4, layer, 0, p])
+            add(kind.sum.at[layer, tile], keep_at, kind.w.at[layer], 0, KEEP, columns)
 
         cond = plane != layer
         if k == 0:
@@ -1582,10 +1630,10 @@
             pl.when(high == 0)(take)
             cond = cond & (high == 0)
         remote(
-            kind.sum.at[layer, tile, keep],
-            kind.end,
-            kind.sent.at[5, layer, 0],
-            kind.got.at[5, 0, 0],
+            kind.sum.at[layer, tile, keep, columns],
+            kind.end.at[:, columns],
+            kind.sent.at[5, layer, 0, p],
+            kind.got.at[5, layer, 0, p],
             to_plane,
             cond,
         )
@@ -1606,12 +1654,17 @@
         else:
             total_ref[...] = acc[step]
 
-    steps = [(layer, k, step) for layer, k in order for step in range(tile_count[k] // 2)]
+    steps = [
+        (layer, k, step, p, columns)
+        for layer, k in order
+        for step in range(tile_count[k] // 2)
+        for p, columns in enumerate(parts(layer, k))
+    ]
     later = {}
     small_at = chunks // 2
-    for at in range(len(steps) + 10):
-        if at < len(steps):
-            stage_product(*steps[at])
+    for at in range(len(steps) + 8):
+        if at < len(steps) and steps[at][3] == 0:
+            stage_product(*steps[at][:3])
         if 0 <= at - 1 < len(steps):
             stage_core(*steps[at - 1])
         if at < chunks // 2:
@@ -1621,26 +1674,34 @@
         if 0 <= at - 3 < len(steps):
             stage_plane(*steps[at - 3])
         if 0 <= at - 5 < len(steps):
-            layer, k, step = steps[at - 5]
-            stage_x(layer, k, step)
+            layer, k, step, p, columns = steps[at - 5]
+            stage_x(layer, k, step, p, columns)
             if step == tile_count[k] // 2 - 1:
-                stage_high(layer, k)
-                later[at + 2] = (layer, k)
+                stage_high(layer, k, p, columns)
+                later[at + 2] = (layer, k, p, columns)
         if at in later:
             stage_end(*later.pop(at))
-    for layer, k in later.values():
-        stage_end(layer, k)
+    for item in later.values():
+        stage_end(*item)
+
     def finish(k):
         kind = kinds[k]
         tile = 2 * (2 * high + low if k == 0 else low) + x
-        landed(kind.end, kind.got.at[5, 0, 0])
+        for layer in range(2):
+
+            @pl.when(plane == layer)
+            def _():
+                for p, columns in enumerate(parts(layer, k)):
+                    landed(kind.end.at[:, columns], kind.got.at[5, layer, 0, p])
+
         own = kind.sum.at[plane, tile]
-        here = pl.ds(pl.multiple_of(256 * plane, 128), 128)
-        there = pl.ds(pl.multiple_of(256 * (1 - plane), 128), 128)
+        here = pl.ds(pl.multiple_of(KEEP * plane, 16), SPLIT)
+        there = pl.ds(pl.multiple_of(KEEP * (1 - plane), 16), SPLIT)
+        middle = slice(SPLIT, KEEP)
         fin[k, here] = own[here]
-        fin[k, there] = kind.end[pl.ds(pl.multiple_of(128 * (1 - plane), 128), 128)]
-        shared = kind.end[pl.ds(pl.multiple_of(128 * plane, 128), 128)].astype(f32)
-        fin[k, 128:256] = (own[128:256].astype(f32) + shared).astype(bf16)
+        fin[k, there] = kind.end[pl.ds(pl.multiple_of(SHARE * (1 - plane), 16), SPLIT)]
+        shared = kind.end[pl.ds(pl.multiple_of(SPLIT * plane, 16), SHARE)].astype(f32)
+        fin[k, middle] = (own[middle].astype(f32) + shared).astype(bf16)
 
     owner = high == 0
     pl.when(owner)(lambda: finish(1))
@@ -1676,14 +1737,14 @@
         scratch += [
             pltpu.VMEM((3, count, 384, D), bf16),
             pltpu.VMEM((count, 384, D), bf16),
-            pltpu.VMEM((2, count, 128, D), bf16),
-            pltpu.VMEM((2, count // 2, 256, D), bf16),
-            pltpu.VMEM((2, count // 4, 256, D), bf16),
-            pltpu.VMEM((2, 256, D), bf16),
-            pltpu.VMEM((256, D), bf16),
+            pltpu.VMEM((2, count, SPLIT, D), bf16),
+            pltpu.VMEM((2, count // 2, KEEP, D), bf16),
+            pltpu.VMEM((2, count // 4, KEEP, D), bf16),
+            pltpu.VMEM((2, KEEP, D), bf16),
+            pltpu.VMEM((KEEP, D), bf16),
             pltpu.SemaphoreType.DMA((2, count)),
-            pltpu.SemaphoreType.DMA((6, 2, count)),
-            pltpu.SemaphoreType.DMA((6, 2, count)),
+            pltpu.SemaphoreType.DMA((6, 2, count, 3)),
+            pltpu.SemaphoreType.DMA((6, 2, count, 3)),
         ]
     small_shape = (SMALL_ROWS + 2 * HIST, 128)
     scratch += [
@@ -1783,27 +1844,33 @@
     tokens = stream_in.shape[0] * 4 * nb
     grad_scale = float(tokens) ** -0.5
 
-    def to_compute(array):
+    def send_rows(array):
+        return swap_sections(jnp.where(low_half, array[..., span:, :], array[..., :span, :]))
+
+    def join_rows(array, got):
         mine = jnp.where(low_half, array[..., :span, :], array[..., span:, :])
-        other = jnp.where(low_half, array[..., span:, :], array[..., :span, :])
-        got = swap_sections(other)
         return jnp.concatenate(
             [jnp.where(low_half, mine, got), jnp.where(low_half, got, mine)], axis=-2
         )
 
+    def to_compute(array):
+        return join_rows(array, send_rows(array))
+
     to_owner = to_compute
 
     block, ends = pack_weights(plan, place, params)
-    gather = gather_weights if nb == 8 else gather_blocks
-    att, mlp, ends = gather(plan, block, ends)
+    if nb == 8:
+        att, mlp, ends, past = gather_weights(plan, mix_weights, block, ends, history)
+    else:
+        att, mlp, ends = gather_blocks(plan, block, ends)
+        past = past_call(mix_weights, history)
     all_vecs = split_ends(plan, ends.reshape(4, nb, 32, 128))
     att_vecs, mlp_vecs = all_vecs[::2], all_vecs[1::2]
 
-    past = past_call(mix_weights, history)
     stream = to_compute(stream_in)
-    cot, past_one, past_two = to_compute(
-        jnp.concatenate([cotangent[None], past], axis=0)
-    )
+    moved_one = send_rows(past[0])
+    later_rows = jnp.stack([past[1], cotangent])
+    moved_two = send_rows(later_rows)
     row_index = jnp.concatenate([s + jnp.arange(span) for s in place.starts])
     position = jnp.where(place.kind == 1, row_index % SEQ_SHORT, row_index)
     place.turn = rotation(position)
@@ -1814,13 +1881,18 @@
     ).astype(jnp.int32)
     cosine, sine = place.turn
 
-    def forward(layer, x, past, extra):
+    def attend(layer, x):
         gain, bias, joint_b, out_b = att_vecs[layer]
         normed, q, kv = qkv_call(
             layer, x, gain, bias, att, joint_b, cosine, sine
         )
         kv_other = swap_cores(kv)
         mixed, lse = att_call(meta, q, kv, kv_other)
+        return x, normed, q, kv, kv_other, mixed, lse
+
+    def feed(layer, kept, past, extra):
+        x, mixed = kept[0], kept[5]
+        out_b = att_vecs[layer][3]
         gain, bias, up_b, down_b = mlp_vecs[layer]
         outs = mlp_call(
             layer,
@@ -1837,7 +1909,7 @@
             past,
             extra,
         )
-        return (x, normed, q, kv, kv_other, mixed, lse), outs
+        return outs
 
     def backward(layer, dy, kept, outs, carried, moved):
         x, normed, q, kv, kv_other, mixed, lse = kept
@@ -1855,9 +1927,16 @@
         vec_a = (sums_a[0], sums_a[1], djb[0], sums[3])
         return dx, moved, sums_a[2], vec_a, vec_m, (n_m, dpre, act, er, normed, dj, mixed, dh)
 
-    kept20, outs20 = forward(0, stream, past_one, ())
+    kept20 = attend(0, stream)
+    mixed, moved_one = lax.optimization_barrier((kept20[5], moved_one))
+    kept20 = kept20[:5] + (mixed, kept20[6])
+    outs20 = feed(0, kept20, join_rows(past[0], moved_one), ())
     y20, c20 = outs20[4:]
-    kept21, outs21 = forward(1, y20, past_two, (c20, cot))
+    kept21 = attend(1, y20)
+    mixed, moved_two = lax.optimization_barrier((kept21[5], moved_two))
+    kept21 = kept21[:5] + (mixed, kept21[6])
+    past_two, cot = join_rows(later_rows, moved_two)
+    outs21 = feed(1, kept21, past_two, (c20, cot))
     y21, sums21 = outs21[4:]
     mix41, mix42 = jnp.sum(sums21[0]), jnp.sum(sums21[1])
     dy20, stream_out, mix20, vec_a21, vec_m21, operands21 = backward(

time: 619 us -> 586 us (0.947)
  Pallas kernels: 495 us -> 462 us
    pallas_call x1, Pallas kernels: 197 us -> 175 us  [reduce_call(): pl.pallas_call(functools.partial(reduce_kernel, counts, scale), in_specs=...]
    pallas_call x2 -> x1, Pallas kernels: 144 us -> 133 us  [gather_weights(): pl.pallas_call(body, in_specs=[SMEM_SPEC] + [any_spec] * 3, out_specs=[an...]
    unnamed x158 -> x162, local copies, waits for them, and re-layouts: 39.9 us -> 46.5 us
  transfers between devices with their start and end apart: 13 -> 14, of which waited for: 2 -> 4; matrix products, arithmetic and copies ran while one was open for 5% -> 3% of each run, Pallas kernels for 31% -> 34%
where the time goes in v5:
time: 586 us; the launch traced here: 581 us
  Pallas kernels  462 us (79%)
  local copies, waits for them, and re-layouts  60.5 us (10%)
  other arithmetic  21.2 us (4%)
  starting transfers between devices  18.2 us (3%)
  waiting for transfers between devices  9.91 us (2%)
  between operations  8.53 us (1%)
    pallas_call x1, Pallas kernels, reduce_call(): pl.pallas_call(functools.partial(reduce_kernel, counts, scale), in_specs=...  175 us
    pallas_call x1, Pallas kernels, gather_weights(): pl.pallas_call(body, in_specs=[SMEM_SPEC] + [any_spec] * 3, out_specs=[an...  133 us
    unnamed x162, local copies, waits for them, and re-layouts  46.5 us
    pallas_call x2, Pallas kernels, att_back_call(): call(att_back_kernel, 'attention_grad_rows', (pairs,), [SMEM_SPEC, pair_s...  38.4 us
    pallas_call x2, Pallas kernels, att_call(): call(att_kernel, 'attention_rows', (pairs,), [SMEM_SPEC, pair_spec(rows),...  25.5 us
    pallas_call x2, Pallas kernels, mlp_call(): call(functools.partial(mlp_kernel, last_layer), 'feed_forward_rows', (FF...  23.1 us
    pallas_call x2, Pallas kernels, mlp_back_call(): call(functools.partial(mlp_back_kernel, last_layer), 'feed_forward_grad_r...  22.5 us
    pallas_call x2, Pallas kernels, qkv_call(): call(qkv_kernel, 'qkv_rows', (6,), [whole_spec((rows, D)), row_spec(D), r...  14.6 us
  transfers between devices with their start and end apart: 14, of which 4 were waited for; matrix products, arithmetic and copies ran while one was open for 3% of the time, Pallas kernels for 34%

profile of v5, /device:TPU:0, one launch (start us, length us, event | category | flops | bytes accessed | tf_op | source)
XLA Modules:
  0.0 580.5 jit_solution(985138309242617070)
XLA Ops:
  1.5 4.8 collective-permute-start
  6.3 1.3 collective-permute-start.1
  7.7 2.1 broadcast_select_fusion.19
  10.4 1.3 dynamic_slice.16
  16.3 1.3 fusion.45
  21.5 2.2 pack_weights.1.block_ref
  23.8 5.5 copy-done.35
  29.2 133.0 %gather_weights.1 = (bf16[2,4,768,768]{3,2,1,0:T(8,128)(2,1)S(1)}, bf16[2,8,768,768]{3,2,1,0:T(8,128)(2,1)}, bf16[32,32,128]{2,1,0:T(8,128)(2,1)S(1)}, bf16[2,512,768]{2,1,0:T(8,128)(2,1)S(1)}) custom-call(f32[43]{0:T(128)S(1)} %copy-done.33, bf16[768,768]{1,0:T(8,128)(2,1)S(1)} %pack_weights.1.block_ref, bf16[32,128]{1,0:T(8,128)(2,1)S(1)} %pad_maximum_fusion.12.vec_ref, ...), custom_call_target="tpu_custom_call" | custom-call | flops 99999997952 | bytes 100000000 | tf_op jit(solution)/shard_map/gather_weights/pallas_call | solution.py:343
  162.2 3.6 copy-done
  168.6 3.7 copy-done.1
  172.3 7.2 %qkv_rows.2 = (bf16[512,768]{1,0:T(8,128)(2,1)S(1)}, bf16[512,768]{1,0:T(8,128)(2,1)S(1)}, bf16[512,1536]{1,0:T(8,128)(2,1)S(1)}) custom-call(bf16[512,768]{1,0:T(8,128)(2,1)S(1)} %pad_maximum_fusion.2.x_ref, f32[1,768]{1,0:T(1,128)S(1)} %get-tuple-element.294.gain_ref, f32[1,768]{1,0:T(1,128)S(1)} %get-tuple-element.295.bias_ref, ...), custom_call_target="tpu_custom_call" | custom-call | flops 1811939328 | bytes 2359296 | tf_op jit(solution)/shard_map/qkv_rows/pallas_call | solution.py:457
  182.7 1.3 collective-permute-done.3.ko_ref.vo_ref
  183.9 12.7 %attention_rows.2 = (bf16[512,768]{1,0:T(8,128)(2,1)S(1)}, f32[6,512,128]{2,1,0:T(8,128)S(1)}) custom-call(s32[4]{0:T(128)S(1)} %pad_add_fusion.2.meta_ref, bf16[512,768]{1,0:T(8,128)(2,1)S(1)} %get-tuple-element.141.q_ref, bf16[512,1536]{1,0:T(8,128)(2,1)S(1)} %get-tuple-element.142.k_ref.v_ref, bf16[512,1536]{1,0:T(8,128)(2,1)S(1)} %get-tuple-element.142.k_ref.v_ref, ...), custom_call_target="tpu_custom_call" | custom-call | flops 4026531840 | bytes 2359296 | tf_op jit(solution)/shard_map/attention_rows/pallas_call | solution.py:571
  198.2 11.3 %feed_forward_rows.2 = (bf16[512,768]{1,0:T(8,128)(2,1)S(1)}, bf16[512,768]{1,0:T(8,128)(2,1)S(1)}, bf16[512,3072]{1,0:T(8,128)(2,1)S(1)}, bf16[512,3072]{1,0:T(...) custom-call(f32[4]{0:T(128)S(1)} %pad_maximum_fusion.13.mix_ref, ...), custom_call_target="tpu_custom_call" | custom-call | flops 5435817984 | bytes 2359296 | tf_op jit(solution)/shard_map/feed_forward_rows/pallas_call | solution.py:665
  209.4 1.6 copy-done.36
  211.9 7.4 %qkv_rows.3 = (bf16[512,768]{1,0:T(8,128)(2,1)S(1)}, bf16[512,768]{1,0:T(8,128)(2,1)S(1)}, bf16[512,1536]{1,0:T(8,128)(2,1)S(1)}) custom-call(bf16[512,768]{1,0:T(8,128)(2,1)S(1)} %get-tuple-element.147.x_ref.dy_ref, f32[1,768]{1,0:T(1,128)S(1)} %get-tuple-element.299.gain_ref, f32[1,768]{1,0:T(1,128)S(1)} %get-tuple-element.300.bias_ref, ...), custom_call_target="tpu_custom_call" | custom-call | flops 1811939328 | bytes 2359296 | tf_op jit(solution)/shard_map/qkv_rows/pallas_call | solution.py:457
  220.7 1.3 copy-done.10
  223.7 12.7 %attention_rows.3 = (bf16[512,768]{1,0:T(8,128)(2,1)S(1)}, f32[6,512,128]{2,1,0:T(8,128)S(1)}) custom-call(s32[4]{0:T(128)S(1)} %pad_add_fusion.2.meta_ref, bf16[512,768]{1,0:T(8,128)(2,1)S(1)} %get-tuple-element.148.q_ref, bf16[512,1536]{1,0:T(8,128)(2,1)S(1)} %get-tuple-element.149.k_ref.v_ref, bf16[512,1536]{1,0:T(8,128)(2,1)S(1)} %get-tuple-element.149.k_ref.v_ref, ...), custom_call_target="tpu_custom_call" | custom-call | flops 4026531840 | bytes 2359296 | tf_op jit(solution)/shard_map/attention_rows/pallas_call | solution.py:571
  236.5 5.1 collective-permute-done.6
  242.1 11.9 %feed_forward_rows.3 = (bf16[512,768]{1,0:T(8,128)(2,1)S(1)}, bf16[512,768]{1,0:T(8,128)(2,1)S(1)}, bf16[512,3072]{1,0:T(8,128)(2,1)S(1)}, bf16[512,3072]{1,0:T(...) custom-call(f32[4]{0:T(128)S(1)} %pad_maximum_fusion.13.mix_ref, ...), custom_call_target="tpu_custom_call" | custom-call | flops 5435817984 | bytes 2359296 | tf_op jit(solution)/shard_map/feed_forward_rows/pallas_call | solution.py:665
  256.0 11.2 %feed_forward_grad_rows.2 = (bf16[512,768]{1,0:T(8,128)(2,1)S(1)}, bf16[512,3072]{1,0:T(8,128)(2,1)S(1)}, f32[1,3072]{1,0:T(1,128)S(1)}, bf16[512,768]{1,0:T(8,1...) custom-call(f32[4]{0:T(128)S(1)} %pad_maximum_fusion.13.mix_ref, ...), custom_call_target="tpu_custom_call" | custom-call | flops 5435817984 | bytes 2359296 | tf_op jit(solution)/shard_map/feed_forward_grad_rows/pallas_call | solution.py:773
  267.2 1.6 copy-done.38
  274.9 1.4 copy-done.65
  276.3 18.9 %attention_grad_rows.2 = (bf16[512,768]{1,0:T(8,128)(2,1)S(1)}, f32[2,512,768]{2,1,0:T(8,128)S(1)}, bf16[2,512,768]{2,1,0:T(8,128)(2,1)S(1)}) custom-call(s32[4]{0:T(128)S(1)} %pad_add_fusion.2.meta_ref, bf16[512,768]{1,0:T(8,128)(2,1)S(1)} %copy-done.59, bf16[512,1536]{1,0:T(8,128)(2,1)S(1)} %copy-done.47, bf16[512,1536]{1,0:T(8,128)(2,1)S(1)} %copy-done.47, ...), custom_call_target="tpu_custom_call" | custom-call | flops 10066329600 | bytes 2359296 | tf_op jit(solution)/shard_map/attention_grad_rows/pallas_call | solution.py:888
  295.5 3.2 collective-permute-done.8.got_ref
  298.7 5.9 %qkv_grad_rows.2 = (bf16[512,2304]{1,0:T(8,128)(2,1)S(1)}, f32[1,2304]{1,0:T(1,128)S(1)}, bf16[512,768]{1,0:T(8,128)(2,1)S(1)}, f32[8,768]{1,0:T(8,128)S(1)}) custom-call(bf16[512,768]{1,0:T(8,128)(2,1)S(1)} %get-tuple-element.161.dq_ref, f32[2,512,768]{2,1,0:T(8,128)S(1)} %get-tuple-element.162.own_ref, ...), custom_call_target="tpu_custom_call" | custom-call | flops 1811939328 | bytes 2359296 | tf_op jit(solution)/shard_map/qkv_grad_rows/pallas_call | solution.py:972
  304.6 1.4 copy-done.40
  307.2 11.3 %feed_forward_grad_rows.3 = (bf16[512,768]{1,0:T(8,128)(2,1)S(1)}, bf16[512,3072]{1,0:T(8,128)(2,1)S(1)}, f32[1,3072]{1,0:T(1,128)S(1)}, bf16[512,768]{1,0:T(8,1...) custom-call(f32[4]{0:T(128)S(1)} %pad_maximum_fusion.13.mix_ref, bf16[512,768]{1,0:T(8,128)(2,1)S(1)} %copy-done.3, ...), custom_call_target="tpu_custom_call" | custom-call | flops 5435817984 | bytes 2359296 | tf_op jit(solution)/shard_map/feed_forward_grad_rows/pallas_call | solution.py:773
  318.5 1.6 copy-done.39
  322.8 19.4 %attention_grad_rows.3 = (bf16[512,768]{1,0:T(8,128)(2,1)S(1)}, f32[2,512,768]{2,1,0:T(8,128)S(1)}, bf16[2,512,768]{2,1,0:T(8,128)(2,1)}) custom-call(s32[4]{0:T(128)S(1)} %pad_add_fusion.2.meta_ref, bf16[512,768]{1,0:T(8,128)(2,1)S(1)} %copy-done.57, bf16[512,1536]{1,0:T(8,128)(2,1)S(1)} %copy-done.43, bf16[512,1536]{1,0:T(8,128)(2,1)S(1)} %copy-done.43, ...), custom_call_target="tpu_custom_call" | custom-call | flops 10066329600 | bytes 2359296 | tf_op jit(solution)/shard_map/attention_grad_rows/pallas_call | solution.py:888
  342.2 1.7 copy-done.21
  348.9 1.4 slice_reduce_fusion.1
  351.8 8.7 %history_grads.1 = bf16[20,512,768]{2,1,0:T(8,128)(2,1)} custom-call(f32[43]{0:T(128)S(1)} %copy-done.33, bf16[512,768]{1,0:T(8,128)(2,1)S(1)} %pad_maximum_fusion.5.dy_ref, bf16[512,768]{1,0:T(8,128)(2,1)S(1)} %copy-done.11), custom_call_target="tpu_custom_call" | custom-call | flops 31457280 | bytes 2359296 | tf_op jit(solution)/shard_map/history_grads/pallas_call | solution.py:1174
  360.6 1.5 copy-done.22
  362.4 7.4 %qkv_grad_rows.3 = (bf16[512,2304]{1,0:T(8,128)(2,1)S(1)}, f32[1,2304]{1,0:T(1,128)S(1)}, bf16[512,768]{1,0:T(8,128)(2,1)S(1)}, f32[8,768]{1,0:T(8,128)S(1)}) custom-call(bf16[512,768]{1,0:T(8,128)(2,1)S(1)} %copy-done.29, f32[2,512,768]{2,1,0:T(8,128)S(1)} %copy-done.22, bf16[2,512,768]{2,1,0:T(8,128)(2,1)} %collective-permute-done.10.got_ref, ...), custom_call_target="tpu_custom_call" | custom-call | flops 1811939328 | bytes 2359296 | tf_op jit(solution)/shard_map/qkv_grad_rows/pallas_call | solution.py:972
  369.9 1.4 copy-done.41
  371.4 2.7 concatenate.170
  374.1 174.9 %reduce_gradients.1 = (bf16[768,768]{1,0:T(8,128)(2,1)}, f32[216,128]{1,0:T(8,128)}) custom-call(f32[176,128]{1,0:T(8,128)} %bitcast.160, bf16[20,512,768]{2,1,0:T(8,128)(2,1)} %hist_ref.3, bf16[512,768]{1,0:T(8,128)(2,1)} %copy-done.18, bf16[512,768]{1,0:T(8,128)(2,1)} %cot_ref.3, bf16[512,768]{1,0:T(8,128)(2,1)} %copy-done.51, ...), custom_call_target="tpu_custom_call" | custom-call | flops 99999997952 | bytes 100000000 | tf_op jit(solution)/shard_map/reduce_gradients/pallas_call | solution.py:1766
  553.1 1.4 convert_element_type.258
  556.2 1.3 collective-permute-start.13
  557.6 4.7 collective-permute-start.12
  562.3 3.0 select_select_fusion.tile_ref
  565.3 1.3 multiply_add_fusion
  567.0 1.7 copy-done.6
  568.6 1.7 copy-done.23
  570.3 1.7 copy-done.24
  572.0 6.0 %adamw_step.1 = (f32[1,590496]{1,0:T(1,128)}, f32[1,590496]{1,0:T(1,128)}, f32[1,590496]{1,0:T(1,128)}, f32[1,590496]{1,0:T(1,128)}) custom-call(s32[3]{0:T(128)S(1)} %pad_add_fusion.3.meta_ref, f32[768,768]{1,0:T(8,128)S(1)} %copy-done.6, f32[6,768]{1,0:T(8,128)S(1)} %fusion.9.before_ref, f32[6,768]{1,0:T(8,128)S(1)} %fusion.6.after_ref, ...), custom_call_target="tpu_custom_call" | custom-call | flops 11809920 | bytes 2359296 | tf_op jit(solution)/shard_map/adamw_step/pallas_call | solution.py:1224
  579.0 1.3 maximum_convert_fusion
  (248 shorter events, 41.3 us)
Async XLA Ops:
  1.5 20.0 %collective-permute-start = (bf16[16,128]{1,0:T(8,128)(2,1)S(1)}, bf16[16,128]{1,0:T(8,128)(2,1)S(1)}, u32[]{:S(2)}, u32[]{:S(2)}) collective-permute-start(bf16[16,128]{1,0:T(8,128)(2,1)S(1)} %bitcast.161), channel_id=1, source_target_pairs={{0,1},{1,2},{2,3},{3,4},{4,5},{5,6},{6,7},{8,9},{9,10},{10,11},{11... | collective-permute-start | bytes 12296 | tf_op jit(solution)/shard_map/ppermute | solution.py:1101
  6.3 15.1 %collective-permute-start.1 = (bf16[16,128]{1,0:T(8,128)(2,1)S(1)}, bf16[16,128]{1,0:T(8,128)(2,1)S(1)}, u32[]{:S(2)}, u32[]{:S(2)}) collective-permute-start(bf16[16,128]{1,0:T(8,128)(2,1)S(1)} %bitcast.163), channel_id=1, source_target_pairs={{1,0},{2,1},{3,2},{4,3},{5,4},{6,5},{7,6},{9,8},{10,9},{11,10},{12... | collective-permute-start | bytes 12296 | tf_op jit(solution)/shard_map/ppermute | solution.py:1102
  7.6 13.8 %copy-start.4 = (f32[1,590496]{1,0:T(1,128)S(1)}, f32[1,590496]{1,0:T(1,128)}, u32[]{:S(2)}) copy-start(f32[1,590496]{1,0:T(1,128)} %p_ref.3) | copy-start | bytes 7085956
  9.7 156.9 %collective-permute-start.2 = (bf16[256,768]{1,0:T(8,128)(2,1)}, bf16[256,768]{1,0:T(8,128)(2,1)}, u32[]{:S(2)}, u32[]{:S(2)}) collective-permute-start(bf16[256,768]{1,0:T(8,128)(2,1)} %broadcast_select_fusion.19), channel_id=1, source_target_pairs={{0,24},{8,16},{16,8},{24,0},{1,25},{9,17},{17,9},{25,1},{2,26},{10... | collective-permute-start | bytes 1179656 | tf_op jit(solution)/shard_map/ppermute | solution.py:54
  20.6 148.1 %copy-start.12 = (f32[512,128]{1,0:T(8,128)}, f32[512,128]{1,0:T(8,128)S(1)}, u32[]{:S(2)}) copy-start(f32[512,128]{1,0:T(8,128)S(1)} %pad_maximum_fusion.7.sin_ref) | copy-start | bytes 786436
  165.8 15.2 %copy-start.16 = (bf16[2,512,768]{2,1,0:T(8,128)(2,1)}, bf16[2,512,768]{2,1,0:T(8,128)(2,1)S(1)}, u32[]{:S(2)}) copy-start(bf16[2,512,768]{2,1,0:T(8,128)(2,1)S(1)} %get-tuple-element.138) | copy-start | bytes 4718596
  180.4 16.3 %copy-start.42 = (bf16[512,1536]{1,0:T(8,128)(2,1)}, bf16[512,1536]{1,0:T(8,128)(2,1)S(1)}, u32[]{:S(2)}) copy-start(bf16[512,1536]{1,0:T(8,128)(2,1)S(1)} %get-tuple-element.142.k_ref.v_ref) | copy-start | bytes 4718596
  180.4 16.3 %copy-start.56 = (bf16[512,768]{1,0:T(8,128)(2,1)}, bf16[512,768]{1,0:T(8,128)(2,1)S(1)}, u32[]{:S(2)}) copy-start(bf16[512,768]{1,0:T(8,128)(2,1)S(1)} %get-tuple-element.141.q_ref) | copy-start | bytes 2359300
  180.4 3.5 collective-permute-start.3
  181.0 15.7 %collective-permute-start.4 = (bf16[256,768]{1,0:T(8,128)(2,1)S(1)}, bf16[256,768]{1,0:T(8,128)(2,1)S(1)}, u32[]{:S(2)}, u32[]{:S(2)}) collective-permute-start(bf16[256,768]{1,0:T(8,128)(2,1)S(1)} %select_bitcast_fusion), channel_id=1, source_target_pairs={{0,24},{8,16},{16,8},{24,0},{1,25},{9,17},{17,9},{25,1},{2,26},{10... | collective-permute-start | bytes 1179656 | tf_op jit(solution)/shard_map/ppermute | solution.py:54
  183.9 12.8 %copy-start.44 = (bf16[512,1536]{1,0:T(8,128)(2,1)}, bf16[512,1536]{1,0:T(8,128)(2,1)S(1)}, u32[]{:S(2)}) copy-start(bf16[512,1536]{1,0:T(8,128)(2,1)S(1)} %collective-permute-done.3.ko_ref.vo_ref) | copy-start | bytes 4718596
  183.9 14.2 %slice-start = ((s8[9437184]{0:T(1024)(128)(4,1)}), s8[4194304]{0:T(1024)(128)(4,1)S(1)}, s32[]{:S(2)}) async-start(s8[9437184]{0:T(1024)(128)(4,1)} %bitcast.140), calls=%async_computation | async-start | bytes 8388608
  183.9 12.8 %copy-start.17 = (bf16[2,512,768]{2,1,0:T(8,128)(2,1)S(1)}, bf16[2,512,768]{2,1,0:T(8,128)(2,1)}, u32[]{:S(2)}) copy-start(bf16[2,512,768]{2,1,0:T(8,128)(2,1)} %copy-done.16) | copy-start | bytes 4718596
  183.9 14.2 %slice-start.1 = ((s8[9437184]{0:T(1024)(128)(4,1)}), s8[4194304]{0:T(1024)(128)(4,1)S(1)}, s32[]{:S(2)}) async-start(s8[9437184]{0:T(1024)(128)(4,1)} %bitcast.140), calls=%async_computation.1 | async-start | bytes 8388608
  183.9 14.2 %slice-start.2 = ((s8[9437184]{0:T(1024)(128)(4,1)}), s8[1048576]{0:T(1024)(128)(4,1)S(1)}, s32[]{:S(2)}) async-start(s8[9437184]{0:T(1024)(128)(4,1)} %bitcast.140), calls=%async_computation.2 | async-start | bytes 2097152
  198.2 13.8 %copy-start.13 = (f32[512,128]{1,0:T(8,128)S(1)}, f32[512,128]{1,0:T(8,128)}, u32[]{:S(2)}) copy-start(f32[512,128]{1,0:T(8,128)} %copy-done.12) | copy-start | bytes 786436
  211.9 30.2 %copy-start.7 = (bf16[512,768]{1,0:T(8,128)(2,1)}, bf16[512,768]{1,0:T(8,128)(2,1)S(1)}, u32[]{:S(2)}) copy-start(bf16[512,768]{1,0:T(8,128)(2,1)S(1)} %get-tuple-element.153.rest_0_.c_ref) | copy-start | bytes 2359300
  220.3 3.4 collective-permute-start.5
  222.1 19.5 %collective-permute-start.6 = (bf16[2,256,768]{2,1,0:T(8,128)(2,1)S(1)}, bf16[2,256,768]{2,1,0:T(8,128)(2,1)S(1)}, u32[]{:S(2)}, u32[]{:S(2)}) collective-permute-start(bf16[2,256,768]{2,1,0:T(8,128)(2,1)S(1)} %broadcast_select_fusion.2), channel_id=1, source_target_pairs={{0,24},{8,16},{16,8},{24,0},{1,25},{9,17},{17,9},{25,1},{2,26},{10... | collective-permute-start | bytes 2359304 | tf_op jit(solution)/shard_map/ppermute | solution.py:54
  223.7 12.7 %copy-start.48 = (bf16[512,1536]{1,0:T(8,128)(2,1)}, bf16[512,1536]{1,0:T(8,128)(2,1)S(1)}, u32[]{:S(2)}) copy-start(bf16[512,1536]{1,0:T(8,128)(2,1)S(1)} %collective-permute-done.5.ko_ref.vo_ref) | copy-start | bytes 4718596
  236.4 34.5 %copy-start.32 = (bf16[512,768]{1,0:T(8,128)(2,1)}, bf16[512,768]{1,0:T(8,128)(2,1)S(1)}, u32[]{:S(2)}) copy-start(bf16[512,768]{1,0:T(8,128)(2,1)S(1)} %get-tuple-element.152.o_ref.refs_14_) | copy-start | bytes 2359300
  242.1 13.9 %copy-start.2 = (bf16[512,768]{1,0:T(8,128)(2,1)}, bf16[512,768]{1,0:T(8,128)(2,1)S(1)}, u32[]{:S(2)}) copy-start(bf16[512,768]{1,0:T(8,128)(2,1)S(1)} %get-tuple-element.236.rest_1_.cot_ref) | copy-start | bytes 2359300
  254.9 12.4 %copy-start.37 = (bf16[512,3072]{1,0:T(8,128)(2,1)}, bf16[512,3072]{1,0:T(8,128)(2,1)S(1)}, u32[]{:S(2)}) copy-start(bf16[512,3072]{1,0:T(8,128)(2,1)S(1)} %get-tuple-element.194.refs_10_) | copy-start | bytes 9437188
  254.9 14.9 %collective-permute-start.7 = (bf16[256,768]{1,0:T(8,128)(2,1)S(1)}, bf16[256,768]{1,0:T(8,128)(2,1)S(1)}, u32[]{:S(2)}, u32[]{:S(2)}) collective-permute-start(bf16[256,768]{1,0:T(8,128)(2,1)S(1)} %broadcast_select_fusion.15), channel_id=1, source_target_pairs={{0,24},{8,16},{16,8},{24,0},{1,25},{9,17},{17,9},{25,1},{2,26},{10... | collective-permute-start | bytes 1179656 | tf_op jit(solution)/shard_map/ppermute | solution.py:54
  269.8 28.9 %copy-start.25 = (bf16[512,768]{1,0:T(8,128)(2,1)}, bf16[512,768]{1,0:T(8,128)(2,1)S(1)}, u32[]{:S(2)}) copy-start(bf16[512,768]{1,0:T(8,128)(2,1)S(1)} %get-tuple-element.164.dh_ref.refs_15_) | copy-start | bytes 2359300
  276.3 22.4 %copy-start.8 = (bf16[512,768]{1,0:T(8,128)(2,1)S(1)}, bf16[512,768]{1,0:T(8,128)(2,1)}, u32[]{:S(2)}) copy-start(bf16[512,768]{1,0:T(8,128)(2,1)} %copy-done.7) | copy-start | bytes 2359300
  295.2 3.5 collective-permute-start.8
  306.1 14.1 %collective-permute-start.9 = (bf16[256,768]{1,0:T(8,128)(2,1)S(1)}, bf16[256,768]{1,0:T(8,128)(2,1)S(1)}, u32[]{:S(2)}, u32[]{:S(2)}) collective-permute-start(bf16[256,768]{1,0:T(8,128)(2,1)S(1)} %broadcast_select_fusion.11), channel_id=1, source_target_pairs={{0,24},{8,16},{16,8},{24,0},{1,25},{9,17},{17,9},{25,1},{2,26},{10... | collective-permute-start | bytes 1179656 | tf_op jit(solution)/shard_map/ppermute | solution.py:54
  307.2 14.1 %copy-start.45 = (bf16[512,1536]{1,0:T(8,128)(2,1)S(1)}, bf16[512,1536]{1,0:T(8,128)(2,1)}, u32[]{:S(2)}) copy-start(bf16[512,1536]{1,0:T(8,128)(2,1)} %copy-done.44) | copy-start | bytes 4718596
  307.2 14.1 %copy-start.63 = (f32[6,512,128]{2,1,0:T(8,128)S(1)}, f32[6,512,128]{2,1,0:T(8,128)}, u32[]{:S(2)}) copy-start(f32[6,512,128]{2,1,0:T(8,128)} %copy-done.62) | copy-start | bytes 4718596
  321.3 30.5 %copy-start.18 = (bf16[512,768]{1,0:T(8,128)(2,1)}, bf16[512,768]{1,0:T(8,128)(2,1)S(1)}, u32[]{:S(2)}) copy-start(bf16[512,768]{1,0:T(8,128)(2,1)S(1)} %pad_maximum_fusion.5.dy_ref) | copy-start | bytes 2359300
  322.8 22.3 %copy-start.74 = (s32[2,8]{1,0:T(2,128)S(1)}, s32[2,8]{1,0:T(2,128)}, u32[]{:S(2)}) copy-start(s32[2,8]{1,0:T(2,128)} %constant.246.clone) | copy-start | bytes 196
  322.8 28.9 %copy-start.11 = (bf16[512,768]{1,0:T(8,128)(2,1)S(1)}, bf16[512,768]{1,0:T(8,128)(2,1)}, u32[]{:S(2)}) copy-start(bf16[512,768]{1,0:T(8,128)(2,1)} %cot_ref.3) | copy-start | bytes 2359300
  344.8 15.8 %collective-permute-start.10 = (bf16[2,512,768]{2,1,0:T(8,128)(2,1)}, bf16[2,512,768]{2,1,0:T(8,128)(2,1)}, u32[]{:S(2)}, u32[]{:S(2)}) collective-permute-start(bf16[2,512,768]{2,1,0:T(8,128)(2,1)} %get-tuple-element.173), channel_id=1, source_target_pairs={{0,8},{8,0},{16,24},{24,16},{1,9},{9,1},{17,25},{25,17},{2,10},{10... | collective-permute-start | bytes 4718600 | tf_op jit(solution)/shard_map/ppermute | solution.py:58
  351.7 8.8 %slice-start.3 = ((s8[9437184]{0:T(1024)(128)(4,1)}), s8[4194304]{0:T(1024)(128)(4,1)S(1)}, s32[]{:S(2)}) async-start(s8[9437184]{0:T(1024)(128)(4,1)} %bitcast.144), calls=%async_computation.3 | async-start | bytes 8388608
  351.8 8.8 %slice-start.4 = ((s8[9437184]{0:T(1024)(128)(4,1)}), s8[4194304]{0:T(1024)(128)(4,1)S(1)}, s32[]{:S(2)}) async-start(s8[9437184]{0:T(1024)(128)(4,1)} %bitcast.144), calls=%async_computation.4 | async-start | bytes 8388608
  351.8 8.8 %slice-start.5 = ((s8[9437184]{0:T(1024)(128)(4,1)}), s8[1048576]{0:T(1024)(128)(4,1)S(1)}, s32[]{:S(2)}) async-start(s8[9437184]{0:T(1024)(128)(4,1)} %bitcast.144), calls=%async_computation.5 | async-start | bytes 2097152
  351.8 8.8 %copy-start.9 = (bf16[512,768]{1,0:T(8,128)(2,1)S(1)}, bf16[512,768]{1,0:T(8,128)(2,1)}, u32[]{:S(2)}) copy-start(bf16[512,768]{1,0:T(8,128)(2,1)} %copy-done.7) | copy-start | bytes 2359300
  351.8 10.3 %copy-start.22 = (f32[2,512,768]{2,1,0:T(8,128)S(1)}, f32[2,512,768]{2,1,0:T(8,128)}, u32[]{:S(2)}) copy-start(f32[2,512,768]{2,1,0:T(8,128)} %copy-done.21) | copy-start | bytes 9437188
  351.8 10.4 %copy-start.27 = (bf16[512,768]{1,0:T(8,128)(2,1)S(1)}, bf16[512,768]{1,0:T(8,128)(2,1)}, u32[]{:S(2)}) copy-start(bf16[512,768]{1,0:T(8,128)(2,1)} %copy-done.26) | copy-start | bytes 2359300
  351.8 10.6 %copy-start.29 = (bf16[512,768]{1,0:T(8,128)(2,1)S(1)}, bf16[512,768]{1,0:T(8,128)(2,1)}, u32[]{:S(2)}) copy-start(bf16[512,768]{1,0:T(8,128)(2,1)} %copy-done.28) | copy-start | bytes 2359300
  362.4 9.0 %copy-start.68 = (f32[768]{0:T(1024)S(1)}, f32[768]{0:T(1024)}, u32[]{:S(2)}) copy-start(f32[768]{0:T(1024)} %get-tuple-element.214) | copy-start | bytes 9220
  362.4 9.0 %copy-start.69 = (f32[768]{0:T(1024)S(1)}, f32[768]{0:T(1024)}, u32[]{:S(2)}) copy-start(f32[768]{0:T(1024)} %get-tuple-element.209) | copy-start | bytes 9220
  362.4 9.0 %copy-start.70 = (f32[768]{0:T(1024)S(1)}, f32[768]{0:T(1024)}, u32[]{:S(2)}) copy-start(f32[768]{0:T(1024)} %get-tuple-element.210) | copy-start | bytes 9220
  556.1 21.8 %collective-permute-start.11 = (bf16[256,768]{1,0:T(8,128)(2,1)}, bf16[256,768]{1,0:T(8,128)(2,1)}, u32[]{:S(2)}, u32[]{:S(2)}) collective-permute-start(bf16[256,768]{1,0:T(8,128)(2,1)} %broadcast_select_fusion.7), channel_id=1, source_target_pairs={{0,24},{8,16},{16,8},{24,0},{1,25},{9,17},{17,9},{25,1},{2,26},{10... | collective-permute-start | bytes 1179656 | tf_op jit(solution)/shard_map/ppermute | solution.py:54
  556.2 10.6 %collective-permute-start.13 = (f32[3,768]{1,0:T(4,128)S(1)}, f32[3,768]{1,0:T(4,128)S(1)}, u32[]{:S(2)}, u32[]{:S(2)}) collective-permute-start(f32[3,768]{1,0:T(4,128)S(1)} %fusion.18), channel_id=1, source_target_pairs={{1,0},{2,1},{3,2},{4,3},{5,4},{6,5},{7,6},{9,8},{10,9},{11,10},{12... | collective-permute-start | bytes 27656 | tf_op jit(solution)/shard_map/ppermute | solution.py:1261
  557.6 9.4 %copy-start.5 = (f32[1,590496]{1,0:T(1,128)S(1)}, f32[1,590496]{1,0:T(1,128)}, u32[]{:S(2)}) copy-start(f32[1,590496]{1,0:T(1,128)} %p_ref.3) | copy-start | bytes 7085956
  557.6 9.3 %collective-permute-start.12 = (f32[3,768]{1,0:T(4,128)S(1)}, f32[3,768]{1,0:T(4,128)S(1)}, u32[]{:S(2)}, u32[]{:S(2)}) collective-permute-start(f32[3,768]{1,0:T(4,128)S(1)} %fusion.21), channel_id=1, source_target_pairs={{0,1},{1,2},{2,3},{3,4},{4,5},{5,6},{6,7},{8,9},{9,10},{10,11},{11... | collective-permute-start | bytes 27656 | tf_op jit(solution)/shard_map/ppermute | solution.py:1260
  (47 other events, 123.6 us)

commit v6 on v5

--- a/solution.py
+++ b/solution.py
@@ -118,9 +118,18 @@
 HIST_CHUNK = 16
 
 
-def gather_kernel(plan, w_ref, block_ref, vec_ref, hist_ref, *refs):
-    att_ref, mlp_ref, vecs_ref, past_ref = refs[:4]
-    att_in, mlp_in, att_core, mlp_core, first_in, vec_in, vec_out, sent, kept, hin, hist_sem = refs[4:]
+def lane_sums(sums):
+    rows = jnp.sum(sums[...], axis=1)
+    total = rows[:, :128]
+    for at in range(128, D, 128):
+        total = total + rows[:, at : at + 128]
+    return total
+
+
+def gather_kernel(plan, w_ref, block_ref, vec_ref, hist_ref, cot_ref, *refs):
+    att_out, mlp_ref, vecs_ref, past_ref, lanes_ref = refs[:5]
+    att_in, mlp_in, att_core, mlp_core, first_in, vec_in, vec_out, sent, kept = refs[5:14]
+    hin, hist_sem, sums, att_ref, out_sem = refs[14:]
     section, b = lax.axis_index("section"), lax.axis_index("batch")
     plane, core = section // 2, section % 2
     z, x = b // 2, b % 2
@@ -138,6 +147,7 @@
         rows = pl.ds(pl.multiple_of(i * HIST_CHUNK, HIST_CHUNK), HIST_CHUNK)
         return pltpu.make_async_copy(hist_ref.at[:, rows], hin.at[slot], hist_sem.at[slot])
 
+    sums[...] = jnp.zeros_like(sums)
     history_in(0, 0).start()
     history_in(1, 1).start()
     pairs = [0]
@@ -150,9 +160,12 @@
             history_in(i, slot).wait()
             for at in range(0, D, 256):
                 columns = slice(at, at + 256)
+                cot = cot_ref[pl.ds(i * HIST_CHUNK, HIST_CHUNK), columns].astype(f32)
 
                 def body(j, totals):
                     row = hin[slot, j, :, columns].astype(f32)
+                    product = row * cot
+                    sums[j, :, columns] += product[:8] + product[8:]
                     return totals[0] + w_ref[j] * row, totals[1] + w_ref[HIST + 1 + j] * row
 
                 zero = jnp.zeros((HIST_CHUNK, 256), f32)
@@ -266,13 +279,14 @@
         column, owned, hops = kinds[k][3][step]
         got = kinds[k][1]
         t = 2 * column + x
-        src = part(k, plane, t)
-        if owned is False:
-            landed(cond, src, got.at[plane, t, 0])
-        for hop, to in hops:
-            remote(both(cond, hop), src, src, got.at[plane, t, 0], to)
-        remote(cond, src, src, got.at[plane, t, 0], to_x)
-        remote(cond, src, src, got.at[plane, t, 0], to_y)
+        for unit in range(2):
+            src = part(k, plane, t, unit)
+            if owned is False:
+                landed(cond, src, got.at[plane, t, unit])
+            for hop, to in hops:
+                remote(both(cond, hop), src, src, got.at[plane, t, unit], to)
+            remote(cond, src, src, got.at[plane, t, unit], to_x)
+            remote(cond, src, src, got.at[plane, t, unit], to_y)
         if owned is False:
             give(cond, k, plane, t)
         average()
@@ -280,11 +294,13 @@
     def corner(k, step):
         column, got = kinds[k][3][step][0], kinds[k][1]
         across, same = 2 * column + (1 - x), 2 * column + x
-        landed(True, part(k, plane, across), got.at[plane, across, 0])
         src = part(k, plane, across, 0)
+        landed(True, src, got.at[plane, across, 0])
         remote(True, src, src, got.at[plane, across, 0], to_y)
-        landed(True, part(k, far, same), got.at[far, same, 0])
+        landed(True, part(k, plane, across, 1), got.at[plane, across, 1])
+        landed(True, part(k, far, same, 0), got.at[far, same, 0])
         src = part(k, far, same, 1)
+        landed(True, src, got.at[far, same, 1])
         remote(True, src, src, got.at[far, same, 1], to_x)
         give(True, k, plane, across)
         give(True, k, far, same)
@@ -322,33 +338,40 @@
     last("m", 3)
     while pairs[0] < chunks // 2:
         average()
+    lanes_ref[...] = lane_sums(sums)
     for k, tiles, skip in (("a", nb // 2, has_att), ("m", nb, True)):
         for layer in range(2):
             for t in range(tiles):
                 other = pl.ds(pl.multiple_of(half * (1 - core), half), half)
                 cond = jnp.logical_not(both((plane == layer) & (b == t), skip))
                 landed(cond, kinds[k][0].at[layer, t, other], kinds[k][2].at[layer, t])
+            if k == "a":
+                pltpu.make_async_copy(att_ref.at[layer], att_out.at[layer], out_sem.at[layer]).start()
     for cond, copy in mine:
         when(cond, copy.wait_send)
+    for layer in range(2):
+        pltpu.make_async_copy(att_ref.at[layer], att_out.at[layer], out_sem.at[layer]).wait()
     each(lambda copy: copy.wait())
     here = pltpu.make_async_copy(vec_ref, vecs_ref.at[me], kept)
     here.start()
     here.wait()
 
 
-def gather_weights(plan, mix_weights, block, vecs, history):
+def gather_weights(plan, mix_weights, block, vecs, history, cotangent):
     nb, rows = plan.nb, plan.rows
     body = functools.partial(gather_kernel, plan)
     any_spec = pl.BlockSpec(memory_space=pltpu.HBM)
+    in_vmem = pl.BlockSpec(memory_space=pltpu.VMEM)
     return pl.pallas_call(
         body,
-        in_specs=[SMEM_SPEC] + [any_spec] * 3,
-        out_specs=[any_spec] * 3 + [pl.BlockSpec(memory_space=pltpu.VMEM)],
+        in_specs=[SMEM_SPEC] + [any_spec] * 3 + [in_vmem],
+        out_specs=[any_spec, any_spec, any_spec, in_vmem, in_vmem],
         out_shape=[
             jax.ShapeDtypeStruct((2, nb // 2, rows, D), bf16),
             jax.ShapeDtypeStruct((2, nb, rows, D), bf16),
             jax.ShapeDtypeStruct((4 * nb,) + vecs.shape, bf16),
             jax.ShapeDtypeStruct((2,) + history.shape[1:], bf16),
+            jax.ShapeDtypeStruct((HIST, 128), f32),
         ],
         scratch_shapes=[
             pltpu.SemaphoreType.DMA((2, nb // 2, 2)),
@@ -358,20 +381,24 @@
             pltpu.SemaphoreType.DMA((2,)),
             pltpu.SemaphoreType.DMA((4 * nb,)),
             pltpu.SemaphoreType.DMA((4 * nb,)),
-            pltpu.SemaphoreType.DMA((96,)),
+            pltpu.SemaphoreType.DMA((128,)),
             pltpu.SemaphoreType.DMA,
             pltpu.VMEM((2, HIST, HIST_CHUNK, D), bf16),
+            pltpu.SemaphoreType.DMA((2,)),
+            pltpu.VMEM((HIST, 8, D), f32),
+            pltpu.VMEM((2, nb // 2, rows, D), bf16),
             pltpu.SemaphoreType.DMA((2,)),
         ],
         name="gather_weights",
         cost_estimate=pl.CostEstimate(flops=10**11, bytes_accessed=10**8, transcendentals=0),
         compiler_params=pltpu.CompilerParams(
-            collective_id=0, has_side_effects=True, vmem_limit_bytes=16 * 1024 * 1024
+            collective_id=0, has_side_effects=True, vmem_limit_bytes=WIDE_LIMIT
         ),
-    )(mix_weights, block, vecs, history)
-
-
-VMEM_LIMIT = 32 * 1024 * 1024
+    )(mix_weights, block, vecs, history, cotangent)
+
+
+VMEM_LIMIT = 24 * 1024 * 1024
+WIDE_LIMIT = 56 * 1024 * 1024
 
 
 def row_spec(width):
@@ -385,7 +412,7 @@
 SMEM_SPEC = pl.BlockSpec(memory_space=pltpu.SMEM)
 
 
-def call(body, name, grid, in_specs, outs, scratch, flops):
+def call(body, name, grid, in_specs, outs, scratch, flops, limit=None):
     return pl.pallas_call(
         body,
         grid=grid,
@@ -397,7 +424,7 @@
         cost_estimate=pl.CostEstimate(
             flops=int(flops), bytes_accessed=4 * D * D, transcendentals=0
         ),
-        compiler_params=pltpu.CompilerParams(vmem_limit_bytes=VMEM_LIMIT),
+        compiler_params=pltpu.CompilerParams(vmem_limit_bytes=limit or VMEM_LIMIT),
     )
 
 
@@ -1237,6 +1264,7 @@
         [out] * 4,
         [pltpu.VMEM((steps * size + 2 * UNDER + 8, 128), f32)],
         20 * plan.shard,
+        WIDE_LIMIT,
     )(meta, tile, before, after, params, first, second)
 
 
@@ -1351,7 +1379,7 @@
 KEEP = SPLIT + SHARE
 
 
-def reduce_kernel(tile_count, scale, small_ref, hist_ref, dy_ref, cot_ref, *refs):
+def reduce_kernel(tile_count, small_ref, hist_ref, dy_ref, *refs):
     operands, refs = refs[:16], refs[16:]
     tile_ref, total_ref = refs[:2]
     refs = refs[2:]
@@ -1449,25 +1477,18 @@
         load_operands(index + 2)
         to = [jnp.where(core == h, layer, 2) for h in range(2)]
 
-        def body(i, carry):
-            columns = pl.ds(pl.multiple_of(i * 256, 256), 256)
-            result = dot_tn(left[slot], right[slot, :, columns]).astype(bf16)
+        for half in range(2):
+            result = dot_tn(left[slot, :, 384 * half : 384 * half + 384], right[slot]).astype(bf16)
             if name == "up":
-                for t in range(4):
+                for t in range(2):
                     row = pl.ds(192 * (j % 2), 192)
-                    store[to[j // 2], t, row, columns] = result[192 * t : 192 * t + 192]
+                    store[to[j // 2], 2 * half + t, row] = result[192 * t : 192 * t + 192]
             elif name == "joint":
-                for t in range(3):
-                    for h in range(2):
-                        at = 256 * t + 128 * h
-                        store[to[h], t, pl.ds(128 * j, 128), columns] = result[at : at + 128]
+                for i in range(3):
+                    t, h = divmod(3 * half + i, 2)
+                    store[to[h], t, pl.ds(128 * j, 128)] = result[128 * i : 128 * i + 128]
             else:
-                tile = 4 + j if name == "down" else 3
-                for h in range(2):
-                    store[to[h], tile, :, columns] = result[384 * h : 384 * h + 384]
-            return carry
-
-        lax.fori_loop(0, 3, body, 0)
+                store[to[half], 4 + j if name == "down" else 3] = result
 
     given = {}
 
@@ -1517,13 +1538,10 @@
             history_in(i, slot).wait()
             rows = pl.ds(i * HIST_CHUNK, HIST_CHUNK)
             dy = dy_ref[rows].astype(f32)
-            g = cot_ref[rows].astype(f32) * scale
 
             def body(j, carry):
-                row = hin[slot, j].astype(f32)
-                one, two = dy * row, g * row
-                sums[j] += one[:8] + one[8:]
-                sums[HIST + j] += two[:8] + two[8:]
+                product = dy * hin[slot, j].astype(f32)
+                sums[j] += product[:8] + product[8:]
                 return carry
 
             lax.fori_loop(0, HIST, body, 0)
@@ -1641,11 +1659,8 @@
     def stage_small(step):
         if step == 0:
             acc[0, :SMALL_ROWS] = small_ref[...]
-            lanes = jnp.sum(sums[...], axis=1)
-            total = lanes[:, :128]
-            for j in range(1, 6):
-                total = total + lanes[:, 128 * j : 128 * j + 128]
-            acc[0, SMALL_ROWS:] = total
+            acc[0, SMALL_ROWS : SMALL_ROWS + HIST] = lane_sums(sums)
+            acc[0, SMALL_ROWS + HIST :] = jnp.zeros((4, 128), f32)
         else:
             landed(part.at[step - 1], small_sem.at[1, step - 1])
             acc[step] = acc[step - 1] + part[step - 1]
@@ -1661,16 +1676,13 @@
         for p, columns in enumerate(parts(layer, k))
     ]
     later = {}
-    small_at = chunks // 2
-    for at in range(len(steps) + 8):
+    history_at = 2
+    small_at = history_at + chunks // 4
+    for at in range(max(len(steps) + 8, small_at + len(peers) + 1)):
         if at < len(steps) and steps[at][3] == 0:
             stage_product(*steps[at][:3])
         if 0 <= at - 1 < len(steps):
             stage_core(*steps[at - 1])
-        if at < chunks // 2:
-            stage_history(at)
-        if 0 <= at - small_at <= len(peers):
-            stage_small(at - small_at)
         if 0 <= at - 3 < len(steps):
             stage_plane(*steps[at - 3])
         if 0 <= at - 5 < len(steps):
@@ -1681,6 +1693,11 @@
                 later[at + 2] = (layer, k, p, columns)
         if at in later:
             stage_end(*later.pop(at))
+        for pair in range(chunks // 2):
+            if at == history_at + pair // 2:
+                stage_history(pair)
+        if 0 <= at - small_at <= len(peers):
+            stage_small(at - small_at)
     for item in later.values():
         stage_end(*item)
 
@@ -1729,7 +1746,7 @@
             pl.when(cond)(copy.wait_send)
 
 
-def reduce_call(scale, small, history, dy, cotangent, operands):
+def reduce_call(small, history, dy, operands):
     counts = (8, 4)
     rows = dy.shape[0]
     scratch = []
@@ -1746,7 +1763,7 @@
             pltpu.SemaphoreType.DMA((6, 2, count, 3)),
             pltpu.SemaphoreType.DMA((6, 2, count, 3)),
         ]
-    small_shape = (SMALL_ROWS + 2 * HIST, 128)
+    small_shape = (SMALL_ROWS + HIST + 4, 128)
     scratch += [
         pltpu.VMEM((2, 384, D), bf16),
         pltpu.VMEM((384, D), bf16),
@@ -1759,13 +1776,13 @@
         pltpu.SemaphoreType.DMA((2, 3)),
         pltpu.SemaphoreType.REGULAR((2,)),
         pltpu.VMEM((2, HIST, HIST_CHUNK, D), bf16),
-        pltpu.VMEM((2 * HIST, 8, D), f32),
+        pltpu.VMEM((HIST, 8, D), f32),
         pltpu.SemaphoreType.DMA((2,)),
     ]
     in_vmem, in_hbm = (pl.BlockSpec(memory_space=space) for space in (pltpu.VMEM, pltpu.HBM))
     return pl.pallas_call(
-        functools.partial(reduce_kernel, counts, scale),
-        in_specs=[in_vmem, in_hbm, in_vmem, in_vmem] + [in_hbm] * 16,
+        functools.partial(reduce_kernel, counts),
+        in_specs=[in_vmem, in_hbm, in_vmem] + [in_hbm] * 16,
         out_specs=[in_vmem, in_vmem],
         out_shape=[
             jax.ShapeDtypeStruct((D, D), bf16),
@@ -1777,7 +1794,7 @@
         compiler_params=pltpu.CompilerParams(
             collective_id=1, has_side_effects=True, vmem_limit_bytes=60 * 1024 * 1024
         ),
-    )(small, history, dy, cotangent, *operands)
+    )(small, history, dy, *operands)
 
 
 def reduce_tiles(place, tiles):
@@ -1860,10 +1877,15 @@
 
     block, ends = pack_weights(plan, place, params)
     if nb == 8:
-        att, mlp, ends, past = gather_weights(plan, mix_weights, block, ends, history)
+        att, mlp, ends, past, cot_sums = gather_weights(
+            plan, mix_weights, block, ends, history, cotangent
+        )
+        cot_sums = jnp.sum(cot_sums, axis=1) * grad_scale
     else:
         att, mlp, ends = gather_blocks(plan, block, ends)
         past = past_call(mix_weights, history)
+        cot_sums = jnp.sum(cotangent.astype(f32)[None] * history.astype(f32), axis=(1, 2))
+        cot_sums = cot_sums * grad_scale
     all_vecs = split_ends(plan, ends.reshape(4, nb, 32, 128))
     att_vecs, mlp_vecs = all_vecs[::2], all_vecs[1::2]
 
@@ -1948,7 +1970,7 @@
     )
     stream_grad = to_owner(dstream).astype(f32)
 
-    own_mix = jnp.stack([mix20, mix41, mix42])
+    own_mix = jnp.concatenate([jnp.stack([mix20, mix41, mix42]), cot_sums])
 
     def flat_vec(v):
         out = jnp.concatenate([line.reshape(-1) for line in v])
@@ -1962,27 +1984,24 @@
     if nb == 8:
         small = jnp.concatenate([small, jnp.zeros((SMALL_ROWS * 128 - small.shape[0],), f32)])
         tile_grad, small = reduce_call(
-            grad_scale,
             small.reshape(SMALL_ROWS, 128),
             history,
             dy20_own,
-            cotangent,
             operands20 + operands21,
         )
-        mix_sums = jnp.sum(small[SMALL_ROWS:], axis=1)
+        mix_sums = jnp.sum(small[SMALL_ROWS : SMALL_ROWS + HIST], axis=1)
         small = small[:SMALL_ROWS].reshape(-1)
     else:
-        rows = [dy20_own.astype(f32), cotangent.astype(f32) * grad_scale]
-        mix_sums = [jnp.sum(r[None] * history.astype(f32), axis=(1, 2)) for r in rows]
+        mix_sums = jnp.sum(dy20_own.astype(f32)[None] * history.astype(f32), axis=(1, 2))
         tiles = [
             mlp_tiles(plan, *ops[:4]) + att_tiles(plan, *ops[4:])
             for ops in (operands20, operands21)
         ]
         tile_grad = reduce_blocks(place, tiles)
-        small = lax.psum(jnp.concatenate([small] + mix_sums), ("section", "batch"))
-        mix_sums = small[-2 * HIST :]
-    own_mix = small[4 * VEC : 4 * VEC + 3]
-    mix_grad = jnp.concatenate([mix_sums[:HIST], own_mix[:1], mix_sums[HIST:], own_mix[1:]])
+        small = lax.psum(jnp.concatenate([small, mix_sums]), ("section", "batch"))
+        mix_sums = small[-HIST:]
+    own_mix = small[4 * VEC : 4 * VEC + 3 + HIST]
+    mix_grad = jnp.concatenate([mix_sums, own_mix[:1], own_mix[3:], own_mix[1:3]])
     vec_rows = small[: 4 * VEC].reshape(4, VEC)
     vec_own = lax.dynamic_index_in_dim(vec_rows, section, 0, keepdims=False)
 

time: 586 us -> 561 us (0.957)
  local copies, waits for them, and re-layouts: 60.5 us -> 36.9 us
    unnamed x162 -> x102, local copies, waits for them, and re-layouts: 46.5 us -> 22.4 us
    pallas_call x2, Pallas kernels: 308 us -> 301 us  [the longest x1 163 us: reduce_call(): pl.pallas_call(functools.partial(reduce_kernel, counts), in_specs=[in_vme...]
  transfers between devices with their start and end apart: 14 -> 14, of which waited for: 4 -> 4; matrix products, arithmetic and copies ran while one was open for 3% -> 4% of each run, Pallas kernels for 34% -> 37%
where the time goes in v6:
time: 561 us; the launch traced here: 556 us
  Pallas kernels  459 us (82%)
  local copies, waits for them, and re-layouts  36.9 us (7%)
  other arithmetic  21.6 us (4%)
  starting transfers between devices  19.7 us (4%)
  waiting for transfers between devices  10.6 us (2%)
  between operations  8.53 us (2%)
    pallas_call x1, Pallas kernels, reduce_call(): pl.pallas_call(functools.partial(reduce_kernel, counts), in_specs=[in_vme...  163 us
    pallas_call x1, Pallas kernels, gather_weights(): pl.pallas_call(body, in_specs=[SMEM_SPEC] + [any_spec] * 3 + [in_vmem], o...  138 us
    pallas_call x2, Pallas kernels, att_back_call(): call(att_back_kernel, 'attention_grad_rows', (pairs,), [SMEM_SPEC, pair_s...  38.3 us
    pallas_call x2, Pallas kernels, att_call(): call(att_kernel, 'attention_rows', (pairs,), [SMEM_SPEC, pair_spec(rows),...  25.5 us
    pallas_call x2, Pallas kernels, mlp_call(): call(functools.partial(mlp_kernel, last_layer), 'feed_forward_rows', (FF...  22.9 us
    pallas_call x2, Pallas kernels, mlp_back_call(): call(functools.partial(mlp_back_kernel, last_layer), 'feed_forward_grad_r...  22.5 us
    unnamed x102, local copies, waits for them, and re-layouts  22.4 us
    pallas_call x2, Pallas kernels, qkv_call(): call(qkv_kernel, 'qkv_rows', (6,), [whole_spec((rows, D)), row_spec(D), r...  14.8 us
  transfers between devices with their start and end apart: 14, of which 4 were waited for; matrix products, arithmetic and copies ran while one was open for 4% of the time, Pallas kernels for 37%

profile of v6, /device:TPU:0, one launch (start us, length us, event | category | flops | bytes accessed | tf_op | source)
XLA Modules:
  0.0 556.2 jit_solution(17708866228334691004)
XLA Ops:
  1.5 4.8 collective-permute-start
  6.3 1.3 collective-permute-start.1
  7.7 2.1 broadcast_select_fusion.19
  10.4 1.3 dynamic_slice.16
  14.3 1.2 slice.380
  16.8 1.3 fusion.44
  22.0 2.5 pack_weights.1.block_ref
  24.5 1.0 copy-done.6
  25.5 137.9 %gather_weights.1 = (bf16[2,4,768,768]{3,2,1,0:T(8,128)(2,1)}, bf16[2,8,768,768]{3,2,1,0:T(8,128)(2,1)}, bf16[32,32,128]{2,1,0:T(8,128)(2,1)}, bf16[2,512,768]{2,1,0:T(8,128)(2,1)}, f32[20,128]{1,0:T(8,128)}) custom-call(f32[43]{0:T(128)} %w_ref.3, bf16[768,768]{1,0:T(8,128)(2,1)} %copy-done.6, bf16[32,128]{1,0:T(8,128)(2,1)} %pad_maximum_fusion.12.vec_ref, ...), custom_call_target="tpu_custom_call" | custom-call | flops 99999997952 | bytes 100000000 | tf_op jit(solution)/shard_map/gather_weights/pallas_call | solution.py:365
  163.4 1.1 fusion.43
  164.9 1.1 broadcast_select_fusion.18
  166.0 3.7 copy-done
  169.7 7.2 %qkv_rows.2 = (bf16[512,768]{1,0:T(8,128)(2,1)S(1)}, bf16[512,768]{1,0:T(8,128)(2,1)S(1)}, bf16[512,1536]{1,0:T(8,128)(2,1)S(1)}) custom-call(bf16[512,768]{1,0:T(8,128)(2,1)S(1)} %pad_maximum_fusion.2.x_ref, f32[1,768]{1,0:T(1,128)S(1)} %get-tuple-element.294.gain_ref, f32[1,768]{1,0:T(1,128)S(1)} %get-tuple-element.295.bias_ref, ...), custom_call_target="tpu_custom_call" | custom-call | flops 1811939328 | bytes 2359296 | tf_op jit(solution)/shard_map/qkv_rows/pallas_call | solution.py:484
  177.9 1.8 collective-permute-start.3
  180.7 2.0 collective-permute-done.3.ko_ref.vo_ref
  182.7 12.7 %attention_rows.2 = (bf16[512,768]{1,0:T(8,128)(2,1)S(1)}, f32[6,512,128]{2,1,0:T(8,128)S(1)}) custom-call(s32[4]{0:T(128)S(1)} %pad_add_fusion.2.meta_ref, bf16[512,768]{1,0:T(8,128)(2,1)S(1)} %get-tuple-element.142.q_ref, bf16[512,1536]{1,0:T(8,128)(2,1)S(1)} %get-tuple-element.143.k_ref.v_ref, bf16[512,1536]{1,0:T(8,128)(2,1)S(1)} %get-tuple-element.143.k_ref.v_ref, ...), custom_call_target="tpu_custom_call" | custom-call | flops 4026531840 | bytes 2359296 | tf_op jit(solution)/shard_map/attention_rows/pallas_call | solution.py:598
  196.9 11.2 %feed_forward_rows.2 = (bf16[512,768]{1,0:T(8,128)(2,1)S(1)}, bf16[512,768]{1,0:T(8,128)(2,1)S(1)}, bf16[512,3072]{1,0:T(8,128)(2,1)S(1)}, bf16[512,3072]{1,0:T(...) custom-call(f32[4]{0:T(128)S(1)} %pad_maximum_fusion.13.mix_ref, ...), custom_call_target="tpu_custom_call" | custom-call | flops 5435817984 | bytes 2359296 | tf_op jit(solution)/shard_map/feed_forward_rows/pallas_call | solution.py:692
  208.1 7.5 %qkv_rows.3 = (bf16[512,768]{1,0:T(8,128)(2,1)S(1)}, bf16[512,768]{1,0:T(8,128)(2,1)S(1)}, bf16[512,1536]{1,0:T(8,128)(2,1)S(1)}) custom-call(bf16[512,768]{1,0:T(8,128)(2,1)S(1)} %get-tuple-element.148.x_ref.dy_ref, f32[1,768]{1,0:T(1,128)S(1)} %get-tuple-element.299.gain_ref, f32[1,768]{1,0:T(1,128)S(1)} %get-tuple-element.300.bias_ref, ...), custom_call_target="tpu_custom_call" | custom-call | flops 1811939328 | bytes 2359296 | tf_op jit(solution)/shard_map/qkv_rows/pallas_call | solution.py:484
  217.3 1.2 collective-permute-start.6
  219.2 12.7 %attention_rows.3 = (bf16[512,768]{1,0:T(8,128)(2,1)S(1)}, f32[6,512,128]{2,1,0:T(8,128)S(1)}) custom-call(s32[4]{0:T(128)S(1)} %pad_add_fusion.2.meta_ref, bf16[512,768]{1,0:T(8,128)(2,1)S(1)} %get-tuple-element.149.q_ref, bf16[512,1536]{1,0:T(8,128)(2,1)S(1)} %get-tuple-element.150.k_ref.v_ref, bf16[512,1536]{1,0:T(8,128)(2,1)S(1)} %get-tuple-element.150.k_ref.v_ref, ...), custom_call_target="tpu_custom_call" | custom-call | flops 4026531840 | bytes 2359296 | tf_op jit(solution)/shard_map/attention_rows/pallas_call | solution.py:598
  232.0 4.8 collective-permute-done.6
  237.3 11.6 %feed_forward_rows.3 = (bf16[512,768]{1,0:T(8,128)(2,1)S(1)}, bf16[512,768]{1,0:T(8,128)(2,1)S(1)}, bf16[512,3072]{1,0:T(8,128)(2,1)S(1)}, bf16[512,3072]{1,0:T(...) custom-call(f32[4]{0:T(128)S(1)} %pad_maximum_fusion.13.mix_ref, ...), custom_call_target="tpu_custom_call" | custom-call | flops 5435817984 | bytes 2359296 | tf_op jit(solution)/shard_map/feed_forward_rows/pallas_call | solution.py:692
  249.0 1.7 copy-done.17
  250.7 1.2 collective-permute-start.7
  251.8 11.2 %feed_forward_grad_rows.2 = (bf16[512,768]{1,0:T(8,128)(2,1)S(1)}, bf16[512,3072]{1,0:T(8,128)(2,1)S(1)}, f32[1,3072]{1,0:T(1,128)S(1)}, bf16[512,768]{1,0:T(8,1...) custom-call(f32[4]{0:T(128)S(1)} %pad_maximum_fusion.13.mix_ref, ...), custom_call_target="tpu_custom_call" | custom-call | flops 5435817984 | bytes 2359296 | tf_op jit(solution)/shard_map/feed_forward_grad_rows/pallas_call | solution.py:800
  263.0 1.6 copy-done.18
  265.9 1.1 copy-done.27
  266.9 18.9 %attention_grad_rows.2 = (bf16[512,768]{1,0:T(8,128)(2,1)S(1)}, f32[2,512,768]{2,1,0:T(8,128)S(1)}, bf16[2,512,768]{2,1,0:T(8,128)(2,1)S(1)}) custom-call(s32[4]{0:T(128)S(1)} %pad_add_fusion.2.meta_ref, bf16[512,768]{1,0:T(8,128)(2,1)S(1)} %get-tuple-element.149.q_ref, bf16[512,1536]{1,0:T(8,128)(2,1)S(1)} %get-tuple-element.150.k_ref.v_ref, ...), custom_call_target="tpu_custom_call" | custom-call | flops 10066329600 | bytes 2359296 | tf_op jit(solution)/shard_map/attention_grad_rows/pallas_call | solution.py:915
  286.2 3.1 collective-permute-done.8.got_ref
  289.3 5.9 %qkv_grad_rows.2 = (bf16[512,2304]{1,0:T(8,128)(2,1)S(1)}, f32[1,2304]{1,0:T(1,128)S(1)}, bf16[512,768]{1,0:T(8,128)(2,1)S(1)}, f32[8,768]{1,0:T(8,128)S(1)}) custom-call(bf16[512,768]{1,0:T(8,128)(2,1)S(1)} %get-tuple-element.162.dq_ref, f32[2,512,768]{2,1,0:T(8,128)S(1)} %get-tuple-element.163.own_ref, ...), custom_call_target="tpu_custom_call" | custom-call | flops 1811939328 | bytes 2359296 | tf_op jit(solution)/shard_map/qkv_grad_rows/pallas_call | solution.py:999
  295.3 1.4 copy-done.20
  297.4 11.3 %feed_forward_grad_rows.3 = (bf16[512,768]{1,0:T(8,128)(2,1)S(1)}, bf16[512,3072]{1,0:T(8,128)(2,1)S(1)}, f32[1,3072]{1,0:T(1,128)S(1)}, bf16[512,768]{1,0:T(8,1...) custom-call(f32[4]{0:T(128)S(1)} %pad_maximum_fusion.13.mix_ref, ...), custom_call_target="tpu_custom_call" | custom-call | flops 5435817984 | bytes 2359296 | tf_op jit(solution)/shard_map/feed_forward_grad_rows/pallas_call | solution.py:800
  308.8 1.6 copy-done.19
  313.1 19.4 %attention_grad_rows.3 = (bf16[512,768]{1,0:T(8,128)(2,1)S(1)}, f32[2,512,768]{2,1,0:T(8,128)S(1)}, bf16[2,512,768]{2,1,0:T(8,128)(2,1)}) custom-call(s32[4]{0:T(128)S(1)} %pad_add_fusion.2.meta_ref, bf16[512,768]{1,0:T(8,128)(2,1)S(1)} %copy-done.35, bf16[512,1536]{1,0:T(8,128)(2,1)S(1)} %copy-done.23, bf16[512,1536]{1,0:T(8,128)(2,1)S(1)} %copy-done.23, ...), custom_call_target="tpu_custom_call" | custom-call | flops 10066329600 | bytes 2359296 | tf_op jit(solution)/shard_map/attention_grad_rows/pallas_call | solution.py:915
  332.5 1.7 copy-done.4
  340.9 1.3 copy-done.3
  342.2 8.6 %history_grads.1 = bf16[20,512,768]{2,1,0:T(8,128)(2,1)} custom-call(f32[43]{0:T(128)S(1)} %copy-done.15, bf16[512,768]{1,0:T(8,128)(2,1)S(1)} %copy-done.3, bf16[512,768]{1,0:T(8,128)(2,1)S(1)} %copy-done.2), custom_call_target="tpu_custom_call" | custom-call | flops 31457280 | bytes 2359296 | tf_op jit(solution)/shard_map/history_grads/pallas_call | solution.py:1201
  350.9 7.4 %qkv_grad_rows.3 = (bf16[512,2304]{1,0:T(8,128)(2,1)S(1)}, f32[1,2304]{1,0:T(1,128)S(1)}, bf16[512,768]{1,0:T(8,128)(2,1)S(1)}, f32[8,768]{1,0:T(8,128)S(1)}) custom-call(bf16[512,768]{1,0:T(8,128)(2,1)S(1)} %copy-done.11, f32[2,512,768]{2,1,0:T(8,128)S(1)} %copy-done.5, bf16[2,512,768]{2,1,0:T(8,128)(2,1)} %collective-permute-done.10.got_ref, ...), custom_call_target="tpu_custom_call" | custom-call | flops 1811939328 | bytes 2359296 | tf_op jit(solution)/shard_map/qkv_grad_rows/pallas_call | solution.py:999
  358.3 1.4 copy-done.21
  359.8 2.7 concatenate.170
  362.5 163.2 %reduce_gradients.1 = (bf16[768,768]{1,0:T(8,128)(2,1)}, f32[200,128]{1,0:T(8,128)}) custom-call(f32[176,128]{1,0:T(8,128)} %bitcast.160, bf16[20,512,768]{2,1,0:T(8,128)(2,1)} %hist_ref.3, bf16[512,768]{1,0:T(8,128)(2,1)} %pad_maximum_fusion.5.dy_ref, bf16[512,768]{1,0:T(8,128)(2,1)} %copy-done.29, bf16[512,3072]{1,0:T(8,128)(2,1)} %copy-done.19, ...), custom_call_target="tpu_custom_call" | custom-call | flops 99999997952 | bytes 100000000 | tf_op jit(solution)/shard_map/reduce_gradients/pallas_call | solution.py:1783
  529.8 2.8 convert_element_type.258
  534.3 1.3 collective-permute-start.13
  535.7 4.5 collective-permute-start.12
  540.3 1.7 select_select_fusion.tile_ref
  542.0 1.3 multiply_add_fusion
  544.9 9.5 %adamw_step.1 = (f32[1,590496]{1,0:T(1,128)}, f32[1,590496]{1,0:T(1,128)}, f32[1,590496]{1,0:T(1,128)}, f32[1,590496]{1,0:T(1,128)}) custom-call(s32[3]{0:T(128)} %pad_add_fusion.3.meta_ref, f32[768,768]{1,0:T(8,128)} %select_select_fusion.tile_ref, f32[6,768]{1,0:T(8,128)} %fusion.9.before_ref, f32[6,768]{1,0:T(8,128)} %fusion.6.after_ref, ...), custom_call_target="tpu_custom_call" | custom-call | flops 11809920 | bytes 2359296 | tf_op jit(solution)/shard_map/adamw_step/pallas_call | solution.py:1251
  554.4 1.3 maximum_convert_fusion
  (190 shorter events, 28.5 us)
Async XLA Ops:
  1.5 20.5 %collective-permute-start = (bf16[16,128]{1,0:T(8,128)(2,1)S(1)}, bf16[16,128]{1,0:T(8,128)(2,1)S(1)}, u32[]{:S(2)}, u32[]{:S(2)}) collective-permute-start(bf16[16,128]{1,0:T(8,128)(2,1)S(1)} %bitcast.161), channel_id=1, source_target_pairs={{0,1},{1,2},{2,3},{3,4},{4,5},{5,6},{6,7},{8,9},{9,10},{10,11},{11... | collective-permute-start | bytes 12296 | tf_op jit(solution)/shard_map/ppermute | solution.py:1128
  6.3 15.6 %collective-permute-start.1 = (bf16[16,128]{1,0:T(8,128)(2,1)S(1)}, bf16[16,128]{1,0:T(8,128)(2,1)S(1)}, u32[]{:S(2)}, u32[]{:S(2)}) collective-permute-start(bf16[16,128]{1,0:T(8,128)(2,1)S(1)} %bitcast.163), channel_id=1, source_target_pairs={{1,0},{2,1},{3,2},{4,3},{5,4},{6,5},{7,6},{9,8},{10,9},{11,10},{12... | collective-permute-start | bytes 12296 | tf_op jit(solution)/shard_map/ppermute | solution.py:1129
  7.6 14.4 %copy-start.1 = (f32[1,590496]{1,0:T(1,128)S(1)}, f32[1,590496]{1,0:T(1,128)}, u32[]{:S(2)}) copy-start(f32[1,590496]{1,0:T(1,128)} %p_ref.3) | copy-start | bytes 7085956
  9.7 155.2 %collective-permute-start.2 = (bf16[256,768]{1,0:T(8,128)(2,1)}, bf16[256,768]{1,0:T(8,128)(2,1)}, u32[]{:S(2)}, u32[]{:S(2)}) collective-permute-start(bf16[256,768]{1,0:T(8,128)(2,1)} %broadcast_select_fusion.19), channel_id=1, source_target_pairs={{0,24},{8,16},{16,8},{24,0},{1,25},{9,17},{17,9},{25,1},{2,26},{10... | collective-permute-start | bytes 1179656 | tf_op jit(solution)/shard_map/ppermute | solution.py:54
  166.0 3.7 copy-start
  169.7 10.1 %copy-start.39 = (bf16[2,512,768]{2,1,0:T(8,128)(2,1)S(1)}, bf16[2,512,768]{2,1,0:T(8,128)(2,1)}, u32[]{:S(2)}) copy-start(bf16[2,512,768]{2,1,0:T(8,128)(2,1)} %get-tuple-element.139) | copy-start | bytes 4718596
  177.9 17.6 %copy-start.22 = (bf16[512,1536]{1,0:T(8,128)(2,1)}, bf16[512,1536]{1,0:T(8,128)(2,1)S(1)}, u32[]{:S(2)}) copy-start(bf16[512,1536]{1,0:T(8,128)(2,1)S(1)} %get-tuple-element.143.k_ref.v_ref) | copy-start | bytes 4718596
  177.9 17.6 %copy-start.34 = (bf16[512,768]{1,0:T(8,128)(2,1)}, bf16[512,768]{1,0:T(8,128)(2,1)S(1)}, u32[]{:S(2)}) copy-start(bf16[512,768]{1,0:T(8,128)(2,1)S(1)} %get-tuple-element.142.q_ref) | copy-start | bytes 2359300
  177.9 4.8 collective-permute-start.3
  179.8 15.7 %collective-permute-start.4 = (bf16[256,768]{1,0:T(8,128)(2,1)S(1)}, bf16[256,768]{1,0:T(8,128)(2,1)S(1)}, u32[]{:S(2)}, u32[]{:S(2)}) collective-permute-start(bf16[256,768]{1,0:T(8,128)(2,1)S(1)} %select_bitcast_fusion), channel_id=1, source_target_pairs={{0,24},{8,16},{16,8},{24,0},{1,25},{9,17},{17,9},{25,1},{2,26},{10... | collective-permute-start | bytes 1179656 | tf_op jit(solution)/shard_map/ppermute | solution.py:54
  182.7 12.8 %copy-start.24 = (bf16[512,1536]{1,0:T(8,128)(2,1)}, bf16[512,1536]{1,0:T(8,128)(2,1)S(1)}, u32[]{:S(2)}) copy-start(bf16[512,1536]{1,0:T(8,128)(2,1)S(1)} %collective-permute-done.3.ko_ref.vo_ref) | copy-start | bytes 4718596
  182.7 14.2 %slice-start = ((s8[9437184]{0:T(1024)(128)(4,1)}), s8[4194304]{0:T(1024)(128)(4,1)S(1)}, s32[]{:S(2)}) async-start(s8[9437184]{0:T(1024)(128)(4,1)} %bitcast.140), calls=%async_computation | async-start | bytes 8388608
  182.7 14.2 %slice-start.1 = ((s8[9437184]{0:T(1024)(128)(4,1)}), s8[4194304]{0:T(1024)(128)(4,1)S(1)}, s32[]{:S(2)}) async-start(s8[9437184]{0:T(1024)(128)(4,1)} %bitcast.140), calls=%async_computation.1 | async-start | bytes 8388608
  182.7 14.2 %slice-start.2 = ((s8[9437184]{0:T(1024)(128)(4,1)}), s8[1048576]{0:T(1024)(128)(4,1)S(1)}, s32[]{:S(2)}) async-start(s8[9437184]{0:T(1024)(128)(4,1)} %bitcast.140), calls=%async_computation.2 | async-start | bytes 2097152
  208.1 7.6 %copy-start.16 = (bf16[512,3072]{1,0:T(8,128)(2,1)}, bf16[512,3072]{1,0:T(8,128)(2,1)S(1)}, u32[]{:S(2)}) copy-start(bf16[512,3072]{1,0:T(8,128)(2,1)S(1)} %get-tuple-element.190.refs_2_) | copy-start | bytes 9437188
  208.1 7.6 %copy-start.29 = (bf16[512,768]{1,0:T(8,128)(2,1)}, bf16[512,768]{1,0:T(8,128)(2,1)S(1)}, u32[]{:S(2)}) copy-start(bf16[512,768]{1,0:T(8,128)(2,1)S(1)} %get-tuple-element.188.refs_0_) | copy-start | bytes 2359300
  215.7 3.5 collective-permute-start.5
  217.3 19.5 %collective-permute-start.6 = (bf16[2,256,768]{2,1,0:T(8,128)(2,1)S(1)}, bf16[2,256,768]{2,1,0:T(8,128)(2,1)S(1)}, u32[]{:S(2)}, u32[]{:S(2)}) collective-permute-start(bf16[2,256,768]{2,1,0:T(8,128)(2,1)S(1)} %broadcast_select_fusion.2), channel_id=1, source_target_pairs={{0,24},{8,16},{16,8},{24,0},{1,25},{9,17},{17,9},{25,1},{2,26},{10... | collective-permute-start | bytes 2359304 | tf_op jit(solution)/shard_map/ppermute | solution.py:54
  219.2 12.7 %copy-start.26 = (bf16[512,1536]{1,0:T(8,128)(2,1)}, bf16[512,1536]{1,0:T(8,128)(2,1)S(1)}, u32[]{:S(2)}) copy-start(bf16[512,1536]{1,0:T(8,128)(2,1)S(1)} %collective-permute-done.5.ko_ref.vo_ref) | copy-start | bytes 4718596
  231.9 33.9 %copy-start.14 = (bf16[512,768]{1,0:T(8,128)(2,1)}, bf16[512,768]{1,0:T(8,128)(2,1)S(1)}, u32[]{:S(2)}) copy-start(bf16[512,768]{1,0:T(8,128)(2,1)S(1)} %get-tuple-element.153.o_ref.refs_14_) | copy-start | bytes 2359300
  248.9 1.7 copy-start.17
  250.6 12.4 %copy-start.31 = (bf16[512,768]{1,0:T(8,128)(2,1)}, bf16[512,768]{1,0:T(8,128)(2,1)S(1)}, u32[]{:S(2)}) copy-start(bf16[512,768]{1,0:T(8,128)(2,1)S(1)} %get-tuple-element.194.refs_8_) | copy-start | bytes 2359300
  250.7 14.0 %collective-permute-start.7 = (bf16[256,768]{1,0:T(8,128)(2,1)S(1)}, bf16[256,768]{1,0:T(8,128)(2,1)S(1)}, u32[]{:S(2)}, u32[]{:S(2)}) collective-permute-start(bf16[256,768]{1,0:T(8,128)(2,1)S(1)} %broadcast_select_fusion.15), channel_id=1, source_target_pairs={{0,24},{8,16},{16,8},{24,0},{1,25},{9,17},{17,9},{25,1},{2,26},{10... | collective-permute-start | bytes 1179656 | tf_op jit(solution)/shard_map/ppermute | solution.py:54
  264.7 24.6 %copy-start.7 = (bf16[512,768]{1,0:T(8,128)(2,1)}, bf16[512,768]{1,0:T(8,128)(2,1)S(1)}, u32[]{:S(2)}) copy-start(bf16[512,768]{1,0:T(8,128)(2,1)S(1)} %get-tuple-element.165.dh_ref.refs_15_) | copy-start | bytes 2359300
  264.7 2.3 copy-start.27
  285.8 3.5 collective-permute-start.8
  296.7 13.7 %collective-permute-start.9 = (bf16[256,768]{1,0:T(8,128)(2,1)S(1)}, bf16[256,768]{1,0:T(8,128)(2,1)S(1)}, u32[]{:S(2)}, u32[]{:S(2)}) collective-permute-start(bf16[256,768]{1,0:T(8,128)(2,1)S(1)} %broadcast_select_fusion.11), channel_id=1, source_target_pairs={{0,24},{8,16},{16,8},{24,0},{1,25},{9,17},{17,9},{25,1},{2,26},{10... | collective-permute-start | bytes 1179656 | tf_op jit(solution)/shard_map/ppermute | solution.py:54
  297.4 14.4 %copy-start.25 = (bf16[512,1536]{1,0:T(8,128)(2,1)S(1)}, bf16[512,1536]{1,0:T(8,128)(2,1)}, u32[]{:S(2)}) copy-start(bf16[512,1536]{1,0:T(8,128)(2,1)} %copy-done.24) | copy-start | bytes 4718596
  297.4 14.4 %copy-start.37 = (f32[6,512,128]{2,1,0:T(8,128)S(1)}, f32[6,512,128]{2,1,0:T(8,128)}, u32[]{:S(2)}) copy-start(f32[6,512,128]{2,1,0:T(8,128)} %copy-done.36) | copy-start | bytes 4718596
  310.4 1.7 copy-start.13
  310.4 2.5 copy-start.23
  310.4 2.7 copy-start.35
  313.1 22.5 %copy-start.44 = (s32[2,8]{1,0:T(2,128)S(1)}, s32[2,8]{1,0:T(2,128)}, u32[]{:S(2)}) copy-start(s32[2,8]{1,0:T(2,128)} %constant.248.clone) | copy-start | bytes 196
  313.1 26.3 %copy-start.41 = (f32[20,128]{1,0:T(8,128)S(1)}, f32[20,128]{1,0:T(8,128)}, u32[]{:S(2)}) copy-start(f32[20,128]{1,0:T(8,128)} %get-tuple-element.187) | copy-start | bytes 30724
  313.1 27.8 %copy-start.15 = (f32[43]{0:T(128)S(1)}, f32[43]{0:T(128)}, u32[]{:S(2)}) copy-start(f32[43]{0:T(128)} %w_ref.3) | copy-start | bytes 520
  335.1 15.7 %collective-permute-start.10 = (bf16[2,512,768]{2,1,0:T(8,128)(2,1)}, bf16[2,512,768]{2,1,0:T(8,128)(2,1)}, u32[]{:S(2)}, u32[]{:S(2)}) collective-permute-start(bf16[2,512,768]{2,1,0:T(8,128)(2,1)} %get-tuple-element.174), channel_id=1, source_target_pairs={{0,8},{8,0},{16,24},{24,16},{1,9},{9,1},{17,25},{25,17},{2,10},{10... | collective-permute-start | bytes 4718600 | tf_op jit(solution)/shard_map/ppermute | solution.py:58
  340.9 10.0 %slice-start.3 = ((s8[9437184]{0:T(1024)(128)(4,1)}), s8[4194304]{0:T(1024)(128)(4,1)S(1)}, s32[]{:S(2)}) async-start(s8[9437184]{0:T(1024)(128)(4,1)} %bitcast.144), calls=%async_computation.3 | async-start | bytes 8388608
  342.2 8.6 %slice-start.4 = ((s8[9437184]{0:T(1024)(128)(4,1)}), s8[4194304]{0:T(1024)(128)(4,1)S(1)}, s32[]{:S(2)}) async-start(s8[9437184]{0:T(1024)(128)(4,1)} %bitcast.144), calls=%async_computation.4 | async-start | bytes 8388608
  342.2 8.6 %slice-start.5 = ((s8[9437184]{0:T(1024)(128)(4,1)}), s8[1048576]{0:T(1024)(128)(4,1)S(1)}, s32[]{:S(2)}) async-start(s8[9437184]{0:T(1024)(128)(4,1)} %bitcast.144), calls=%async_computation.5 | async-start | bytes 2097152
  342.2 8.6 %copy-start.5 = (f32[2,512,768]{2,1,0:T(8,128)S(1)}, f32[2,512,768]{2,1,0:T(8,128)}, u32[]{:S(2)}) copy-start(f32[2,512,768]{2,1,0:T(8,128)} %copy-done.4) | copy-start | bytes 9437188
  342.2 8.6 %copy-start.9 = (bf16[512,768]{1,0:T(8,128)(2,1)S(1)}, bf16[512,768]{1,0:T(8,128)(2,1)}, u32[]{:S(2)}) copy-start(bf16[512,768]{1,0:T(8,128)(2,1)} %copy-done.8) | copy-start | bytes 2359300
  342.2 8.7 %copy-start.11 = (bf16[512,768]{1,0:T(8,128)(2,1)S(1)}, bf16[512,768]{1,0:T(8,128)(2,1)}, u32[]{:S(2)}) copy-start(bf16[512,768]{1,0:T(8,128)(2,1)} %copy-done.10) | copy-start | bytes 2359300
  532.6 7.6 %copy-start.38 = (bf16[768,768]{1,0:T(8,128)(2,1)S(1)}, bf16[768,768]{1,0:T(8,128)(2,1)}, u32[]{:S(2)}) copy-start(bf16[768,768]{1,0:T(8,128)(2,1)} %get-tuple-element.201) | copy-start | bytes 3538948
  533.4 20.9 %collective-permute-start.11 = (bf16[256,768]{1,0:T(8,128)(2,1)S(1)}, bf16[256,768]{1,0:T(8,128)(2,1)S(1)}, u32[]{:S(2)}, u32[]{:S(2)}) collective-permute-start(bf16[256,768]{1,0:T(8,128)(2,1)S(1)} %broadcast_select_fusion.7), channel_id=1, source_target_pairs={{0,24},{8,16},{16,8},{24,0},{1,25},{9,17},{17,9},{25,1},{2,26},{10... | collective-permute-start | bytes 1179656 | tf_op jit(solution)/shard_map/ppermute | solution.py:54
  534.3 9.3 %collective-permute-start.13 = (f32[3,768]{1,0:T(4,128)S(1)}, f32[3,768]{1,0:T(4,128)S(1)}, u32[]{:S(2)}, u32[]{:S(2)}) collective-permute-start(f32[3,768]{1,0:T(4,128)S(1)} %fusion.18), channel_id=1, source_target_pairs={{1,0},{2,1},{3,2},{4,3},{5,4},{6,5},{7,6},{9,8},{10,9},{11,10},{12... | collective-permute-start | bytes 27656 | tf_op jit(solution)/shard_map/ppermute | solution.py:1289
  535.7 6.3 %copy-start.42 = (f32[43]{0:T(128)S(1)}, f32[43]{0:T(128)}, u32[]{:S(2)}) copy-start(f32[43]{0:T(128)} %param.31) | copy-start | bytes 520
  535.7 6.3 %copy-start.43 = (f32[43]{0:T(128)S(1)}, f32[43]{0:T(128)}, u32[]{:S(2)}) copy-start(f32[43]{0:T(128)} %param.30) | copy-start | bytes 520
  535.7 7.9 %collective-permute-start.12 = (f32[3,768]{1,0:T(4,128)S(1)}, f32[3,768]{1,0:T(4,128)S(1)}, u32[]{:S(2)}, u32[]{:S(2)}) collective-permute-start(f32[3,768]{1,0:T(4,128)S(1)} %fusion.21), channel_id=1, source_target_pairs={{0,1},{1,2},{2,3},{3,4},{4,5},{5,6},{6,7},{8,9},{9,10},{10,11},{11... | collective-permute-start | bytes 27656 | tf_op jit(solution)/shard_map/ppermute | solution.py:1288
  (17 other events, 22.7 us)

commit v7 on v6

--- a/solution.py
+++ b/solution.py
@@ -1020,6 +1020,7 @@
         ],
         [pltpu.VMEM((rows, D), f32)],
         2 * rows * D * 3 * D,
+        VMEM_LIMIT if layer else WIDE_LIMIT,
     )(
         dq,
         own,
@@ -1213,7 +1214,7 @@
 
 
 def update_kernel(
-    plan, meta_ref, tile_ref, before_ref, after_ref, p_ref, m_ref, v_ref, g_ref, s_ref, mn_ref, vn_ref, wide
+    plan, meta_ref, tile_ref, first_ref, before_ref, after_ref, p_ref, m_ref, v_ref, g_ref, s_ref, mn_ref, vn_ref, wide
 ):
     step = pl.program_id(0)
     end = UNDER + plan.tile // 128
@@ -1232,7 +1233,12 @@
                     for j in range(6):
                         wide[pl.ds(UNDER + 6 * line + j, rows, stride=6 * stride)] = tile_ref[
                             row : row + rows, 128 * j : 128 * j + 128
-                        ]
+                        ].astype(f32)
+
+        @pl.when(meta_ref[3] == 1)
+        def _():
+            for j in range(6):
+                wide[UNDER + j : UNDER + j + 1] = first_ref[:, 128 * j : 128 * j + 128]
 
     size = g_ref.shape[1] // 128
     grad = take_shifted(wide, meta_ref[1] + step * size, meta_ref[2], size)
@@ -1243,7 +1249,7 @@
     )
 
 
-def update_call(plan, meta, tile, before, after, params, first, second):
+def update_call(plan, meta, tile, first_line, before, after, params, first, second):
     size = min(STEP_ROWS, -(-plan.shard // 1024) * 8)
     steps = pl.cdiv(plan.shard, size * 128)
     flat = pl.BlockSpec((1, size * 128), lambda i: (0, i))
@@ -1255,6 +1261,7 @@
         [
             SMEM_SPEC,
             whole_spec((plan.rows, D)),
+            whole_spec((1, D)),
             whole_spec((6, D)),
             whole_spec((6, D)),
             flat,
@@ -1265,15 +1272,14 @@
         [pltpu.VMEM((steps * size + 2 * UNDER + 8, 128), f32)],
         20 * plan.shard,
         WIDE_LIMIT,
-    )(meta, tile, before, after, params, first, second)
+    )(meta, tile, first_line, before, after, params, first, second)
 
 
 def update_weights(plan, place, tile, vecs, params, first, second):
     nb, b = plan.nb, place.b
-    tile = tile.astype(f32)
 
     def lines(rows):
-        return jnp.concatenate([tile[r : r + 1] for r in rows], axis=0)
+        return jnp.concatenate([tile[r : r + 1] for r in rows], axis=0).astype(f32)
 
     def ends(role):
         pieces = line_pieces(plan, role)
@@ -1317,8 +1323,7 @@
         ),
     )
     empty = att & (b >= four)
-    line = jnp.arange(plan.rows)[:, None]
-    tile = jnp.where(empty, jnp.where((line == 0) & (b == four), vecs[5:6], 0.0), tile)
+    first_line = jnp.where(b == four, vecs[5:6], 0.0)
     offsets = [
         [UNDER * 128 + shard_at - starts[i] for i, shard_at in enumerate(range(0, nb * plan.shard, plan.shard))]
         for starts in (plan.att_start, plan.mlp_start)
@@ -1326,9 +1331,9 @@
     for i in range(four + 1, nb):
         offsets[0][i] = offsets[0][four]
     offset = jnp.array(offsets, jnp.int32)[place.core, b]
-    meta = jnp.stack([place.role, offset // 128, offset % 128]).astype(jnp.int32)
+    meta = jnp.stack([place.role, offset // 128, offset % 128, empty]).astype(jnp.int32)
     before = jnp.where(att & (b > four), none, before)
-    return update_call(plan, meta, tile, before, after, params, first, second)
+    return update_call(plan, meta, tile, first_line, before, after, params, first, second)
 
 
 def mlp_tiles(plan, normed, dpre, active, er):
@@ -1979,7 +1984,6 @@
     small = jnp.concatenate(
         [flat_vec(v) for v in (vec_a20, vec_m20, vec_a21, vec_m21)] + [own_mix]
     )
-    history_grad = history_call(grad_scale, mix_weights, dy20_own, cotangent)
 
     if nb == 8:
         small = jnp.concatenate([small, jnp.zeros((SMALL_ROWS * 128 - small.shape[0],), f32)])
@@ -2000,6 +2004,8 @@
         tile_grad = reduce_blocks(place, tiles)
         small = lax.psum(jnp.concatenate([small, mix_sums]), ("section", "batch"))
         mix_sums = small[-HIST:]
+    dy20_own, tile_grad = lax.optimization_barrier((dy20_own, tile_grad))
+    history_grad = history_call(grad_scale, mix_weights, dy20_own, cotangent)
     own_mix = small[4 * VEC : 4 * VEC + 3 + HIST]
     mix_grad = jnp.concatenate([mix_sums, own_mix[:1], own_mix[3:], own_mix[1:3]])
     vec_rows = small[: 4 * VEC].reshape(4, VEC)

time: 561 us -> 559 us (level)
    unnamed x102 -> x100, local copies, waits for them, and re-layouts: 22.4 us -> 23.4 us
  transfers between devices with their start and end apart: 14 -> 14, of which waited for: 4 -> 4; matrix products, arithmetic and copies ran while one was open for 4% -> 3% of each run, Pallas kernels for 37% -> 37%
where the time goes in v7:
time: 559 us; the launch traced here: 553 us
  Pallas kernels  461 us (82%)
  local copies, waits for them, and re-layouts  38.8 us (7%)
  other arithmetic  18.2 us (3%)
  starting transfers between devices  16.4 us (3%)
  waiting for transfers between devices  10.6 us (2%)
  between operations  8.46 us (2%)
    pallas_call x1, Pallas kernels, reduce_call(): pl.pallas_call(functools.partial(reduce_kernel, counts), in_specs=[in_vme...  163 us
    pallas_call x1, Pallas kernels, gather_weights(): pl.pallas_call(body, in_specs=[SMEM_SPEC] + [any_spec] * 3 + [in_vmem], o...  138 us
    pallas_call x2, Pallas kernels, att_back_call(): call(att_back_kernel, 'attention_grad_rows', (pairs,), [SMEM_SPEC, pair_s...  38.3 us
    pallas_call x2, Pallas kernels, att_call(): call(att_kernel, 'attention_rows', (pairs,), [SMEM_SPEC, pair_spec(rows),...  25.5 us
    unnamed x100, local copies, waits for them, and re-layouts  23.4 us
    pallas_call x2, Pallas kernels, mlp_call(): call(functools.partial(mlp_kernel, last_layer), 'feed_forward_rows', (FF...  22.9 us
    pallas_call x2, Pallas kernels, mlp_back_call(): call(functools.partial(mlp_back_kernel, last_layer), 'feed_forward_grad_r...  22.4 us
    pallas_call x2, Pallas kernels, qkv_back_call(): call(qkv_back_kernel, 'qkv_grad_rows', (3,), [full, whole_spec((2, rows,...  16.2 us
  transfers between devices with their start and end apart: 14, of which 4 were waited for; matrix products, arithmetic and copies ran while one was open for 3% of the time, Pallas kernels for 37%

profile of v7, /device:TPU:0, one launch (start us, length us, event | category | flops | bytes accessed | tf_op | source)
XLA Modules:
  0.0 553.2 jit_solution(5289032227432917760)
XLA Ops:
  1.5 4.8 collective-permute-start
  6.3 1.3 collective-permute-start.1
  7.7 2.1 broadcast_select_fusion.19
  10.4 1.3 dynamic_slice.16
  14.3 1.2 slice.380
  16.8 1.3 fusion.42
  19.5 1.0 fusion.4
  22.0 2.5 pack_weights.1.block_ref
  24.5 1.0 copy-done.10
  25.5 137.9 %gather_weights.1 = (bf16[2,4,768,768]{3,2,1,0:T(8,128)(2,1)}, bf16[2,8,768,768]{3,2,1,0:T(8,128)(2,1)}, bf16[32,32,128]{2,1,0:T(8,128)(2,1)}, bf16[2,512,768]{2,1,0:T(8,128)(2,1)}, f32[20,128]{1,0:T(8,128)}) custom-call(f32[43]{0:T(128)} %w_ref.3, bf16[768,768]{1,0:T(8,128)(2,1)} %copy-done.10, bf16[32,128]{1,0:T(8,128)(2,1)} %pad_maximum_fusion.8.vec_ref, ...), custom_call_target="tpu_custom_call" | custom-call | flops 99999997952 | bytes 100000000 | tf_op jit(solution)/shard_map/gather_weights/pallas_call | solution.py:365
  163.5 1.1 fusion.41
  164.9 1.1 broadcast_select_fusion.18
  166.1 4.0 copy-done
  170.1 7.0 %qkv_rows.2 = (bf16[512,768]{1,0:T(8,128)(2,1)S(1)}, bf16[512,768]{1,0:T(8,128)(2,1)S(1)}, bf16[512,1536]{1,0:T(8,128)(2,1)S(1)}) custom-call(bf16[512,768]{1,0:T(8,128)(2,1)S(1)} %pad_maximum_fusion.2.x_ref, f32[1,768]{1,0:T(1,128)S(1)} %get-tuple-element.294.gain_ref, f32[1,768]{1,0:T(1,128)S(1)} %get-tuple-element.295.bias_ref, ...), custom_call_target="tpu_custom_call" | custom-call | flops 1811939328 | bytes 2359296 | tf_op jit(solution)/shard_map/qkv_rows/pallas_call | solution.py:484
  178.0 1.8 collective-permute-start.3
  180.9 2.0 collective-permute-done.3.ko_ref.vo_ref
  182.9 12.7 %attention_rows.2 = (bf16[512,768]{1,0:T(8,128)(2,1)S(1)}, f32[6,512,128]{2,1,0:T(8,128)S(1)}) custom-call(s32[4]{0:T(128)S(1)} %pad_add_fusion.2.meta_ref, bf16[512,768]{1,0:T(8,128)(2,1)S(1)} %get-tuple-element.144.q_ref, bf16[512,1536]{1,0:T(8,128)(2,1)S(1)} %get-tuple-element.145.k_ref.v_ref, bf16[512,1536]{1,0:T(8,128)(2,1)S(1)} %get-tuple-element.145.k_ref.v_ref, ...), custom_call_target="tpu_custom_call" | custom-call | flops 4026531840 | bytes 2359296 | tf_op jit(solution)/shard_map/attention_rows/pallas_call | solution.py:598
  195.8 1.0 copy-done.37
  196.8 11.3 %feed_forward_rows.2 = (bf16[512,768]{1,0:T(8,128)(2,1)S(1)}, bf16[512,768]{1,0:T(8,128)(2,1)S(1)}, bf16[512,3072]{1,0:T(8,128)(2,1)S(1)}, bf16[512,3072]{1,0:T(...) custom-call(f32[4]{0:T(128)S(1)} %pad_maximum_fusion.9.mix_ref, ...), custom_call_target="tpu_custom_call" | custom-call | flops 5435817984 | bytes 2359296 | tf_op jit(solution)/shard_map/feed_forward_rows/pallas_call | solution.py:692
  208.2 1.7 copy-done.18
  210.7 7.3 %qkv_rows.3 = (bf16[512,768]{1,0:T(8,128)(2,1)S(1)}, bf16[512,768]{1,0:T(8,128)(2,1)S(1)}, bf16[512,1536]{1,0:T(8,128)(2,1)S(1)}) custom-call(bf16[512,768]{1,0:T(8,128)(2,1)S(1)} %get-tuple-element.150.x_ref.dy_ref, f32[1,768]{1,0:T(1,128)S(1)} %get-tuple-element.299.gain_ref, f32[1,768]{1,0:T(1,128)S(1)} %get-tuple-element.300.bias_ref, ...), custom_call_target="tpu_custom_call" | custom-call | flops 1811939328 | bytes 2359296 | tf_op jit(solution)/shard_map/qkv_rows/pallas_call | solution.py:484
  219.7 1.2 collective-permute-start.6
  221.5 12.7 %attention_rows.3 = (bf16[512,768]{1,0:T(8,128)(2,1)S(1)}, f32[6,512,128]{2,1,0:T(8,128)S(1)}) custom-call(s32[4]{0:T(128)S(1)} %pad_add_fusion.2.meta_ref, bf16[512,768]{1,0:T(8,128)(2,1)S(1)} %get-tuple-element.151.q_ref, bf16[512,1536]{1,0:T(8,128)(2,1)S(1)} %get-tuple-element.152.k_ref.v_ref, bf16[512,1536]{1,0:T(8,128)(2,1)S(1)} %get-tuple-element.152.k_ref.v_ref, ...), custom_call_target="tpu_custom_call" | custom-call | flops 4026531840 | bytes 2359296 | tf_op jit(solution)/shard_map/attention_rows/pallas_call | solution.py:598
  234.3 4.8 collective-permute-done.6
  239.6 11.6 %feed_forward_rows.3 = (bf16[512,768]{1,0:T(8,128)(2,1)S(1)}, bf16[512,768]{1,0:T(8,128)(2,1)S(1)}, bf16[512,3072]{1,0:T(8,128)(2,1)S(1)}, bf16[512,3072]{1,0:T(...) custom-call(f32[4]{0:T(128)S(1)} %pad_maximum_fusion.9.mix_ref, ...), custom_call_target="tpu_custom_call" | custom-call | flops 5435817984 | bytes 2359296 | tf_op jit(solution)/shard_map/feed_forward_rows/pallas_call | solution.py:692
  251.3 1.7 copy-done.19
  253.0 1.1 collective-permute-start.7
  254.1 11.1 %feed_forward_grad_rows.2 = (bf16[512,768]{1,0:T(8,128)(2,1)S(1)}, bf16[512,3072]{1,0:T(8,128)(2,1)S(1)}, f32[1,3072]{1,0:T(1,128)S(1)}, bf16[512,768]{1,0:T(8,1...) custom-call(f32[4]{0:T(128)S(1)} %pad_maximum_fusion.9.mix_ref, ...), custom_call_target="tpu_custom_call" | custom-call | flops 5435817984 | bytes 2359296 | tf_op jit(solution)/shard_map/feed_forward_grad_rows/pallas_call | solution.py:800
  265.3 1.6 copy-done.20
  268.1 1.1 copy-done.28
  269.2 18.9 %attention_grad_rows.2 = (bf16[512,768]{1,0:T(8,128)(2,1)S(1)}, f32[2,512,768]{2,1,0:T(8,128)S(1)}, bf16[2,512,768]{2,1,0:T(8,128)(2,1)S(1)}) custom-call(s32[4]{0:T(128)S(1)} %pad_add_fusion.2.meta_ref, bf16[512,768]{1,0:T(8,128)(2,1)S(1)} %get-tuple-element.151.q_ref, bf16[512,1536]{1,0:T(8,128)(2,1)S(1)} %get-tuple-element.152.k_ref.v_ref, ...), custom_call_target="tpu_custom_call" | custom-call | flops 10066329600 | bytes 2359296 | tf_op jit(solution)/shard_map/attention_grad_rows/pallas_call | solution.py:915
  288.4 3.2 collective-permute-done.8.got_ref
  291.6 5.8 %qkv_grad_rows.2 = (bf16[512,2304]{1,0:T(8,128)(2,1)S(1)}, f32[1,2304]{1,0:T(1,128)S(1)}, bf16[512,768]{1,0:T(8,128)(2,1)S(1)}, f32[8,768]{1,0:T(8,128)S(1)}) custom-call(bf16[512,768]{1,0:T(8,128)(2,1)S(1)} %get-tuple-element.164.dq_ref, f32[2,512,768]{2,1,0:T(8,128)S(1)} %get-tuple-element.165.own_ref, ...), custom_call_target="tpu_custom_call" | custom-call | flops 1811939328 | bytes 2359296 | tf_op jit(solution)/shard_map/qkv_grad_rows/pallas_call | solution.py:999
  297.4 1.4 copy-done.22
  299.7 11.3 %feed_forward_grad_rows.3 = (bf16[512,768]{1,0:T(8,128)(2,1)S(1)}, bf16[512,3072]{1,0:T(8,128)(2,1)S(1)}, f32[1,3072]{1,0:T(1,128)S(1)}, bf16[512,768]{1,0:T(8,1...) custom-call(f32[4]{0:T(128)S(1)} %pad_maximum_fusion.9.mix_ref, ...), custom_call_target="tpu_custom_call" | custom-call | flops 5435817984 | bytes 2359296 | tf_op jit(solution)/shard_map/feed_forward_grad_rows/pallas_call | solution.py:800
  311.0 1.6 copy-done.21
  315.3 19.4 %attention_grad_rows.3 = (bf16[512,768]{1,0:T(8,128)(2,1)S(1)}, f32[2,512,768]{2,1,0:T(8,128)S(1)}, bf16[2,512,768]{2,1,0:T(8,128)(2,1)}) custom-call(s32[4]{0:T(128)S(1)} %pad_add_fusion.2.meta_ref, bf16[512,768]{1,0:T(8,128)(2,1)S(1)} %copy-done.36, bf16[512,1536]{1,0:T(8,128)(2,1)S(1)} %copy-done.24, bf16[512,1536]{1,0:T(8,128)(2,1)S(1)} %copy-done.24, ...), custom_call_target="tpu_custom_call" | custom-call | flops 10066329600 | bytes 2359296 | tf_op jit(solution)/shard_map/attention_grad_rows/pallas_call | solution.py:915
  334.7 1.7 copy-done.9
  342.9 1.1 copy-done.42
  344.0 10.4 %qkv_grad_rows.3 = (bf16[512,2304]{1,0:T(8,128)(2,1)}, f32[1,2304]{1,0:T(1,128)}, bf16[512,768]{1,0:T(8,128)(2,1)}, f32[8,768]{1,0:T(8,128)}) custom-call(bf16[512,768]{1,0:T(8,128)(2,1)} %copy-done.13, f32[2,512,768]{2,1,0:T(8,128)} %copy-done.9, bf16[2,512,768]{2,1,0:T(8,128)(2,1)} %copy-done.42, f32[512,128]{1,0:T(8,128)} %copy-done.6, ...), custom_call_target="tpu_custom_call" | custom-call | flops 1811939328 | bytes 2359296 | tf_op jit(solution)/shard_map/qkv_grad_rows/pallas_call | solution.py:999
  356.0 2.7 concatenate.220
  358.7 163.4 %reduce_gradients.1 = (bf16[768,768]{1,0:T(8,128)(2,1)}, f32[200,128]{1,0:T(8,128)}) custom-call(f32[176,128]{1,0:T(8,128)} %bitcast.171, bf16[20,512,768]{2,1,0:T(8,128)(2,1)} %hist_ref.3, bf16[512,768]{1,0:T(8,128)(2,1)} %pad_maximum_fusion.5.dy_ref, bf16[512,768]{1,0:T(8,128)(2,1)} %copy-done.30, bf16[512,3072]{1,0:T(8,128)(2,1)} %copy-done.21, ...), custom_call_target="tpu_custom_call" | custom-call | flops 99999997952 | bytes 100000000 | tf_op jit(solution)/shard_map/reduce_gradients/pallas_call | solution.py:1788
  527.2 1.3 collective-permute-start.12
  528.5 1.3 collective-permute-start.13
  531.3 1.3 multiply_add_fusion
  532.9 8.2 %history_grads.1 = bf16[20,512,768]{2,1,0:T(8,128)(2,1)} custom-call(f32[43]{0:T(128)S(1)} %copy-done.17, bf16[512,768]{1,0:T(8,128)(2,1)S(1)} %copy-done.8, bf16[512,768]{1,0:T(8,128)(2,1)S(1)} %copy-done.5), custom_call_target="tpu_custom_call" | custom-call | flops 31457280 | bytes 2359296 | tf_op jit(solution)/shard_map/history_grads/pallas_call | solution.py:1202
  542.4 9.1 %adamw_step.1 = (f32[1,590496]{1,0:T(1,128)}, f32[1,590496]{1,0:T(1,128)}, f32[1,590496]{1,0:T(1,128)}, f32[1,590496]{1,0:T(1,128)}) custom-call(s32[4]{0:T(128)} %pad_add_fusion.3.meta_ref, bf16[768,768]{1,0:T(8,128)(2,1)} %get-tuple-element.204.tile_ref, f32[1,768]{1,0:T(1,128)} %broadcast_select_fusion.22.first_ref, f32[6,768]{1,0:T(8,128)} %fusion.9.before_ref, ...), custom_call_target="tpu_custom_call" | custom-call | flops 11809920 | bytes 2359296 | tf_op jit(solution)/shard_map/adamw_step/pallas_call | solution.py:1257
  551.5 1.3 maximum_convert_fusion
  (182 shorter events, 29.2 us)
Async XLA Ops:
  1.5 20.6 %collective-permute-start = (bf16[16,128]{1,0:T(8,128)(2,1)S(1)}, bf16[16,128]{1,0:T(8,128)(2,1)S(1)}, u32[]{:S(2)}, u32[]{:S(2)}) collective-permute-start(bf16[16,128]{1,0:T(8,128)(2,1)S(1)} %bitcast.172), channel_id=1, source_target_pairs={{0,1},{1,2},{2,3},{3,4},{4,5},{5,6},{6,7},{8,9},{9,10},{10,11},{11... | collective-permute-start | bytes 12296 | tf_op jit(solution)/shard_map/ppermute | solution.py:1129
  6.3 15.6 %collective-permute-start.1 = (bf16[16,128]{1,0:T(8,128)(2,1)S(1)}, bf16[16,128]{1,0:T(8,128)(2,1)S(1)}, u32[]{:S(2)}, u32[]{:S(2)}) collective-permute-start(bf16[16,128]{1,0:T(8,128)(2,1)S(1)} %bitcast.174), channel_id=1, source_target_pairs={{1,0},{2,1},{3,2},{4,3},{5,4},{6,5},{7,6},{9,8},{10,9},{11,10},{12... | collective-permute-start | bytes 12296 | tf_op jit(solution)/shard_map/ppermute | solution.py:1130
  7.6 14.4 %copy-start.2 = (f32[1,590496]{1,0:T(1,128)S(1)}, f32[1,590496]{1,0:T(1,128)}, u32[]{:S(2)}) copy-start(f32[1,590496]{1,0:T(1,128)} %p_ref.3) | copy-start | bytes 7085956
  9.7 155.2 %collective-permute-start.2 = (bf16[256,768]{1,0:T(8,128)(2,1)}, bf16[256,768]{1,0:T(8,128)(2,1)}, u32[]{:S(2)}, u32[]{:S(2)}) collective-permute-start(bf16[256,768]{1,0:T(8,128)(2,1)} %broadcast_select_fusion.19), channel_id=1, source_target_pairs={{0,24},{8,16},{16,8},{24,0},{1,25},{9,17},{17,9},{25,1},{2,26},{10... | collective-permute-start | bytes 1179656 | tf_op jit(solution)/shard_map/ppermute | solution.py:54
  20.8 293.2 %copy-start.6 = (f32[512,128]{1,0:T(8,128)}, f32[512,128]{1,0:T(8,128)S(1)}, u32[]{:S(2)}) copy-start(f32[512,128]{1,0:T(8,128)S(1)} %pad_maximum_fusion.6.cos_ref) | copy-start | bytes 786436
  21.1 292.9 %copy-start.7 = (f32[512,128]{1,0:T(8,128)}, f32[512,128]{1,0:T(8,128)S(1)}, u32[]{:S(2)}) copy-start(f32[512,128]{1,0:T(8,128)S(1)} %pad_maximum_fusion.7.sin_ref) | copy-start | bytes 786436
  166.1 30.7 %copy-start.1 = (bf16[512,768]{1,0:T(8,128)(2,1)}, bf16[512,768]{1,0:T(8,128)(2,1)S(1)}, u32[]{:S(2)}) copy-start(bf16[512,768]{1,0:T(8,128)(2,1)S(1)} %pad_maximum_fusion.2.x_ref) | copy-start | bytes 2359300
  166.1 4.0 copy-start
  170.1 9.9 %copy-start.39 = (bf16[2,512,768]{2,1,0:T(8,128)(2,1)S(1)}, bf16[2,512,768]{2,1,0:T(8,128)(2,1)}, u32[]{:S(2)}) copy-start(bf16[2,512,768]{2,1,0:T(8,128)(2,1)} %get-tuple-element.141) | copy-start | bytes 4718596
  178.0 17.6 %copy-start.23 = (bf16[512,1536]{1,0:T(8,128)(2,1)}, bf16[512,1536]{1,0:T(8,128)(2,1)S(1)}, u32[]{:S(2)}) copy-start(bf16[512,1536]{1,0:T(8,128)(2,1)S(1)} %get-tuple-element.145.k_ref.v_ref) | copy-start | bytes 4718596
  178.0 17.6 %copy-start.35 = (bf16[512,768]{1,0:T(8,128)(2,1)}, bf16[512,768]{1,0:T(8,128)(2,1)S(1)}, u32[]{:S(2)}) copy-start(bf16[512,768]{1,0:T(8,128)(2,1)S(1)} %get-tuple-element.144.q_ref) | copy-start | bytes 2359300
  178.0 4.9 collective-permute-start.3
  180.0 15.7 %collective-permute-start.4 = (bf16[256,768]{1,0:T(8,128)(2,1)S(1)}, bf16[256,768]{1,0:T(8,128)(2,1)S(1)}, u32[]{:S(2)}, u32[]{:S(2)}) collective-permute-start(bf16[256,768]{1,0:T(8,128)(2,1)S(1)} %select_bitcast_fusion), channel_id=1, source_target_pairs={{0,24},{8,16},{16,8},{24,0},{1,25},{9,17},{17,9},{25,1},{2,26},{10... | collective-permute-start | bytes 1179656 | tf_op jit(solution)/shard_map/ppermute | solution.py:54
  182.9 12.8 %copy-start.25 = (bf16[512,1536]{1,0:T(8,128)(2,1)}, bf16[512,1536]{1,0:T(8,128)(2,1)S(1)}, u32[]{:S(2)}) copy-start(bf16[512,1536]{1,0:T(8,128)(2,1)S(1)} %collective-permute-done.3.ko_ref.vo_ref) | copy-start | bytes 4718596
  182.9 13.9 %slice-start = ((s8[9437184]{0:T(1024)(128)(4,1)}), s8[4194304]{0:T(1024)(128)(4,1)S(1)}, s32[]{:S(2)}) async-start(s8[9437184]{0:T(1024)(128)(4,1)} %bitcast.154), calls=%async_computation | async-start | bytes 8388608
  182.9 13.9 %slice-start.1 = ((s8[9437184]{0:T(1024)(128)(4,1)}), s8[4194304]{0:T(1024)(128)(4,1)S(1)}, s32[]{:S(2)}) async-start(s8[9437184]{0:T(1024)(128)(4,1)} %bitcast.154), calls=%async_computation.1 | async-start | bytes 8388608
  182.9 13.9 %slice-start.2 = ((s8[9437184]{0:T(1024)(128)(4,1)}), s8[1048576]{0:T(1024)(128)(4,1)S(1)}, s32[]{:S(2)}) async-start(s8[9437184]{0:T(1024)(128)(4,1)} %bitcast.154), calls=%async_computation.2 | async-start | bytes 2097152
  195.7 118.3 %copy-start.14 = (bf16[512,768]{1,0:T(8,128)(2,1)}, bf16[512,768]{1,0:T(8,128)(2,1)S(1)}, u32[]{:S(2)}) copy-start(bf16[512,768]{1,0:T(8,128)(2,1)S(1)} %get-tuple-element.147.o_ref.refs_6_) | copy-start | bytes 2359300
  208.1 1.7 copy-start.18
  210.7 80.9 %copy-start.3 = (bf16[512,768]{1,0:T(8,128)(2,1)}, bf16[512,768]{1,0:T(8,128)(2,1)S(1)}, u32[]{:S(2)}) copy-start(bf16[512,768]{1,0:T(8,128)(2,1)S(1)} %get-tuple-element.156.rest_0_.c_ref) | copy-start | bytes 2359300
  218.0 3.5 collective-permute-start.5
  219.7 19.4 %collective-permute-start.6 = (bf16[2,256,768]{2,1,0:T(8,128)(2,1)S(1)}, bf16[2,256,768]{2,1,0:T(8,128)(2,1)S(1)}, u32[]{:S(2)}, u32[]{:S(2)}) collective-permute-start(bf16[2,256,768]{2,1,0:T(8,128)(2,1)S(1)} %broadcast_select_fusion.2), channel_id=1, source_target_pairs={{0,24},{8,16},{16,8},{24,0},{1,25},{9,17},{17,9},{25,1},{2,26},{10... | collective-permute-start | bytes 2359304 | tf_op jit(solution)/shard_map/ppermute | solution.py:54
  221.5 12.7 %copy-start.27 = (bf16[512,1536]{1,0:T(8,128)(2,1)}, bf16[512,1536]{1,0:T(8,128)(2,1)S(1)}, u32[]{:S(2)}) copy-start(bf16[512,1536]{1,0:T(8,128)(2,1)S(1)} %collective-permute-done.5.ko_ref.vo_ref) | copy-start | bytes 4718596
  234.3 33.8 %copy-start.15 = (bf16[512,768]{1,0:T(8,128)(2,1)}, bf16[512,768]{1,0:T(8,128)(2,1)S(1)}, u32[]{:S(2)}) copy-start(bf16[512,768]{1,0:T(8,128)(2,1)S(1)} %get-tuple-element.155.o_ref.refs_14_) | copy-start | bytes 2359300
  251.2 1.7 copy-start.19
  253.0 13.9 %collective-permute-start.7 = (bf16[256,768]{1,0:T(8,128)(2,1)S(1)}, bf16[256,768]{1,0:T(8,128)(2,1)S(1)}, u32[]{:S(2)}, u32[]{:S(2)}) collective-permute-start(bf16[256,768]{1,0:T(8,128)(2,1)S(1)} %broadcast_select_fusion.15), channel_id=1, source_target_pairs={{0,24},{8,16},{16,8},{24,0},{1,25},{9,17},{17,9},{25,1},{2,26},{10... | collective-permute-start | bytes 1179656 | tf_op jit(solution)/shard_map/ppermute | solution.py:54
  265.3 1.6 copy-start.20
  266.9 24.7 %copy-start.11 = (bf16[512,768]{1,0:T(8,128)(2,1)}, bf16[512,768]{1,0:T(8,128)(2,1)S(1)}, u32[]{:S(2)}) copy-start(bf16[512,768]{1,0:T(8,128)(2,1)S(1)} %get-tuple-element.167.dh_ref.refs_15_) | copy-start | bytes 2359300
  266.9 2.3 copy-start.28
  288.1 3.5 collective-permute-start.8
  298.8 13.8 %collective-permute-start.9 = (bf16[256,768]{1,0:T(8,128)(2,1)S(1)}, bf16[256,768]{1,0:T(8,128)(2,1)S(1)}, u32[]{:S(2)}, u32[]{:S(2)}) collective-permute-start(bf16[256,768]{1,0:T(8,128)(2,1)S(1)} %broadcast_select_fusion.11), channel_id=1, source_target_pairs={{0,24},{8,16},{16,8},{24,0},{1,25},{9,17},{17,9},{25,1},{2,26},{10... | collective-permute-start | bytes 1179656 | tf_op jit(solution)/shard_map/ppermute | solution.py:54
  299.7 14.4 %copy-start.36 = (bf16[512,768]{1,0:T(8,128)(2,1)S(1)}, bf16[512,768]{1,0:T(8,128)(2,1)}, u32[]{:S(2)}) copy-start(bf16[512,768]{1,0:T(8,128)(2,1)} %copy-done.35) | copy-start | bytes 2359300
  299.7 14.4 %copy-start.38 = (f32[6,512,128]{2,1,0:T(8,128)S(1)}, f32[6,512,128]{2,1,0:T(8,128)}, u32[]{:S(2)}) copy-start(f32[6,512,128]{2,1,0:T(8,128)} %copy-done.37) | copy-start | bytes 4718596
  312.6 2.3 copy-start.24
  312.6 2.7 copy-start.26
  315.3 22.3 %copy-start.46 = (s32[2,8]{1,0:T(2,128)S(1)}, s32[2,8]{1,0:T(2,128)}, u32[]{:S(2)}) copy-start(s32[2,8]{1,0:T(2,128)} %constant.247.clone) | copy-start | bytes 196
  315.3 26.1 %copy-start.43 = (f32[20,128]{1,0:T(8,128)S(1)}, f32[20,128]{1,0:T(8,128)}, u32[]{:S(2)}) copy-start(f32[20,128]{1,0:T(8,128)} %get-tuple-element.189) | copy-start | bytes 30724
  334.7 1.7 copy-start.9
  337.3 5.6 %collective-permute-start.10 = (bf16[2,512,768]{2,1,0:T(8,128)(2,1)}, bf16[2,512,768]{2,1,0:T(8,128)(2,1)S(1)}, u32[]{:S(2)}, u32[]{:S(2)}) collective-permute-start(bf16[2,512,768]{2,1,0:T(8,128)(2,1)} %get-tuple-element.176), channel_id=1, source_target_pairs={{0,8},{8,0},{16,24},{24,16},{1,9},{9,1},{17,25},{25,17},{2,10},{10... | collective-permute-start | bytes 4718600 | tf_op jit(solution)/shard_map/ppermute | solution.py:58
  358.7 172.5 %copy-start.41 = (bf16[512,768]{1,0:T(8,128)(2,1)S(1)}, bf16[512,768]{1,0:T(8,128)(2,1)}, u32[]{:S(2)}) copy-start(bf16[512,768]{1,0:T(8,128)(2,1)} %get-tuple-element.178) | copy-start | bytes 2359300
  522.1 9.2 %copy-start.17 = (f32[43]{0:T(128)S(1)}, f32[43]{0:T(128)}, u32[]{:S(2)}) copy-start(f32[43]{0:T(128)} %w_ref.3) | copy-start | bytes 520
  522.1 9.2 %copy-start.44 = (f32[43]{0:T(128)S(1)}, f32[43]{0:T(128)}, u32[]{:S(2)}) copy-start(f32[43]{0:T(128)} %param.31) | copy-start | bytes 520
  522.1 9.2 %copy-start.45 = (f32[43]{0:T(128)S(1)}, f32[43]{0:T(128)}, u32[]{:S(2)}) copy-start(f32[43]{0:T(128)} %param.30) | copy-start | bytes 520
  522.1 10.7 %copy-start.5 = (bf16[512,768]{1,0:T(8,128)(2,1)S(1)}, bf16[512,768]{1,0:T(8,128)(2,1)}, u32[]{:S(2)}) copy-start(bf16[512,768]{1,0:T(8,128)(2,1)} %cot_ref.3) | copy-start | bytes 2359300
  522.1 10.7 %copy-start.8 = (bf16[512,768]{1,0:T(8,128)(2,1)S(1)}, bf16[512,768]{1,0:T(8,128)(2,1)}, u32[]{:S(2)}) copy-start(bf16[512,768]{1,0:T(8,128)(2,1)} %pad_maximum_fusion.5.dy_ref) | copy-start | bytes 2359300
  527.2 13.9 %collective-permute-start.12 = (f32[3,768]{1,0:T(4,128)S(1)}, f32[3,768]{1,0:T(4,128)S(1)}, u32[]{:S(2)}, u32[]{:S(2)}) collective-permute-start(f32[3,768]{1,0:T(4,128)S(1)} %convert_bitcast_fusion.1), channel_id=1, source_target_pairs={{0,1},{1,2},{2,3},{3,4},{4,5},{5,6},{6,7},{8,9},{9,10},{10,11},{11... | collective-permute-start | bytes 27656 | tf_op jit(solution)/shard_map/ppermute | solution.py:1294
  528.5 12.6 %collective-permute-start.13 = (f32[3,768]{1,0:T(4,128)S(1)}, f32[3,768]{1,0:T(4,128)S(1)}, u32[]{:S(2)}, u32[]{:S(2)}) collective-permute-start(f32[3,768]{1,0:T(4,128)S(1)} %convert_bitcast_fusion), channel_id=1, source_target_pairs={{1,0},{2,1},{3,2},{4,3},{5,4},{6,5},{7,6},{9,8},{10,9},{11,10},{12... | collective-permute-start | bytes 27656 | tf_op jit(solution)/shard_map/ppermute | solution.py:1295
  531.2 20.3 %collective-permute-start.11 = (bf16[256,768]{1,0:T(8,128)(2,1)S(1)}, bf16[256,768]{1,0:T(8,128)(2,1)S(1)}, u32[]{:S(2)}, u32[]{:S(2)}) collective-permute-start(bf16[256,768]{1,0:T(8,128)(2,1)S(1)} %broadcast_select_fusion.7), channel_id=1, source_target_pairs={{0,24},{8,16},{16,8},{24,0},{1,25},{9,17},{17,9},{25,1},{2,26},{10... | collective-permute-start | bytes 1179656 | tf_op jit(solution)/shard_map/ppermute | solution.py:54
  (16 other events, 19.8 us)

commit v8 on v7

--- a/solution.py
+++ b/solution.py
@@ -942,6 +942,7 @@
             pltpu.VMEM((2 * rows, 128), f32),
         ],
         50 * rows * rows * D,
+        WIDE_LIMIT,
     )(meta, q, kv, kv, kv_other, kv_other, datt, mixed, lse, cosine, sine)
 
 

time: 559 us -> 562 us (level)
    unnamed x100 -> x116, local copies, waits for them, and re-layouts: 23.4 us -> 23.8 us
where the time goes in v8:
time: 562 us; the launch traced here: 556 us
  Pallas kernels  462 us (82%)
  local copies, waits for them, and re-layouts  39.2 us (7%)
  other arithmetic  18.4 us (3%)
  starting transfers between devices  17.5 us (3%)
  waiting for transfers between devices  10.7 us (2%)
  between operations  8.57 us (2%)
    pallas_call x1, Pallas kernels, reduce_call(): pl.pallas_call(functools.partial(reduce_kernel, counts), in_specs=[in_vme...  164 us
    pallas_call x1, Pallas kernels, gather_weights(): pl.pallas_call(body, in_specs=[SMEM_SPEC] + [any_spec] * 3 + [in_vmem], o...  138 us
    pallas_call x2, Pallas kernels, att_back_call(): call(att_back_kernel, 'attention_grad_rows', (pairs,), [SMEM_SPEC, pair_s...  39 us
    pallas_call x2, Pallas kernels, att_call(): call(att_kernel, 'attention_rows', (pairs,), [SMEM_SPEC, pair_spec(rows),...  25.5 us
    unnamed x116, local copies, waits for them, and re-layouts  23.8 us
    pallas_call x2, Pallas kernels, mlp_call(): call(functools.partial(mlp_kernel, last_layer), 'feed_forward_rows', (FF...  22.8 us
    pallas_call x2, Pallas kernels, mlp_back_call(): call(functools.partial(mlp_back_kernel, last_layer), 'feed_forward_grad_r...  22.2 us
    pallas_call x2, Pallas kernels, qkv_back_call(): call(qkv_back_kernel, 'qkv_grad_rows', (3,), [full, whole_spec((2, rows,...  16.2 us
  transfers between devices with their start and end apart: 14, of which 4 were waited for; matrix products, arithmetic and copies ran while one was open for 3% of the time, Pallas kernels for 37%

profile of v8, /device:TPU:0, one launch (start us, length us, event | category | flops | bytes accessed | tf_op | source)
XLA Modules:
  0.0 556.2 jit_solution(17813423553995874270)
XLA Ops:
  1.5 4.8 collective-permute-start
  6.3 1.3 collective-permute-start.1
  7.7 2.1 broadcast_select_fusion.19
  10.4 1.3 dynamic_slice.16
  14.2 1.2 slice.380
  16.8 1.3 fusion.42
  22.0 2.5 pack_weights.1.block_ref
  25.5 137.9 %gather_weights.1 = (bf16[2,4,768,768]{3,2,1,0:T(8,128)(2,1)}, bf16[2,8,768,768]{3,2,1,0:T(8,128)(2,1)}, bf16[32,32,128]{2,1,0:T(8,128)(2,1)}, bf16[2,512,768]{2,1,0:T(8,128)(2,1)}, f32[20,128]{1,0:T(8,128)}) custom-call(f32[43]{0:T(128)} %w_ref.3, bf16[768,768]{1,0:T(8,128)(2,1)} %copy-done.15, bf16[32,128]{1,0:T(8,128)(2,1)} %pad_maximum_fusion.8.vec_ref, ...), custom_call_target="tpu_custom_call" | custom-call | flops 99999997952 | bytes 100000000 | tf_op jit(solution)/shard_map/gather_weights/pallas_call | solution.py:365
  163.5 1.1 fusion.41
  164.9 1.1 broadcast_select_fusion.18
  166.1 4.0 copy-done
  170.1 7.2 %qkv_rows.2 = (bf16[512,768]{1,0:T(8,128)(2,1)S(1)}, bf16[512,768]{1,0:T(8,128)(2,1)S(1)}, bf16[512,1536]{1,0:T(8,128)(2,1)S(1)}) custom-call(bf16[512,768]{1,0:T(8,128)(2,1)S(1)} %pad_maximum_fusion.2.x_ref, f32[1,768]{1,0:T(1,128)S(1)} %get-tuple-element.294.gain_ref, f32[1,768]{1,0:T(1,128)S(1)} %get-tuple-element.295.bias_ref, ...), custom_call_target="tpu_custom_call" | custom-call | flops 1811939328 | bytes 2359296 | tf_op jit(solution)/shard_map/qkv_rows/pallas_call | solution.py:484
  178.2 1.8 collective-permute-start.3
  181.1 2.0 collective-permute-done.3.ko_ref.vo_ref
  183.0 12.7 %attention_rows.2 = (bf16[512,768]{1,0:T(8,128)(2,1)S(1)}, f32[6,512,128]{2,1,0:T(8,128)S(1)}) custom-call(s32[4]{0:T(128)S(1)} %pad_add_fusion.2.meta_ref, bf16[512,768]{1,0:T(8,128)(2,1)S(1)} %get-tuple-element.144.q_ref, bf16[512,1536]{1,0:T(8,128)(2,1)S(1)} %get-tuple-element.145.k_ref.v_ref, bf16[512,1536]{1,0:T(8,128)(2,1)S(1)} %get-tuple-element.145.k_ref.v_ref, ...), custom_call_target="tpu_custom_call" | custom-call | flops 4026531840 | bytes 2359296 | tf_op jit(solution)/shard_map/attention_rows/pallas_call | solution.py:598
  196.0 1.0 copy-done.45
  197.2 11.2 %feed_forward_rows.2 = (bf16[512,768]{1,0:T(8,128)(2,1)S(1)}, bf16[512,768]{1,0:T(8,128)(2,1)S(1)}, bf16[512,3072]{1,0:T(8,128)(2,1)S(1)}, bf16[512,3072]{1,0:T(...) custom-call(f32[4]{0:T(128)S(1)} %pad_maximum_fusion.9.mix_ref, ...), custom_call_target="tpu_custom_call" | custom-call | flops 5435817984 | bytes 2359296 | tf_op jit(solution)/shard_map/feed_forward_rows/pallas_call | solution.py:692
  209.3 7.5 %qkv_rows.3 = (bf16[512,768]{1,0:T(8,128)(2,1)S(1)}, bf16[512,768]{1,0:T(8,128)(2,1)S(1)}, bf16[512,1536]{1,0:T(8,128)(2,1)S(1)}) custom-call(bf16[512,768]{1,0:T(8,128)(2,1)S(1)} %get-tuple-element.150.x_ref.dy_ref, f32[1,768]{1,0:T(1,128)S(1)} %get-tuple-element.299.gain_ref, f32[1,768]{1,0:T(1,128)S(1)} %get-tuple-element.300.bias_ref, ...), custom_call_target="tpu_custom_call" | custom-call | flops 1811939328 | bytes 2359296 | tf_op jit(solution)/shard_map/qkv_rows/pallas_call | solution.py:484
  217.4 1.2 copy-done.5
  218.9 1.2 collective-permute-start.6
  220.4 12.7 %attention_rows.3 = (bf16[512,768]{1,0:T(8,128)(2,1)S(1)}, f32[6,512,128]{2,1,0:T(8,128)S(1)}) custom-call(s32[4]{0:T(128)S(1)} %pad_add_fusion.2.meta_ref, bf16[512,768]{1,0:T(8,128)(2,1)S(1)} %get-tuple-element.151.q_ref, bf16[512,1536]{1,0:T(8,128)(2,1)S(1)} %get-tuple-element.152.k_ref.v_ref, bf16[512,1536]{1,0:T(8,128)(2,1)S(1)} %get-tuple-element.152.k_ref.v_ref, ...), custom_call_target="tpu_custom_call" | custom-call | flops 4026531840 | bytes 2359296 | tf_op jit(solution)/shard_map/attention_rows/pallas_call | solution.py:598
  233.2 5.1 collective-permute-done.6
  238.8 11.6 %feed_forward_rows.3 = (bf16[512,768]{1,0:T(8,128)(2,1)S(1)}, bf16[512,768]{1,0:T(8,128)(2,1)S(1)}, bf16[512,3072]{1,0:T(8,128)(2,1)S(1)}, bf16[512,3072]{1,0:T(...) custom-call(f32[4]{0:T(128)S(1)} %pad_maximum_fusion.9.mix_ref, ...), custom_call_target="tpu_custom_call" | custom-call | flops 5435817984 | bytes 2359296 | tf_op jit(solution)/shard_map/feed_forward_rows/pallas_call | solution.py:692
  250.5 1.7 copy-done.27
  252.2 1.2 collective-permute-start.7
  253.3 11.1 %feed_forward_grad_rows.2 = (bf16[512,768]{1,0:T(8,128)(2,1)S(1)}, bf16[512,3072]{1,0:T(8,128)(2,1)S(1)}, f32[1,3072]{1,0:T(1,128)S(1)}, bf16[512,768]{1,0:T(8,1...) custom-call(f32[4]{0:T(128)S(1)} %pad_maximum_fusion.9.mix_ref, ...), custom_call_target="tpu_custom_call" | custom-call | flops 5435817984 | bytes 2359296 | tf_op jit(solution)/shard_map/feed_forward_grad_rows/pallas_call | solution.py:800
  264.5 1.6 copy-done.28
  266.2 1.1 pad_maximum_fusion.4
  267.6 19.6 %attention_grad_rows.2 = (bf16[512,768]{1,0:T(8,128)(2,1)}, f32[2,512,768]{2,1,0:T(8,128)}, bf16[2,512,768]{2,1,0:T(8,128)(2,1)}) custom-call(s32[4]{0:T(128)} %copy-done.25, bf16[512,768]{1,0:T(8,128)(2,1)} %copy-done.42, bf16[512,1536]{1,0:T(8,128)(2,1)} %copy-done.33, bf16[512,1536]{1,0:T(8,128)(2,1)} %copy-done.33, bf16[512,1536]{1,0:T(8,128)(2,1)} %copy-done.34, ...), custom_call_target="tpu_custom_call" | custom-call | flops 10066329600 | bytes 2359296 | tf_op jit(solution)/shard_map/attention_grad_rows/pallas_call | solution.py:915
  287.5 3.3 collective-permute-done.8.got_ref
  290.9 3.7 copy-done.1
  294.5 1.9 copy-done.14
  296.4 1.1 copy-done.18
  297.6 5.8 %qkv_grad_rows.2 = (bf16[512,2304]{1,0:T(8,128)(2,1)S(1)}, f32[1,2304]{1,0:T(1,128)S(1)}, bf16[512,768]{1,0:T(8,128)(2,1)S(1)}, f32[8,768]{1,0:T(8,128)S(1)}) custom-call(bf16[512,768]{1,0:T(8,128)(2,1)S(1)} %copy-done.18, f32[2,512,768]{2,1,0:T(8,128)S(1)} %copy-done.14, bf16[2,512,768]{2,1,0:T(8,128)(2,1)S(1)} %collective-permute-done.8.got_ref, ...), custom_call_target="tpu_custom_call" | custom-call | flops 1811939328 | bytes 2359296 | tf_op jit(solution)/shard_map/qkv_grad_rows/pallas_call | solution.py:1000
  305.1 11.0 %feed_forward_grad_rows.3 = (bf16[512,768]{1,0:T(8,128)(2,1)S(1)}, bf16[512,3072]{1,0:T(8,128)(2,1)S(1)}, f32[1,3072]{1,0:T(1,128)S(1)}, bf16[512,768]{1,0:T(8,1...) custom-call(f32[4]{0:T(128)S(1)} %pad_maximum_fusion.9.mix_ref, ...), custom_call_target="tpu_custom_call" | custom-call | flops 5435817984 | bytes 2359296 | tf_op jit(solution)/shard_map/feed_forward_grad_rows/pallas_call | solution.py:800
  316.1 1.6 copy-done.29
  317.9 1.1 pad_maximum_fusion.5.dy_ref
  319.4 19.5 %attention_grad_rows.3 = (bf16[512,768]{1,0:T(8,128)(2,1)}, f32[2,512,768]{2,1,0:T(8,128)}, bf16[2,512,768]{2,1,0:T(8,128)(2,1)}) custom-call(s32[4]{0:T(128)} %copy-done.25, bf16[512,768]{1,0:T(8,128)(2,1)} %copy-done.41, bf16[512,1536]{1,0:T(8,128)(2,1)} %copy-done.31, bf16[512,1536]{1,0:T(8,128)(2,1)} %copy-done.31, bf16[512,1536]{1,0:T(8,128)(2,1)} %copy-done.32, ...), custom_call_target="tpu_custom_call" | custom-call | flops 10066329600 | bytes 2359296 | tf_op jit(solution)/shard_map/attention_grad_rows/pallas_call | solution.py:915
  344.7 1.1 copy-done.50
  345.8 10.4 %qkv_grad_rows.3 = (bf16[512,2304]{1,0:T(8,128)(2,1)}, f32[1,2304]{1,0:T(1,128)}, bf16[512,768]{1,0:T(8,128)(2,1)}, f32[8,768]{1,0:T(8,128)}) custom-call(bf16[512,768]{1,0:T(8,128)(2,1)} %get-tuple-element.174.dq_ref, f32[2,512,768]{2,1,0:T(8,128)} %get-tuple-element.175.own_ref, bf16[2,512,768]{2,1,0:T(8,128)(2,1)} %copy-done.50, f32[512,128]{1,0:T(8,128)} %copy-done.7, ...), custom_call_target="tpu_custom_call" | custom-call | flops 1811939328 | bytes 2359296 | tf_op jit(solution)/shard_map/qkv_grad_rows/pallas_call | solution.py:1000
  357.8 2.7 concatenate.220
  360.4 163.6 %reduce_gradients.1 = (bf16[768,768]{1,0:T(8,128)(2,1)}, f32[200,128]{1,0:T(8,128)}) custom-call(f32[176,128]{1,0:T(8,128)} %bitcast.171, bf16[20,512,768]{2,1,0:T(8,128)(2,1)} %hist_ref.3, bf16[512,768]{1,0:T(8,128)(2,1)} %pad_maximum_fusion.5.dy_ref, bf16[512,768]{1,0:T(8,128)(2,1)} %copy-done.36, bf16[512,3072]{1,0:T(8,128)(2,1)} %copy-done.29, ...), custom_call_target="tpu_custom_call" | custom-call | flops 99999997952 | bytes 100000000 | tf_op jit(solution)/shard_map/reduce_gradients/pallas_call | solution.py:1789
  529.1 2.3 collective-permute-start.12
  531.5 1.3 collective-permute-start.13
  534.2 1.3 multiply_add_fusion
  535.8 8.2 %history_grads.1 = bf16[20,512,768]{2,1,0:T(8,128)(2,1)} custom-call(f32[43]{0:T(128)S(1)} %copy-done.24, bf16[512,768]{1,0:T(8,128)(2,1)S(1)} %copy-done.11, bf16[512,768]{1,0:T(8,128)(2,1)S(1)} %copy-done.6), custom_call_target="tpu_custom_call" | custom-call | flops 31457280 | bytes 2359296 | tf_op jit(solution)/shard_map/history_grads/pallas_call | solution.py:1203
  545.3 9.1 %adamw_step.1 = (f32[1,590496]{1,0:T(1,128)}, f32[1,590496]{1,0:T(1,128)}, f32[1,590496]{1,0:T(1,128)}, f32[1,590496]{1,0:T(1,128)}) custom-call(s32[4]{0:T(128)} %pad_add_fusion.3.meta_ref, bf16[768,768]{1,0:T(8,128)(2,1)} %get-tuple-element.204.tile_ref, f32[1,768]{1,0:T(1,128)} %broadcast_select_fusion.22.first_ref, f32[6,768]{1,0:T(8,128)} %fusion.9.before_ref, ...), custom_call_target="tpu_custom_call" | custom-call | flops 11809920 | bytes 2359296 | tf_op jit(solution)/shard_map/adamw_step/pallas_call | solution.py:1258
  554.5 1.3 maximum_convert_fusion
  (198 shorter events, 27.3 us)
Async XLA Ops:
  1.5 20.6 %collective-permute-start = (bf16[16,128]{1,0:T(8,128)(2,1)S(1)}, bf16[16,128]{1,0:T(8,128)(2,1)S(1)}, u32[]{:S(2)}, u32[]{:S(2)}) collective-permute-start(bf16[16,128]{1,0:T(8,128)(2,1)S(1)} %bitcast.172), channel_id=1, source_target_pairs={{0,1},{1,2},{2,3},{3,4},{4,5},{5,6},{6,7},{8,9},{9,10},{10,11},{11... | collective-permute-start | bytes 12296 | tf_op jit(solution)/shard_map/ppermute | solution.py:1130
  6.3 15.6 %collective-permute-start.1 = (bf16[16,128]{1,0:T(8,128)(2,1)S(1)}, bf16[16,128]{1,0:T(8,128)(2,1)S(1)}, u32[]{:S(2)}, u32[]{:S(2)}) collective-permute-start(bf16[16,128]{1,0:T(8,128)(2,1)S(1)} %bitcast.174), channel_id=1, source_target_pairs={{1,0},{2,1},{3,2},{4,3},{5,4},{6,5},{7,6},{9,8},{10,9},{11,10},{12... | collective-permute-start | bytes 12296 | tf_op jit(solution)/shard_map/ppermute | solution.py:1131
  7.6 14.4 %copy-start.3 = (f32[1,590496]{1,0:T(1,128)S(1)}, f32[1,590496]{1,0:T(1,128)}, u32[]{:S(2)}) copy-start(f32[1,590496]{1,0:T(1,128)} %p_ref.3) | copy-start | bytes 7085956
  9.7 155.2 %collective-permute-start.2 = (bf16[256,768]{1,0:T(8,128)(2,1)}, bf16[256,768]{1,0:T(8,128)(2,1)}, u32[]{:S(2)}, u32[]{:S(2)}) collective-permute-start(bf16[256,768]{1,0:T(8,128)(2,1)} %broadcast_select_fusion.19), channel_id=1, source_target_pairs={{0,24},{8,16},{16,8},{24,0},{1,25},{9,17},{17,9},{25,1},{2,26},{10... | collective-permute-start | bytes 1179656 | tf_op jit(solution)/shard_map/ppermute | solution.py:54
  20.8 188.5 %copy-start.7 = (f32[512,128]{1,0:T(8,128)}, f32[512,128]{1,0:T(8,128)S(1)}, u32[]{:S(2)}) copy-start(f32[512,128]{1,0:T(8,128)S(1)} %pad_maximum_fusion.6.cos_ref) | copy-start | bytes 786436
  21.1 188.2 %copy-start.9 = (f32[512,128]{1,0:T(8,128)}, f32[512,128]{1,0:T(8,128)S(1)}, u32[]{:S(2)}) copy-start(f32[512,128]{1,0:T(8,128)S(1)} %pad_maximum_fusion.7.sin_ref) | copy-start | bytes 786436
  166.1 30.9 %copy-start.2 = (bf16[512,768]{1,0:T(8,128)(2,1)}, bf16[512,768]{1,0:T(8,128)(2,1)S(1)}, u32[]{:S(2)}) copy-start(bf16[512,768]{1,0:T(8,128)(2,1)S(1)} %pad_maximum_fusion.2.x_ref) | copy-start | bytes 2359300
  166.1 4.0 copy-start
  170.1 10.0 %copy-start.47 = (bf16[2,512,768]{2,1,0:T(8,128)(2,1)S(1)}, bf16[2,512,768]{2,1,0:T(8,128)(2,1)}, u32[]{:S(2)}) copy-start(bf16[2,512,768]{2,1,0:T(8,128)(2,1)} %get-tuple-element.141) | copy-start | bytes 4718596
  178.2 17.6 %copy-start.31 = (bf16[512,1536]{1,0:T(8,128)(2,1)}, bf16[512,1536]{1,0:T(8,128)(2,1)S(1)}, u32[]{:S(2)}) copy-start(bf16[512,1536]{1,0:T(8,128)(2,1)S(1)} %get-tuple-element.145.k_ref.v_ref) | copy-start | bytes 4718596
  178.2 17.6 %copy-start.41 = (bf16[512,768]{1,0:T(8,128)(2,1)}, bf16[512,768]{1,0:T(8,128)(2,1)S(1)}, u32[]{:S(2)}) copy-start(bf16[512,768]{1,0:T(8,128)(2,1)S(1)} %get-tuple-element.144.q_ref) | copy-start | bytes 2359300
  178.2 4.8 collective-permute-start.3
  180.1 40.3 %copy-start.25 = (s32[4]{0:T(128)}, s32[4]{0:T(128)S(1)}, u32[]{:S(2)}) copy-start(s32[4]{0:T(128)S(1)} %pad_add_fusion.2.meta_ref) | copy-start | bytes 52
  180.1 15.7 %collective-permute-start.4 = (bf16[256,768]{1,0:T(8,128)(2,1)S(1)}, bf16[256,768]{1,0:T(8,128)(2,1)S(1)}, u32[]{:S(2)}, u32[]{:S(2)}) collective-permute-start(bf16[256,768]{1,0:T(8,128)(2,1)S(1)} %select_bitcast_fusion), channel_id=1, source_target_pairs={{0,24},{8,16},{16,8},{24,0},{1,25},{9,17},{17,9},{25,1},{2,26},{10... | collective-permute-start | bytes 1179656 | tf_op jit(solution)/shard_map/ppermute | solution.py:54
  183.0 12.8 %copy-start.32 = (bf16[512,1536]{1,0:T(8,128)(2,1)}, bf16[512,1536]{1,0:T(8,128)(2,1)S(1)}, u32[]{:S(2)}) copy-start(bf16[512,1536]{1,0:T(8,128)(2,1)S(1)} %collective-permute-done.3.ko_ref.vo_ref) | copy-start | bytes 4718596
  183.0 14.2 %slice-start = ((s8[9437184]{0:T(1024)(128)(4,1)}), s8[4194304]{0:T(1024)(128)(4,1)S(1)}, s32[]{:S(2)}) async-start(s8[9437184]{0:T(1024)(128)(4,1)} %bitcast.154), calls=%async_computation | async-start | bytes 8388608
  183.0 14.2 %slice-start.1 = ((s8[9437184]{0:T(1024)(128)(4,1)}), s8[4194304]{0:T(1024)(128)(4,1)S(1)}, s32[]{:S(2)}) async-start(s8[9437184]{0:T(1024)(128)(4,1)} %bitcast.154), calls=%async_computation.1 | async-start | bytes 8388608
  183.0 14.2 %slice-start.2 = ((s8[9437184]{0:T(1024)(128)(4,1)}), s8[1048576]{0:T(1024)(128)(4,1)S(1)}, s32[]{:S(2)}) async-start(s8[9437184]{0:T(1024)(128)(4,1)} %bitcast.154), calls=%async_computation.2 | async-start | bytes 2097152
  209.3 7.6 %copy-start.12 = (bf16[512,3072]{1,0:T(8,128)(2,1)}, bf16[512,3072]{1,0:T(8,128)(2,1)S(1)}, u32[]{:S(2)}) copy-start(bf16[512,3072]{1,0:T(8,128)(2,1)S(1)} %get-tuple-element.170.slope_ref) | copy-start | bytes 9437188
  209.3 7.6 %copy-start.26 = (bf16[512,3072]{1,0:T(8,128)(2,1)}, bf16[512,3072]{1,0:T(8,128)(2,1)S(1)}, u32[]{:S(2)}) copy-start(bf16[512,3072]{1,0:T(8,128)(2,1)S(1)} %get-tuple-element.192.refs_2_) | copy-start | bytes 9437188
  209.3 7.6 %copy-start.36 = (bf16[512,768]{1,0:T(8,128)(2,1)}, bf16[512,768]{1,0:T(8,128)(2,1)S(1)}, u32[]{:S(2)}) copy-start(bf16[512,768]{1,0:T(8,128)(2,1)S(1)} %get-tuple-element.190.refs_0_) | copy-start | bytes 2359300
  209.3 81.5 %copy-start.4 = (bf16[512,768]{1,0:T(8,128)(2,1)}, bf16[512,768]{1,0:T(8,128)(2,1)S(1)}, u32[]{:S(2)}) copy-start(bf16[512,768]{1,0:T(8,128)(2,1)S(1)} %get-tuple-element.156.rest_0_.c_ref) | copy-start | bytes 2359300
  216.9 3.5 collective-permute-start.5
  218.9 19.4 %collective-permute-start.6 = (bf16[2,256,768]{2,1,0:T(8,128)(2,1)S(1)}, bf16[2,256,768]{2,1,0:T(8,128)(2,1)S(1)}, u32[]{:S(2)}, u32[]{:S(2)}) collective-permute-start(bf16[2,256,768]{2,1,0:T(8,128)(2,1)S(1)} %broadcast_select_fusion.2), channel_id=1, source_target_pairs={{0,24},{8,16},{16,8},{24,0},{1,25},{9,17},{17,9},{25,1},{2,26},{10... | collective-permute-start | bytes 2359304 | tf_op jit(solution)/shard_map/ppermute | solution.py:54
  220.4 12.8 %copy-start.34 = (bf16[512,1536]{1,0:T(8,128)(2,1)}, bf16[512,1536]{1,0:T(8,128)(2,1)S(1)}, u32[]{:S(2)}) copy-start(bf16[512,1536]{1,0:T(8,128)(2,1)S(1)} %collective-permute-done.5.ko_ref.vo_ref) | copy-start | bytes 4718596
  233.2 5.5 copy-start.46
  233.2 5.6 %copy-start.20 = (bf16[512,768]{1,0:T(8,128)(2,1)}, bf16[512,768]{1,0:T(8,128)(2,1)S(1)}, u32[]{:S(2)}) copy-start(bf16[512,768]{1,0:T(8,128)(2,1)S(1)} %get-tuple-element.155.o_ref.refs_14_) | copy-start | bytes 2359300
  252.1 12.4 %copy-start.38 = (bf16[512,768]{1,0:T(8,128)(2,1)}, bf16[512,768]{1,0:T(8,128)(2,1)S(1)}, u32[]{:S(2)}) copy-start(bf16[512,768]{1,0:T(8,128)(2,1)S(1)} %get-tuple-element.196.refs_8_) | copy-start | bytes 2359300
  252.2 14.0 %collective-permute-start.7 = (bf16[256,768]{1,0:T(8,128)(2,1)S(1)}, bf16[256,768]{1,0:T(8,128)(2,1)S(1)}, u32[]{:S(2)}, u32[]{:S(2)}) collective-permute-start(bf16[256,768]{1,0:T(8,128)(2,1)S(1)} %broadcast_select_fusion.15), channel_id=1, source_target_pairs={{0,24},{8,16},{16,8},{24,0},{1,25},{9,17},{17,9},{25,1},{2,26},{10... | collective-permute-start | bytes 1179656 | tf_op jit(solution)/shard_map/ppermute | solution.py:54
  266.1 24.7 %copy-start.16 = (bf16[512,768]{1,0:T(8,128)(2,1)}, bf16[512,768]{1,0:T(8,128)(2,1)S(1)}, u32[]{:S(2)}) copy-start(bf16[512,768]{1,0:T(8,128)(2,1)S(1)} %get-tuple-element.167.dh_ref.refs_15_) | copy-start | bytes 2359300
  267.6 23.3 %copy-start.8 = (f32[512,128]{1,0:T(8,128)S(1)}, f32[512,128]{1,0:T(8,128)}, u32[]{:S(2)}) copy-start(f32[512,128]{1,0:T(8,128)} %copy-done.7) | copy-start | bytes 786436
  267.6 23.3 %copy-start.10 = (f32[512,128]{1,0:T(8,128)S(1)}, f32[512,128]{1,0:T(8,128)}, u32[]{:S(2)}) copy-start(f32[512,128]{1,0:T(8,128)} %copy-done.9) | copy-start | bytes 786436
  287.2 3.7 collective-permute-start.8
  297.6 6.6 %copy-start.13 = (bf16[512,3072]{1,0:T(8,128)(2,1)S(1)}, bf16[512,3072]{1,0:T(8,128)(2,1)}, u32[]{:S(2)}) copy-start(bf16[512,3072]{1,0:T(8,128)(2,1)} %copy-done.12) | copy-start | bytes 9437188
  303.4 12.8 %copy-start.30 = (bf16[512,2304]{1,0:T(8,128)(2,1)}, bf16[512,2304]{1,0:T(8,128)(2,1)S(1)}, u32[]{:S(2)}) copy-start(bf16[512,2304]{1,0:T(8,128)(2,1)S(1)} %get-tuple-element.201.refs_13_) | copy-start | bytes 7077892
  303.4 14.3 %collective-permute-start.9 = (bf16[256,768]{1,0:T(8,128)(2,1)S(1)}, bf16[256,768]{1,0:T(8,128)(2,1)S(1)}, u32[]{:S(2)}, u32[]{:S(2)}) collective-permute-start(bf16[256,768]{1,0:T(8,128)(2,1)S(1)} %broadcast_select_fusion.11), channel_id=1, source_target_pairs={{0,24},{8,16},{16,8},{24,0},{1,25},{9,17},{17,9},{25,1},{2,26},{10... | collective-permute-start | bytes 1179656 | tf_op jit(solution)/shard_map/ppermute | solution.py:54
  319.4 20.0 %copy-start.54 = (s32[2,8]{1,0:T(2,128)S(1)}, s32[2,8]{1,0:T(2,128)}, u32[]{:S(2)}) copy-start(s32[2,8]{1,0:T(2,128)} %constant.247.clone) | copy-start | bytes 196
  319.4 23.8 %copy-start.51 = (f32[20,128]{1,0:T(8,128)S(1)}, f32[20,128]{1,0:T(8,128)}, u32[]{:S(2)}) copy-start(f32[20,128]{1,0:T(8,128)} %get-tuple-element.189) | copy-start | bytes 30724
  338.9 5.7 %collective-permute-start.10 = (bf16[2,512,768]{2,1,0:T(8,128)(2,1)}, bf16[2,512,768]{2,1,0:T(8,128)(2,1)S(1)}, u32[]{:S(2)}, u32[]{:S(2)}) collective-permute-start(bf16[2,512,768]{2,1,0:T(8,128)(2,1)} %get-tuple-element.176), channel_id=1, source_target_pairs={{0,8},{8,0},{16,24},{24,16},{1,9},{9,1},{17,25},{25,17},{2,10},{10... | collective-permute-start | bytes 4718600 | tf_op jit(solution)/shard_map/ppermute | solution.py:58
  360.4 173.7 %copy-start.49 = (bf16[512,768]{1,0:T(8,128)(2,1)S(1)}, bf16[512,768]{1,0:T(8,128)(2,1)}, u32[]{:S(2)}) copy-start(bf16[512,768]{1,0:T(8,128)(2,1)} %get-tuple-element.178) | copy-start | bytes 2359300
  524.0 10.2 %copy-start.24 = (f32[43]{0:T(128)S(1)}, f32[43]{0:T(128)}, u32[]{:S(2)}) copy-start(f32[43]{0:T(128)} %w_ref.3) | copy-start | bytes 520
  524.0 10.2 %copy-start.52 = (f32[43]{0:T(128)S(1)}, f32[43]{0:T(128)}, u32[]{:S(2)}) copy-start(f32[43]{0:T(128)} %param.31) | copy-start | bytes 520
  524.0 10.2 %copy-start.53 = (f32[43]{0:T(128)S(1)}, f32[43]{0:T(128)}, u32[]{:S(2)}) copy-start(f32[43]{0:T(128)} %param.30) | copy-start | bytes 520
  524.1 11.7 %copy-start.6 = (bf16[512,768]{1,0:T(8,128)(2,1)S(1)}, bf16[512,768]{1,0:T(8,128)(2,1)}, u32[]{:S(2)}) copy-start(bf16[512,768]{1,0:T(8,128)(2,1)} %cot_ref.3) | copy-start | bytes 2359300
  524.1 11.7 %copy-start.11 = (bf16[512,768]{1,0:T(8,128)(2,1)S(1)}, bf16[512,768]{1,0:T(8,128)(2,1)}, u32[]{:S(2)}) copy-start(bf16[512,768]{1,0:T(8,128)(2,1)} %pad_maximum_fusion.5.dy_ref) | copy-start | bytes 2359300
  529.1 14.9 %collective-permute-start.12 = (f32[3,768]{1,0:T(4,128)S(1)}, f32[3,768]{1,0:T(4,128)S(1)}, u32[]{:S(2)}, u32[]{:S(2)}) collective-permute-start(f32[3,768]{1,0:T(4,128)S(1)} %convert_bitcast_fusion.1), channel_id=1, source_target_pairs={{0,1},{1,2},{2,3},{3,4},{4,5},{5,6},{6,7},{8,9},{9,10},{10,11},{11... | collective-permute-start | bytes 27656 | tf_op jit(solution)/shard_map/ppermute | solution.py:1295
  531.5 12.6 %collective-permute-start.13 = (f32[3,768]{1,0:T(4,128)S(1)}, f32[3,768]{1,0:T(4,128)S(1)}, u32[]{:S(2)}, u32[]{:S(2)}) collective-permute-start(f32[3,768]{1,0:T(4,128)S(1)} %convert_bitcast_fusion), channel_id=1, source_target_pairs={{1,0},{2,1},{3,2},{4,3},{5,4},{6,5},{7,6},{9,8},{10,9},{11,10},{12... | collective-permute-start | bytes 27656 | tf_op jit(solution)/shard_map/ppermute | solution.py:1296
  534.1 20.3 %collective-permute-start.11 = (bf16[256,768]{1,0:T(8,128)(2,1)S(1)}, bf16[256,768]{1,0:T(8,128)(2,1)S(1)}, u32[]{:S(2)}, u32[]{:S(2)}) collective-permute-start(bf16[256,768]{1,0:T(8,128)(2,1)S(1)} %broadcast_select_fusion.7), channel_id=1, source_target_pairs={{0,24},{8,16},{16,8},{24,0},{1,25},{9,17},{17,9},{25,1},{2,26},{10... | collective-permute-start | bytes 1179656 | tf_op jit(solution)/shard_map/ppermute | solution.py:54
  (24 other events, 40.4 us)
